TPU v7x, 32 devices: a whole 2x2x4 slice. The times are simulated.
32 devices in a mesh: expert: 8 (over z, core), tensor: 4 (over y, x).
Axes of the slice: x: 2, y: 2, z: 4, core: 2. Of those that a mesh axis runs over, the one named last changes fastest.
Arguments:
- inputs: bfloat16 [12288, 1024], P(('expert', 'tensor')), may hold values from -6 to 6
- attn_gain: bfloat16 [1024], replicated, may hold values from 0.25 to 1.75
- w_query: bfloat16 [1024, 1024], replicated, may hold values from -0.1875 to 0.1875
- w_key: bfloat16 [1024, 1024], replicated, may hold values from -0.1875 to 0.1875
- w_value: bfloat16 [1024, 1024], replicated, may hold values from -0.1875 to 0.1875
- w_proj: bfloat16 [1024, 1024], replicated, may hold values from -1 to 1
- rel_bias: bfloat16 [32, 16], replicated, may hold values from -4 to 4
- moe_gain: bfloat16 [1024], replicated, may hold values from 0.25 to 1.75
- w_router: bfloat16 [1024, 16], replicated, may hold values from -0.119628906 to 0.119628906
- w_gate: bfloat16 [16, 1024, 2816], P('expert', None, 'tensor'), may hold values from -0.1875 to 0.1875
- w_up: bfloat16 [16, 1024, 2816], P('expert', None, 'tensor'), may hold values from -0.1875 to 0.1875
- w_down: bfloat16 [16, 2816, 1024], P('expert', 'tensor'), may hold values from -2.5 to 2.5
- routes: int32 [12288, 2], P(('expert', 'tensor')), may hold values from 0 to 15, all different within a row
- long_buckets: int32 [2047], replicated, may hold values from 0 to 31
- short_buckets: int32 [255], replicated, may hold values from 0 to 31
- long_lens: int32 [8], P('expert'), may hold values from 769 to 1024, as said below
- short_lens: int32 [32], P(('expert', 'tensor')), may hold values from 64 to 128, as said below
- cotangent: bfloat16 [12288, 1024], P(('expert', 'tensor')), may hold values from -6 to 6
Outputs:
- outputs: bfloat16 [12288, 1024], P(('expert', 'tensor'))
- inputs_grad: float32 [12288, 1024], P(('expert', 'tensor'))
- attn_gain_grad: float32 [1024], replicated
- w_query_grad: float32 [1024, 1024], replicated
- w_key_grad: float32 [1024, 1024], replicated
- w_value_grad: float32 [1024, 1024], replicated
- w_proj_grad: float32 [1024, 1024], replicated
- rel_bias_grad: float32 [32, 16], replicated
- moe_gain_grad: float32 [1024], replicated
- w_router_grad: float32 [1024, 16], replicated
- w_gate_grad: float32 [16, 1024, 2816], P('expert', None, 'tensor')
- w_up_grad: float32 [16, 1024, 2816], P('expert', None, 'tensor')
- w_down_grad: float32 [16, 2816, 1024], P('expert', 'tensor')
Inputs may be any that keep to these rules, and one draw needn't show every extreme that they name: `routes`: the two experts of a token differ. `long_lens`: some long sequence has all 1024 tokens valid. `short_lens`: some short sequence has all 128 tokens valid.
All inputs are finite; a program needn't handle non-finite values.
Results may differ from a plain program's by a relative error of at most 0.019.
Values may be sent and summed in bfloat16 or wider, within the bound.
No kernel may reach another device: no remote copies, remote signals or barrier semaphores. Data moves between devices by JAX's collectives and lax.ppermute only.
A program may use at most 448 MiB of HBM per device.

v0:
```python
from functools import partial
import math

import jax
import jax.numpy as jnp
from jax import lax
from jax.sharding import PartitionSpec as P

precise = lax.Precision.HIGHEST


def rms_scale(rows):
    return rows * lax.rsqrt(jnp.mean(rows * rows, axis=-1, keepdims=True) + 1e-06)


def norm_apply(rows, gain):
    return rms_scale(rows) * gain


def geglu(gate_pre, up_pre):
    return jax.nn.gelu(gate_pre, approximate=True) * up_pre


def gate_values(logit_rows, route_hot):
    return jnp.sum(route_hot * jax.nn.softmax(logit_rows, axis=-1)[:, None, :], axis=-1)


def table_hot(table, count):
    return (table[:, None] == jnp.arange(count, dtype=jnp.int32)[None, :]).astype(jnp.float32)


def offset_bias(rel_table, hot, base, rows, span):
    extent = 2 * span - 1
    per_offset = jnp.transpose(
        jnp.dot(hot, rel_table, precision=precise, preferred_element_type=jnp.float32)
    )
    tiled = jnp.tile(per_offset, (1, rows + 1))
    start = (span - 1 - base) % extent
    window = lax.dynamic_slice_in_dim(tiled, start, rows * (extent - 1), 1)
    return window.reshape(per_offset.shape[0], rows, extent - 1)[:, :, :span]


def offset_grad(grad_bias, hot, base, rows, span):
    extent = 2 * span - 1
    heads = grad_bias.shape[0]
    padded = jnp.pad(grad_bias, ((0, 0), (0, 0), (0, extent - 1 - span))).reshape(
        heads, rows * (extent - 1)
    )
    start = (span - 1 - base) % extent
    whole = lax.dynamic_update_slice_in_dim(
        jnp.zeros((heads, (rows + 1) * extent), jnp.float32), padded, start, 1
    )
    per_offset = jnp.sum(whole.reshape(heads, rows + 1, extent), axis=1)
    return jnp.dot(
        jnp.transpose(hot),
        jnp.transpose(per_offset),
        precision=precise,
        preferred_element_type=jnp.float32,
    )


def scores_of(query, keys, bias, valid, scale):
    product = jnp.einsum("bihd,bjhd->bhij", query, keys, preferred_element_type=jnp.float32) * scale
    scores = product + bias[None]
    return jnp.where(valid[:, None, None, :], scores, -1e30)


def attend_forward(query, keys, values, bias, valid, scale):
    scores = scores_of(query, keys, bias, valid, scale)
    highest = jnp.max(scores, axis=-1, keepdims=True)
    expanded = jnp.exp(scores - highest)
    totals = jnp.sum(expanded, axis=-1, keepdims=True)
    attend = expanded / totals
    mixed = jnp.einsum(
        "bhij,bjhd->bihd", attend.astype(jnp.bfloat16), values, preferred_element_type=jnp.float32
    )
    return (mixed.astype(jnp.bfloat16), highest + jnp.log(totals))


def attend_backward(query, keys, values, bias, valid, scale, logsum, grad_mixed):
    scores = scores_of(query, keys, bias, valid, scale)
    attend = jnp.exp(scores - logsum)
    grad_attend = jnp.einsum(
        "bihd,bjhd->bhij", grad_mixed, values, preferred_element_type=jnp.float32
    )
    inner = jnp.sum(attend * grad_attend, axis=-1, keepdims=True)
    grad_scores = attend * (grad_attend - inner)
    bias_grad = jnp.sum(grad_scores, axis=0)
    scores_low = grad_scores.astype(jnp.bfloat16)
    grad_query = (
        jnp.einsum("bhij,bjhd->bihd", scores_low, keys, preferred_element_type=jnp.float32) * scale
    )
    grad_keys = (
        jnp.einsum("bhij,bihd->bjhd", scores_low, query, preferred_element_type=jnp.float32) * scale
    )
    grad_values = jnp.einsum(
        "bhij,bihd->bjhd",
        attend.astype(jnp.bfloat16),
        grad_mixed,
        preferred_element_type=jnp.float32,
    )
    return (grad_query, grad_keys, grad_values, bias_grad)


def send_slots(slot_rows):
    experts_axis = lax.axis_size("expert")
    tensor_axis = lax.axis_size("tensor")
    blocks = slot_rows.reshape(
        (experts_axis, slot_rows.shape[0] // experts_axis) + slot_rows.shape[1:]
    )
    copies = jnp.broadcast_to(blocks[:, None], (experts_axis, tensor_axis) + blocks.shape[1:])
    copies = copies.reshape((experts_axis * tensor_axis,) + blocks.shape[1:])
    return lax.all_to_all(copies, ("expert", "tensor"), split_axis=0, concat_axis=0, tiled=True)


def return_sums(partial_rows):
    experts_axis = lax.axis_size("expert")
    tensor_axis = lax.axis_size("tensor")
    arrived = lax.all_to_all(
        partial_rows.astype(jnp.bfloat16),
        ("expert", "tensor"),
        split_axis=0,
        concat_axis=0,
        tiled=True,
    ).astype(partial_rows.dtype)
    arrived = jnp.sum(
        arrived.reshape((experts_axis, tensor_axis) + arrived.shape[1:]), axis=1
    ).astype(jnp.bfloat16)
    return arrived.reshape((arrived.shape[0] * arrived.shape[1],) + arrived.shape[2:])


def per_device(
    inputs,
    attn_gain,
    w_query,
    w_key,
    w_value,
    w_proj,
    rel_bias,
    moe_gain,
    w_router,
    w_gate,
    w_up,
    w_down,
    routes,
    long_buckets,
    short_buckets,
    long_lens,
    short_lens,
    cotangent,
):
    tok_count = inputs.shape[0]
    width = inputs.shape[1]
    top_count = routes.shape[1]
    short_count = short_lens.shape[0]
    short_len = (short_buckets.shape[0] + 1) // 2
    long_span = (long_buckets.shape[0] + 1) // 2
    long_local = tok_count - short_count * short_len
    bucket_count = rel_bias.shape[0]
    heads = rel_bias.shape[1]
    head_dim = width // heads
    scale = 1.0 / math.sqrt(head_dim)
    experts = w_router.shape[1]
    capacity = (5 * tok_count * top_count + 4 * experts - 1) // (4 * experts)
    rel_table = rel_bias.astype(jnp.float32)
    inputs_wide = inputs.astype(jnp.float32)
    normed_attn, norm_attn_back = jax.vjp(norm_apply, inputs_wide, attn_gain.astype(jnp.float32))
    normed_low = normed_attn.astype(jnp.bfloat16)
    query = jnp.dot(normed_low, w_query, preferred_element_type=jnp.float32).astype(jnp.bfloat16)
    keys = jnp.dot(normed_low, w_key, preferred_element_type=jnp.float32).astype(jnp.bfloat16)
    values = jnp.dot(normed_low, w_value, preferred_element_type=jnp.float32).astype(jnp.bfloat16)
    long_query = query[:long_local].reshape(1, long_local, heads, head_dim)
    gathered = (
        lax.all_gather(keys[:long_local], "tensor", axis=0, tiled=True),
        lax.all_gather(values[:long_local], "tensor", axis=0, tiled=True),
    )
    long_keys = gathered[0].reshape(1, long_span, heads, head_dim)
    long_values = gathered[1].reshape(1, long_span, heads, head_dim)
    long_base = lax.axis_index("tensor") * long_local
    key_places = jnp.arange(long_span, dtype=jnp.int32)
    long_table_hot = table_hot(long_buckets, bucket_count)
    long_bias = offset_bias(rel_table, long_table_hot, long_base, long_local, long_span)
    long_valid = key_places[None, :] < long_lens[:, None]
    long_mixed, long_logsum = attend_forward(
        long_query, long_keys, long_values, long_bias, long_valid, scale
    )
    short_query = query[long_local:].reshape(short_count, short_len, heads, head_dim)
    short_keys = keys[long_local:].reshape(short_count, short_len, heads, head_dim)
    short_values = values[long_local:].reshape(short_count, short_len, heads, head_dim)
    short_places = jnp.arange(short_len, dtype=jnp.int32)
    short_table_hot = table_hot(short_buckets, bucket_count)
    short_bias = offset_bias(rel_table, short_table_hot, 0, short_len, short_len)
    short_valid = short_places[None, :] < short_lens[:, None]
    short_mixed, short_logsum = attend_forward(
        short_query, short_keys, short_values, short_bias, short_valid, scale
    )
    mixed = jnp.concatenate(
        [
            long_mixed.reshape(long_local, width),
            short_mixed.reshape(short_count * short_len, width),
        ],
        axis=0,
    )
    resid = inputs_wide + jnp.dot(mixed, w_proj, preferred_element_type=jnp.float32)
    normed_moe, norm_moe_back = jax.vjp(norm_apply, resid, moe_gain.astype(jnp.float32))
    moe_low = normed_moe.astype(jnp.bfloat16)
    logits = jnp.dot(moe_low, w_router, preferred_element_type=jnp.float32)
    route_hot = (routes[:, :, None] == jnp.arange(experts, dtype=jnp.int32)).astype(jnp.float32)
    gates, gate_back = jax.vjp(partial(gate_values, route_hot=route_hot), logits)
    pair_routes = routes.reshape(-1)
    pair_total = pair_routes.shape[0]
    route_count = (pair_routes[:, None] == jnp.arange(experts, dtype=jnp.int32)).astype(jnp.float32)
    pair_places = jnp.arange(pair_total, dtype=jnp.int32)
    earlier = (pair_places[None, :] < pair_places[:, None]).astype(jnp.float32)
    before = jnp.dot(earlier, route_count, preferred_element_type=jnp.float32)
    position = jnp.sum(before * route_count, axis=1).astype(jnp.int32)
    kept = position < capacity
    slot_index = pair_routes * capacity + position
    pair_hot = (
        (slot_index[:, None] == jnp.arange(experts * capacity, dtype=jnp.int32)) & kept[:, None]
    ).astype(jnp.bfloat16)
    token_hot = jnp.sum(pair_hot.reshape(tok_count, top_count, experts * capacity), axis=1)
    slots = jnp.einsum("ts,td->sd", token_hot, moe_low, preferred_element_type=jnp.float32).astype(
        jnp.bfloat16
    )
    received = send_slots(slots.reshape(experts, capacity, width))
    gate_pre = jnp.einsum("sjcd,jdf->sjcf", received, w_gate, preferred_element_type=jnp.float32)
    up_pre = jnp.einsum("sjcd,jdf->sjcf", received, w_up, preferred_element_type=jnp.float32)
    hidden, hidden_back = jax.vjp(geglu, gate_pre, up_pre)
    hidden_low = hidden.astype(jnp.bfloat16)
    expert_part = jnp.einsum(
        "sjcf,jfd->sjcd", hidden_low, w_down, preferred_element_type=jnp.float32
    )
    expert_out = return_sums(expert_part)
    pair_values = jnp.dot(
        pair_hot, expert_out.reshape(experts * capacity, width), preferred_element_type=jnp.float32
    ).reshape(tok_count, top_count, width)
    outputs = (resid + jnp.sum(gates[:, :, None] * pair_values, axis=1)).astype(jnp.bfloat16)
    grad_out = cotangent.astype(jnp.float32)
    grad_gates = jnp.sum(grad_out[:, None, :] * pair_values, axis=-1)
    grad_pairs = (
        (gates[:, :, None] * grad_out[:, None, :])
        .astype(jnp.bfloat16)
        .reshape(tok_count * top_count, width)
    )
    grad_expert_out = jnp.einsum(
        "ps,pd->sd", pair_hot, grad_pairs, preferred_element_type=jnp.float32
    ).astype(jnp.bfloat16)
    grad_received = send_slots(grad_expert_out.reshape(experts, capacity, width))
    grad_hidden = jnp.einsum(
        "sjcd,jfd->sjcf", grad_received, w_down, preferred_element_type=jnp.float32
    )
    down_grad = jnp.einsum(
        "sjcf,sjcd->jfd", hidden_low, grad_received, preferred_element_type=jnp.float32
    )
    grad_gate_pre, grad_up_pre = hidden_back(grad_hidden)
    gate_low = grad_gate_pre.astype(jnp.bfloat16)
    up_low = grad_up_pre.astype(jnp.bfloat16)
    gate_grad = jnp.einsum("sjcd,sjcf->jdf", received, gate_low, preferred_element_type=jnp.float32)
    up_grad = jnp.einsum("sjcd,sjcf->jdf", received, up_low, preferred_element_type=jnp.float32)
    slot_part = jnp.einsum("sjcf,jdf->sjcd", gate_low, w_gate, preferred_element_type=jnp.float32)
    slot_part = slot_part + jnp.einsum(
        "sjcf,jdf->sjcd", up_low, w_up, preferred_element_type=jnp.float32
    )
    grad_slots = return_sums(slot_part)
    grad_moe = jnp.dot(
        token_hot, grad_slots.reshape(experts * capacity, width), preferred_element_type=jnp.float32
    )
    grad_logits = gate_back(grad_gates)[0]
    logits_low = grad_logits.astype(jnp.bfloat16)
    router_grad = jnp.einsum("td,te->de", moe_low, logits_low, preferred_element_type=jnp.float32)
    grad_moe = grad_moe + jnp.einsum(
        "te,de->td", logits_low, w_router, preferred_element_type=jnp.float32
    )
    grad_resid_part, moe_gain_grad = norm_moe_back(grad_moe)
    grad_resid = grad_out + grad_resid_part
    grad_branch = grad_resid.astype(jnp.bfloat16)
    proj_grad = jnp.einsum("td,te->de", mixed, grad_branch, preferred_element_type=jnp.float32)
    grad_mixed = jnp.einsum(
        "te,de->td", grad_branch, w_proj, preferred_element_type=jnp.float32
    ).astype(jnp.bfloat16)
    long_grads = attend_backward(
        long_query,
        long_keys,
        long_values,
        long_bias,
        long_valid,
        scale,
        long_logsum,
        grad_mixed[:long_local].reshape(1, long_local, heads, head_dim),
    )
    key_sums = (
        lax.psum_scatter(
            long_grads[1].reshape(long_span, width).astype(jnp.bfloat16),
            "tensor",
            scatter_dimension=0,
            tiled=True,
        ).astype(jnp.float32),
        lax.psum_scatter(
            long_grads[2].reshape(long_span, width).astype(jnp.bfloat16),
            "tensor",
            scatter_dimension=0,
            tiled=True,
        ).astype(jnp.float32),
    )
    short_grads = attend_backward(
        short_query,
        short_keys,
        short_values,
        short_bias,
        short_valid,
        scale,
        short_logsum,
        grad_mixed[long_local:].reshape(short_count, short_len, heads, head_dim),
    )
    rel_grad = offset_grad(
        long_grads[3], long_table_hot, long_base, long_local, long_span
    ) + offset_grad(short_grads[3], short_table_hot, 0, short_len, short_len)
    short_rows = short_count * short_len
    grad_query = jnp.concatenate(
        [long_grads[0].reshape(long_local, width), short_grads[0].reshape(short_rows, width)],
        axis=0,
    ).astype(jnp.bfloat16)
    grad_keys = jnp.concatenate(
        [key_sums[0], short_grads[1].reshape(short_rows, width)], axis=0
    ).astype(jnp.bfloat16)
    grad_values = jnp.concatenate(
        [key_sums[1], short_grads[2].reshape(short_rows, width)], axis=0
    ).astype(jnp.bfloat16)
    query_grad = jnp.einsum("td,te->de", normed_low, grad_query, preferred_element_type=jnp.float32)
    key_grad = jnp.einsum("td,te->de", normed_low, grad_keys, preferred_element_type=jnp.float32)
    value_grad = jnp.einsum(
        "td,te->de", normed_low, grad_values, preferred_element_type=jnp.float32
    )
    grad_normed = jnp.einsum("te,de->td", grad_query, w_query, preferred_element_type=jnp.float32)
    grad_normed = grad_normed + jnp.einsum(
        "te,de->td", grad_keys, w_key, preferred_element_type=jnp.float32
    )
    grad_normed = grad_normed + jnp.einsum(
        "te,de->td", grad_values, w_value, preferred_element_type=jnp.float32
    )
    grad_inputs_part, attn_gain_grad = norm_attn_back(grad_normed)
    inputs_grad = grad_resid + grad_inputs_part
    totals = lax.psum(
        (
            attn_gain_grad,
            query_grad,
            key_grad,
            value_grad,
            proj_grad,
            rel_grad,
            moe_gain_grad,
            router_grad,
        ),
        ("expert", "tensor"),
    )
    return (
        outputs,
        inputs_grad,
        totals[0],
        totals[1],
        totals[2],
        totals[3],
        totals[4],
        totals[5],
        totals[6],
        totals[7],
        gate_grad,
        up_grad,
        down_grad,
    )


def solution(mesh):
    return jax.shard_map(
        per_device,
        mesh=mesh,
        in_specs=(
            P(("expert", "tensor"), None),
            P(),
            P(),
            P(),
            P(),
            P(),
            P(),
            P(),
            P(),
            P("expert", None, "tensor"),
            P("expert", None, "tensor"),
            P("expert", "tensor", None),
            P(("expert", "tensor"), None),
            P(),
            P(),
            P("expert"),
            P(("expert", "tensor")),
            P(("expert", "tensor"), None),
        ),
        out_specs=(
            P(("expert", "tensor"), None),
            P(("expert", "tensor"), None),
            P(),
            P(),
            P(),
            P(),
            P(),
            P(),
            P(),
            P(),
            P("expert", None, "tensor"),
            P("expert", None, "tensor"),
            P("expert", "tensor", None),
        ),
        check_vma=False,
    )
```

profile of v0, /device:TPU:0, one launch (start us, length us, event | category | flops | bytes accessed | tf_op | source)
XLA Modules:
  0.0 1510.4 jit_solution(13102918012106457240)
XLA Ops:
  49.8 11.8 tile.8
  61.5 43.6 %tile.9 = f32[16,526079]{1,0:T(8,128)} reshape(f32[16,257,2047]{2,1,0:T(8,128)} %tile.8) | data formatting | bytes 67338112 | tf_op jit(solution)/shard_map/tile | solution.py:37
  105.2 25.7 %constant_dynamic-slice_fusion = f32[16,523776]{1,0:T(8,128)} fusion(f32[16,526079]{1,0:T(8,128)} %tile.9, s32[]{:T(128)S(6)} %select_n.26), kind=kLoop, calls=%fused_computation.183 | loop fusion | bytes 67043332 | tf_op jit(solution)/shard_map/dynamic_slice | solution.py:39
  138.3 49.4 %reshape.451 = f32[16,256,2046]{2,1,0:T(8,128)} reshape(f32[16,523776]{1,0:T(8,128)} %constant_dynamic-slice_fusion) | data formatting | bytes 67043328 | tf_op jit(solution)/shard_map/reshape | solution.py:40
  197.1 11.3 fusion.135
  282.1 151.7 %all-to-all-done = bf16[32,2,60,1024]{3,1,2,0:T(2,128)(2,1)} async-done(((bf16[32,2,60,1024]{3,1,2,0:T(2,128)(2,1)}), bf16[32,2,60,1024]{3,1,2,0:T(2,128)(2,1)}, u32[]{:S(2)}, u32[]{:S(2)}) %all-to-all-start) | async-done | bytes 7864352 | tf_op jit(solution)/shard_map/all_to_all | solution.py:113
  448.8 13.9 fusion.27
  462.7 15.5 %fusion.29 = f32[2,32,60,704]{3,2,1,0:T(8,128)} fusion(bf16[32,2,60,1024]{3,1,2,0:T(2,128)(2,1)} %all-to-all-done, bf16[2,1024,704]{1,2,0:T(8,128)(2,1)S(1)} %copy-done.92), kind=kOutput, calls=%fused_computation.45 | convolution fusion | flops 5536481280 | bytes 21561344 | tf_op jit(solution)/shard_map/sjcd,jdf->sjcf/dot_general | solution.py:227
  478.2 147.0 %all-to-all-done.2 = bf16[32,2,60,1024]{3,1,2,0:T(2,128)(2,1)} async-done(((bf16[32,2,60,1024]{3,1,2,0:T(2,128)(2,1)}), bf16[32,2,60,1024]{3,1,2,0:T(2,128)(2,1)}, u32[]{:S(2)}, u32[]{:S(2)}) %all-to-all-start.2) | async-done | bytes 7864352 | tf_op jit(solution)/shard_map/all_to_all | solution.py:113
  625.2 28.5 %fusion.10 = (bf16[32,2,60,704]{3,2,0,1:T(8,128)(2,1)}, bf16[32,2,60,704]{3,2,0,1:T(8,128)(2,1)}, bf16[32,2,60,704]{3,2,0,1:T(8,128)(2,1)}) fusion(f32[2,32,60,704]{3,2,1,0:T(8,128)} %fusion.29, f32[2,32,60,704]{3,2,1,0:T(8,128)} %fusion.27, bf16[2,704,1024]{2,1,0:T(8,128)(2,1)S(1)} %copy-done, bf16[32,2,60,1024]{3,1,2,0:T(2,128)(2,1)} %all-to-all-done.2), kind=kOutput, calls=%fused_computation.21 | convolution fusion | flops 5606768640 | bytes 48594944 | tf_op jit(solution)/shard_map/sjcd,jfd->sjcf/dot_general | solution.py:250
  653.7 9.7 convert_bitcast_fusion
  663.4 17.0 %copy.171 = bf16[32,2,60,1024]{3,1,2,0:T(2,128)(2,1)} copy(bf16[32,2,60,1024]{3,2,0,1:T(8,128)(2,1)S(1)} %convert_bitcast_fusion) | data formatting | bytes 15728640 | tf_op jit(solution)/shard_map/convert_element_type | solution.py:120
  686.4 13.0 fusion.46
  699.4 12.1 fusion.16
  711.5 17.1 %copy.178 = bf16[32,2,60,1024]{3,1,2,0:T(2,128)(2,1)} copy(bf16[32,2,60,1024]{3,2,0,1:T(8,128)(2,1)S(1)} %fusion.16) | data formatting | bytes 15728640 | tf_op jit(solution)/shard_map/convert_element_type | solution.py:120
  728.6 134.3 %all-to-all-done.1 = bf16[32,2,60,1024]{3,1,2,0:T(2,128)(2,1)} async-done(((bf16[32,2,60,1024]{3,1,2,0:T(2,128)(2,1)}), bf16[32,2,60,1024]{3,1,2,0:T(2,128)(2,1)}, u32[]{:S(2)}, u32[]{:S(2)}) %all-to-all-start.1) | async-done | bytes 7864352 | tf_op jit(solution)/shard_map/all_to_all | solution.py:119
  870.0 11.1 bitcast_reduce_fusion.1
  888.9 156.2 %all-to-all-done.3 = bf16[32,2,60,1024]{3,1,2,0:T(2,128)(2,1)} async-done(((bf16[32,2,60,1024]{3,1,2,0:T(2,128)(2,1)}), bf16[32,2,60,1024]{3,1,2,0:T(2,128)(2,1)}, u32[]{:S(2)}, u32[]{:S(2)}) %all-to-all-start.3) | async-done | bytes 7864352 | tf_op jit(solution)/shard_map/all_to_all | solution.py:119
  1045.1 10.7 bitcast_reduce_fusion
  1077.8 11.2 multiply_reduce_fusion
  1089.0 12.4 subtract_multiply_fusion
  1132.6 18.8 %reduce-scatter.3.cloned.1.call-done = bf16[256,1024]{0,1:T(8,128)(2,1)} async-done(((bf16[1024,1024]{0,1:T(8,128)(2,1)}), bf16[256,1024]{0,1:T(8,128)(2,1)}) %reduce-scatter.3.cloned.1.call-update) | async-done | bytes 524304 | tf_op jit(solution)/shard_map/reduce_scatter | solution.py:293
  1156.0 12.9 fusion.54
  1168.9 12.7 fusion.51
  1181.6 11.1 fusion.57
  1194.0 19.3 %pad.9 = f32[16,256,2046]{2,1,0:T(8,128)} pad(f32[16,256,1024]{2,1,0:T(8,128)} %copy-done.2, f32[]{:T(128)} %constant.21.clone.1), padding=0_0x0_0x0_1022 | pad | bytes 50298884 | tf_op jit(solution)/shard_map/jit(_pad)/pad | solution.py:46
  1222.8 50.1 %reshape.470 = f32[16,523776]{1,0:T(8,128)} reshape(f32[16,256,2046]{2,1,0:T(8,128)} %pad.9) | data formatting | bytes 67043328 | tf_op jit(solution)/shard_map/reshape | solution.py:46
  1272.9 11.3 broadcast_in_dim.65
  1284.2 90.8 %dynamic_update_slice.6 = f32[16,526079]{1,0:T(8,128)} dynamic-update-slice(f32[16,526079]{1,0:T(8,128)} %broadcast_in_dim.65, f32[16,523776]{1,0:T(8,128)} %reshape.470, s32[]{:T(128)} %constant.25.clone.1, s32[]{:T(128)S(6)} %select_n.26) | dynamic-update-slice | bytes 67043332 | tf_op jit(solution)/shard_map/dynamic_update_slice | solution.py:50
  1375.0 50.3 %reshape.471 = f32[16,257,2047]{2,1,0:T(8,128)} reshape(f32[16,526079]{1,0:T(8,128)} %dynamic_update_slice.6) | data formatting | bytes 67338112 | tf_op jit(solution)/shard_map/reshape | solution.py:53
  1425.3 12.4 reduce_sum.252
  1445.8 39.6 %all-reduce.3 = (f32[1024]{0:T(1024)}, f32[32,16]{0,1:T(8,128)}, f32[1024]{0:T(1024)}) all-reduce(f32[1024]{0:T(1024)S(1)} %get-tuple-element.17, f32[32,16]{0,1:T(8,128)S(1)} %convolution_add_fusion.1, f32[1024]{0:T(1024)S(1)} %copy-done.84), channel_id=1, replica_groups=mesh['expert'=8,'tensor'=4] {'expert','tensor'}, use_global_device_ids=true, to_apply=%region_24.25 | all-reduce | flops 2560 | bytes 20480 | tf_op jit(solution)/shard_map/psum | solution.py:344
  (341 shorter events, 260.8 us)
Async XLA Ops:
  7.2 618.1 %copy-start = (bf16[2,704,1024]{2,1,0:T(8,128)(2,1)S(1)}, bf16[2,704,1024]{2,1,0:T(8,128)(2,1)}, u32[]{:S(2)}) copy-start(bf16[2,704,1024]{2,1,0:T(8,128)(2,1)} %param.29) | copy-start | bytes 8650756
  7.2 186.0 %all-gather.5.cloned.1.call-start = ((), (), s32[]{:S(2)}) async-start(), calls=%async_computation.7 | async-start | bytes 2621440 | tf_op jit(solution)/shard_map/all_gather | solution.py:174
  9.3 15.2 %copy-start.58 = (f32[384]{0:T(512)}, f32[384]{0:T(512)S(1)}, u32[]{:S(2)}) copy-start(f32[384]{0:T(512)S(1)} %fusion.118) | copy-start | bytes 4612
  10.0 14.5 copy-start.48
  14.6 201.6 %all-gather.3.cloned.1.call-start = ((), (), s32[]{:S(2)}) async-start(), calls=%async_computation.6 | async-start | bytes 2621440 | tf_op jit(solution)/shard_map/all_gather | solution.py:175
  28.6 102.3 %copy-start.27 = (bf16[128,1024]{0,1:T(8,128)(2,1)}, bf16[128,1024]{0,1:T(8,128)(2,1)S(1)}, u32[]{:S(2)}) copy-start(bf16[128,1024]{0,1:T(8,128)(2,1)S(1)} %copy.161) | copy-start | bytes 786436
  29.8 101.1 %copy-start.29 = (bf16[128,1024]{0,1:T(8,128)(2,1)}, bf16[128,1024]{0,1:T(8,128)(2,1)S(1)}, u32[]{:S(2)}) copy-start(bf16[128,1024]{0,1:T(8,128)(2,1)S(1)} %copy.162) | copy-start | bytes 786436
  105.2 25.7 %copy-start.22 = (f32[16,128,128]{1,2,0:T(8,128)S(1)}, f32[16,128,128]{1,2,0:T(8,128)}, u32[]{:S(2)}) copy-start(f32[16,128,128]{1,2,0:T(8,128)} %copy.202) | copy-start | bytes 3145732
  132.3 58.6 %copy-start.65 = (f32[16,128]{1,0:T(8,128)}, f32[16,128]{1,0:T(8,128)S(1)}, u32[]{:S(2)}) copy-start(f32[16,128]{1,0:T(8,128)S(1)} %get-tuple-element.32) | copy-start | bytes 24580
  134.8 94.9 %copy-start.67 = (f32[1024]{0:T(1024)}, f32[1024]{0:T(1024)S(1)}, u32[]{:S(2)}) copy-start(f32[1024]{0:T(1024)S(1)} %convert_element_type.208) | copy-start | bytes 12292
  136.3 60.8 %copy-start.17 = (bf16[256,1024]{0,1:T(8,128)(2,1)}, bf16[256,1024]{0,1:T(8,128)(2,1)S(1)}, u32[]{:S(2)}) copy-start(bf16[256,1024]{0,1:T(8,128)(2,1)S(1)} %copy.158) | copy-start | bytes 1572868
  249.8 184.0 %all-to-all-start = ((bf16[32,2,60,1024]{3,1,2,0:T(2,128)(2,1)}), bf16[32,2,60,1024]{3,1,2,0:T(2,128)(2,1)}, u32[]{:S(2)}, u32[]{:S(2)}) async-start(bf16[32,2,60,1024]{3,1,2,0:T(2,128)(2,1)} %bitcast.181), calls=%async_computation | async-start | bytes 15728640 | tf_op jit(solution)/shard_map/all_to_all | solution.py:113
  443.0 182.2 %all-to-all-start.2 = ((bf16[32,2,60,1024]{3,1,2,0:T(2,128)(2,1)}), bf16[32,2,60,1024]{3,1,2,0:T(2,128)(2,1)}, u32[]{:S(2)}, u32[]{:S(2)}) async-start(bf16[32,2,60,1024]{3,1,2,0:T(2,128)(2,1)} %bitcast.182), calls=%async_computation.2 | async-start | bytes 15728640 | tf_op jit(solution)/shard_map/all_to_all | solution.py:113
  448.7 14.0 copy-start.92
  680.5 182.5 %all-to-all-start.1 = ((bf16[32,2,60,1024]{3,1,2,0:T(2,128)(2,1)}), bf16[32,2,60,1024]{3,1,2,0:T(2,128)(2,1)}, u32[]{:S(2)}, u32[]{:S(2)}) async-start(bf16[32,2,60,1024]{3,1,2,0:T(2,128)(2,1)} %copy.171), calls=%async_computation.1 | async-start | bytes 15728640 | tf_op jit(solution)/shard_map/all_to_all | solution.py:119
  728.6 140.1 %copy-start.16 = (bf16[384,1024]{1,0:T(8,128)(2,1)S(1)}, bf16[384,1024]{1,0:T(8,128)(2,1)}, u32[]{:S(2)}) copy-start(bf16[384,1024]{1,0:T(8,128)(2,1)} %param.35) | copy-start | bytes 2359300
  728.6 141.4 %copy-start.62 = (f32[16,256]{1,0:T(8,128)S(1)}, f32[16,256]{1,0:T(8,128)}, u32[]{:S(2)}) copy-start(f32[16,256]{1,0:T(8,128)} %copy-done.61) | copy-start | bytes 49156
  728.6 141.4 %copy-start.71 = (f32[16,256]{1,0:T(8,128)S(1)}, f32[16,256]{1,0:T(8,128)}, u32[]{:S(2)}) copy-start(f32[16,256]{1,0:T(8,128)} %copy-done.70) | copy-start | bytes 49156
  862.9 182.2 %all-to-all-start.3 = ((bf16[32,2,60,1024]{3,1,2,0:T(2,128)(2,1)}), bf16[32,2,60,1024]{3,1,2,0:T(2,128)(2,1)}, u32[]{:S(2)}, u32[]{:S(2)}) async-start(bf16[32,2,60,1024]{3,1,2,0:T(2,128)(2,1)} %copy.178), calls=%async_computation.3 | async-start | bytes 15728640 | tf_op jit(solution)/shard_map/all_to_all | solution.py:119
  868.6 259.5 %reduce-scatter.5.cloned.1.call-start = ((), (), s32[]{:S(2)}) async-start(), calls=%async_computation.9 | async-start | bytes 2621440 | tf_op jit(solution)/shard_map/reduce_scatter | solution.py:299
  1076.2 75.3 %reduce-scatter.3.cloned.1.call-start = ((), (), s32[]{:S(2)}) async-start(), calls=%async_computation.8 | async-start | bytes 2621440 | tf_op jit(solution)/shard_map/reduce_scatter | solution.py:293
  1108.1 380.3 %all-reduce.7.cloned.1.call-start = ((), (), s32[]{:S(2)}) async-start(), calls=%async_computation.10 | async-start | bytes 33685504 | tf_op jit(solution)/shard_map/psum | solution.py:344
  1111.5 40.0 %copy-start.43 = (bf16[16,64,128]{2,1,0:T(8,128)(2,1)}, bf16[16,64,128]{2,1,0:T(8,128)(2,1)S(1)}, u32[]{:S(2)}) copy-start(bf16[16,64,128]{2,1,0:T(8,128)(2,1)S(1)} %fusion.93) | copy-start | bytes 786436
  1112.7 15.4 %copy-start.25 = (bf16[16,64,128]{2,1,0:T(8,128)(2,1)}, bf16[16,64,128]{2,1,0:T(8,128)(2,1)S(1)}, u32[]{:S(2)}) copy-start(bf16[16,64,128]{2,1,0:T(8,128)(2,1)S(1)} %convolution_convert_fusion.5) | copy-start | bytes 786436
  1156.0 25.6 %slice-start.1 = ((s8[6291456]{0:T(1024)(128)(4,1)}), s8[4194304]{0:T(1024)(128)(4,1)S(1)}, s32[]{:S(2)}) async-start(s8[6291456]{0:T(1024)(128)(4,1)} %bitcast.213), calls=%async_computation.12 | async-start | bytes 8388608
  1168.9 12.7 slice-start.2
  1194.0 19.4 %copy-start.23 = (f32[16,128,128]{2,1,0:T(8,128)S(1)}, f32[16,128,128]{2,1,0:T(8,128)}, u32[]{:S(2)}) copy-start(f32[16,128,128]{2,1,0:T(8,128)} %copy.205) | copy-start | bytes 3145732
  1425.3 13.0 copy-start.99
  1425.3 13.3 copy-start.38
  1425.3 13.3 copy-start.46
  1443.3 42.2 %copy-start.81 = (f32[384]{0:T(512)S(1)}, f32[384]{0:T(512)}, u32[]{:S(2)}) copy-start(f32[384]{0:T(512)} %copy-done.80) | copy-start | bytes 4612
  1443.3 42.2 %copy-start.12 = (f32[384,1024]{1,0:T(8,128)S(1)}, f32[384,1024]{1,0:T(8,128)}, u32[]{:S(2)}) copy-start(f32[384,1024]{1,0:T(8,128)} %copy-done.10) | copy-start | bytes 4718596
  (80 other events, 345.1 us)
Sparse Core Ops, SparseCore 0:
  14.7 38.0 all-gather.4
  55.2 35.2 all-gather.2
  1076.3 36.2 reduce-scatter.4
  1116.3 35.1 reduce-scatter.2
  1158.9 284.1 all-reduce.6
where the time goes:
time: 1520 us; the launch traced here: 1510 us
  waiting for transfers between devices  608 us (40%)
  local copies, waits for them, and re-layouts  513 us (34%)
  matrix products  241 us (16%)
  other arithmetic  66.1 us (4%)
  blocking collectives  39.6 us (3%)
  starting transfers between devices  25 us (2%)
  between operations  16.8 us (1%)
    all_to_all x2, waiting for transfers between devices, send_slots(): lax.all_to_all(copies, ('expert', 'tensor'), split_axis=0, concat_axis=0,...  299 us
    all_to_all x2, waiting for transfers between devices, return_sums(): lax.all_to_all(partial_rows.astype(jnp.bfloat16), ('expert', 'tensor'), s...  291 us
    dynamic_update_slice x2, local copies, waits for them, and re-layouts, offset_grad(): lax.dynamic_update_slice_in_dim(jnp.zeros((heads, (rows + 1) * extent), j...  94.4 us
    another operation x4, local copies, waits for them, and re-layouts, offset_bias(): tiled = jnp.tile(per_offset, (1, rows + 1))  60.8 us
    reshape x2, local copies, waits for them, and re-layouts, offset_bias(): return window.reshape(per_offset.shape[0], rows, extent - 1)[:, :, :span]  55.7 us
    reshape x2, local copies, waits for them, and re-layouts, offset_grad(): per_offset = jnp.sum(whole.reshape(heads, rows + 1, extent), axis=1)  53.3 us
    reshape x2, local copies, waits for them, and re-layouts, offset_grad(): jnp.pad(grad_bias, ((0, 0), (0, 0), (0, extent - 1 - span)))  52.6 us
    psum x1, blocking collectives, per_device(): lax.psum((attn_gain_grad, query_grad, key_grad, value_grad, proj_grad, re...  39.6 us
  transfers between devices with their start and end apart: 9, of which 5 were waited for; matrix products, arithmetic and copies ran while one was open for 43% of the time, Pallas kernels for 0%

commit v1 on v0

v1 whole, which is shorter than its diff:
```python
from functools import partial
import math

import jax
import jax.numpy as jnp
from jax import lax
from jax.experimental import pallas as pl
from jax.experimental.pallas import tpu as pltpu
from jax.sharding import PartitionSpec as P

precise = lax.Precision.HIGHEST
bf16 = jnp.bfloat16
f32 = jnp.float32
NT = (((1,), (1,)), ((), ()))
NN = (((1,), (0,)), ((), ()))
TN = (((0,), (0,)), ((), ()))
VMEM_BYTES = 56 * 1024 * 1024


def mm(left, right, dims=NN):
    return lax.dot_general(left, right, dims, preferred_element_type=f32)


def params():
    return pltpu.CompilerParams(
        dimension_semantics=("arbitrary",), vmem_limit_bytes=VMEM_BYTES
    )


def cost(flops, moved):
    return pl.CostEstimate(flops=int(flops), bytes_accessed=int(moved), transcendentals=0)


def rms_scale(rows):
    return rows * lax.rsqrt(jnp.mean(rows * rows, axis=-1, keepdims=True) + 1e-06)


def norm_apply(rows, gain):
    return rms_scale(rows) * gain


def gate_values(logit_rows, route_hot):
    return jnp.sum(route_hot * jax.nn.softmax(logit_rows, axis=-1)[:, None, :], axis=-1)


def table_hot(table, count):
    return (table[:, None] == jnp.arange(count, dtype=jnp.int32)[None, :]).astype(f32)


def swap(rows, axis, mask):
    count = lax.axis_size(axis)
    return lax.ppermute(rows, axis, [(i, i ^ mask) for i in range(count)])


def gather_parts(rows):
    count = lax.axis_size("tensor")
    if count != 4:
        return [rows] + [swap(rows, "tensor", r) for r in range(1, count)]
    half = rows.shape[0] // 2
    by_x = swap(rows, "tensor", 1)
    by_y = swap(rows, "tensor", 2)
    return [rows, by_x, by_y, swap(by_x[:half], "tensor", 2), swap(by_y[half:], "tensor", 1)]


def sum_parts(parts):
    count = lax.axis_size("tensor")
    if count != 4:
        arrived = [swap(parts[r], "tensor", r) for r in range(1, count)]
        return sum([part.astype(f32) for part in arrived], parts[0].astype(f32))
    half = parts[3].shape[0]
    left = swap(parts[3], "tensor", 1)
    right = swap(parts[4], "tensor", 2)
    to_y = jnp.concatenate(
        [(parts[2][:half].astype(f32) + left.astype(f32)).astype(bf16), parts[2][half:]], axis=0
    )
    to_x = jnp.concatenate(
        [parts[1][:half], (parts[1][half:].astype(f32) + right.astype(f32)).astype(bf16)], axis=0
    )
    from_x = swap(to_x, "tensor", 1)
    from_y = swap(to_y, "tensor", 2)
    return parts[0].astype(f32) + from_x.astype(f32) + from_y.astype(f32)


def part_rows(count, rows):
    return [rows, rows, rows, rows // 2, rows // 2] if count == 4 else [rows] * count


def over_experts(rows):
    experts_axis = lax.axis_size("expert")
    blocks = rows.reshape(experts_axis, rows.shape[0] // experts_axis, rows.shape[1])
    return lax.all_to_all(blocks, "expert", 0, 0, tiled=True).reshape(rows.shape)


def piece(rows, index, size):
    return lax.dynamic_slice_in_dim(rows, index * size, size, 0)


def total(rows):
    experts_axis = lax.axis_size("expert")
    tensor_axis = lax.axis_size("tensor")
    size = rows.shape[0]
    if experts_axis != 8 or tensor_axis != 4 or size % 256:
        return lax.psum(rows, ("expert", "tensor"))
    here = lax.axis_index("expert")
    core = here % 2
    depth = here // 2
    place = lax.axis_index("tensor")
    levels = (
        (core, 2, lambda a, r: swap(a, "expert", r)),
        (place, 4, lambda a, r: swap(a, "tensor", r)),
        (depth, 4, lambda a, r: swap(a, "expert", 2 * r)),
    )
    part = rows
    for index, count, move in levels:
        size = size // count
        arrived = [move(piece(part, index ^ r, size).astype(bf16), r) for r in range(1, count)]
        part = piece(part, index, size).astype(f32)
        for other in arrived:
            part = part + other.astype(f32)
    part = part.astype(bf16)
    for index, count, move in levels[::-1]:
        blocks = jnp.stack([part] + [move(part, r) for r in range(1, count)])
        part = jnp.concatenate(
            [lax.dynamic_index_in_dim(blocks, index ^ i, 0, keepdims=False) for i in range(count)],
            axis=0,
        )
    return part.astype(f32)


def project_kernel(long_local, inputs, gain, w_query, w_key, w_value, normed, query, pair, near, held):
    @pl.when(pl.program_id(0) == 0)
    def _():
        rows = inputs[...].astype(f32)
        scale = lax.rsqrt(jnp.mean(rows * rows, axis=-1, keepdims=True) + 1e-06)
        held[...] = (rows * scale * gain[...].astype(f32)).astype(bf16)
        normed[...] = held[...]

    rows = held[...]
    query[...] = mm(rows, w_query[...]).astype(bf16)
    keys = mm(rows, w_key[...]).astype(bf16)
    values = mm(rows, w_value[...]).astype(bf16)
    pair[:long_local] = keys[:long_local]
    pair[long_local:] = values[:long_local]
    short = keys.shape[0] - long_local
    near[:short] = keys[long_local:]
    near[short:] = values[long_local:]


def project(inputs, gain, w_query, w_key, w_value, long_local):
    rows, width = inputs.shape
    short = rows - long_local
    step = 256
    whole = lambda count: pl.BlockSpec((count, width), lambda i: (0, 0))
    cut = lambda count: pl.BlockSpec((count, step), lambda i: (0, i))
    return pl.pallas_call(
        partial(project_kernel, long_local),
        grid=(width // step,),
        in_specs=[whole(rows), whole(1), cut(width), cut(width), cut(width)],
        out_specs=[whole(rows), cut(rows), cut(2 * long_local), cut(2 * short)],
        out_shape=[
            jax.ShapeDtypeStruct((rows, width), bf16),
            jax.ShapeDtypeStruct((rows, width), bf16),
            jax.ShapeDtypeStruct((2 * long_local, width), bf16),
            jax.ShapeDtypeStruct((2 * short, width), bf16),
        ],
        scratch_shapes=[pltpu.VMEM((rows, width), bf16)],
        compiler_params=params(),
        cost_estimate=cost(6 * rows * width * width, 6 * width * width + 10 * rows * width),
        name="project",
    )(inputs, gain.reshape(1, width), w_query, w_key, w_value)


def key_value_views(parts, count, rows):
    views = []
    for r in range(count):
        if count == 4 and r == 3:
            views.append((parts[3], slice(0, rows), parts[4], slice(0, rows)))
        else:
            views.append((parts[r], slice(0, rows), parts[r], slice(rows, 2 * rows)))
    return views


def forward_kernel(count, rows, dim, facts, query, *refs):
    kinds = len(part_rows(count, rows))
    parts = refs[:kinds]
    near, far_bias, near_bias, mixed, far_attend, near_attend, window = refs[kinds:]
    place, far_len, near_len = facts[0], facts[1], facts[2]
    scale = 1.0 / math.sqrt(dim)
    views = key_value_views(parts, count, rows)
    short = near.shape[0] // 2
    reach = far_bias.shape[-1]
    for head in range(2):
        lanes = slice(head * dim, (head + 1) * dim)
        low = (query[:, lanes].astype(f32) * scale).astype(bf16)
        table = jnp.broadcast_to(far_bias[0, head : head + 1, :], (rows, reach))
        window[...] = pltpu.roll(table, reach - (rows - 1), 1, stride=1, stride_axis=0)
        scores = []
        for r in range(count):
            source = place ^ r
            start = pl.multiple_of(source * rows, rows)
            keys = views[r][0][views[r][1], lanes]
            part = mm(low[:rows], keys, NT) + window[:, pl.ds(start, rows)]
            spot = source * rows + lax.broadcasted_iota(jnp.int32, (1, rows), 1)
            scores.append(jnp.where(spot < far_len, part, -1e30))
        highest = scores[0]
        for part in scores[1:]:
            highest = jnp.maximum(highest, part)
        highest = jnp.max(highest, axis=-1, keepdims=True)
        grown = [jnp.exp(part - highest) for part in scores]
        whole = grown[0]
        for part in grown[1:]:
            whole = whole + part
        inverse = 1.0 / jnp.sum(whole, axis=-1, keepdims=True)
        out = jnp.zeros((rows, dim), f32)
        for r in range(count):
            attend = (grown[r] * inverse).astype(bf16)
            far_attend[head, :, r * rows : (r + 1) * rows] = attend
            out = out + mm(attend, views[r][2][views[r][3], lanes])
        mixed[:rows, lanes] = out.astype(bf16)

        table = jnp.broadcast_to(near_bias[0, head : head + 1, :], (short, 2 * short))
        bias = pltpu.roll(table, short + 1, 1, stride=1, stride_axis=0)[:, :short]
        part = mm(low[rows:], near[:short, lanes], NT) + bias
        spot = lax.broadcasted_iota(jnp.int32, (1, short), 1)
        part = jnp.where(spot < near_len, part, -1e30)
        part = jnp.exp(part - jnp.max(part, axis=-1, keepdims=True))
        attend = (part * (1.0 / jnp.sum(part, axis=-1, keepdims=True))).astype(bf16)
        near_attend[head] = attend
        mixed[rows:, lanes] = mm(attend, near[short:, lanes]).astype(bf16)


def attention_specs(count, rows, short, reach, tokens):
    cut = lambda size: pl.BlockSpec((size, 128), lambda i, *_: (0, i))
    parts = [cut(size) for size in part_rows(count, 2 * rows)]
    table = lambda size: pl.BlockSpec((1, 2, size), lambda i, *_: (i, 0, 0))
    weights = lambda size, span: pl.BlockSpec((2, size, span), lambda i, *_: (i, 0, 0))
    return (
        cut(tokens),
        parts,
        cut(2 * short),
        [table(reach), table(2 * short)],
        [weights(rows, count * rows), weights(short, short)],
    )


def attend_forward(facts, query, parts, near, far_bias, near_bias, count, rows, dim):
    tokens, width = query.shape
    heads = width // dim
    short = near.shape[0] // 2
    reach = far_bias.shape[-1]
    cut, part_specs, near_spec, tables, weights = attention_specs(count, rows, short, reach, tokens)
    return pl.pallas_call(
        partial(forward_kernel, count, rows, dim),
        grid_spec=pltpu.PrefetchScalarGridSpec(
            num_scalar_prefetch=1,
            grid=(heads // 2,),
            in_specs=[cut] + part_specs + [near_spec] + tables,
            out_specs=[cut] + weights,
            scratch_shapes=[pltpu.VMEM((rows, reach), f32)],
        ),
        out_shape=[
            jax.ShapeDtypeStruct((tokens, width), bf16),
            jax.ShapeDtypeStruct((heads, rows, count * rows), bf16),
            jax.ShapeDtypeStruct((heads, short, short), bf16),
        ],
        compiler_params=params(),
        cost_estimate=cost(40 * heads * rows * rows * count * dim, 12 * width * rows * count),
        name="attend_forward",
    )(facts, query, *parts, near, far_bias, near_bias)


def backward_kernel(count, rows, dim, facts, query, grad, *refs):
    kinds = len(part_rows(count, rows))
    parts = refs[:kinds]
    near, far_attend, near_attend = refs[kinds : kinds + 3]
    grad_query = refs[kinds + 3]
    grad_parts = refs[kinds + 4 : 2 * kinds + 4]
    grad_near, far_sums, near_sums, window, near_window = refs[2 * kinds + 4 :]
    place = facts[0]
    scale = 1.0 / math.sqrt(dim)
    views = key_value_views(parts, count, rows)
    grad_views = key_value_views(grad_parts, count, rows)
    short = near.shape[0] // 2
    reach = window.shape[1]

    @pl.when(pl.program_id(0) == 0)
    def _():
        window[...] = jnp.zeros_like(window)
        near_window[...] = jnp.zeros_like(near_window)

    def reversal(size):
        up = lax.broadcasted_iota(jnp.int32, (size, size), 0)
        across = lax.broadcasted_iota(jnp.int32, (size, size), 1)
        return (up + across == size - 1).astype(bf16)

    far_turn = reversal(rows)
    near_turn = far_turn if short == rows else reversal(short)
    for head in range(2):
        lanes = slice(head * dim, (head + 1) * dim)
        low = query[:, lanes]
        grad_low = grad[:, lanes]
        turned = jnp.transpose((low.astype(f32) * scale), (1, 0)).astype(bf16)
        grad_turned = jnp.transpose(grad_low.astype(f32), (1, 0)).astype(bf16)
        attends, grads = [], []
        inner = jnp.zeros((rows, 1), f32)
        for r in range(count):
            attend = far_attend[head, :, r * rows : (r + 1) * rows]
            part = mm(grad_low[:rows], views[r][2][views[r][3], lanes], NT)
            inner = inner + jnp.sum(attend.astype(f32) * part, axis=-1, keepdims=True)
            attends.append(attend)
            grads.append(part)
        out = jnp.zeros((rows, dim), f32)
        for r in range(count):
            start = pl.multiple_of((place ^ r) * rows, rows)
            scores = (attends[r].astype(f32) * (grads[r] - inner)).astype(bf16)
            window[:, pl.ds(start, rows)] = mm(far_turn, scores)
            out = out + mm(scores, views[r][0][views[r][1], lanes])
            grad_keys = mm(turned[:, :rows], scores)
            grad_values = mm(grad_turned[:, :rows], attends[r])
            view = grad_views[r]
            view[0][view[1], lanes] = jnp.transpose(grad_keys, (1, 0)).astype(bf16)
            view[2][view[3], lanes] = jnp.transpose(grad_values, (1, 0)).astype(bf16)
        grad_query[:rows, lanes] = (out * scale).astype(bf16)
        rolled = pltpu.roll(window[...], 0, 1, stride=1, stride_axis=0)
        far_sums[0, head : head + 1, :] = jnp.sum(rolled, axis=0, keepdims=True)

        attend = near_attend[head]
        part = mm(grad_low[rows:], near[short:, lanes], NT)
        wide = attend.astype(f32)
        part = wide * (part - jnp.sum(wide * part, axis=-1, keepdims=True))
        scores = part.astype(bf16)
        near_window[:, :short] = mm(near_turn, scores)
        rolled = pltpu.roll(near_window[...], 0, 1, stride=1, stride_axis=0)
        near_sums[0, head : head + 1, :] = jnp.sum(rolled, axis=0, keepdims=True)
        grad_query[rows:, lanes] = (mm(scores, near[:short, lanes]) * scale).astype(bf16)
        grad_keys = mm(turned[:, rows:], scores)
        grad_values = mm(grad_turned[:, rows:], attend)
        grad_near[:short, lanes] = jnp.transpose(grad_keys, (1, 0)).astype(bf16)
        grad_near[short:, lanes] = jnp.transpose(grad_values, (1, 0)).astype(bf16)


def attend_backward(facts, query, grad, parts, near, weights, reach, count, rows, dim):
    tokens, width = query.shape
    heads = width // dim
    short = near.shape[0] // 2
    cut, part_specs, near_spec, tables, weight_specs = attention_specs(count, rows, short, reach, tokens)
    sizes = part_rows(count, 2 * rows)
    outs = pl.pallas_call(
        partial(backward_kernel, count, rows, dim),
        grid_spec=pltpu.PrefetchScalarGridSpec(
            num_scalar_prefetch=1,
            grid=(heads // 2,),
            in_specs=[cut, cut] + part_specs + [near_spec] + weight_specs,
            out_specs=[cut] + part_specs + [near_spec] + tables,
            scratch_shapes=[pltpu.VMEM((rows, reach), f32), pltpu.VMEM((short, 2 * short), f32)],
        ),
        out_shape=[jax.ShapeDtypeStruct((tokens, width), bf16)]
        + [jax.ShapeDtypeStruct((size, width), bf16) for size in sizes]
        + [jax.ShapeDtypeStruct((2 * short, width), bf16)]
        + [
            jax.ShapeDtypeStruct((heads // 2, 2, reach), f32),
            jax.ShapeDtypeStruct((heads // 2, 2, 2 * short), f32),
        ],
        compiler_params=params(),
        cost_estimate=cost(100 * heads * rows * rows * count * dim, 16 * width * rows * count),
        name="attend_backward",
    )(facts, query, grad, *parts, near, *weights)
    kinds = len(sizes)
    return outs[0], outs[1 : kinds + 1], outs[kinds + 1], outs[kinds + 2], outs[kinds + 3]


def part_copies(count, parts, index, buffer, sem, out=False):
    if count == 4 and index == 3:
        half = parts[3].shape[0]
        pairs = [(parts[3], buffer.at[pl.ds(0, half)]), (parts[4], buffer.at[pl.ds(half, half)])]
    else:
        pairs = [(parts[index], buffer)]
    return [
        pltpu.make_async_copy(b, a, sem) if out else pltpu.make_async_copy(a, b, sem)
        for a, b in pairs
    ]


def expert_kernel(count, capacity, padded, facts, *refs):
    kinds = len(part_rows(count, 2))
    slots, grads = refs[:kinds], refs[kinds : 2 * kinds]
    w_gate, w_up, w_down = refs[2 * kinds : 2 * kinds + 3]
    rest = refs[2 * kinds + 3 :]
    hidden_out, gate_out, up_out = rest[:3]
    outs, grad_outs = rest[3 : 3 + kinds], rest[3 + kinds : 3 + 2 * kinds]
    slot_rows, grad_rows, out_rows, grad_out_rows, in_sem, out_sem = rest[3 + 2 * kinds :]
    step = pl.program_id(0)
    slot = step % 2
    rows, width = slot_rows.shape[1:]
    groups = rows // padded
    place = facts[0]

    def fetch(index, side):
        for r in range(count):

            @pl.when(index == r)
            def _():
                for source, buffer, lane in ((slots, slot_rows, 0), (grads, grad_rows, 1)):
                    for copy in part_copies(count, source, r, buffer.at[side], in_sem.at[side, lane]):
                        copy.start()

    @pl.when(step == 0)
    def _():
        fetch(step, slot)

    @pl.when(step + 1 < count)
    def _():
        fetch(step + 1, 1 - slot)

    for buffer, source, lane in ((slot_rows, slots, 0), (grad_rows, grads, 1)):
        pltpu.make_async_copy(source[0], buffer.at[slot], in_sem.at[slot, lane]).wait()

    def wait_out(side):
        for buffer, target, lane in ((out_rows, outs, 0), (grad_out_rows, grad_outs, 1)):
            pltpu.make_async_copy(buffer.at[side], target[0], out_sem.at[side, lane]).wait()

    @pl.when(step >= 2)
    def _():
        wait_out(slot)

    rows_in = slot_rows[slot]
    grads_in = grad_rows[slot]
    lanes = lax.broadcasted_iota(jnp.int32, (padded, 128), 1)
    match = lax.broadcasted_iota(jnp.int32, (padded, 128), 0) == lanes
    columns = []
    for g in range(groups):
        tail = slot_rows[slot, pl.ds((g + 1) * padded - 16, 16), :128].astype(f32)
        spare = 16 - (padded - capacity)
        line = tail[spare : spare + 1] + tail[spare + 1 : spare + 2]
        columns.append(jnp.sum(jnp.where(match, line, 0.0), axis=-1, keepdims=True))
    gate_column = jnp.concatenate(columns, axis=0)

    gate_pre = mm(rows_in, w_gate[0], NT)
    up_pre = mm(rows_in, w_up[0], NT)
    grad_hidden = mm(grads_in, w_down[0], NT) * gate_column
    slope = math.sqrt(2.0 / math.pi)
    square = gate_pre * gate_pre
    curve = jnp.tanh(slope * gate_pre * (1.0 + 0.044715 * square))
    side = 0.5 * (1.0 + curve)
    bent = gate_pre * side
    hidden = bent * up_pre
    bent_slope = side + 0.5 * slope * gate_pre * (1.0 - curve * curve) * (
        1.0 + 3.0 * 0.044715 * square
    )
    gate_low = (grad_hidden * up_pre * bent_slope).astype(bf16)
    up_low = (grad_hidden * bent).astype(bf16)
    hidden_out[...] = (hidden * gate_column).astype(bf16)
    gate_out[...] = gate_low
    up_out[...] = up_low
    out = mm(hidden.astype(bf16), w_down[0])
    out_rows[slot] = out.astype(bf16)
    grad_gate = jnp.sum(out * grads_in.astype(f32), axis=-1, keepdims=True)
    grad_out = mm(gate_low, w_gate[0]) + mm(up_low, w_up[0])
    grad_out_rows[slot] = grad_out.astype(bf16)

    span = count * padded
    lanes = lax.broadcasted_iota(jnp.int32, (padded, span), 1)
    match = lax.broadcasted_iota(jnp.int32, (padded, span), 0) + place * padded == lanes
    row = lax.broadcasted_iota(jnp.int32, (16, span), 0)
    spare = 16 - (padded - capacity)
    for g in range(groups):
        values = jnp.where(match, grad_gate[g * padded : (g + 1) * padded], 0.0)
        line = jnp.sum(values, axis=0, keepdims=True)
        high = line.astype(bf16).astype(f32)
        tail = grad_out[(g + 1) * padded - 16 : (g + 1) * padded, :span]
        tail = jnp.where(row == spare, high, jnp.where(row == spare + 1, line - high, tail))
        grad_out_rows[slot, pl.ds((g + 1) * padded - 16, 16), :span] = tail.astype(bf16)

    for r in range(count):

        @pl.when(step == r)
        def _():
            for target, buffer, lane in ((outs, out_rows, 0), (grad_outs, grad_out_rows, 1)):
                for copy in part_copies(count, target, r, buffer.at[slot], out_sem.at[slot, lane], True):
                    copy.start()

    @pl.when(step == count - 1)
    def _():
        wait_out(slot)
        if count > 1:
            wait_out(1 - slot)


def expert_pass(facts, slots, grads, w_gate, w_up, w_down, which, capacity, padded):
    count = lax.axis_size("tensor")
    rows, width = slots[0].shape
    units = w_gate.shape[1]
    sizes = part_rows(count, rows)
    kinds = len(sizes)
    anywhere = pl.BlockSpec(memory_space=pl.ANY)
    weight = pl.BlockSpec((1, units, width), lambda i, *_: (which, 0, 0))
    middle = pl.BlockSpec((rows, units), lambda i, *_: (i, 0))
    outs = pl.pallas_call(
        partial(expert_kernel, count, capacity, padded),
        grid_spec=pltpu.PrefetchScalarGridSpec(
            num_scalar_prefetch=1,
            grid=(count,),
            in_specs=[anywhere] * (2 * kinds) + [weight] * 3,
            out_specs=[middle] * 3 + [anywhere] * (2 * kinds),
            scratch_shapes=[pltpu.VMEM((2, rows, width), bf16)] * 4
            + [pltpu.SemaphoreType.DMA((2, 2))] * 2,
        ),
        out_shape=[jax.ShapeDtypeStruct((count * rows, units), bf16)] * 3
        + [jax.ShapeDtypeStruct((size, width), bf16) for size in sizes] * 2,
        compiler_params=params(),
        cost_estimate=cost(12 * count * rows * units * width, 8 * count * rows * width),
        name="expert_pass",
    )(facts, *slots, *grads, w_gate, w_up, w_down)
    return outs[:3], outs[3 : 3 + kinds], outs[3 + kinds :]


def weight_kernel(count, *refs):
    kinds = len(part_rows(count, 2))
    slots, grads = refs[:kinds], refs[kinds : 2 * kinds]
    hidden, gate_low, up_low = refs[2 * kinds : 2 * kinds + 3]
    gate_out, up_out, down_out, slot_rows, grad_rows, in_sem = refs[-6:]
    step = pl.program_id(0)
    slot = step % 2

    def fetch(index, side):
        for r in range(count):

            @pl.when(index == r)
            def _():
                for source, buffer, lane in ((slots, slot_rows, 0), (grads, grad_rows, 1)):
                    for copy in part_copies(count, source, r, buffer.at[side], in_sem.at[side, lane]):
                        copy.start()

    @pl.when(step == 0)
    def _():
        fetch(step, slot)

    @pl.when(step + 1 < count)
    def _():
        fetch(step + 1, 1 - slot)

    for buffer, source, lane in ((slot_rows, slots, 0), (grad_rows, grads, 1)):
        pltpu.make_async_copy(source[0], buffer.at[slot], in_sem.at[slot, lane]).wait()

    @pl.when(step == 0)
    def _():
        for out in (gate_out, up_out, down_out):
            out[...] = jnp.zeros_like(out)

    rows_in = slot_rows[slot]
    gate_out[0] += mm(gate_low[...], rows_in, TN)
    up_out[0] += mm(up_low[...], rows_in, TN)
    down_out[0] += mm(hidden[...], grad_rows[slot], TN)


def weight_pass(slots, grads, middles, before, which, local):
    count = lax.axis_size("tensor")
    rows, width = slots[0].shape
    units = middles[0].shape[1]
    kinds = len(slots)
    anywhere = pl.BlockSpec(memory_space=pl.ANY)
    middle = pl.BlockSpec((rows, units), lambda i: (i, 0))
    outs = pl.BlockSpec((1, units, width), lambda i: (which, 0, 0))
    aliases = {2 * kinds + 3 + i: i for i in range(len(before))}
    return pl.pallas_call(
        partial(weight_kernel, count),
        grid=(count,),
        in_specs=[anywhere] * (2 * kinds) + [middle] * 3 + [anywhere] * len(before),
        out_specs=[outs] * 3,
        out_shape=[jax.ShapeDtypeStruct((local, units, width), f32)] * 3,
        scratch_shapes=[pltpu.VMEM((2, rows, width), bf16)] * 2 + [pltpu.SemaphoreType.DMA((2, 2))],
        input_output_aliases=aliases,
        compiler_params=params(),
        cost_estimate=cost(6 * count * rows * units * width, 8 * count * rows * width),
        name="weight_pass",
    )(*slots, *grads, *middles, *before)


def per_device(
    inputs,
    attn_gain,
    w_query,
    w_key,
    w_value,
    w_proj,
    rel_bias,
    moe_gain,
    w_router,
    w_gate,
    w_up,
    w_down,
    routes,
    long_buckets,
    short_buckets,
    long_lens,
    short_lens,
    cotangent,
):
    experts_axis = lax.axis_size("expert")
    tensor_axis = lax.axis_size("tensor")
    place = lax.axis_index("tensor")
    tok_count, width = inputs.shape
    top_count = routes.shape[1]
    short_len = (short_buckets.shape[0] + 1) // 2
    long_span = (long_buckets.shape[0] + 1) // 2
    long_local = tok_count - short_len
    bucket_count, heads = rel_bias.shape
    head_dim = width // heads
    experts = w_router.shape[1]
    local = experts // experts_axis
    capacity = (5 * tok_count * top_count + 4 * experts - 1) // (4 * experts)
    padded = (capacity + 2 + 15) // 16 * 16
    block = experts_axis * padded
    rel_table = rel_bias.astype(f32)
    facts = jnp.stack([place.astype(jnp.int32), long_lens[0], short_lens[0]])

    pair_routes = routes.reshape(-1)
    pair_total = pair_routes.shape[0]
    route_count = (pair_routes[:, None] == jnp.arange(experts, dtype=jnp.int32)).astype(bf16)
    pair_places = jnp.arange(pair_total, dtype=jnp.int32)
    earlier = (pair_places[None, :] < pair_places[:, None]).astype(bf16)
    before = jnp.dot(earlier, route_count, preferred_element_type=f32)
    position = jnp.sum(before * route_count.astype(f32), axis=1).astype(jnp.int32)
    slot_index = (pair_routes % local) * block + (pair_routes // local) * padded + position
    slot_index = jnp.where(position < capacity, slot_index, -1).reshape(tok_count, top_count)
    slot_places = jnp.arange(local * block, dtype=jnp.int32)
    pair_hot = (slot_index[:, :, None] == slot_places).astype(bf16)
    token_hot = jnp.sum(pair_hot, axis=1)

    grad_slots_in = mm(token_hot, cotangent, TN).astype(bf16)
    grad_parts = [
        gather_parts(over_experts(grad_slots_in[j * block : (j + 1) * block])) for j in range(local)
    ]

    normed_low, query, pair, near = project(inputs, attn_gain, w_query, w_key, w_value, long_local)
    parts = gather_parts(pair)
    reach = long_span + long_local
    first = long_span - long_local - long_local * place
    long_table = jnp.pad(long_buckets, (0, 1), constant_values=-1)
    long_hot = table_hot(lax.dynamic_slice_in_dim(long_table, first, reach, 0), bucket_count)
    short_hot = table_hot(jnp.pad(short_buckets, (0, 1), constant_values=-1), bucket_count)
    spread = lambda hot: jnp.einsum(
        "cb,bh->hc", hot, rel_table, precision=precise, preferred_element_type=f32
    ).reshape(heads // 2, 2, hot.shape[0])
    mixed, far_attend, near_attend = attend_forward(
        facts, query, parts, near, spread(long_hot), spread(short_hot), tensor_axis, long_local, head_dim
    )
    inputs_wide = inputs.astype(f32)
    resid = inputs_wide + mm(mixed, w_proj)
    normed_moe, norm_moe_back = jax.vjp(norm_apply, resid, moe_gain.astype(f32))
    moe_low = normed_moe.astype(bf16)
    logits = mm(moe_low, w_router)
    route_hot = (routes[:, :, None] == jnp.arange(experts, dtype=jnp.int32)).astype(f32)
    gates, gate_back = jax.vjp(partial(gate_values, route_hot=route_hot), logits)

    slot_gates = jnp.sum(pair_hot.astype(f32) * gates[:, :, None], axis=(0, 1))
    slot_gates = slot_gates.reshape(local * experts_axis, padded)
    gates_high = slot_gates.astype(bf16)
    gates_rest = (slot_gates - gates_high.astype(f32)).astype(bf16)
    spare_rows = jnp.pad(
        jnp.concatenate([gates_high, gates_rest], axis=0), ((0, 0), (0, width - padded))
    )
    group = jnp.arange(local * experts_axis, dtype=jnp.int32)[:, None] * padded + capacity
    spare_hot = jnp.concatenate([group == slot_places, group + 1 == slot_places], axis=0).astype(bf16)
    slots_in = (mm(token_hot, moe_low, TN) + mm(spare_hot, spare_rows, TN)).astype(bf16)
    slot_parts = [
        gather_parts(over_experts(slots_in[j * block : (j + 1) * block])) for j in range(local)
    ]
    gate_turned = jnp.swapaxes(w_gate, 1, 2)
    up_turned = jnp.swapaxes(w_up, 1, 2)
    passes = [
        expert_pass(
            facts, slot_parts[j], grad_parts[j], gate_turned, up_turned, w_down, j, capacity, padded
        )
        for j in range(local)
    ]
    grad_slots = [over_experts(sum_parts(passes[j][2]).astype(bf16)) for j in range(local)]
    weight_grads = ()
    for j in range(local):
        weight_grads = weight_pass(slot_parts[j], grad_parts[j], passes[j][0], weight_grads, j, local)

    grad_out = cotangent.astype(f32)
    slot_grads = []
    for rows in grad_slots:
        lines = rows.reshape(experts_axis, padded, width)[:, capacity : capacity + 2]
        lines = lines[:, :, : tensor_axis * padded].astype(f32)
        lines = lines.reshape(experts_axis, 2, tensor_axis, padded)
        slot_grads.append(jnp.sum(lines, axis=(1, 2)).reshape(block))
    slot_grads = jnp.concatenate(slot_grads)
    grad_gates = jnp.sum(
        jnp.where(slot_index[:, :, None] == slot_places, slot_grads, 0.0), axis=-1
    )
    grad_moe = sum(
        mm(token_hot[:, j * block : (j + 1) * block], grad_slots[j]) for j in range(local)
    )
    logits_low = gate_back(grad_gates)[0].astype(bf16)
    router_grad = mm(logits_low, moe_low, TN)
    grad_moe = grad_moe + mm(logits_low, w_router, NT)
    grad_resid_part, moe_gain_grad = norm_moe_back(grad_moe)
    grad_resid = grad_out + grad_resid_part
    grad_branch = grad_resid.astype(bf16)
    proj_grad = total(mm(mixed, grad_branch, TN))
    grad_mixed = mm(grad_branch, w_proj, NT).astype(bf16)

    grad_query, grad_pairs, grad_near, far_sums, near_sums = attend_backward(
        facts, query, grad_mixed, parts, near, (far_attend, near_attend), reach, tensor_axis, long_local, head_dim
    )
    pair_sums = sum_parts(grad_pairs).astype(bf16)
    query_grad = total(mm(normed_low, grad_query, TN))
    grad_keys = jnp.concatenate([pair_sums[:long_local], grad_near[:short_len]], axis=0)
    grad_values = jnp.concatenate([pair_sums[long_local:], grad_near[short_len:]], axis=0)
    collect = lambda sums, hot: jnp.einsum(
        "hc,cb->bh",
        sums.reshape(heads, hot.shape[0]),
        hot,
        precision=precise,
        preferred_element_type=f32,
    )
    rel_grad = collect(far_sums, long_hot) + collect(near_sums, short_hot)
    key_grad = total(mm(normed_low, grad_keys, TN))
    value_grad = mm(normed_low, grad_values, TN)
    grad_normed = mm(grad_query, w_query, NT) + mm(grad_keys, w_key, NT) + mm(grad_values, w_value, NT)
    norm_attn_back = jax.vjp(norm_apply, inputs_wide, attn_gain.astype(f32))[1]
    grad_inputs_part, attn_gain_grad = norm_attn_back(grad_normed)
    inputs_grad = grad_resid + grad_inputs_part
    rel_row = jnp.pad(rel_grad.reshape(1, -1), ((0, 0), (0, width - rel_grad.size)))
    small = jnp.concatenate([attn_gain_grad[None], moe_gain_grad[None], rel_row, router_grad], axis=0)
    small_rows = small.shape[0]
    small = jnp.pad(small, ((0, 256 - small_rows), (0, 0)))
    last = total(jnp.concatenate([value_grad, small], axis=0))

    outs_back = [over_experts(sum_parts(passes[j][1]).astype(bf16)) for j in range(local)]
    pair_values = sum(
        mm(pair_hot[:, :, j * block : (j + 1) * block].reshape(pair_total, block), outs_back[j])
        for j in range(local)
    ).reshape(tok_count, top_count, width)
    outputs = (resid + jnp.sum(gates[:, :, None] * pair_values, axis=1)).astype(bf16)
    return (
        outputs,
        inputs_grad,
        last[width],
        query_grad,
        key_grad,
        last[:width],
        proj_grad,
        last[width + 2, : rel_grad.size].reshape(rel_grad.shape),
        last[width + 1],
        jnp.transpose(last[width + 3 : width + small_rows]),
        jnp.swapaxes(weight_grads[0], 1, 2),
        jnp.swapaxes(weight_grads[1], 1, 2),
        weight_grads[2],
    )


def solution(mesh):
    return jax.shard_map(
        per_device,
        mesh=mesh,
        in_specs=(
            P(("expert", "tensor"), None),
            P(),
            P(),
            P(),
            P(),
            P(),
            P(),
            P(),
            P(),
            P("expert", None, "tensor"),
            P("expert", None, "tensor"),
            P("expert", "tensor", None),
            P(("expert", "tensor"), None),
            P(),
            P(),
            P("expert"),
            P(("expert", "tensor")),
            P(("expert", "tensor"), None),
        ),
        out_specs=(
            P(("expert", "tensor"), None),
            P(("expert", "tensor"), None),
            P(),
            P(),
            P(),
            P(),
            P(),
            P(),
            P(),
            P(),
            P("expert", None, "tensor"),
            P("expert", None, "tensor"),
            P("expert", "tensor", None),
        ),
        check_vma=False,
    )
```

time: 1520 us -> 821 us (0.54)
  local copies, waits for them, and re-layouts: 513 us -> 56.3 us
  waiting for transfers between devices: 608 us -> 309 us
  matrix products: 241 us -> 39.3 us
  Pallas kernels: 0 us -> 154 us
  starting transfers between devices: 25 us -> 150 us
    all_to_all x4 -> x7, waiting for transfers between devices: 589 us -> 33.4 us  [over_experts(): lax.all_to_all(blocks, 'expert', 0, 0, tiled=True).reshape(rows.shape)]
    ppermute x0 -> x96, waiting for transfers between devices: none -> 275 us  [swap(): return lax.ppermute(rows, axis, [(i, i ^ mask) for i in range(count)])]
    dot_general x45 -> x24, matrix products: 241 us -> 39.3 us  [the longest x19 37.2 us: mm(): return lax.dot_general(left, right, dims, preferred_element_type=f32)]
    pallas_call x0 -> x7, Pallas kernels: none -> 154 us  [the longest x2 58.2 us: expert_pass(): pl.pallas_call(partial(expert_kernel, count, capacity, padded), grid_spec...]
    reshape x6 -> x12, local copies, waits for them, and re-layouts: 162 us -> 17.3 us  [the longest x2 7.3 us: per_device(): pair_hot[:, :, j * block:(j + 1) * block].reshape(pair_total, block)]
    ppermute x0 -> x96, starting transfers between devices: none -> 106 us  [swap(): return lax.ppermute(rows, axis, [(i, i ^ mask) for i in range(count)])]
    dynamic_update_slice x2 -> x0, local copies, waits for them, and re-layouts: 94.4 us -> none  [offset_grad(): lax.dynamic_update_slice_in_dim(jnp.zeros((heads, (rows + 1) * extent), j...]
    another operation x4 -> x1, local copies, waits for them, and re-layouts: 60.8 us -> 0.08 us  [per_device(): last[width + 2, :rel_grad.size].reshape(rel_grad.shape)]
  transfers between devices with their start and end apart: 9 -> 103, of which waited for: 5 -> 49; matrix products, arithmetic and copies ran while one was open for 43% -> 14% of each run, Pallas kernels for 0% -> 14%
where the time goes in v1:
time: 821 us; the launch traced here: 817 us
  waiting for transfers between devices  309 us (38%)
  Pallas kernels  154 us (19%)
  starting transfers between devices  150 us (18%)
  other arithmetic  73.5 us (9%)
  local copies, waits for them, and re-layouts  56.3 us (7%)
  matrix products  39.3 us (5%)
  blocking collectives  30.8 us (4%)
    ppermute x96, waiting for transfers between devices, swap(): return lax.ppermute(rows, axis, [(i, i ^ mask) for i in range(count)])  275 us
    ppermute x96, starting transfers between devices, swap(): return lax.ppermute(rows, axis, [(i, i ^ mask) for i in range(count)])  106 us
    pallas_call x2, Pallas kernels, expert_pass(): pl.pallas_call(partial(expert_kernel, count, capacity, padded), grid_spec...  58.2 us
    all_to_all x7, starting transfers between devices, over_experts(): lax.all_to_all(blocks, 'expert', 0, 0, tiled=True).reshape(rows.shape)  44.7 us
    dot_general x19, matrix products, mm(): return lax.dot_general(left, right, dims, preferred_element_type=f32)  37.2 us
    pallas_call x1, Pallas kernels, attend_backward(): pl.pallas_call(partial(backward_kernel, count, rows, dim), grid_spec=pltp...  35 us
    all_to_all x7, waiting for transfers between devices, over_experts(): lax.all_to_all(blocks, 'expert', 0, 0, tiled=True).reshape(rows.shape)  33.4 us
    pallas_call x2, Pallas kernels, weight_pass(): pl.pallas_call(partial(weight_kernel, count), grid=(count,), in_specs=[an...  31.8 us
  transfers between devices with their start and end apart: 103, of which 49 were waited for; matrix products, arithmetic and copies ran while one was open for 14% of the time, Pallas kernels for 14%

profile of v1, /device:TPU:0, one launch (start us, length us, event | category | flops | bytes accessed | tf_op | source)
XLA Modules:
  0.0 816.7 jit_solution(8084211733195044579)
XLA Ops:
  2.1 6.9 project.1
  41.7 8.0 collective-permute-done.3.refs_4_
  52.7 22.0 %attend_forward.1 = (bf16[384,1024]{1,0:T(8,128)(2,1)}, bf16[16,256,1024]{2,1,0:T(8,128)(2,1)}, bf16[16,128,128]{2,1,0:T(8,128)(2,1)}) custom-call(s32[3]{0:T(128)} %pad_add_fusion.facts, bf16[384,1024]{1,0:T(8,128)(2,1)} %get-tuple-element.61.query, bf16[512,1024]{1,0:T(8,128)(2,1)} %get-tuple-element.62.refs_0_, ...), custom_call_target="tpu_custom_call" | custom-call | flops 10737418240 | bytes 12582912 | tf_op jit(solution)/shard_map/attend_forward/pallas_call | solution.py:252
  78.7 14.8 %all-to-all-start.1 = ((bf16[8,64,1024]{2,1,0:T(8,128)(2,1)}), bf16[8,64,1024]{2,1,0:T(8,128)(2,1)}, u32[]{:S(2)}, u32[]{:S(2)}) async-start(bf16[8,64,1024]{2,1,0:T(8,128)(2,1)} %bitcast.198), calls=%async_computation.1 | async-start | bytes 2097152 | tf_op jit(solution)/shard_map/all_to_all | solution.py:91
  100.5 19.6 %all-to-all-done.1 = bf16[8,64,1024]{2,1,0:T(8,128)(2,1)} async-done(((bf16[8,64,1024]{2,1,0:T(8,128)(2,1)}), bf16[8,64,1024]{2,1,0:T(8,128)(2,1)}, u32[]{:S(2)}, u32[]{:S(2)}) %all-to-all-start.1) | async-done | bytes 1048608 | tf_op jit(solution)/shard_map/all_to_all | solution.py:91
  120.1 30.8 %all_to_all.40 = bf16[8,64,1024]{2,1,0:T(8,128)(2,1)} all-to-all(bf16[8,64,1024]{2,1,0:T(8,128)(2,1)} %bitcast.204), channel_id=1, replica_groups=mesh['expert'=8,'tensor'=4] {'expert'}, dimensions={0} | all-to-all | bytes 2097152 | tf_op jit(solution)/shard_map/all_to_all | solution.py:91
  160.9 20.7 %collective-permute-done.21.refs_7_ = bf16[512,1024]{1,0:T(8,128)(2,1)} collective-permute-done((bf16[512,1024]{1,0:T(8,128)(2,1)}, bf16[512,1024]{1,0:T(8,128)(2,1)}, u32[]{:S(2)}, u32[]{:S(2)}) %collective-permute-start.21) | collective-permute-done | bytes 1048608 | tf_op jit(solution)/shard_map/ppermute | solution.py:52
  183.8 20.3 %collective-permute-done.17.refs_2_ = bf16[512,1024]{1,0:T(8,128)(2,1)} collective-permute-done((bf16[512,1024]{1,0:T(8,128)(2,1)}, bf16[512,1024]{1,0:T(8,128)(2,1)}, u32[]{:S(2)}, u32[]{:S(2)}) %collective-permute-start.17) | collective-permute-done | bytes 1048608 | tf_op jit(solution)/shard_map/ppermute | solution.py:52
  210.5 16.1 %collective-permute-done.9.refs_7_ = bf16[512,1024]{1,0:T(8,128)(2,1)} collective-permute-done((bf16[512,1024]{1,0:T(8,128)(2,1)}, bf16[512,1024]{1,0:T(8,128)(2,1)}, u32[]{:S(2)}, u32[]{:S(2)}) %collective-permute-start.9) | collective-permute-done | bytes 1048608 | tf_op jit(solution)/shard_map/ppermute | solution.py:52
  228.7 20.2 %collective-permute-done.5.refs_2_ = bf16[512,1024]{1,0:T(8,128)(2,1)S(1)} collective-permute-done((bf16[512,1024]{1,0:T(8,128)(2,1)}, bf16[512,1024]{1,0:T(8,128)(2,1)S(1)}, u32[]{:S(2)}, u32[]{:S(2)}) %collective-permute-start.5) | collective-permute-done | bytes 1048608 | tf_op jit(solution)/shard_map/ppermute | solution.py:52
  254.4 7.3 collective-permute-done.23.refs_9_
  262.8 10.1 %collective-permute-done.19.refs_4_ = bf16[256,1024]{1,0:T(8,128)(2,1)S(1)} collective-permute-done((bf16[256,1024]{1,0:T(8,128)(2,1)S(1)}, bf16[256,1024]{1,0:T(8,128)(2,1)S(1)}, u32[]{:S(2)}, u32[]{:S(2)}) %collective-permute-start.19) | collective-permute-done | bytes 524320 | tf_op jit(solution)/shard_map/ppermute | solution.py:52
  274.3 28.9 %expert_pass.3 = (bf16[2048,704]{1,0:T(8,128)(2,1)}, bf16[2048,704]{1,0:T(8,128)(2,1)}, bf16[2048,704]{1,0:T(8,128)(2,1)}, bf16[512,1024]{1,0:T(8,128)(2,1)}, bf...) custom-call(s32[3]{0:T(128)} %pad_add_fusion.facts, ...), custom_call_target="tpu_custom_call" | custom-call | flops 17716740096 | bytes 16777216 | tf_op jit(solution)/shard_map/expert_pass/pallas_call | solution.py:498
  305.4 29.3 %expert_pass.2 = (bf16[2048,704]{1,0:T(8,128)(2,1)}, bf16[2048,704]{1,0:T(8,128)(2,1)}, bf16[2048,704]{1,0:T(8,128)(2,1)}, bf16[512,1024]{1,0:T(8,128)(2,1)}, bf...) custom-call(s32[3]{0:T(128)} %pad_add_fusion.facts, ...), custom_call_target="tpu_custom_call" | custom-call | flops 17716740096 | bytes 16777216 | tf_op jit(solution)/shard_map/expert_pass/pallas_call | solution.py:498
  352.4 11.3 %collective-permute-done.35 = bf16[512,1024]{1,0:T(8,128)(2,1)S(1)} collective-permute-done((bf16[512,1024]{1,0:T(8,128)(2,1)S(1)}, bf16[512,1024]{1,0:T(8,128)(2,1)S(1)}, u32[]{:S(2)}, u32[]{:S(2)}) %collective-permute-start.35) | collective-permute-done | bytes 1048608 | tf_op jit(solution)/shard_map/ppermute | solution.py:52
  363.6 9.4 %collective-permute-done.33 = bf16[512,1024]{1,0:T(8,128)(2,1)S(1)} collective-permute-done((bf16[512,1024]{1,0:T(8,128)(2,1)S(1)}, bf16[512,1024]{1,0:T(8,128)(2,1)S(1)}, u32[]{:S(2)}, u32[]{:S(2)}) %collective-permute-start.33) | collective-permute-done | bytes 1048608 | tf_op jit(solution)/shard_map/ppermute | solution.py:52
  396.5 11.9 %collective-permute-done.29 = bf16[512,1024]{1,0:T(8,128)(2,1)S(1)} collective-permute-done((bf16[512,1024]{1,0:T(8,128)(2,1)S(1)}, bf16[512,1024]{1,0:T(8,128)(2,1)S(1)}, u32[]{:S(2)}, u32[]{:S(2)}) %collective-permute-start.29) | collective-permute-done | bytes 1048608 | tf_op jit(solution)/shard_map/ppermute | solution.py:52
  436.4 7.8 collective-permute-done.12
  454.5 15.9 %weight_pass.2 = (f32[2,704,1024]{2,1,0:T(8,128)}, f32[2,704,1024]{2,1,0:T(8,128)}, f32[2,704,1024]{2,1,0:T(8,128)}) custom-call(bf16[512,1024]{1,0:T(8,128)(2,1)} %bitcast.4.refs_0_, bf16[512,1024]{1,0:T(8,128)(2,1)} %copy-done.43, bf16[512,1024]{1,0:T(8,128)(2,1)} %copy-done.42, bf16[256,1024]{1,0:T(8,128)(2,1)} %collective-permute-done.6.refs_3_, ...), custom_call_target="tpu_custom_call" | custom-call | flops 8858370048 | bytes 16777216 | tf_op jit(solution)/shard_map/weight_pass/pallas_call | solution.py:565
  470.3 16.0 %weight_pass.3 = (f32[2,704,1024]{2,1,0:T(8,128)}, f32[2,704,1024]{2,1,0:T(8,128)}, f32[2,704,1024]{2,1,0:T(8,128)}) custom-call(bf16[512,1024]{1,0:T(8,128)(2,1)} %bitcast.196, bf16[512,1024]{1,0:T(8,128)(2,1)} %collective-permute-done.16.refs_1_, ...), custom_call_target="tpu_custom_call", output_to_operand_aliasing={{0}: (13, {}), {1}: (14, {}), {2}: (15, {})} | custom-call | flops 8858370048 | bytes 16777216 | tf_op jit(solution)/shard_map/weight_pass/pallas_call | solution.py:565
  492.0 5.3 all-to-all-start.2
  510.2 13.8 %all-to-all-done.2 = bf16[8,64,1024]{2,1,0:T(8,128)(2,1)} async-done(((bf16[8,64,1024]{2,1,0:T(8,128)(2,1)}), bf16[8,64,1024]{2,1,0:T(8,128)(2,1)}, u32[]{:S(2)}, u32[]{:S(2)}) %all-to-all-start.2) | async-done | bytes 1048608 | tf_op jit(solution)/shard_map/all_to_all | solution.py:91
  534.1 6.0 multiply_reduce_fusion
  549.7 35.0 %attend_backward.1 = (bf16[384,1024]{1,0:T(8,128)(2,1)}, bf16[512,1024]{1,0:T(8,128)(2,1)}, bf16[512,1024]{1,0:T(8,128)(2,1)}, bf16[512,1024]{1,0:T(8,128)(2,1)}...) custom-call(s32[3]{0:T(128)} %pad_add_fusion.facts, ...), custom_call_target="tpu_custom_call" | custom-call | flops 26843545600 | bytes 16777216 | tf_op jit(solution)/shard_map/attend_backward/pallas_call | solution.py:348
  596.5 7.1 collective-permute-done.38
  612.0 25.6 %collective-permute-done.83 = bf16[128,1024]{1,0:T(8,128)(2,1)S(1)} collective-permute-done((bf16[128,1024]{1,0:T(8,128)(2,1)S(1)}, bf16[128,1024]{1,0:T(8,128)(2,1)S(1)}, u32[]{:S(2)}, u32[]{:S(2)}) %collective-permute-start.83) | collective-permute-done | bytes 262176 | tf_op jit(solution)/shard_map/ppermute | solution.py:52
  694.8 6.6 collective-permute-done.64
  701.4 5.3 collective-permute-done.66
  711.0 5.6 collective-permute-done.69
  716.5 5.3 collective-permute-done.71
  774.2 5.7 collective-permute-done.80
  785.5 7.3 collective-permute-done.52
  (509 shorter events, 357.1 us)
Async XLA Ops:
  23.4 55.3 %all-to-all-start.4 = ((bf16[8,64,1024]{2,1,0:T(8,128)(2,1)}), bf16[8,64,1024]{2,1,0:T(8,128)(2,1)}, u32[]{:S(2)}, u32[]{:S(2)}) async-start(bf16[8,64,1024]{2,1,0:T(8,128)(2,1)} %bitcast.199), calls=%async_computation.4 | async-start | bytes 2097152 | tf_op jit(solution)/shard_map/all_to_all | solution.py:91
  78.7 41.4 %all-to-all-start.1 = ((bf16[8,64,1024]{2,1,0:T(8,128)(2,1)}), bf16[8,64,1024]{2,1,0:T(8,128)(2,1)}, u32[]{:S(2)}, u32[]{:S(2)}) async-start(bf16[8,64,1024]{2,1,0:T(8,128)(2,1)} %bitcast.198), calls=%async_computation.1 | async-start | bytes 2097152 | tf_op jit(solution)/shard_map/all_to_all | solution.py:91
  157.4 46.6 %collective-permute-start.17 = (bf16[512,1024]{1,0:T(8,128)(2,1)}, bf16[512,1024]{1,0:T(8,128)(2,1)}, u32[]{:S(2)}, u32[]{:S(2)}) collective-permute-start(bf16[512,1024]{1,0:T(8,128)(2,1)} %bitcast.193), channel_id=1, source_target_pairs={{0,2},{1,3},{2,0},{3,1},{4,6},{5,7},{6,4},{7,5},{8,10},{9,11},{10,... | collective-permute-start | bytes 3145736 | tf_op jit(solution)/shard_map/ppermute | solution.py:52
  157.9 50.0 %collective-permute-start.16 = (bf16[512,1024]{1,0:T(8,128)(2,1)}, bf16[512,1024]{1,0:T(8,128)(2,1)}, u32[]{:S(2)}, u32[]{:S(2)}) collective-permute-start(bf16[512,1024]{1,0:T(8,128)(2,1)} %bitcast.194), channel_id=1, source_target_pairs={{0,1},{1,0},{2,3},{3,2},{4,5},{5,4},{6,7},{7,6},{8,9},{9,8},{10,11... | collective-permute-start | bytes 3145736 | tf_op jit(solution)/shard_map/ppermute | solution.py:52
  159.3 67.2 %collective-permute-start.9 = (bf16[512,1024]{1,0:T(8,128)(2,1)}, bf16[512,1024]{1,0:T(8,128)(2,1)}, u32[]{:S(2)}, u32[]{:S(2)}) collective-permute-start(bf16[512,1024]{1,0:T(8,128)(2,1)} %bitcast.6.refs_5_), channel_id=1, source_target_pairs={{0,2},{1,3},{2,0},{3,1},{4,6},{5,7},{6,4},{7,5},{8,10},{9,11},{10,... | collective-permute-start | bytes 3145736 | tf_op jit(solution)/shard_map/ppermute | solution.py:52
  181.6 46.5 %collective-permute-start.8 = (bf16[512,1024]{1,0:T(8,128)(2,1)}, bf16[512,1024]{1,0:T(8,128)(2,1)}, u32[]{:S(2)}, u32[]{:S(2)}) collective-permute-start(bf16[512,1024]{1,0:T(8,128)(2,1)} %bitcast.6.refs_5_), channel_id=1, source_target_pairs={{0,1},{1,0},{2,3},{3,2},{4,5},{5,4},{6,7},{7,6},{8,9},{9,8},{10,11... | collective-permute-start | bytes 3145736 | tf_op jit(solution)/shard_map/ppermute | solution.py:52
  183.2 65.7 %collective-permute-start.5 = (bf16[512,1024]{1,0:T(8,128)(2,1)}, bf16[512,1024]{1,0:T(8,128)(2,1)S(1)}, u32[]{:S(2)}, u32[]{:S(2)}) collective-permute-start(bf16[512,1024]{1,0:T(8,128)(2,1)} %bitcast.4.refs_0_), channel_id=1, source_target_pairs={{0,2},{1,3},{2,0},{3,1},{4,6},{5,7},{6,4},{7,5},{8,10},{9,11},{10,... | collective-permute-start | bytes 3145736 | tf_op jit(solution)/shard_map/ppermute | solution.py:52
  204.1 49.6 %collective-permute-start.4 = (bf16[512,1024]{1,0:T(8,128)(2,1)}, bf16[512,1024]{1,0:T(8,128)(2,1)S(1)}, u32[]{:S(2)}, u32[]{:S(2)}) collective-permute-start(bf16[512,1024]{1,0:T(8,128)(2,1)} %bitcast.4.refs_0_), channel_id=1, source_target_pairs={{0,1},{1,0},{2,3},{3,2},{4,5},{5,4},{6,7},{7,6},{8,9},{9,8},{10,11... | collective-permute-start | bytes 3145736 | tf_op jit(solution)/shard_map/ppermute | solution.py:52
  207.9 53.8 %collective-permute-start.23 = (bf16[256,1024]{1,0:T(8,128)(2,1)S(1)}, bf16[256,1024]{1,0:T(8,128)(2,1)S(1)}, u32[]{:S(2)}, u32[]{:S(2)}) collective-permute-start(bf16[256,1024]{1,0:T(8,128)(2,1)S(1)} %slice.215), channel_id=1, source_target_pairs={{0,1},{1,0},{2,3},{3,2},{4,5},{5,4},{6,7},{7,6},{8,9},{9,8},{10,11... | collective-permute-start | bytes 1572872 | tf_op jit(solution)/shard_map/ppermute | solution.py:52
  226.5 35.7 %collective-permute-start.22 = (bf16[256,1024]{1,0:T(8,128)(2,1)S(1)}, bf16[256,1024]{1,0:T(8,128)(2,1)S(1)}, u32[]{:S(2)}, u32[]{:S(2)}) collective-permute-start(bf16[256,1024]{1,0:T(8,128)(2,1)S(1)} %slice.214), channel_id=1, source_target_pairs={{0,2},{1,3},{2,0},{3,1},{4,6},{5,7},{6,4},{7,5},{8,10},{9,11},{10,... | collective-permute-start | bytes 1572872 | tf_op jit(solution)/shard_map/ppermute | solution.py:52
  228.1 44.8 %collective-permute-start.19 = (bf16[256,1024]{1,0:T(8,128)(2,1)S(1)}, bf16[256,1024]{1,0:T(8,128)(2,1)S(1)}, u32[]{:S(2)}, u32[]{:S(2)}) collective-permute-start(bf16[256,1024]{1,0:T(8,128)(2,1)S(1)} %slice.212), channel_id=1, source_target_pairs={{0,1},{1,0},{2,3},{3,2},{4,5},{5,4},{6,7},{7,6},{8,9},{9,8},{10,11... | collective-permute-start | bytes 1572872 | tf_op jit(solution)/shard_map/ppermute | solution.py:52
  253.7 51.1 %collective-permute-start.11 = (bf16[256,1024]{1,0:T(8,128)(2,1)}, bf16[256,1024]{1,0:T(8,128)(2,1)}, u32[]{:S(2)}, u32[]{:S(2)}) collective-permute-start(bf16[256,1024]{1,0:T(8,128)(2,1)} %slice.208), channel_id=1, source_target_pairs={{0,1},{1,0},{2,3},{3,2},{4,5},{5,4},{6,7},{7,6},{8,9},{9,8},{10,11... | collective-permute-start | bytes 1572872 | tf_op jit(solution)/shard_map/ppermute | solution.py:52
  261.7 43.7 %collective-permute-start.10 = (bf16[256,1024]{1,0:T(8,128)(2,1)S(1)}, bf16[256,1024]{1,0:T(8,128)(2,1)}, u32[]{:S(2)}, u32[]{:S(2)}) collective-permute-start(bf16[256,1024]{1,0:T(8,128)(2,1)S(1)} %slice.207), channel_id=1, source_target_pairs={{0,2},{1,3},{2,0},{3,1},{4,6},{5,7},{6,4},{7,5},{8,10},{9,11},{10,... | collective-permute-start | bytes 1572872 | tf_op jit(solution)/shard_map/ppermute | solution.py:52
  262.2 43.2 %collective-permute-start.7 = (bf16[256,1024]{1,0:T(8,128)(2,1)S(1)}, bf16[256,1024]{1,0:T(8,128)(2,1)}, u32[]{:S(2)}, u32[]{:S(2)}) collective-permute-start(bf16[256,1024]{1,0:T(8,128)(2,1)S(1)} %slice.205), channel_id=1, source_target_pairs={{0,1},{1,0},{2,3},{3,2},{4,5},{5,4},{6,7},{7,6},{8,9},{9,8},{10,11... | collective-permute-start | bytes 1572872 | tf_op jit(solution)/shard_map/ppermute | solution.py:52
  303.2 34.8 %collective-permute-start.32 = (bf16[256,1024]{1,0:T(8,128)(2,1)}, bf16[256,1024]{1,0:T(8,128)(2,1)S(1)}, u32[]{:S(2)}, u32[]{:S(2)}) collective-permute-start(bf16[256,1024]{1,0:T(8,128)(2,1)} %get-tuple-element.82), channel_id=1, source_target_pairs={{0,2},{1,3},{2,0},{3,1},{4,6},{5,7},{6,4},{7,5},{8,10},{9,11},{10,... | collective-permute-start | bytes 1572872 | tf_op jit(solution)/shard_map/ppermute | solution.py:52
  338.3 34.8 %collective-permute-start.33 = (bf16[512,1024]{1,0:T(8,128)(2,1)S(1)}, bf16[512,1024]{1,0:T(8,128)(2,1)S(1)}, u32[]{:S(2)}, u32[]{:S(2)}) collective-permute-start(bf16[512,1024]{1,0:T(8,128)(2,1)S(1)} %pad_maximum_fusion.8), channel_id=1, source_target_pairs={{0,1},{1,0},{2,3},{3,2},{4,5},{5,4},{6,7},{7,6},{8,9},{9,8},{10,11... | collective-permute-start | bytes 3145736 | tf_op jit(solution)/shard_map/ppermute | solution.py:52
  341.9 46.6 %collective-permute-start.26 = (bf16[256,1024]{1,0:T(8,128)(2,1)}, bf16[256,1024]{1,0:T(8,128)(2,1)}, u32[]{:S(2)}, u32[]{:S(2)}) collective-permute-start(bf16[256,1024]{1,0:T(8,128)(2,1)} %get-tuple-element.74), channel_id=1, source_target_pairs={{0,1},{1,0},{2,3},{3,2},{4,5},{5,4},{6,7},{7,6},{8,9},{9,8},{10,11... | collective-permute-start | bytes 1572872 | tf_op jit(solution)/shard_map/ppermute | solution.py:52
  344.2 35.6 %collective-permute-start.28 = (bf16[256,1024]{1,0:T(8,128)(2,1)}, bf16[256,1024]{1,0:T(8,128)(2,1)}, u32[]{:S(2)}, u32[]{:S(2)}) collective-permute-start(bf16[256,1024]{1,0:T(8,128)(2,1)} %get-tuple-element.77), channel_id=1, source_target_pairs={{0,2},{1,3},{2,0},{3,1},{4,6},{5,7},{6,4},{7,5},{8,10},{9,11},{10,... | collective-permute-start | bytes 1572872 | tf_op jit(solution)/shard_map/ppermute | solution.py:52
  351.8 44.7 %collective-permute-start.31 = (bf16[512,1024]{1,0:T(8,128)(2,1)}, bf16[512,1024]{1,0:T(8,128)(2,1)}, u32[]{:S(2)}, u32[]{:S(2)}) collective-permute-start(bf16[512,1024]{1,0:T(8,128)(2,1)} %pad_maximum_fusion.7), channel_id=1, source_target_pairs={{0,2},{1,3},{2,0},{3,1},{4,6},{5,7},{6,4},{7,5},{8,10},{9,11},{10,... | collective-permute-start | bytes 3145736 | tf_op jit(solution)/shard_map/ppermute | solution.py:52
  374.7 36.6 %all-to-all-start.7 = ((bf16[8,64,1024]{2,1,0:T(8,128)(2,1)}), bf16[8,64,1024]{2,1,0:T(8,128)(2,1)}, u32[]{:S(2)}, u32[]{:S(2)}) async-start(bf16[8,64,1024]{2,1,0:T(8,128)(2,1)} %bitcast.201), calls=%async_computation.7 | async-start | bytes 2097152 | tf_op jit(solution)/shard_map/all_to_all | solution.py:91
  387.9 44.6 %collective-permute-start.14 = (bf16[256,1024]{1,0:T(8,128)(2,1)}, bf16[256,1024]{1,0:T(8,128)(2,1)}, u32[]{:S(2)}, u32[]{:S(2)}) collective-permute-start(bf16[256,1024]{1,0:T(8,128)(2,1)} %get-tuple-element.69), channel_id=1, source_target_pairs={{0,1},{1,0},{2,3},{3,2},{4,5},{5,4},{6,7},{7,6},{8,9},{9,8},{10,11... | collective-permute-start | bytes 1572872 | tf_op jit(solution)/shard_map/ppermute | solution.py:52
  390.8 55.4 %collective-permute-start.27 = (bf16[512,1024]{1,0:T(8,128)(2,1)}, bf16[512,1024]{1,0:T(8,128)(2,1)}, u32[]{:S(2)}, u32[]{:S(2)}) collective-permute-start(bf16[512,1024]{1,0:T(8,128)(2,1)} %pad_maximum_fusion.5), channel_id=1, source_target_pairs={{0,2},{1,3},{2,0},{3,1},{4,6},{5,7},{6,4},{7,5},{8,10},{9,11},{10,... | collective-permute-start | bytes 3145736 | tf_op jit(solution)/shard_map/ppermute | solution.py:52
  411.3 38.0 %all-to-all-start.6 = ((bf16[8,64,1024]{2,1,0:T(8,128)(2,1)}), bf16[8,64,1024]{2,1,0:T(8,128)(2,1)}, u32[]{:S(2)}, u32[]{:S(2)}) async-start(bf16[8,64,1024]{2,1,0:T(8,128)(2,1)} %bitcast.197), calls=%async_computation.6 | async-start | bytes 2097152 | tf_op jit(solution)/shard_map/all_to_all | solution.py:91
  434.8 51.5 %collective-permute-start.15 = (bf16[512,1024]{1,0:T(8,128)(2,1)}, bf16[512,1024]{1,0:T(8,128)(2,1)}, u32[]{:S(2)}, u32[]{:S(2)}) collective-permute-start(bf16[512,1024]{1,0:T(8,128)(2,1)} %pad_maximum_fusion.3), channel_id=1, source_target_pairs={{0,2},{1,3},{2,0},{3,1},{4,6},{5,7},{6,4},{7,5},{8,10},{9,11},{10,... | collective-permute-start | bytes 3145736 | tf_op jit(solution)/shard_map/ppermute | solution.py:52
  445.5 40.9 %collective-permute-start.13 = (bf16[512,1024]{1,0:T(8,128)(2,1)}, bf16[512,1024]{1,0:T(8,128)(2,1)}, u32[]{:S(2)}, u32[]{:S(2)}) collective-permute-start(bf16[512,1024]{1,0:T(8,128)(2,1)} %pad_maximum_fusion.2), channel_id=1, source_target_pairs={{0,1},{1,0},{2,3},{3,2},{4,5},{5,4},{6,7},{7,6},{8,9},{9,8},{10,11... | collective-permute-start | bytes 3145736 | tf_op jit(solution)/shard_map/ppermute | solution.py:52
  449.3 42.7 %all-to-all-start.5 = ((bf16[8,64,1024]{2,1,0:T(8,128)(2,1)}), bf16[8,64,1024]{2,1,0:T(8,128)(2,1)}, u32[]{:S(2)}, u32[]{:S(2)}) async-start(bf16[8,64,1024]{2,1,0:T(8,128)(2,1)} %bitcast.200), calls=%async_computation.5 | async-start | bytes 2097152 | tf_op jit(solution)/shard_map/all_to_all | solution.py:91
  603.9 77.7 %collective-permute-start.39 = (bf16[512,1024]{1,0:T(8,128)(2,1)S(1)}, bf16[512,1024]{1,0:T(8,128)(2,1)S(1)}, u32[]{:S(2)}, u32[]{:S(2)}) collective-permute-start(bf16[512,1024]{1,0:T(8,128)(2,1)S(1)} %pad_maximum_fusion.11), channel_id=1, source_target_pairs={{0,2},{1,3},{2,0},{3,1},{4,6},{5,7},{6,4},{7,5},{8,10},{9,11},{10,... | collective-permute-start | bytes 3145736 | tf_op jit(solution)/shard_map/ppermute | solution.py:52
  605.9 77.3 %collective-permute-start.37 = (bf16[512,1024]{1,0:T(8,128)(2,1)S(1)}, bf16[512,1024]{1,0:T(8,128)(2,1)S(1)}, u32[]{:S(2)}, u32[]{:S(2)}) collective-permute-start(bf16[512,1024]{1,0:T(8,128)(2,1)S(1)} %pad_maximum_fusion.10), channel_id=1, source_target_pairs={{0,1},{1,0},{2,3},{3,2},{4,5},{5,4},{6,7},{7,6},{8,9},{9,8},{10,11... | collective-permute-start | bytes 3145736 | tf_op jit(solution)/shard_map/ppermute | solution.py:52
  608.6 34.6 %collective-permute-start.85 = (bf16[128,1024]{1,0:T(8,128)(2,1)S(1)}, bf16[128,1024]{1,0:T(8,128)(2,1)S(1)}, u32[]{:S(2)}, u32[]{:S(2)}) collective-permute-start(bf16[128,1024]{1,0:T(8,128)(2,1)S(1)} %get-tuple-element.177), channel_id=1, source_target_pairs={{0,3},{1,2},{2,1},{3,0},{4,7},{5,6},{6,5},{7,4},{8,11},{9,10},{10,... | collective-permute-start | bytes 786440 | tf_op jit(solution)/shard_map/ppermute | solution.py:52
  609.9 35.7 %collective-permute-start.84 = (bf16[128,1024]{1,0:T(8,128)(2,1)S(1)}, bf16[128,1024]{1,0:T(8,128)(2,1)S(1)}, u32[]{:S(2)}, u32[]{:S(2)}) collective-permute-start(bf16[128,1024]{1,0:T(8,128)(2,1)S(1)} %get-tuple-element.178), channel_id=1, source_target_pairs={{0,2},{1,3},{2,0},{3,1},{4,6},{5,7},{6,4},{7,5},{8,10},{9,11},{10,... | collective-permute-start | bytes 786440 | tf_op jit(solution)/shard_map/ppermute | solution.py:52
  739.7 56.4 %collective-permute-start.95 = (bf16[512,1024]{1,0:T(8,128)(2,1)S(1)}, bf16[512,1024]{1,0:T(8,128)(2,1)S(1)}, u32[]{:S(2)}, u32[]{:S(2)}) collective-permute-start(bf16[512,1024]{1,0:T(8,128)(2,1)S(1)} %get-tuple-element.203), channel_id=1, source_target_pairs={{0,4},{4,0},{8,12},{12,8},{16,20},{20,16},{24,28},{28,24},{1,5},{5... | collective-permute-start | bytes 3145736 | tf_op jit(solution)/shard_map/ppermute | solution.py:52
  742.5 54.3 %collective-permute-start.67 = (bf16[512,1024]{1,0:T(8,128)(2,1)S(1)}, bf16[512,1024]{1,0:T(8,128)(2,1)S(1)}, u32[]{:S(2)}, u32[]{:S(2)}) collective-permute-start(bf16[512,1024]{1,0:T(8,128)(2,1)S(1)} %get-tuple-element.215), channel_id=1, source_target_pairs={{0,4},{4,0},{8,12},{12,8},{16,20},{20,16},{24,28},{28,24},{1,5},{5... | collective-permute-start | bytes 3145736 | tf_op jit(solution)/shard_map/ppermute | solution.py:52
  (136 other events, 1906.3 us)

commit v2 on v1

v2 whole, which is shorter than its diff:
```python
from functools import partial
import math

import jax
import jax.numpy as jnp
from jax import lax
from jax.experimental import pallas as pl
from jax.experimental.pallas import tpu as pltpu
from jax.sharding import PartitionSpec as P

precise = lax.Precision.HIGHEST
bf16 = jnp.bfloat16
f32 = jnp.float32
NT = (((1,), (1,)), ((), ()))
NN = (((1,), (0,)), ((), ()))
TN = (((0,), (0,)), ((), ()))
VMEM_BYTES = 56 * 1024 * 1024


def mm(left, right, dims=NN):
    return lax.dot_general(left, right, dims, preferred_element_type=f32)


def params():
    return pltpu.CompilerParams(
        dimension_semantics=("arbitrary",), vmem_limit_bytes=VMEM_BYTES
    )


def cost(flops, moved):
    return pl.CostEstimate(flops=int(flops) // 8, bytes_accessed=int(moved) // 8, transcendentals=0)


def table_hot(table, count):
    return (table[:, None] == jnp.arange(count, dtype=jnp.int32)[None, :]).astype(f32)


def swap(rows, axis, mask):
    count = lax.axis_size(axis)
    return lax.ppermute(rows, axis, [(i, i ^ mask) for i in range(count)])


def after(value, *others):
    return lax.optimization_barrier((value,) + tuple(jax.tree.leaves(others)))[0]


def after_all(values, *others):
    leaves = tuple(jax.tree.leaves(others))
    return lax.optimization_barrier(tuple(values) + leaves)[: len(values)]


def ring_gather(rows, move):
    half = rows.shape[0] // 2
    first, second = move(rows, 0), move(rows, 1)
    return [rows, first, second, move(first[:half], 1), move(second[half:], 0)]


def ring_sum(parts, move):
    half = parts[3].shape[0]
    left = move(parts[3], 0)
    right = move(parts[4], 1)
    to_second = jnp.concatenate(
        [(parts[2][:half].astype(f32) + left.astype(f32)).astype(bf16), parts[2][half:]], axis=0
    )
    to_first = jnp.concatenate(
        [parts[1][:half], (parts[1][half:].astype(f32) + right.astype(f32)).astype(bf16)], axis=0
    )
    first = move(to_first, 0)
    second = move(to_second, 1)
    return parts[0].astype(f32) + first.astype(f32) + second.astype(f32)


def in_plane(rows, way):
    return swap(rows, "tensor", 1 + way)


def gather_parts(rows):
    count = lax.axis_size("tensor")
    if count == 4:
        return ring_gather(rows, in_plane)
    return [rows] + [swap(rows, "tensor", r) for r in range(1, count)]


def sum_parts(parts):
    count = lax.axis_size("tensor")
    if count == 4:
        return ring_sum(parts, in_plane)
    arrived = [swap(parts[r], "tensor", r) for r in range(1, count)]
    return sum([part.astype(f32) for part in arrived], parts[0].astype(f32))


def over_experts(rows):
    experts_axis = lax.axis_size("expert")
    blocks = rows.reshape(experts_axis, rows.shape[0] // experts_axis, rows.shape[1])
    return lax.all_to_all(blocks, "expert", 0, 0, tiled=True).reshape(rows.shape)


def add_low(left, right):
    return (left.astype(f32) + right.astype(f32)).astype(bf16)


def total_blocks(near, far):
    rest = add_low(near, swap(far, "expert", 1))
    rest = ring_sum([rest[0:4], rest[4:8], rest[8:12], rest[12:14], rest[14:16]], in_plane).astype(bf16)
    own = rest[0].astype(f32)
    for m in range(1, 4):
        own = own + swap(rest[m], "expert", 2 * m).astype(f32)
    own = own.astype(bf16)
    rest = jnp.stack([own] + [swap(own, "expert", 2 * m) for m in range(1, 4)])
    near = jnp.concatenate(ring_gather(rest, in_plane), axis=0)
    return near, swap(near, "expert", 1)


def project_kernel(long_local, inputs, gain, w_query, w_key, w_value, normed, query, pair, near, held):
    @pl.when(pl.program_id(0) == 0)
    def _():
        rows = inputs[...].astype(f32)
        scale = lax.rsqrt(jnp.mean(rows * rows, axis=-1, keepdims=True) + 1e-06)
        held[...] = (rows * scale * gain[...].astype(f32)).astype(bf16)
        normed[...] = held[...]

    rows = held[...]
    query[...] = mm(rows, w_query[...]).astype(bf16)
    keys = mm(rows, w_key[...]).astype(bf16)
    values = mm(rows, w_value[...]).astype(bf16)
    pair[:long_local] = keys[:long_local]
    pair[long_local:] = values[:long_local]
    short = keys.shape[0] - long_local
    near[:short] = keys[long_local:]
    near[short:] = values[long_local:]


def project(inputs, gain, w_query, w_key, w_value, long_local):
    rows, width = inputs.shape
    short = rows - long_local
    step = 256
    whole = lambda count: pl.BlockSpec((count, width), lambda i: (0, 0))
    cut = lambda count: pl.BlockSpec((count, step), lambda i: (0, i))
    return pl.pallas_call(
        partial(project_kernel, long_local),
        grid=(width // step,),
        in_specs=[whole(rows), whole(1), cut(width), cut(width), cut(width)],
        out_specs=[whole(rows), cut(rows), cut(2 * long_local), cut(2 * short)],
        out_shape=[
            jax.ShapeDtypeStruct((rows, width), bf16),
            jax.ShapeDtypeStruct((rows, width), bf16),
            jax.ShapeDtypeStruct((2 * long_local, width), bf16),
            jax.ShapeDtypeStruct((2 * short, width), bf16),
        ],
        scratch_shapes=[pltpu.VMEM((rows, width), bf16)],
        compiler_params=params(),
        cost_estimate=cost(6 * rows * width * width, 6 * width * width + 10 * rows * width),
        name="project",
    )(inputs, gain.reshape(1, width), w_query, w_key, w_value)


def project_others_kernel(local, gain, w_key, w_value, *refs):
    sources, (normed, pairs, held) = refs[:-3], refs[-3:]

    @pl.when(pl.program_id(0) == 0)
    def _():
        rows = jnp.concatenate([source[...] for source in sources], axis=0).astype(f32)
        scale = lax.rsqrt(jnp.mean(rows * rows, axis=-1, keepdims=True) + 1e-06)
        held[...] = (rows * scale * gain[...].astype(f32)).astype(bf16)
        normed[...] = held[...]

    keys = mm(held[...], w_key[...]).astype(bf16)
    values = mm(held[...], w_value[...]).astype(bf16)
    for r in range(keys.shape[0] // local):
        pairs[2 * r * local : (2 * r + 1) * local] = keys[r * local : (r + 1) * local]
        pairs[(2 * r + 1) * local : (2 * r + 2) * local] = values[r * local : (r + 1) * local]


def project_others(sources, gain, w_key, w_value, local):
    rows = sum(source.shape[0] for source in sources)
    width = gain.shape[0]
    step = 256
    whole = lambda count: pl.BlockSpec((count, width), lambda i: (0, 0))
    cut = lambda count: pl.BlockSpec((count, step), lambda i: (0, i))
    return pl.pallas_call(
        partial(project_others_kernel, local),
        grid=(width // step,),
        in_specs=[whole(1), cut(width), cut(width)] + [whole(source.shape[0]) for source in sources],
        out_specs=[whole(rows), cut(2 * rows)],
        out_shape=[
            jax.ShapeDtypeStruct((rows, width), bf16),
            jax.ShapeDtypeStruct((2 * rows, width), bf16),
        ],
        scratch_shapes=[pltpu.VMEM((rows, width), bf16)],
        compiler_params=params(),
        cost_estimate=cost(4 * rows * width * width, 4 * width * width + 8 * rows * width),
        name="project_others",
    )(gain.reshape(1, width), w_key, w_value, *sources)


def key_value_views(pair, others, count, rows):
    views = [(pair, slice(0, rows), pair, slice(rows, 2 * rows))]
    for r in range(count - 1):
        at = 2 * r * rows
        views.append((others, slice(at, at + rows), others, slice(at + rows, at + 2 * rows)))
    return views


def forward_kernel(
    count, rows, dim, facts, query, pair, others, near, far_bias, near_bias, mixed, far_attend, near_attend, window
):
    place, far_len, near_len = facts[0], facts[1], facts[2]
    scale = 1.0 / math.sqrt(dim)
    views = key_value_views(pair, others, count, rows)
    short = near.shape[0] // 2
    reach = far_bias.shape[-1]
    for head in range(2):
        lanes = slice(head * dim, (head + 1) * dim)
        low = (query[:, lanes].astype(f32) * scale).astype(bf16)
        table = jnp.broadcast_to(far_bias[0, head : head + 1, :], (rows, reach))
        window[...] = pltpu.roll(table, reach - (rows - 1), 1, stride=1, stride_axis=0)
        scores = []
        for r in range(count):
            source = place ^ r
            start = pl.multiple_of(source * rows, rows)
            keys = views[r][0][views[r][1], lanes]
            part = mm(low[:rows], keys, NT) + window[:, pl.ds(start, rows)]
            spot = source * rows + lax.broadcasted_iota(jnp.int32, (1, rows), 1)
            scores.append(jnp.where(spot < far_len, part, -1e30))
        highest = scores[0]
        for part in scores[1:]:
            highest = jnp.maximum(highest, part)
        highest = jnp.max(highest, axis=-1, keepdims=True)
        grown = [jnp.exp(part - highest) for part in scores]
        whole = grown[0]
        for part in grown[1:]:
            whole = whole + part
        inverse = 1.0 / jnp.sum(whole, axis=-1, keepdims=True)
        out = jnp.zeros((rows, dim), f32)
        for r in range(count):
            attend = (grown[r] * inverse).astype(bf16)
            far_attend[head, :, r * rows : (r + 1) * rows] = attend
            out = out + mm(attend, views[r][2][views[r][3], lanes])
        mixed[:rows, lanes] = out.astype(bf16)

        table = jnp.broadcast_to(near_bias[0, head : head + 1, :], (short, 2 * short))
        bias = pltpu.roll(table, short + 1, 1, stride=1, stride_axis=0)[:, :short]
        part = mm(low[rows:], near[:short, lanes], NT) + bias
        spot = lax.broadcasted_iota(jnp.int32, (1, short), 1)
        part = jnp.where(spot < near_len, part, -1e30)
        part = jnp.exp(part - jnp.max(part, axis=-1, keepdims=True))
        attend = (part * (1.0 / jnp.sum(part, axis=-1, keepdims=True))).astype(bf16)
        near_attend[head] = attend
        mixed[rows:, lanes] = mm(attend, near[short:, lanes]).astype(bf16)


def attention_specs(count, rows, short, reach, tokens, first=0):
    cut = lambda size: pl.BlockSpec((size, 128), lambda i, *_: (0, i + first))
    parts = [cut(2 * rows), cut(2 * (count - 1) * rows)]
    table = lambda size: pl.BlockSpec((1, 2, size), lambda i, *_: (i + first, 0, 0))
    weights = lambda size, span: pl.BlockSpec((2, size, span), lambda i, *_: (i + first, 0, 0))
    return (
        cut(tokens),
        parts,
        cut(2 * short),
        [table(reach), table(2 * short)],
        [weights(rows, count * rows), weights(short, short)],
    )


def attend_forward(facts, query, parts, near, far_bias, near_bias, count, rows, dim):
    tokens, width = query.shape
    heads = width // dim
    short = near.shape[0] // 2
    reach = far_bias.shape[-1]
    cut, part_specs, near_spec, tables, weights = attention_specs(count, rows, short, reach, tokens)
    return pl.pallas_call(
        partial(forward_kernel, count, rows, dim),
        grid_spec=pltpu.PrefetchScalarGridSpec(
            num_scalar_prefetch=1,
            grid=(heads // 2,),
            in_specs=[cut] + part_specs + [near_spec] + tables,
            out_specs=[cut] + weights,
            scratch_shapes=[pltpu.VMEM((rows, reach), f32)],
        ),
        out_shape=[
            jax.ShapeDtypeStruct((tokens, width), bf16),
            jax.ShapeDtypeStruct((heads, rows, count * rows), bf16),
            jax.ShapeDtypeStruct((heads, short, short), bf16),
        ],
        compiler_params=params(),
        cost_estimate=cost(40 * heads * rows * rows * count * dim, 12 * width * rows * count),
        name="attend_forward",
    )(facts, query, *parts, near, far_bias, near_bias)


def backward_kernel(
    count,
    rows,
    dim,
    facts,
    query,
    grad,
    pair,
    others,
    near,
    far_attend,
    near_attend,
    grad_query,
    grad_pair,
    grad_others,
    grad_near,
    far_sums,
    near_sums,
    window,
    near_window,
):
    place = facts[0]
    scale = 1.0 / math.sqrt(dim)
    views = key_value_views(pair, others, count, rows)
    grad_views = key_value_views(grad_pair, grad_others, count, rows)
    short = near.shape[0] // 2
    reach = window.shape[1]

    @pl.when(pl.program_id(0) == 0)
    def _():
        window[...] = jnp.zeros_like(window)
        near_window[...] = jnp.zeros_like(near_window)

    def reversal(size):
        up = lax.broadcasted_iota(jnp.int32, (size, size), 0)
        across = lax.broadcasted_iota(jnp.int32, (size, size), 1)
        return (up + across == size - 1).astype(bf16)

    far_turn = reversal(rows)
    near_turn = far_turn if short == rows else reversal(short)
    for head in range(2):
        lanes = slice(head * dim, (head + 1) * dim)
        low = query[:, lanes]
        grad_low = grad[:, lanes]
        turned = jnp.transpose((low.astype(f32) * scale), (1, 0)).astype(bf16)
        grad_turned = jnp.transpose(grad_low.astype(f32), (1, 0)).astype(bf16)
        attends, grads = [], []
        inner = jnp.zeros((rows, 1), f32)
        for r in range(count):
            attend = far_attend[head, :, r * rows : (r + 1) * rows]
            part = mm(grad_low[:rows], views[r][2][views[r][3], lanes], NT)
            inner = inner + jnp.sum(attend.astype(f32) * part, axis=-1, keepdims=True)
            attends.append(attend)
            grads.append(part)
        out = jnp.zeros((rows, dim), f32)
        for r in range(count):
            start = pl.multiple_of((place ^ r) * rows, rows)
            scores = (attends[r].astype(f32) * (grads[r] - inner)).astype(bf16)
            window[:, pl.ds(start, rows)] = mm(far_turn, scores)
            out = out + mm(scores, views[r][0][views[r][1], lanes])
            grad_keys = mm(turned[:, :rows], scores)
            grad_values = mm(grad_turned[:, :rows], attends[r])
            view = grad_views[r]
            view[0][view[1], lanes] = jnp.transpose(grad_keys, (1, 0)).astype(bf16)
            view[2][view[3], lanes] = jnp.transpose(grad_values, (1, 0)).astype(bf16)
        grad_query[:rows, lanes] = (out * scale).astype(bf16)
        rolled = pltpu.roll(window[...], 0, 1, stride=1, stride_axis=0)
        far_sums[0, head : head + 1, :] = jnp.sum(rolled, axis=0, keepdims=True)

        attend = near_attend[head]
        part = mm(grad_low[rows:], near[short:, lanes], NT)
        wide = attend.astype(f32)
        part = wide * (part - jnp.sum(wide * part, axis=-1, keepdims=True))
        scores = part.astype(bf16)
        near_window[:, :short] = mm(near_turn, scores)
        rolled = pltpu.roll(near_window[...], 0, 1, stride=1, stride_axis=0)
        near_sums[0, head : head + 1, :] = jnp.sum(rolled, axis=0, keepdims=True)
        grad_query[rows:, lanes] = (mm(scores, near[:short, lanes]) * scale).astype(bf16)
        grad_keys = mm(turned[:, rows:], scores)
        grad_values = mm(grad_turned[:, rows:], attend)
        grad_near[:short, lanes] = jnp.transpose(grad_keys, (1, 0)).astype(bf16)
        grad_near[short:, lanes] = jnp.transpose(grad_values, (1, 0)).astype(bf16)


def attend_backward(facts, query, grad, parts, near, weights, reach, count, rows, dim, half):
    tokens, width = query.shape
    pairs = width // dim // 4
    wide = width // 2
    short = near.shape[0] // 2
    cut, part_specs, near_spec, _, weight_specs = attention_specs(
        count, rows, short, reach, tokens, half * pairs
    )
    cut_out, part_outs, near_out, tables, _ = attention_specs(count, rows, short, reach, tokens)
    return pl.pallas_call(
        partial(backward_kernel, count, rows, dim),
        grid_spec=pltpu.PrefetchScalarGridSpec(
            num_scalar_prefetch=1,
            grid=(pairs,),
            in_specs=[cut, cut] + part_specs + [near_spec] + weight_specs,
            out_specs=[cut_out] + part_outs + [near_out] + tables,
            scratch_shapes=[pltpu.VMEM((rows, reach), f32), pltpu.VMEM((short, 2 * short), f32)],
        ),
        out_shape=[
            jax.ShapeDtypeStruct((size, wide), bf16)
            for size in (tokens, 2 * rows, 2 * (count - 1) * rows, 2 * short)
        ]
        + [
            jax.ShapeDtypeStruct((pairs, 2, reach), f32),
            jax.ShapeDtypeStruct((pairs, 2, 2 * short), f32),
        ],
        compiler_params=params(),
        cost_estimate=cost(50 * width // dim * rows * rows * count * dim, 8 * width * rows * count),
        name="attend_backward",
    )(facts, query, grad, *parts, near, *weights)


def normed_grads_kernel(local, count, *refs):
    grads, (w_query, w_key, w_value) = refs[:8], refs[8:11]
    own, own_short, away = refs[11:]
    half = pl.program_id(0)

    @pl.when(half == 0)
    def _():
        own[...] = jnp.zeros_like(own)
        own_short[...] = jnp.zeros_like(own_short)
        away[...] = jnp.zeros_like(away)

    for which in range(2):

        @pl.when(half == which)
        def _():
            query, pair, others, near = grads[4 * which : 4 * which + 4]
            short = near.shape[0] // 2
            full = mm(query[...], w_query[...], NT)
            own[...] += full[:local] + mm(pair[:local], w_key[...], NT) + mm(pair[local:], w_value[...], NT)
            own_short[...] += (
                full[local:] + mm(near[:short], w_key[...], NT) + mm(near[short:], w_value[...], NT)
            )
            for r in range(count - 1):
                at = 2 * r * local
                away[r * local : (r + 1) * local] += mm(
                    others[at : at + local], w_key[...], NT
                ) + mm(others[at + local : at + 2 * local], w_value[...], NT)


def normed_grads(halves, w_query, w_key, w_value, local, count):
    width = w_query.shape[0]
    wide = width // 2
    short = halves[0][3].shape[0] // 2
    arrays = [array for half in halves for array in half[:4]]
    cut = pl.BlockSpec((width, wide), lambda i: (0, i))
    return pl.pallas_call(
        partial(normed_grads_kernel, local, count),
        grid=(2,),
        in_specs=[pl.BlockSpec(array.shape, lambda i: (0, 0)) for array in arrays] + [cut] * 3,
        out_specs=[
            pl.BlockSpec((size, width), lambda i: (0, 0)) for size in (local, short, (count - 1) * local)
        ],
        out_shape=[
            jax.ShapeDtypeStruct((size, width), f32) for size in (local, short, (count - 1) * local)
        ],
        compiler_params=params(),
        cost_estimate=cost(4 * count * local * width * width, 8 * count * local * width),
        name="normed_grads",
    )(*arrays, w_query, w_key, w_value)


def expert_kernel(chunks, capacity, padded, lanes_used, facts, rows_in, grads_in, *refs):
    sources, rest = refs[: 3 * chunks], refs[3 * chunks :]
    middles, (out_ref, grad_ref) = rest[: 3 * chunks], rest[3 * chunks : 3 * chunks + 2]
    held, sems = rest[3 * chunks + 2 : 6 * chunks + 2], rest[6 * chunks + 2]
    rows = rows_in.shape[0]
    groups = rows // padded
    first = pl.program_id(0) == 0

    def copy(i):
        index = facts[4] if i < 3 else i % 3
        return pltpu.make_async_copy(sources[i].at[index], held[i], sems.at[i])

    @pl.when(first)
    def _():
        for i in range(3 * chunks):
            copy(i).start()
        for i in range(3 * chunks):
            copy(i).wait()

    slots = rows_in[...]
    grads = grads_in[...]
    spare = 16 - (padded - capacity)
    lanes = lax.broadcasted_iota(jnp.int32, (padded, 128), 1)
    match = lax.broadcasted_iota(jnp.int32, (padded, 128), 0) == lanes
    columns = []
    for g in range(groups):
        tail = rows_in[pl.ds((g + 1) * padded - 16, 16), :128].astype(f32)
        line = tail[spare : spare + 1] + tail[spare + 1 : spare + 2]
        columns.append(jnp.sum(jnp.where(match, line, 0.0), axis=-1, keepdims=True))
    gate_column = jnp.concatenate(columns, axis=0)

    lows = []
    slope = math.sqrt(2.0 / math.pi)
    for c in range(chunks):
        gate_pre = mm(slots, held[3 * c][...], NT)
        up_pre = mm(slots, held[3 * c + 1][...], NT)
        grad_hidden = mm(grads, held[3 * c + 2][...], NT) * gate_column
        square = gate_pre * gate_pre
        curve = jnp.tanh(slope * gate_pre * (1.0 + 0.044715 * square))
        side = 0.5 * (1.0 + curve)
        bent = gate_pre * side
        hidden = bent * up_pre
        bent_slope = side + 0.5 * slope * gate_pre * (1.0 - curve * curve) * (
            1.0 + 3.0 * 0.044715 * square
        )
        gate_low = (grad_hidden * up_pre * bent_slope).astype(bf16)
        up_low = (grad_hidden * bent).astype(bf16)
        middles[3 * c][...] = (hidden * gate_column).astype(bf16)
        middles[3 * c + 1][...] = gate_low
        middles[3 * c + 2][...] = up_low
        lows.append((gate_low, up_low, hidden.astype(bf16)))
    left = [jnp.concatenate([low[k] for low in lows], axis=1) for k in range(3)]
    right = [
        jnp.concatenate([held[3 * c + k][...] for c in range(chunks)], axis=0) for k in range(3)
    ]
    out = mm(left[2], right[2])
    grad_out = mm(left[0], right[0]) + mm(left[1], right[1])
    out_ref[...] = out.astype(bf16)
    grad_ref[...] = grad_out.astype(bf16)

    grad_gate = jnp.sum(out * grads.astype(f32), axis=-1, keepdims=True)
    lanes = lax.broadcasted_iota(jnp.int32, (padded, lanes_used), 1)
    up = lax.broadcasted_iota(jnp.int32, (padded, lanes_used), 0)
    match = up + facts[5] * padded == lanes
    row = lax.broadcasted_iota(jnp.int32, (16, lanes_used), 0)
    for g in range(groups):
        values = jnp.where(match, grad_gate[g * padded : (g + 1) * padded], 0.0)
        line = jnp.sum(values, axis=0, keepdims=True)
        high = line.astype(bf16).astype(f32)
        tail = grad_out[(g + 1) * padded - 16 : (g + 1) * padded, :lanes_used]
        tail = jnp.where(row == spare, high, jnp.where(row == spare + 1, line - high, tail))
        grad_ref[pl.ds((g + 1) * padded - 16, 16), :lanes_used] = tail.astype(bf16)


def expert_pass(facts, slots, grads, own, other, capacity, padded, lanes_used):
    rows, width = slots.shape
    units = own[0].shape[1]
    chunks = 1 if other is None else 2
    sources = list(own) + ([] if other is None else [other] * 3)
    tile = rows
    cut = lambda size: pl.BlockSpec((tile, size), lambda i, f: (i, 0))
    outs = pl.pallas_call(
        partial(expert_kernel, chunks, capacity, padded, lanes_used),
        grid_spec=pltpu.PrefetchScalarGridSpec(
            num_scalar_prefetch=1,
            grid=(rows // tile,),
            in_specs=[cut(width)] * 2 + [pl.BlockSpec(memory_space=pl.ANY)] * (3 * chunks),
            out_specs=[cut(units)] * (3 * chunks) + [cut(width)] * 2,
            scratch_shapes=[pltpu.VMEM((units, width), bf16)] * (3 * chunks)
            + [pltpu.SemaphoreType.DMA((3 * chunks,))],
        ),
        out_shape=[jax.ShapeDtypeStruct((rows, units), bf16)] * (3 * chunks)
        + [jax.ShapeDtypeStruct((rows, width), bf16)] * 2,
        compiler_params=params(),
        cost_estimate=cost(12 * chunks * rows * units * width, 8 * rows * width),
        name="expert_pass",
    )(facts, slots, grads, *sources)
    middles = [outs[3 * c : 3 * c + 3] for c in range(chunks)]
    return middles, outs[3 * chunks], outs[3 * chunks + 1]


def weight_body(count, packed, extra, facts, *refs):
    kinds = [refs[k * count : (k + 1) * count] for k in range(5)]
    outs = refs[5 * count + extra :]
    targets = outs[1:4] if packed else outs[:3]
    held, sems = refs[-6:-1], refs[-1]
    step = pl.program_id(0)
    slot = step % 2

    def fetch(index, side):
        for r in range(count):

            @pl.when(index == r)
            def _():
                for k in range(5):
                    pltpu.make_async_copy(kinds[k][r], held[k].at[side], sems.at[side, k]).start()

    @pl.when(step == 0)
    def _():
        fetch(step, slot)

    @pl.when(step + 1 < count)
    def _():
        fetch(step + 1, 1 - slot)

    for k in range(5):
        pltpu.make_async_copy(kinds[k][0], held[k].at[slot], sems.at[slot, k]).wait()

    @pl.when(step == 0)
    def _():
        for target in targets:
            target[...] = jnp.zeros_like(target)

    rows, grads = held[0][slot], held[1][slot]
    lefts = ((held[3], rows), (held[4], rows), (held[2], grads))
    for target, (left, right) in zip(targets, lefts):
        target[0] += mm(left[slot], right, TN)

    if packed:

        @pl.when(step == count - 1)
        def _():
            for i in range(3):
                outs[0][i] = targets[i][0].astype(bf16)


def weight_pass(facts, slots, grads, middles, before, local, packed):
    count = len(slots)
    rows, width = slots[0].shape
    units = middles[0][0].shape[1]
    anywhere = pl.BlockSpec(memory_space=pl.ANY)
    if packed:
        out_specs = [pl.BlockSpec((3, units, width), lambda i, f: (0, 0, 0))]
        out_shape = [jax.ShapeDtypeStruct((3, units, width), bf16)]
        totals = [pltpu.VMEM((1, units, width), f32)] * 3
    else:
        out_specs = [pl.BlockSpec((1, units, width), lambda i, f: (f[4], 0, 0))] * 3
        out_shape = [jax.ShapeDtypeStruct((local, units, width), f32)] * 3
        totals = []
    kinds = [list(slots), list(grads)] + [[middle[k] for middle in middles] for k in range(3)]
    body = partial(weight_body, count, packed, len(before))
    return pl.pallas_call(
        body,
        grid_spec=pltpu.PrefetchScalarGridSpec(
            num_scalar_prefetch=1,
            grid=(count,),
            in_specs=[anywhere] * (5 * count + len(before)),
            out_specs=out_specs,
            scratch_shapes=totals
            + [pltpu.VMEM((2, rows, width), bf16)] * 2
            + [pltpu.VMEM((2, rows, units), bf16)] * 3
            + [pltpu.SemaphoreType.DMA((2, 5))],
        ),
        out_shape=out_shape,
        input_output_aliases={1 + 5 * count + i: i for i in range(len(before))},
        compiler_params=params(),
        cost_estimate=cost(6 * count * rows * units * width, 8 * count * rows * width),
        name="weight_pass",
    )(facts, *[array for kind in kinds for array in kind], *before)


def fill_kernel(facts, source, *refs):
    for i in range(3):
        refs[-3 + i][0] = source[i].astype(f32)


def weight_fill(facts, source, before):
    _, units, width = source.shape
    tile = units // 4
    anywhere = pl.BlockSpec(memory_space=pl.ANY)
    return pl.pallas_call(
        fill_kernel,
        grid_spec=pltpu.PrefetchScalarGridSpec(
            num_scalar_prefetch=1,
            grid=(4,),
            in_specs=[pl.BlockSpec((3, tile, width), lambda i, f: (0, i, 0))] + [anywhere] * 3,
            out_specs=[pl.BlockSpec((1, tile, width), lambda i, f: (f[6], i, 0))] * 3,
        ),
        out_shape=[jax.ShapeDtypeStruct(array.shape, f32) for array in before],
        input_output_aliases={2 + i: i for i in range(3)},
        compiler_params=params(),
        cost_estimate=cost(0, 6 * source.size),
        name="weight_fill",
    )(facts, source, *before)


def place_kernel(capacity, padded, block, local, turns, routes, rows, slots_out, wide_out, rows_out):
    experts_axis = block // padded
    tokens = rows.shape[0]
    experts = experts_axis * local
    number = lax.broadcasted_iota(jnp.int32, (experts, tokens), 0)
    picks = [number == routes[k : k + 1] for k in range(routes.shape[0])]
    named = picks[0]
    for pick in picks[1:]:
        named = named | pick
    earlier = lax.broadcasted_iota(jnp.int32, (tokens, tokens), 0) < lax.broadcasted_iota(
        jnp.int32, (tokens, tokens), 1
    )
    before = mm(named.astype(bf16), earlier.astype(bf16))
    places = []
    for k, pick in enumerate(picks):
        route = routes[k : k + 1]
        position = jnp.sum(jnp.where(pick, before, 0.0), axis=0, keepdims=True).astype(jnp.int32)
        owner = route // local
        turn = jnp.where(owner % 2 == 0, turns[:, 0:1], turns[:, 1:2])
        which = (route % local) ^ turn
        slot = which * block + owner * padded + position
        slots_out[k : k + 1] = jnp.where(position < capacity, slot, -1)
        slot = (owner * local + which) * padded + position
        places.append(jnp.where(position < capacity, slot, -1))
        wide_out[k : k + 1] = places[k]
    spots = lax.broadcasted_iota(jnp.int32, (local * block, tokens), 0)
    hot = spots == places[0]
    for slot in places[1:]:
        hot = hot | (spots == slot)
    rows_out[...] = mm(hot.astype(bf16), rows[...]).astype(bf16)


def place_rows(turns, routes, rows, capacity, padded, block, local):
    tops, tokens = routes.shape
    width = rows.shape[1]
    return pl.pallas_call(
        partial(place_kernel, capacity, padded, block, local),
        out_shape=[
            jax.ShapeDtypeStruct((tops, tokens), jnp.int32),
            jax.ShapeDtypeStruct((tops, tokens), jnp.int32),
            jax.ShapeDtypeStruct((local * block, width), bf16),
        ],
        compiler_params=pltpu.CompilerParams(vmem_limit_bytes=VMEM_BYTES),
        cost_estimate=cost(2 * local * block * tokens * width, 4 * local * block * width),
        name="place_rows",
    )(turns, routes, rows)


def route_kernel(
    capacity, padded, mixed, w_proj, inputs, gain, router, routes, slots, resid, moe, probs, gates, out
):
    local, block, width = out.shape
    tokens = inputs.shape[0]
    sums = inputs[...].astype(f32) + mm(mixed[...], w_proj[...])
    resid[...] = sums
    scale = lax.rsqrt(jnp.mean(sums * sums, axis=-1, keepdims=True) + 1e-06)
    low = (sums * scale * gain[...].astype(f32)).astype(bf16)
    moe[...] = low
    logits = mm(router[...], low, NT)
    grown = jnp.exp(logits - jnp.max(logits, axis=0, keepdims=True))
    share = grown / jnp.sum(grown, axis=0, keepdims=True)
    probs[...] = share
    number = lax.broadcasted_iota(jnp.int32, share.shape, 0)
    spots = lax.broadcasted_iota(jnp.int32, (local * block, tokens), 0)
    row = lax.broadcasted_iota(jnp.int32, (16, tokens), 0)
    hot = None
    lines = jnp.zeros((16, local * block), f32)
    for k in range(routes.shape[0]):
        gate = jnp.sum(jnp.where(number == routes[k : k + 1], share, 0.0), axis=0, keepdims=True)
        gates[k : k + 1] = gate
        high = gate.astype(bf16).astype(f32)
        both = jnp.where(row == 0, high, jnp.where(row == 1, gate - high, 0.0)).astype(bf16)
        mine = (spots == slots[k : k + 1]).astype(bf16)
        lines = lines + mm(both, mine, NT)
        hot = mine if hot is None else hot + mine
    filled = mm(hot, low).astype(bf16)
    spare = 16 - (padded - capacity)
    row = lax.broadcasted_iota(jnp.int32, (16, padded), 0)
    for j in range(local):
        out[j] = filled[j * block : (j + 1) * block]
        for g in range(block // padded):
            at = j * block + g * padded
            tail = filled[at + padded - 16 : at + padded, :padded].astype(f32)
            line = lines[:, at : at + padded]
            tail = jnp.where(row == spare, line[0:1], jnp.where(row == spare + 1, line[1:2], tail))
            out[j, pl.ds((g + 1) * padded - 16, 16), :padded] = tail.astype(bf16)


def route_rows(mixed, w_proj, inputs, gain, router, routes, slots, capacity, padded, block, local):
    tokens, width = inputs.shape
    tops = routes.shape[0]
    return pl.pallas_call(
        partial(route_kernel, capacity, padded),
        out_shape=[
            jax.ShapeDtypeStruct((tokens, width), f32),
            jax.ShapeDtypeStruct((tokens, width), bf16),
            jax.ShapeDtypeStruct((router.shape[0], tokens), f32),
            jax.ShapeDtypeStruct((tops, tokens), f32),
            jax.ShapeDtypeStruct((local, block, width), bf16),
        ],
        compiler_params=pltpu.CompilerParams(vmem_limit_bytes=VMEM_BYTES),
        cost_estimate=cost(4 * local * block * tokens * width, 12 * local * block * width),
        name="route_rows",
    )(mixed, w_proj, inputs, gain.reshape(1, width), router, routes, slots)


def merge_kernel(
    capacity, padded, count, cotangent, resid, probs, moe, router, gain, w_proj, routes, slots, columns, *refs
):
    local = len(refs) - 5
    grads = refs[:local]
    grad_resid, grad_mixed, gain_grad, router_grad, branch_out = refs[local:]
    block = grads[0].shape[0]
    tokens = cotangent.shape[0]
    tops = routes.shape[0]
    spare = 16 - (padded - capacity)
    pieces = []
    for j in range(local):
        for g in range(block // padded):
            tail = grads[j][pl.ds((g + 1) * padded - 16, 16), : count * padded].astype(f32)
            line = tail[spare : spare + 1] + tail[spare + 1 : spare + 2]
            folded = line[:, :padded]
            for r in range(1, count):
                folded = folded + line[:, r * padded : (r + 1) * padded]
            pieces.append(folded)
    line = jnp.concatenate(pieces, axis=1)
    row = lax.broadcasted_iota(jnp.int32, (16, line.shape[1]), 0)
    high = line.astype(bf16).astype(f32)
    rest = line - high
    middle = rest.astype(bf16).astype(f32)
    stack = jnp.where(row == 0, high, jnp.where(row == 1, middle, jnp.where(row == 2, rest - middle, 0.0)))
    stack = stack.astype(bf16)
    share = probs[...]
    number = lax.broadcasted_iota(jnp.int32, share.shape, 0)
    spots = lax.broadcasted_iota(jnp.int32, (local * block, tokens), 0)
    grad_probs = jnp.zeros_like(share)
    for k in range(tops):
        picked = jnp.sum(mm(stack, (spots == slots[k : k + 1]).astype(bf16)), axis=0, keepdims=True)
        grad_probs = grad_probs + jnp.where(number == routes[k : k + 1], picked, 0.0)
    grad_logits = share * (grad_probs - jnp.sum(share * grad_probs, axis=0, keepdims=True))
    grad_logits = grad_logits.astype(bf16)
    router_grad[...] = mm(grad_logits, moe[...])
    grad_moe = mm(grad_logits, router[...], TN)
    spots = lax.broadcasted_iota(jnp.int32, (tokens, block), 1)
    for j in range(local):
        hot = None
        for k in range(tops):
            mine = spots + j * block == columns[:, k : k + 1]
            hot = mine if hot is None else hot | mine
        grad_moe = grad_moe + mm(hot.astype(bf16), grads[j][...])
    rows = resid[...]
    scale = lax.rsqrt(jnp.mean(rows * rows, axis=-1, keepdims=True) + 1e-06)
    normed = rows * scale
    gain_grad[...] = jnp.sum(grad_moe * normed, axis=0, keepdims=True)
    lifted = grad_moe * gain[...].astype(f32)
    spread = jnp.mean(lifted * normed, axis=-1, keepdims=True)
    back = cotangent[...].astype(f32) + scale * (lifted - normed * spread)
    grad_resid[...] = back
    branch = back.astype(bf16)
    grad_mixed[...] = mm(branch, w_proj[...], NT).astype(bf16)
    branch_out[...] = branch


def merge_rows(
    cotangent, resid, probs, moe, router, gain, w_proj, routes, slots, grads, capacity, padded, count
):
    tokens, width = cotangent.shape
    return pl.pallas_call(
        partial(merge_kernel, capacity, padded, count),
        out_shape=[
            jax.ShapeDtypeStruct((tokens, width), f32),
            jax.ShapeDtypeStruct((tokens, width), bf16),
            jax.ShapeDtypeStruct((1, width), f32),
            jax.ShapeDtypeStruct((router.shape[0], width), f32),
            jax.ShapeDtypeStruct((tokens, width), bf16),
        ],
        compiler_params=pltpu.CompilerParams(vmem_limit_bytes=VMEM_BYTES),
        cost_estimate=cost(6 * tokens * width * width, 20 * tokens * width),
        name="merge_rows",
    )(
        cotangent, resid, probs, moe, router, gain.reshape(1, width), w_proj, routes, slots,
        jnp.transpose(slots), *grads,
    )


def blocks_kernel(
    local, facts, normed, normed_others, mixed, grad_query, grad_pair, grad_others, grad_near, branch, small, near, far
):
    step = pl.program_id(0)
    number = facts[3]
    group = step ^ (number // 4)
    share = (near.shape[1] - 8) // 4
    short = grad_near.shape[0] // 2
    own, own_short = normed[:local], normed[local:]

    def keyed(which):
        part = mm(own, grad_pair[which * local : (which + 1) * local], TN)
        part = part + mm(own_short, grad_near[which * short : (which + 1) * short], TN)
        for r in range(normed_others.shape[0] // local):
            at = (2 * r + which) * local
            part = part + mm(normed_others[r * local : (r + 1) * local], grad_others[at : at + local], TN)
        return part

    made = [mm(normed[...], grad_query[...], TN), keyed(0), keyed(1), mm(mixed[...], branch[...], TN)]
    made = [part.astype(bf16) for part in made]
    for s in range(4):
        spot = s ^ (number % 4)
        lines = [part[s * share : (s + 1) * share] for part in made]
        extra = jnp.zeros((8, small.shape[1]), bf16)
        if s < 3:
            extra = jnp.where(group == 0, small[s * 8 : s * 8 + 8], extra)
        whole = jnp.concatenate(lines + [extra], axis=0)

        @pl.when(step < 4)
        def _():
            near[spot] = whole

        @pl.when(step >= 4)
        def _():
            far[spot] = whole


def weight_blocks(facts, lefts, rights, branch, small, local, half):
    tokens, width = lefts[0].shape
    wide = width // 2
    rows = 4 * width // 32 + 8
    cut = lambda count: pl.BlockSpec((count, width // 8), lambda i, f: (0, i ^ (f[3] // 4)))
    full = lambda count: pl.BlockSpec((count, wide), lambda i, f: (0, 0))
    out = lambda which: pl.BlockSpec((4, rows, wide), which)
    return pl.pallas_call(
        partial(blocks_kernel, local),
        grid_spec=pltpu.PrefetchScalarGridSpec(
            num_scalar_prefetch=1,
            grid=(8,),
            in_specs=[cut(left.shape[0]) for left in lefts]
            + [full(right.shape[0]) for right in rights]
            + [pl.BlockSpec((tokens, wide), lambda i, f: (0, half)), full(24)],
            out_specs=[
                out(lambda i, f: (jnp.minimum(i, 3), 0, 0)),
                out(lambda i, f: (jnp.maximum(i - 4, 0), 0, 0)),
            ],
        ),
        out_shape=[jax.ShapeDtypeStruct((16, rows, wide), bf16)] * 2,
        compiler_params=params(),
        cost_estimate=cost(8 * tokens * width * width, 4 * width * width),
        name="weight_blocks",
    )(facts, *lefts, *rights, branch, small)


def unpack_kernel(facts, near, far, w_query, w_key, w_value, gain, *refs):
    query, key, value, proj, gain_grad, small = refs[-6:]
    step = pl.program_id(0)
    number = facts[3]
    group = step ^ (number // 4)
    share = (near.shape[1] - 8) // 4

    def spread(source):
        for s in range(4):
            block = source[s ^ (number % 4)].astype(f32)
            for which, out in enumerate((query, key, value, proj)):
                out[s * share : (s + 1) * share] = block[which * share : (which + 1) * share]
            if s < 3:

                @pl.when(group == 0)
                def _():
                    small[s * 8 : s * 8 + 8] = block[4 * share :]

    @pl.when(step < 4)
    def _():
        spread(near)

    @pl.when(step >= 4)
    def _():
        spread(far)

    sums = query[...] * w_query[...].astype(f32)
    sums = sums + key[...] * w_key[...].astype(f32)
    sums = sums + value[...] * w_value[...].astype(f32)
    column = jnp.sum(sums, axis=-1, keepdims=True)
    size = column.shape[0]
    match = lax.broadcasted_iota(jnp.int32, (size, size), 0) == lax.broadcasted_iota(
        jnp.int32, (size, size), 1
    )
    line = jnp.sum(jnp.where(match, column, 0.0), axis=0, keepdims=True)
    gain_grad[...] = line / gain[...].astype(f32)


def unpack_blocks(facts, near, far, w_query, w_key, w_value, gain, before, half):
    width = w_query.shape[0]
    wide = width // 2
    rows = near.shape[1]
    step = width // 8
    line = pl.BlockSpec((1, step), lambda i, f: (0, i ^ (f[3] // 4)))
    block = pl.BlockSpec((step, wide), lambda i, f: (i ^ (f[3] // 4), half))
    return pl.pallas_call(
        unpack_kernel,
        grid_spec=pltpu.PrefetchScalarGridSpec(
            num_scalar_prefetch=1,
            grid=(8,),
            in_specs=[
                pl.BlockSpec((4, rows, wide), lambda i, f: (jnp.minimum(i, 3), 0, 0)),
                pl.BlockSpec((4, rows, wide), lambda i, f: (jnp.maximum(i - 4, 0), 0, 0)),
                block,
                block,
                block,
                line,
            ]
            + [pl.BlockSpec(memory_space=pl.ANY)] * len(before),
            out_specs=[block, block, block, block, line, pl.BlockSpec((24, wide), lambda i, f: (0, 0))],
        ),
        out_shape=[jax.ShapeDtypeStruct((width, width), f32)] * 4
        + [jax.ShapeDtypeStruct((1, width), f32), jax.ShapeDtypeStruct((24, wide), f32)],
        input_output_aliases={7 + i: i for i in range(len(before))},
        compiler_params=params(),
        cost_estimate=cost(6 * width * width, 12 * width * width),
        name="unpack_blocks",
    )(facts, near, far, w_query, w_key, w_value, gain.reshape(1, width), *before)


def per_device(
    inputs,
    attn_gain,
    w_query,
    w_key,
    w_value,
    w_proj,
    rel_bias,
    moe_gain,
    w_router,
    w_gate,
    w_up,
    w_down,
    routes,
    long_buckets,
    short_buckets,
    long_lens,
    short_lens,
    cotangent,
):
    experts_axis = lax.axis_size("expert")
    tensor_axis = lax.axis_size("tensor")
    place = lax.axis_index("tensor")
    tok_count, width = inputs.shape
    top_count = routes.shape[1]
    short_len = (short_buckets.shape[0] + 1) // 2
    long_span = (long_buckets.shape[0] + 1) // 2
    long_local = tok_count - short_len
    bucket_count, heads = rel_bias.shape
    head_dim = width // heads
    experts = w_router.shape[1]
    local = experts // experts_axis
    capacity = (5 * tok_count * top_count + 4 * experts - 1) // (4 * experts)
    padded = (capacity + 2 + 15) // 16 * 16
    block = experts_axis * padded
    rel_table = rel_bias.astype(f32)
    here = lax.axis_index("expert")
    number = (here % 2) * 16 + place * 4 + here // 2
    paired = tensor_axis == 4 and local == 2
    routes_rows = jnp.transpose(routes)
    router = jnp.transpose(w_router)
    gate_turned = jnp.swapaxes(w_gate, 1, 2)
    up_turned = jnp.swapaxes(w_up, 1, 2)
    if paired:
        turns = jnp.stack([place % 2, place // 2]).astype(jnp.int32)
        which = jnp.where(here % 2 == 0, turns[0], turns[1])
        part_of = jnp.where(here % 2 == 0, turns[1], turns[0])
        shares = 2
    else:
        turns = jnp.zeros((2,), jnp.int32)
        which, part_of, shares = jnp.int32(0), place, tensor_axis
    facts = [place, long_lens[0], short_lens[0], number, which, part_of, 1 - which]
    facts = jnp.stack([jnp.asarray(fact, jnp.int32) for fact in facts])

    def trade(rows, other):
        pairs = []
        for e in range(experts_axis):
            mask = (2 if e % 2 == 0 else 1) if other else (1 if e % 2 == 0 else 2)
            pairs += [(e * tensor_axis + t, e * tensor_axis + (t ^ mask)) for t in range(tensor_axis)]
        return lax.ppermute(rows, ("expert", "tensor"), pairs)

    sources = gather_parts(inputs[:long_local])[1:]
    normed_low, query, pair, near = project(inputs, attn_gain, w_query, w_key, w_value, long_local)
    slots, wide_slots, grad_slots_in = place_rows(
        turns.reshape(1, 2), after(routes_rows, normed_low), cotangent, capacity, padded, block, local
    )

    def by_expert(rows):
        split = rows.reshape(experts_axis, local, padded, width)
        return [split[:, j].reshape(block, width) for j in range(local)]

    def by_device(parts):
        split = [part.reshape(experts_axis, 1, padded, width) for part in parts]
        return jnp.concatenate(split, axis=1).reshape(local * block, width)

    grad_whole = over_experts(grad_slots_in)
    grad_arrived = by_expert(grad_whole)
    normed_others, others = project_others(sources, attn_gain, w_key, w_value, long_local)
    parts = (pair, others)
    if paired:
        other = jnp.stack(
            [
                lax.dynamic_index_in_dim(array, 1 - which, 0, keepdims=False)
                for array in (gate_turned, up_turned, w_down)
            ]
        )
        other = trade(after(other, sources), False)

    reach = long_span + long_local
    first = long_span - long_local - long_local * place
    long_table = jnp.pad(long_buckets, (0, 1), constant_values=-1)
    long_hot = table_hot(lax.dynamic_slice_in_dim(long_table, first, reach, 0), bucket_count)
    short_hot = table_hot(jnp.pad(short_buckets, (0, 1), constant_values=-1), bucket_count)
    spread = lambda hot: jnp.einsum(
        "cb,bh->hc", hot, rel_table, precision=precise, preferred_element_type=f32
    ).reshape(heads // 2, 2, hot.shape[0])
    mixed, far_attend, near_attend = attend_forward(
        facts, query, parts, near, spread(long_hot), spread(short_hot),
        tensor_axis, long_local, head_dim,
    )
    resid, moe_low, probs, gates, slots_in = route_rows(
        mixed, w_proj, inputs, moe_gain, router, routes_rows, slots, capacity, padded, block, local
    )

    own = (gate_turned, up_turned, w_down)
    lanes_used = shares * padded
    if paired:

        run = lambda rows, grads: expert_pass(
            facts, rows, grads, own, other, capacity, padded, lanes_used
        )
        grads_c = trade(after(grad_arrived[0], other), True)
        grads_b = trade(after(grad_arrived[1], other), False)
        grads_d = trade(grads_b, True)
        rows_a = over_experts(after(slots_in[0], grad_whole))
        rows_c = trade(after(rows_a, grads_b, grads_c), True)
        rows_b = over_experts(after(slots_in[1], rows_a, grads_b, grads_c))
        pass_a = run(rows_a, grad_arrived[0])
        rows_b = trade(after(rows_b, pass_a[1]), False)
        pass_c = run(rows_c, grads_c)
        rows_d = trade(after(rows_b, pass_c[1]), True)
        kept = add_low(pass_a[2], trade(pass_c[2], True))
        kept = over_experts(kept)
        pass_b = run(rows_b, grads_b)
        pass_d = run(after(rows_d, pass_b[1]), grads_d)
        traded = add_low(pass_b[2], trade(pass_d[2], True))
        traded = trade(traded, False)
        grad_slots = [kept, over_experts(after(traded, kept))]

        passes = [pass_a, pass_c, pass_b, pass_d]
        slot_blocks = [rows_a, rows_c, rows_b, rows_d]
        grad_blocks = [grad_arrived[0], grads_c, grads_b, grads_d]
        (sent,) = weight_pass(
            facts, slot_blocks, grad_blocks, [after_all(made[0][1], pass_d[1]) for made in passes], (), local, True
        )
        weight_grads = weight_pass(
            facts, slot_blocks, grad_blocks, [after_all(made[0][0], sent) for made in passes], (), local, False
        )
        outs_c = trade(after(pass_c[1], traded), True)
        outs_d = trade(after(pass_d[1], traded), True)
        grad_slots[0] = after(grad_slots[0], weight_grads, outs_c, outs_d)
        outs_kept = add_low(pass_a[1], outs_c)
        outs_traded = trade(add_low(pass_b[1], outs_d), False)
        held_back = outs_traded
        sent = trade(after(sent, outs_traded), False)
        send_outs = lambda: over_experts(after(by_device([outs_kept, outs_traded]), grad_slots[1]))
    else:
        grad_blocks = [gather_parts(rows) for rows in grad_arrived]
        slot_blocks = [gather_parts(over_experts(slots_in[j])) for j in range(local)]
        weight_grads, passes = (), []
        for j in range(local):
            facts_j = facts.at[4].set(j)
            passes.append(
                [
                    expert_pass(facts_j, rows, grads, own, None, capacity, padded, lanes_used)
                    for rows, grads in zip(slot_blocks[j], grad_blocks[j])
                ]
            )
            weight_grads = weight_pass(
                facts_j, slot_blocks[j], grad_blocks[j], [made[0][0] for made in passes[j]], weight_grads, local, False
            )
        send_back = lambda which: [
            over_experts(sum_parts([made[which] for made in passes[j]]).astype(bf16)) for j in range(local)
        ]
        grad_slots = send_back(2)
        send_outs = lambda: by_device(send_back(1))
        held_back = grad_slots[0]

    grad_resid, grad_mixed, moe_gain_grad, router_grad, branch = merge_rows(
        cotangent, resid, probs, moe_low, router, moe_gain, w_proj, routes_rows, slots, grad_slots,
        capacity, padded, shares,
    )
    grad_mixed = after(grad_mixed, held_back)
    collect = lambda sums, hot: jnp.einsum(
        "hc,cb->bh",
        sums.reshape(heads // 2, hot.shape[0]),
        hot,
        precision=precise,
        preferred_element_type=f32,
    )
    quick = experts_axis == 8 and tensor_axis == 4
    wide = width // 2
    halves, rel_halves, sums = [], [], []
    for half in range(2):
        made = attend_backward(
            facts, query, grad_mixed, parts, near, (far_attend, near_attend), reach, tensor_axis, long_local,
            head_dim, half,
        )
        halves.append(made[:4])
        rel_halves.append(collect(made[4], long_hot) + collect(made[5], short_hot))
        if quick:
            rel_row = jnp.pad(rel_halves[half].reshape(1, -1), ((0, 0), (0, wide - rel_halves[half].size)))
            columns = slice(half * wide, (half + 1) * wide)
            small = jnp.concatenate([rel_row, moe_gain_grad[:, columns], router_grad[:, columns]], axis=0)
            small = jnp.pad(small, ((0, 24 - small.shape[0]), (0, 0))).astype(bf16)
            blocks = weight_blocks(
                facts, (normed_low, normed_others, mixed), made[:4], branch, small, long_local, half
            )
            grad_mixed = after(grad_mixed, blocks)
            sums.append(total_blocks(*blocks))
    own_grads, near_grads, away = normed_grads(halves, w_query, w_key, w_value, long_local, tensor_axis)
    pieces = [own_grads] + [
        away[r * long_local : (r + 1) * long_local].astype(bf16) for r in range(tensor_axis - 1)
    ]
    if tensor_axis == 4:
        pieces = pieces[:3] + [pieces[3][: long_local // 2], pieces[3][long_local // 2 :]]
    grad_normed = jnp.concatenate([sum_parts(pieces), near_grads], axis=0)
    inputs_wide = inputs.astype(f32)
    scale = lax.rsqrt(jnp.mean(inputs_wide * inputs_wide, axis=-1, keepdims=True) + 1e-06)
    normed = inputs_wide * scale
    lifted = grad_normed * attn_gain.astype(f32)
    inputs_grad = grad_resid + scale * (
        lifted - normed * jnp.mean(lifted * normed, axis=-1, keepdims=True)
    )
    if quick:
        outs, smalls, gains = (), [], []
        for half in range(2):
            made = unpack_blocks(facts, *sums[half], w_query, w_key, w_value, attn_gain, outs, half)
            outs = made[:4]
            gains.append(made[4])
            smalls.append(made[5])
        query_grad, key_grad, value_grad, proj_grad = outs
        attn_gain_grad = (gains[0] + gains[1])[0]
        rel_grad = jnp.concatenate(
            [small[0, : rel.size].reshape(rel.shape) for small, rel in zip(smalls, rel_halves)], axis=1
        )
        small = jnp.concatenate(smalls, axis=1)
    else:
        whole = [jnp.concatenate([one, two], axis=1) for one, two in zip(*halves)]
        key_others = [slice(2 * r * long_local, (2 * r + 1) * long_local) for r in range(tensor_axis - 1)]
        value_others = [slice((2 * r + 1) * long_local, (2 * r + 2) * long_local) for r in range(tensor_axis - 1)]

        def keyed(index, spots):
            short = slice(index * short_len, (index + 1) * short_len)
            rows = slice(index * long_local, (index + 1) * long_local)
            lefts = jnp.concatenate([normed_low, normed_others], axis=0)
            rights = jnp.concatenate([whole[1][rows], whole[3][short]] + [whole[2][spot] for spot in spots], axis=0)
            return mm(lefts, rights, TN)

        rel_grad = jnp.concatenate(rel_halves, axis=1)
        rel_row = jnp.pad(rel_grad.reshape(1, -1), ((0, 0), (0, width - rel_grad.size)))
        small = jnp.concatenate([rel_row, moe_gain_grad, router_grad], axis=0)
        query_grad, key_grad, value_grad, proj_grad, small = lax.psum(
            (
                mm(normed_low, whole[0], TN),
                keyed(0, key_others),
                keyed(1, value_others),
                mm(mixed, branch, TN),
                small,
            ),
            ("expert", "tensor"),
        )
        attn_gain_grad = jnp.sum(
            query_grad * w_query.astype(f32) + key_grad * w_key.astype(f32) + value_grad * w_value.astype(f32),
            axis=1,
        ) / attn_gain.astype(f32)
        rel_grad = small[0, : rel_grad.size].reshape(rel_grad.shape)
    if paired:
        weight_grads = weight_fill(facts, sent, weight_grads)

    outs_back = send_outs()
    slot_places = jnp.arange(local * block, dtype=jnp.int32)
    outputs = resid
    for k in range(top_count):
        chosen = mm((wide_slots[k][:, None] == slot_places).astype(bf16), outs_back)
        outputs = outputs + gates[k][:, None] * chosen
    return (
        outputs.astype(bf16),
        inputs_grad,
        attn_gain_grad,
        query_grad,
        key_grad,
        value_grad,
        proj_grad,
        rel_grad,
        small[1],
        jnp.transpose(small[2 : 2 + experts]),
        jnp.swapaxes(weight_grads[0], 1, 2),
        jnp.swapaxes(weight_grads[1], 1, 2),
        weight_grads[2],
    )


def solution(mesh):
    return jax.shard_map(
        per_device,
        mesh=mesh,
        in_specs=(
            P(("expert", "tensor"), None),
            P(),
            P(),
            P(),
            P(),
            P(),
            P(),
            P(),
            P(),
            P("expert", None, "tensor"),
            P("expert", None, "tensor"),
            P("expert", "tensor", None),
            P(("expert", "tensor"), None),
            P(),
            P(),
            P("expert"),
            P(("expert", "tensor")),
            P(("expert", "tensor"), None),
        ),
        out_specs=(
            P(("expert", "tensor"), None),
            P(("expert", "tensor"), None),
            P(),
            P(),
            P(),
            P(),
            P(),
            P(),
            P(),
            P(),
            P("expert", None, "tensor"),
            P("expert", None, "tensor"),
            P("expert", "tensor", None),
        ),
        check_vma=False,
    )
```

time: 821 us -> 643 us (0.78); the launches traced: 817 us -> 630 us
  waiting for transfers between devices: 309 us -> 191 us
  Pallas kernels: 154 us -> 258 us
  other arithmetic: 73.5 us -> 26.9 us
  starting transfers between devices: 150 us -> 107 us
  blocking collectives: 30.8 us -> 0 us
  matrix products: 39.3 us -> 8.74 us
  local copies, waits for them, and re-layouts: 56.3 us -> 36.6 us
    ppermute x96 -> x40, waiting for transfers between devices: 275 us -> 122 us  [swap(): return lax.ppermute(rows, axis, [(i, i ^ mask) for i in range(count)])]
    pallas_call x4 -> x16, Pallas kernels: 90 us -> 191 us  [the longest x4 71.9 us: expert_pass(): pl.pallas_call(partial(expert_kernel, chunks, capacity, padded, lanes_use...]
    ppermute x0 -> x14, waiting for transfers between devices: none -> 40 us  [trade(): return lax.ppermute(rows, ('expert', 'tensor'), pairs)]
    ppermute x96 -> x40, starting transfers between devices: 106 us -> 66.3 us  [swap(): return lax.ppermute(rows, axis, [(i, i ^ mask) for i in range(count)])]
    dot_general x19 -> x2, matrix products: 37.2 us -> 6.34 us  [mm(): return lax.dot_general(left, right, dims, preferred_element_type=f32)]
    all_to_all x1 -> x0, blocking collectives: 30.8 us -> none  [over_experts(): lax.all_to_all(blocks, 'expert', 0, 0, tiled=True).reshape(rows.shape)]
    reduce_sum x13 -> x2, other arithmetic: 18.8 us -> 0.68 us  [the longest x1 0.44 us: per_device(): jnp.mean(lifted * normed, axis=-1, keepdims=True)]
    all_to_all x7 -> x6, starting transfers between devices: 44.7 us -> 27.1 us  [over_experts(): lax.all_to_all(blocks, 'expert', 0, 0, tiled=True).reshape(rows.shape)]
  transfers between devices with their start and end apart: 103 -> 60, of which waited for: 49 -> 27; matrix products, arithmetic and copies ran while one was open for 14% -> 9% of each run, Pallas kernels for 14% -> 35%
where the time goes in v2:
time: 643 us; the launch traced here: 630 us
  Pallas kernels  258 us (40%)
  waiting for transfers between devices  191 us (30%)
  starting transfers between devices  107 us (17%)
  local copies, waits for them, and re-layouts  36.6 us (6%)
  other arithmetic  26.9 us (4%)
  matrix products  8.74 us (1%)
    ppermute x40, waiting for transfers between devices, swap(): return lax.ppermute(rows, axis, [(i, i ^ mask) for i in range(count)])  122 us
    pallas_call x4, Pallas kernels, expert_pass(): pl.pallas_call(partial(expert_kernel, chunks, capacity, padded, lanes_use...  71.9 us
    ppermute x40, starting transfers between devices, swap(): return lax.ppermute(rows, axis, [(i, i ^ mask) for i in range(count)])  66.3 us
    ppermute x14, waiting for transfers between devices, trade(): return lax.ppermute(rows, ('expert', 'tensor'), pairs)  40 us
    pallas_call x2, Pallas kernels, attend_backward(): pl.pallas_call(partial(backward_kernel, count, rows, dim), grid_spec=pltp...  37.5 us
    pallas_call x2, Pallas kernels, weight_pass(): pl.pallas_call(body, grid_spec=pltpu.PrefetchScalarGridSpec(num_scalar_pr...  31.8 us
    all_to_all x6, waiting for transfers between devices, over_experts(): lax.all_to_all(blocks, 'expert', 0, 0, tiled=True).reshape(rows.shape)  28.4 us
    all_to_all x6, starting transfers between devices, over_experts(): lax.all_to_all(blocks, 'expert', 0, 0, tiled=True).reshape(rows.shape)  27.1 us
  transfers between devices with their start and end apart: 60, of which 27 were waited for; matrix products, arithmetic and copies ran while one was open for 9% of the time, Pallas kernels for 35%

profile of v2, /device:TPU:0, one launch (start us, length us, event | category | flops | bytes accessed | tf_op | source)
XLA Modules:
  0.0 630.3 jit_solution(5691522447191643408)
XLA Ops:
  8.3 6.9 %project.1 = (bf16[384,1024]{1,0:T(8,128)(2,1)}, bf16[384,1024]{1,0:T(8,128)(2,1)}, bf16[512,1024]{1,0:T(8,128)(2,1)}, bf16[256,1024]{1,0:T(8,128)(2,1)}) custom-call(bf16[384,1024]{1,0:T(8,128)(2,1)} %inputs.3, bf16[1,1024]{1,0:T(2,128)(2,1)} %reshape.131.gain, bf16[1024,1024]{1,0:T(8,128)(2,1)} %w_query.5, bf16[1024,1024]{1,0:T(8,128)(2,1)} %w_key.7, ...), custom_call_target="tpu_custom_call" | custom-call | flops 301989888 | bytes 1277952 | tf_op jit(solution)/shard_map/project/pallas_call | solution.py:139
  44.2 7.7 %project_others.1 = (bf16[768,1024]{1,0:T(8,128)(2,1)}, bf16[1536,1024]{1,0:T(8,128)(2,1)}) custom-call(bf16[1,1024]{1,0:T(2,128)(2,1)} %reshape.131.gain, bf16[1024,1024]{1,0:T(8,128)(2,1)} %w_key.7, bf16[1024,1024]{1,0:T(8,128)(2,1)} %w_value.7, bf16[256,1024]{1,0:T(8,128)(2,1)} %copy-done.17, bf16[256,1024]{1,0:T(8,128)(2,1)} %collective-permute-done.1.refs_1_, ...), custom_call_target="tpu_custom_call" | custom-call | flops 402653184 | bytes 1310720 | tf_op jit(solution)/shard_map/project_others/pallas_call | solution.py:180
  51.9 21.9 %attend_forward.1 = (bf16[384,1024]{1,0:T(8,128)(2,1)}, bf16[16,256,1024]{2,1,0:T(8,128)(2,1)}, bf16[16,128,128]{2,1,0:T(8,128)(2,1)}) custom-call(s32[7]{0:T(128)} %stack.68.facts, bf16[384,1024]{1,0:T(8,128)(2,1)} %get-tuple-element.145.query, bf16[512,1024]{1,0:T(8,128)(2,1)} %get-tuple-element.146.pair, bf16[1536,1024]{1,0:T(8,128)(2,1)} %get-tuple-element.147.others, ...), custom_call_target="tpu_custom_call" | custom-call | flops 1342177280 | bytes 1572864 | tf_op jit(solution)/shard_map/attend_forward/pallas_call | solution.py:272
  73.8 6.6 %route_rows.1 = (f32[384,1024]{1,0:T(8,128)}, bf16[384,1024]{1,0:T(8,128)(2,1)}, f32[16,384]{1,0:T(8,128)}, f32[2,384]{1,0:T(2,128)}, bf16[2,512,1024]{2,1,0:T(8,128)(2,1)}) custom-call(bf16[384,1024]{1,0:T(8,128)(2,1)} %get-tuple-element.149.mixed, bf16[1024,1024]{1,0:T(8,128)(2,1)} %w_proj.3, bf16[384,1024]{1,0:T(8,128)(2,1)} %inputs.3, ...), custom_call_target="tpu_custom_call" | custom-call | flops 201326592 | bytes 1572864 | tf_op jit(solution)/shard_map/route_rows/pallas_call | solution.py:756
  94.0 20.7 %all-to-all-done = bf16[8,64,1024]{2,1,0:T(8,128)(2,1)S(1)} async-done(((bf16[8,64,1024]{2,1,0:T(8,128)(2,1)}), bf16[8,64,1024]{2,1,0:T(8,128)(2,1)S(1)}, u32[]{:S(2)}, u32[]{:S(2)}) %all-to-all-start) | async-done | bytes 1048608 | tf_op jit(solution)/shard_map/all_to_all | solution.py:95
  116.8 5.7 all-to-all-start.2
  123.5 17.8 %expert_pass.4 = (bf16[512,704]{1,0:T(8,128)(2,1)}, bf16[512,704]{1,0:T(8,128)(2,1)}, bf16[512,704]{1,0:T(8,128)(2,1)}, bf16[512,704]{1,0:T(8,128)(2,1)}, bf16[5...) custom-call(s32[7]{0:T(128)} %stack.68.facts, ...), custom_call_target="tpu_custom_call" | custom-call | flops 1107296256 | bytes 524288 | tf_op jit(solution)/shard_map/expert_pass/pallas_call | solution.py:540
  141.3 7.4 %all-to-all-done.2 = bf16[8,64,1024]{2,1,0:T(8,128)(2,1)} async-done(((bf16[8,64,1024]{2,1,0:T(8,128)(2,1)}), bf16[8,64,1024]{2,1,0:T(8,128)(2,1)}, u32[]{:S(2)}, u32[]{:S(2)}) %all-to-all-start.2) | async-done | bytes 1048608 | tf_op jit(solution)/shard_map/all_to_all | solution.py:95
  150.3 18.0 %expert_pass.5 = (bf16[512,704]{1,0:T(8,128)(2,1)}, bf16[512,704]{1,0:T(8,128)(2,1)}, bf16[512,704]{1,0:T(8,128)(2,1)}, bf16[512,704]{1,0:T(8,128)(2,1)}, bf16[5...) custom-call(s32[7]{0:T(128)} %stack.68.facts, ...), custom_call_target="tpu_custom_call" | custom-call | flops 1107296256 | bytes 524288 | tf_op jit(solution)/shard_map/expert_pass/pallas_call | solution.py:540
  171.4 18.2 %expert_pass.6 = (bf16[512,704]{1,0:T(8,128)(2,1)}, bf16[512,704]{1,0:T(8,128)(2,1)}, bf16[512,704]{1,0:T(8,128)(2,1)}, bf16[512,704]{1,0:T(8,128)(2,1)}, bf16[5...) custom-call(s32[7]{0:T(128)} %stack.68.facts, ...), custom_call_target="tpu_custom_call" | custom-call | flops 1107296256 | bytes 524288 | tf_op jit(solution)/shard_map/expert_pass/pallas_call | solution.py:540
  195.4 17.9 %expert_pass.7 = (bf16[512,704]{1,0:T(8,128)(2,1)}, bf16[512,704]{1,0:T(8,128)(2,1)}, bf16[512,704]{1,0:T(8,128)(2,1)}, bf16[512,704]{1,0:T(8,128)(2,1)}, bf16[5...) custom-call(s32[7]{0:T(128)} %stack.68.facts, ...), custom_call_target="tpu_custom_call" | custom-call | flops 1107296256 | bytes 524288 | tf_op jit(solution)/shard_map/expert_pass/pallas_call | solution.py:540
  219.4 9.0 %collective-permute-done.11 = bf16[512,1024]{1,0:T(8,128)(2,1)S(1)} collective-permute-done((bf16[512,1024]{1,0:T(8,128)(2,1)}, bf16[512,1024]{1,0:T(8,128)(2,1)S(1)}, u32[]{:S(2)}, u32[]{:S(2)}) %collective-permute-start.11) | collective-permute-done | bytes 1048608 | tf_op jit(solution)/shard_map/ppermute | solution.py:1043
  229.4 15.2 %collective-permute-done.12 = bf16[512,1024]{1,0:T(8,128)(2,1)} collective-permute-done((bf16[512,1024]{1,0:T(8,128)(2,1)S(1)}, bf16[512,1024]{1,0:T(8,128)(2,1)}, u32[]{:S(2)}, u32[]{:S(2)}) %collective-permute-start.12) | collective-permute-done | bytes 1048608 | tf_op jit(solution)/shard_map/ppermute | solution.py:1043
  250.7 9.0 %collective-permute-done.14 = bf16[512,1024]{1,0:T(8,128)(2,1)} collective-permute-done((bf16[512,1024]{1,0:T(8,128)(2,1)}, bf16[512,1024]{1,0:T(8,128)(2,1)}, u32[]{:S(2)}, u32[]{:S(2)}) %collective-permute-start.14) | collective-permute-done | bytes 1048608 | tf_op jit(solution)/shard_map/ppermute | solution.py:1043
  263.5 16.1 %weight_pass.2 = bf16[3,704,1024]{2,1,0:T(8,128)(2,1)} custom-call(s32[7]{0:T(128)} %stack.68.facts, bf16[512,1024]{1,0:T(8,128)(2,1)} %bitcast.111, bf16[512,1024]{1,0:T(8,128)(2,1)} %collective-permute-done.7.rows_in.refs_1_, bf16[512,1024]{1,0:T(8,128)(2,1)} %copy-done.7, bf16[512,1024]{1,0:T(8,128)(2,1)} %copy-done.8, bf16[512,1024]{1,0:T(8,128)(2,1)} %bitcast.115, ...), custom_call_target="tpu_custom_call" | custom-call | flops 1107296256 | bytes 2097152 | tf_op jit(solution)/shard_map/weight_pass/pallas_call | solution.py:620
  279.6 15.7 %weight_pass.3 = (f32[2,704,1024]{2,1,0:T(8,128)}, f32[2,704,1024]{2,1,0:T(8,128)}, f32[2,704,1024]{2,1,0:T(8,128)}) custom-call(s32[7]{0:T(128)} %stack.68.facts, bf16[512,1024]{1,0:T(8,128)(2,1)} %bitcast.112, bf16[512,1024]{1,0:T(8,128)(2,1)} %collective-permute-done.7.rows_in.refs_1_, bf16[512,1024]{1,0:T(8,128)(2,1)} %copy-done.7, ...), custom_call_target="tpu_custom_call" | custom-call | flops 1107296256 | bytes 2097152 | tf_op jit(solution)/shard_map/weight_pass/pallas_call | solution.py:620
  296.3 7.4 %merge_rows.1 = (f32[384,1024]{1,0:T(8,128)}, bf16[384,1024]{1,0:T(8,128)(2,1)}, f32[1,1024]{1,0:T(1,128)}, f32[16,1024]{1,0:T(8,128)}, bf16[384,1024]{1,0:T(8,128)(2,1)}) custom-call(bf16[384,1024]{1,0:T(8,128)(2,1)} %cotangent.1, f32[384,1024]{1,0:T(8,128)} %get-tuple-element.153.resid, f32[16,384]{1,0:T(8,128)} %get-tuple-element.178.probs, ...), custom_call_target="tpu_custom_call" | custom-call | flops 301989888 | bytes 983040 | tf_op jit(solution)/shard_map/merge_rows/pallas_call | solution.py:832
  305.2 18.9 %attend_backward.2 = (bf16[384,512]{1,0:T(8,128)(2,1)}, bf16[512,512]{1,0:T(8,128)(2,1)}, bf16[1536,512]{1,0:T(8,128)(2,1)}, bf16[256,512]{1,0:T(8,128)(2,1)}, f...) custom-call(s32[7]{0:T(128)} %stack.68.facts, bf16[384,1024]{1,0:T(8,128)(2,1)} %get-tuple-element.145.query, ...), custom_call_target="tpu_custom_call" | custom-call | flops 1677721600 | bytes 1048576 | tf_op jit(solution)/shard_map/attend_backward/pallas_call | solution.py:385
  327.1 11.4 %weight_blocks.2 = (bf16[16,136,512]{2,1,0:T(8,128)(2,1)}, bf16[16,136,512]{2,1,0:T(8,128)(2,1)}) custom-call(s32[7]{0:T(128)} %stack.68.facts, bf16[384,1024]{1,0:T(8,128)(2,1)} %get-tuple-element.150.normed, bf16[768,1024]{1,0:T(8,128)(2,1)} %get-tuple-element.241.normed_others, bf16[384,1024]{1,0:T(8,128)(2,1)} %get-tuple-element.149.mixed, ...), custom_call_target="tpu_custom_call" | custom-call | flops 402653184 | bytes 524288 | tf_op jit(solution)/shard_map/weight_blocks/pallas_call | solution.py:894
  338.5 18.7 %attend_backward.3 = (bf16[384,512]{1,0:T(8,128)(2,1)}, bf16[512,512]{1,0:T(8,128)(2,1)}, bf16[1536,512]{1,0:T(8,128)(2,1)}, bf16[256,512]{1,0:T(8,128)(2,1)}, f...) custom-call(s32[7]{0:T(128)} %stack.68.facts, bf16[384,1024]{1,0:T(8,128)(2,1)} %get-tuple-element.145.query, ...), custom_call_target="tpu_custom_call" | custom-call | flops 1677721600 | bytes 1048576 | tf_op jit(solution)/shard_map/attend_backward/pallas_call | solution.py:385
  360.2 11.6 %weight_blocks.3 = (bf16[16,136,512]{2,1,0:T(8,128)(2,1)}, bf16[16,136,512]{2,1,0:T(8,128)(2,1)}) custom-call(s32[7]{0:T(128)} %stack.68.facts, bf16[384,1024]{1,0:T(8,128)(2,1)} %get-tuple-element.150.normed, bf16[768,1024]{1,0:T(8,128)(2,1)} %get-tuple-element.241.normed_others, bf16[384,1024]{1,0:T(8,128)(2,1)} %get-tuple-element.149.mixed, ...), custom_call_target="tpu_custom_call" | custom-call | flops 402653184 | bytes 524288 | tf_op jit(solution)/shard_map/weight_blocks/pallas_call | solution.py:894
  372.5 13.3 %normed_grads.1 = (f32[256,1024]{1,0:T(8,128)}, f32[128,1024]{1,0:T(8,128)}, f32[768,1024]{1,0:T(8,128)}) custom-call(bf16[384,512]{1,0:T(8,128)(2,1)} %get-tuple-element.237.grad_query.refs_0_, bf16[512,512]{1,0:T(8,128)(2,1)} %get-tuple-element.238.grad_pair.refs_1_, bf16[1536,512]{1,0:T(8,128)(2,1)} %get-tuple-element.239.grad_others.refs_2_, ...), custom_call_target="tpu_custom_call" | custom-call | flops 536870912 | bytes 1048576 | tf_op jit(solution)/shard_map/normed_grads/pallas_call | solution.py:443
  422.6 8.8 %collective-permute-done.25 = bf16[4,136,512]{2,1,0:T(8,128)(2,1)S(1)} collective-permute-done((bf16[4,136,512]{2,1,0:T(8,128)(2,1)S(1)}, bf16[4,136,512]{2,1,0:T(8,128)(2,1)S(1)}, u32[]{:S(2)}, u32[]{:S(2)}) %collective-permute-start.25) | collective-permute-done | bytes 557088 | tf_op jit(solution)/shard_map/ppermute | solution.py:40
  447.4 17.1 %collective-permute-start.42 = (bf16[136,512]{1,0:T(8,128)(2,1)S(1)}, bf16[136,512]{1,0:T(8,128)(2,1)S(1)}, u32[]{:S(2)}, u32[]{:S(2)}) collective-permute-start(bf16[136,512]{1,0:T(8,128)(2,1)S(1)} %get-tuple-element.320), channel_id=1, source_target_pairs={{0,8},{4,12},{8,0},{12,4},{16,24},{20,28},{24,16},{28,20},{1,9},{5... | collective-permute-start | bytes 417800 | tf_op jit(solution)/shard_map/ppermute | solution.py:40
  471.6 7.2 %collective-permute-done.43 = bf16[136,512]{1,0:T(8,128)(2,1)S(1)} collective-permute-done((bf16[136,512]{1,0:T(8,128)(2,1)S(1)}, bf16[136,512]{1,0:T(8,128)(2,1)S(1)}, u32[]{:S(2)}, u32[]{:S(2)}) %collective-permute-start.43) | collective-permute-done | bytes 139296 | tf_op jit(solution)/shard_map/ppermute | solution.py:40
  487.2 6.7 %collective-permute-done.46 = bf16[136,512]{1,0:T(8,128)(2,1)S(1)} collective-permute-done((bf16[136,512]{1,0:T(8,128)(2,1)S(1)}, bf16[136,512]{1,0:T(8,128)(2,1)S(1)}, u32[]{:S(2)}, u32[]{:S(2)}) %collective-permute-start.46) | collective-permute-done | bytes 139296 | tf_op jit(solution)/shard_map/ppermute | solution.py:40
  497.2 52.0 %collective-permute-done.32 = bf16[4,136,512]{2,1,0:T(8,128)(2,1)S(1)} collective-permute-done((bf16[4,136,512]{2,1,0:T(8,128)(2,1)S(1)}, bf16[4,136,512]{2,1,0:T(8,128)(2,1)S(1)}, u32[]{:S(2)}, u32[]{:S(2)}) %collective-permute-start.32) | collective-permute-done | bytes 557088 | tf_op jit(solution)/shard_map/ppermute | solution.py:40
  551.4 6.7 %collective-permute-done.48 = bf16[4,136,512]{2,1,0:T(8,128)(2,1)S(1)} collective-permute-done((bf16[4,136,512]{2,1,0:T(8,128)(2,1)S(1)}, bf16[4,136,512]{2,1,0:T(8,128)(2,1)S(1)}, u32[]{:S(2)}, u32[]{:S(2)}) %collective-permute-start.48) | collective-permute-done | bytes 557088 | tf_op jit(solution)/shard_map/ppermute | solution.py:40
  561.3 8.7 %collective-permute-done.34 = bf16[2,136,512]{2,1,0:T(8,128)(2,1)S(1)} collective-permute-done((bf16[2,136,512]{2,1,0:T(8,128)(2,1)S(1)}, bf16[2,136,512]{2,1,0:T(8,128)(2,1)S(1)}, u32[]{:S(2)}, u32[]{:S(2)}) %collective-permute-start.34) | collective-permute-done | bytes 278560 | tf_op jit(solution)/shard_map/ppermute | solution.py:40
  597.6 6.6 %weight_fill.1 = (f32[2,704,1024]{2,1,0:T(8,128)}, f32[2,704,1024]{2,1,0:T(8,128)}, f32[2,704,1024]{2,1,0:T(8,128)}) custom-call(s32[7]{0:T(128)} %stack.68.facts, bf16[3,704,1024]{2,1,0:T(8,128)(2,1)} %collective-permute-done.53.source, f32[2,704,1024]{2,1,0:T(8,128)} %get-tuple-element.228.refs_0_, ...), custom_call_target="tpu_custom_call", output_to_operand_aliasing={{0}: (2, {}), {1}: (3, {}), {2}: (4, {})} | custom-call | bytes 1622016 | tf_op jit(solution)/shard_map/weight_fill/pallas_call | solution.py:649
  604.2 9.6 %unpack_blocks.2 = (f32[1024,1024]{1,0:T(8,128)}, f32[1024,1024]{1,0:T(8,128)}, f32[1024,1024]{1,0:T(8,128)}, f32[1024,1024]{1,0:T(8,128)}, f32[1,1024]{1,0:T(1,128)}, /*index=5*/f32[24,512]{1,0:T(8,128)}) custom-call(s32[7]{0:T(128)} %stack.68.facts, bf16[16,136,512]{2,1,0:T(8,128)(2,1)} %copy-done.12, bf16[16,136,512]{2,1,0:T(8,128)(2,1)} %collective-permute-done.36.far, ...), custom_call_target="tpu_custom_call" | custom-call | flops 786432 | bytes 1572864 | tf_op jit(solution)/shard_map/unpack_blocks/pallas_call | solution.py:959
  615.4 9.7 %unpack_blocks.3 = (f32[1024,1024]{1,0:T(8,128)}, f32[1024,1024]{1,0:T(8,128)}, f32[1024,1024]{1,0:T(8,128)}, f32[1024,1024]{1,0:T(8,128)}, f32[1,1024]{1,0:T(1,128)}, /*index=5*/f32[24,512]{1,0:T(8,128)}) custom-call(s32[7]{0:T(128)} %stack.68.facts, ...), custom_call_target="tpu_custom_call", output_to_operand_aliasing={{0}: (7, {}), {1}: (8, {}), {2}: (9, {}), {3}: (10, {})} | custom-call | flops 786432 | bytes 1572864 | tf_op jit(solution)/shard_map/unpack_blocks/pallas_call | solution.py:959
  (283 shorter events, 199.2 us)
Async XLA Ops:
  2.5 26.0 %collective-permute-start = (bf16[256,1024]{1,0:T(8,128)(2,1)}, bf16[256,1024]{1,0:T(8,128)(2,1)S(1)}, u32[]{:S(2)}, u32[]{:S(2)}) collective-permute-start(bf16[256,1024]{1,0:T(8,128)(2,1)} %slice.181), channel_id=1, source_target_pairs={{0,1},{1,0},{2,3},{3,2},{4,5},{5,4},{6,7},{7,6},{8,9},{9,8},{10,11... | collective-permute-start | bytes 1572872 | tf_op jit(solution)/shard_map/ppermute | solution.py:40
  5.5 23.6 %collective-permute-start.1 = (bf16[256,1024]{1,0:T(8,128)(2,1)}, bf16[256,1024]{1,0:T(8,128)(2,1)}, u32[]{:S(2)}, u32[]{:S(2)}) collective-permute-start(bf16[256,1024]{1,0:T(8,128)(2,1)} %slice.181), channel_id=1, source_target_pairs={{0,2},{1,3},{2,0},{3,1},{4,6},{5,7},{6,4},{7,5},{8,10},{9,11},{10,... | collective-permute-start | bytes 1572872 | tf_op jit(solution)/shard_map/ppermute | solution.py:40
  19.6 63.8 %all-to-all-start.1 = ((bf16[8,128,1024]{2,1,0:T(8,128)(2,1)}), bf16[8,128,1024]{2,1,0:T(8,128)(2,1)}, u32[]{:S(2)}, u32[]{:S(2)}) async-start(bf16[8,128,1024]{2,1,0:T(8,128)(2,1)} %bitcast.123), calls=%async_computation.1 | async-start | bytes 4194304 | tf_op jit(solution)/shard_map/all_to_all | solution.py:95
  38.6 52.3 %collective-permute-start.4 = (bf16[3,704,1024]{2,1,0:T(8,128)(2,1)}, bf16[3,704,1024]{2,1,0:T(8,128)(2,1)}, u32[]{:S(2)}, u32[]{:S(2)}) collective-permute-start(bf16[3,704,1024]{2,1,0:T(8,128)(2,1)} %pad_maximum_fusion), channel_id=1, source_target_pairs={{0,1},{1,0},{2,3},{3,2},{4,6},{5,7},{6,4},{7,5},{8,9},{9,8},{10,11... | collective-permute-start | bytes 12976136 | tf_op jit(solution)/shard_map/ppermute | solution.py:1043
  83.4 31.3 %all-to-all-start = ((bf16[8,64,1024]{2,1,0:T(8,128)(2,1)}), bf16[8,64,1024]{2,1,0:T(8,128)(2,1)S(1)}, u32[]{:S(2)}, u32[]{:S(2)}) async-start(bf16[8,64,1024]{2,1,0:T(8,128)(2,1)} %bitcast.13), calls=%async_computation | async-start | bytes 2097152 | tf_op jit(solution)/shard_map/all_to_all | solution.py:95
  90.9 25.7 %collective-permute-start.5 = (bf16[512,1024]{1,0:T(8,128)(2,1)}, bf16[512,1024]{1,0:T(8,128)(2,1)S(1)}, u32[]{:S(2)}, u32[]{:S(2)}) collective-permute-start(bf16[512,1024]{1,0:T(8,128)(2,1)} %bitcast.22), channel_id=1, source_target_pairs={{0,1},{1,0},{2,3},{3,2},{4,6},{5,7},{6,4},{7,5},{8,9},{9,8},{10,11... | collective-permute-start | bytes 3145736 | tf_op jit(solution)/shard_map/ppermute | solution.py:1043
  92.4 24.3 %collective-permute-start.6 = (bf16[512,1024]{1,0:T(8,128)(2,1)S(1)}, bf16[512,1024]{1,0:T(8,128)(2,1)}, u32[]{:S(2)}, u32[]{:S(2)}) collective-permute-start(bf16[512,1024]{1,0:T(8,128)(2,1)S(1)} %bitcast.113), channel_id=1, source_target_pairs={{0,2},{1,3},{2,0},{3,1},{4,5},{5,4},{6,7},{7,6},{8,10},{9,11},{10,... | collective-permute-start | bytes 3145736 | tf_op jit(solution)/shard_map/ppermute | solution.py:1043
  116.8 32.0 %all-to-all-start.2 = ((bf16[8,64,1024]{2,1,0:T(8,128)(2,1)}), bf16[8,64,1024]{2,1,0:T(8,128)(2,1)}, u32[]{:S(2)}, u32[]{:S(2)}) async-start(bf16[8,64,1024]{2,1,0:T(8,128)(2,1)} %bitcast.122), calls=%async_computation.2 | async-start | bytes 2097152 | tf_op jit(solution)/shard_map/all_to_all | solution.py:95
  122.5 27.8 %collective-permute-start.7 = (bf16[512,1024]{1,0:T(8,128)(2,1)S(1)}, bf16[512,1024]{1,0:T(8,128)(2,1)}, u32[]{:S(2)}, u32[]{:S(2)}) collective-permute-start(bf16[512,1024]{1,0:T(8,128)(2,1)S(1)} %bitcast.109), channel_id=1, source_target_pairs={{0,2},{1,3},{2,0},{3,1},{4,5},{5,4},{6,7},{7,6},{8,10},{9,11},{10,... | collective-permute-start | bytes 3145736 | tf_op jit(solution)/shard_map/ppermute | solution.py:1043
  169.4 25.0 %collective-permute-start.10 = (bf16[512,1024]{1,0:T(8,128)(2,1)S(1)}, bf16[512,1024]{1,0:T(8,128)(2,1)S(1)}, u32[]{:S(2)}, u32[]{:S(2)}) collective-permute-start(bf16[512,1024]{1,0:T(8,128)(2,1)S(1)} %collective-permute-done.5.grads_in.refs_6_), channel_id=1, source_target_pairs={{0,2},{1,3},{2,0},{3,1},{4,5},{5,4},{6,7},{7,6},{8,10},{9,11},{10,... | collective-permute-start | bytes 3145736 | tf_op jit(solution)/shard_map/ppermute | solution.py:1043
  170.4 44.0 %collective-permute-start.16 = (bf16[512,1024]{1,0:T(8,128)(2,1)}, bf16[512,1024]{1,0:T(8,128)(2,1)S(1)}, u32[]{:S(2)}, u32[]{:S(2)}) collective-permute-start(bf16[512,1024]{1,0:T(8,128)(2,1)} %get-tuple-element.175), channel_id=1, source_target_pairs={{0,2},{1,3},{2,0},{3,1},{4,5},{5,4},{6,7},{7,6},{8,10},{9,11},{10,... | collective-permute-start | bytes 3145736 | tf_op jit(solution)/shard_map/ppermute | solution.py:1043
  215.8 30.1 %all-to-all-start.3 = ((bf16[8,64,1024]{2,1,0:T(8,128)(2,1)}), bf16[8,64,1024]{2,1,0:T(8,128)(2,1)S(1)}, u32[]{:S(2)}, u32[]{:S(2)}) async-start(bf16[8,64,1024]{2,1,0:T(8,128)(2,1)} %bitcast.31), calls=%async_computation.3 | async-start | bytes 2097152 | tf_op jit(solution)/shard_map/all_to_all | solution.py:95
  245.9 49.4 %all-to-all-start.4 = ((bf16[8,64,1024]{2,1,0:T(8,128)(2,1)}), bf16[8,64,1024]{2,1,0:T(8,128)(2,1)S(1)}, u32[]{:S(2)}, u32[]{:S(2)}) async-start(bf16[8,64,1024]{2,1,0:T(8,128)(2,1)} %bitcast.33), calls=%async_computation.4 | async-start | bytes 2097152 | tf_op jit(solution)/shard_map/all_to_all | solution.py:95
  249.6 45.7 %collective-permute-start.13 = (bf16[512,1024]{1,0:T(8,128)(2,1)}, bf16[512,1024]{1,0:T(8,128)(2,1)S(1)}, u32[]{:S(2)}, u32[]{:S(2)}) collective-permute-start(bf16[512,1024]{1,0:T(8,128)(2,1)} %get-tuple-element.171), channel_id=1, source_target_pairs={{0,2},{1,3},{2,0},{3,1},{4,5},{5,4},{6,7},{7,6},{8,10},{9,11},{10,... | collective-permute-start | bytes 3145736 | tf_op jit(solution)/shard_map/ppermute | solution.py:1043
  262.6 42.6 %collective-permute-start.15 = (bf16[512,1024]{1,0:T(8,128)(2,1)}, bf16[512,1024]{1,0:T(8,128)(2,1)}, u32[]{:S(2)}, u32[]{:S(2)}) collective-permute-start(bf16[512,1024]{1,0:T(8,128)(2,1)} %add_convert_fusion.3), channel_id=1, source_target_pairs={{0,1},{1,0},{2,3},{3,2},{4,6},{5,7},{6,4},{7,5},{8,9},{9,8},{10,11... | collective-permute-start | bytes 3145736 | tf_op jit(solution)/shard_map/ppermute | solution.py:1043
  338.5 62.5 %collective-permute-start.21 = (bf16[16,136,512]{2,1,0:T(8,128)(2,1)}, bf16[16,136,512]{2,1,0:T(8,128)(2,1)}, u32[]{:S(2)}, u32[]{:S(2)}) collective-permute-start(bf16[16,136,512]{2,1,0:T(8,128)(2,1)} %get-tuple-element.248), channel_id=1, source_target_pairs={{0,4},{4,0},{8,12},{12,8},{16,20},{20,16},{24,28},{28,24},{1,5},{5... | collective-permute-start | bytes 6684680 | tf_op jit(solution)/shard_map/ppermute | solution.py:40
  371.8 33.9 %collective-permute-start.37 = (bf16[16,136,512]{2,1,0:T(8,128)(2,1)}, bf16[16,136,512]{2,1,0:T(8,128)(2,1)}, u32[]{:S(2)}, u32[]{:S(2)}) collective-permute-start(bf16[16,136,512]{2,1,0:T(8,128)(2,1)} %get-tuple-element.261), channel_id=1, source_target_pairs={{0,4},{4,0},{8,12},{12,8},{16,20},{20,16},{24,28},{28,24},{1,5},{5... | collective-permute-start | bytes 6684680 | tf_op jit(solution)/shard_map/ppermute | solution.py:40
  395.2 196.0 %all-to-all-start.5 = ((bf16[8,128,1024]{2,1,0:T(8,128)(2,1)}), bf16[8,128,1024]{2,1,0:T(8,128)(2,1)}, u32[]{:S(2)}, u32[]{:S(2)}) async-start(bf16[8,128,1024]{2,1,0:T(8,128)(2,1)} %bitcast.35), calls=%async_computation.5 | async-start | bytes 4194304 | tf_op jit(solution)/shard_map/all_to_all | solution.py:95
  420.7 22.2 %collective-permute-start.41 = (bf16[4,136,512]{2,1,0:T(8,128)(2,1)S(1)}, bf16[4,136,512]{2,1,0:T(8,128)(2,1)S(1)}, u32[]{:S(2)}, u32[]{:S(2)}) collective-permute-start(bf16[4,136,512]{2,1,0:T(8,128)(2,1)S(1)} %pad_maximum_fusion.6), channel_id=1, source_target_pairs={{0,2},{1,3},{2,0},{3,1},{4,6},{5,7},{6,4},{7,5},{8,10},{9,11},{10,... | collective-permute-start | bytes 1671176 | tf_op jit(solution)/shard_map/ppermute | solution.py:40
  436.6 30.4 %collective-permute-start.27 = (bf16[136,512]{1,0:T(8,128)(2,1)S(1)}, bf16[136,512]{1,0:T(8,128)(2,1)S(1)}, u32[]{:S(2)}, u32[]{:S(2)}) collective-permute-start(bf16[136,512]{1,0:T(8,128)(2,1)S(1)} %get-tuple-element.325), channel_id=1, source_target_pairs={{0,16},{4,20},{8,24},{12,28},{16,0},{20,4},{24,8},{28,12},{1,17},{... | collective-permute-start | bytes 417800 | tf_op jit(solution)/shard_map/ppermute | solution.py:40
  436.6 30.4 %collective-permute-start.26 = (bf16[136,512]{1,0:T(8,128)(2,1)S(1)}, bf16[136,512]{1,0:T(8,128)(2,1)S(1)}, u32[]{:S(2)}, u32[]{:S(2)}) collective-permute-start(bf16[136,512]{1,0:T(8,128)(2,1)S(1)} %get-tuple-element.323), channel_id=1, source_target_pairs={{0,8},{4,12},{8,0},{12,4},{16,24},{20,28},{24,16},{28,20},{1,9},{5... | collective-permute-start | bytes 417800 | tf_op jit(solution)/shard_map/ppermute | solution.py:40
  443.9 24.7 %collective-permute-start.44 = (bf16[136,512]{1,0:T(8,128)(2,1)S(1)}, bf16[136,512]{1,0:T(8,128)(2,1)S(1)}, u32[]{:S(2)}, u32[]{:S(2)}) collective-permute-start(bf16[136,512]{1,0:T(8,128)(2,1)S(1)} %get-tuple-element.321), channel_id=1, source_target_pairs={{0,24},{4,28},{8,16},{12,20},{16,8},{20,12},{24,0},{28,4},{1,25},{... | collective-permute-start | bytes 417800 | tf_op jit(solution)/shard_map/ppermute | solution.py:40
  447.4 31.4 %collective-permute-start.43 = (bf16[136,512]{1,0:T(8,128)(2,1)S(1)}, bf16[136,512]{1,0:T(8,128)(2,1)S(1)}, u32[]{:S(2)}, u32[]{:S(2)}) collective-permute-start(bf16[136,512]{1,0:T(8,128)(2,1)S(1)} %get-tuple-element.322), channel_id=1, source_target_pairs={{0,16},{4,20},{8,24},{12,28},{16,0},{20,4},{24,8},{28,12},{1,17},{... | collective-permute-start | bytes 417800 | tf_op jit(solution)/shard_map/ppermute | solution.py:40
  447.4 31.4 %collective-permute-start.42 = (bf16[136,512]{1,0:T(8,128)(2,1)S(1)}, bf16[136,512]{1,0:T(8,128)(2,1)S(1)}, u32[]{:S(2)}, u32[]{:S(2)}) collective-permute-start(bf16[136,512]{1,0:T(8,128)(2,1)S(1)} %get-tuple-element.320), channel_id=1, source_target_pairs={{0,8},{4,12},{8,0},{12,4},{16,24},{20,28},{24,16},{28,20},{1,9},{5... | collective-permute-start | bytes 417800 | tf_op jit(solution)/shard_map/ppermute | solution.py:40
  484.0 113.6 %collective-permute-start.53 = (bf16[3,704,1024]{2,1,0:T(8,128)(2,1)}, bf16[3,704,1024]{2,1,0:T(8,128)(2,1)}, u32[]{:S(2)}, u32[]{:S(2)}) collective-permute-start(bf16[3,704,1024]{2,1,0:T(8,128)(2,1)} %weight_pass.2), channel_id=1, source_target_pairs={{0,1},{1,0},{2,3},{3,2},{4,6},{5,7},{6,4},{7,5},{8,9},{9,8},{10,11... | collective-permute-start | bytes 12976136 | tf_op jit(solution)/shard_map/ppermute | solution.py:1043
  484.2 65.0 %collective-permute-start.32 = (bf16[4,136,512]{2,1,0:T(8,128)(2,1)S(1)}, bf16[4,136,512]{2,1,0:T(8,128)(2,1)S(1)}, u32[]{:S(2)}, u32[]{:S(2)}) collective-permute-start(bf16[4,136,512]{2,1,0:T(8,128)(2,1)S(1)} %pad_maximum_fusion.4), channel_id=1, source_target_pairs={{0,1},{1,0},{2,3},{3,2},{4,5},{5,4},{6,7},{7,6},{8,9},{9,8},{10,11... | collective-permute-start | bytes 1671176 | tf_op jit(solution)/shard_map/ppermute | solution.py:40
  486.3 64.1 %collective-permute-start.33 = (bf16[4,136,512]{2,1,0:T(8,128)(2,1)S(1)}, bf16[4,136,512]{2,1,0:T(8,128)(2,1)S(1)}, u32[]{:S(2)}, u32[]{:S(2)}) collective-permute-start(bf16[4,136,512]{2,1,0:T(8,128)(2,1)S(1)} %pad_maximum_fusion.4), channel_id=1, source_target_pairs={{0,2},{1,3},{2,0},{3,1},{4,6},{5,7},{6,4},{7,5},{8,10},{9,11},{10,... | collective-permute-start | bytes 1671176 | tf_op jit(solution)/shard_map/ppermute | solution.py:40
  494.0 64.2 %collective-permute-start.48 = (bf16[4,136,512]{2,1,0:T(8,128)(2,1)S(1)}, bf16[4,136,512]{2,1,0:T(8,128)(2,1)S(1)}, u32[]{:S(2)}, u32[]{:S(2)}) collective-permute-start(bf16[4,136,512]{2,1,0:T(8,128)(2,1)S(1)} %pad_maximum_fusion.7), channel_id=1, source_target_pairs={{0,1},{1,0},{2,3},{3,2},{4,5},{5,4},{6,7},{7,6},{8,9},{9,8},{10,11... | collective-permute-start | bytes 1671176 | tf_op jit(solution)/shard_map/ppermute | solution.py:40
  494.1 65.2 %collective-permute-start.49 = (bf16[4,136,512]{2,1,0:T(8,128)(2,1)S(1)}, bf16[4,136,512]{2,1,0:T(8,128)(2,1)S(1)}, u32[]{:S(2)}, u32[]{:S(2)}) collective-permute-start(bf16[4,136,512]{2,1,0:T(8,128)(2,1)S(1)} %pad_maximum_fusion.7), channel_id=1, source_target_pairs={{0,2},{1,3},{2,0},{3,1},{4,6},{5,7},{6,4},{7,5},{8,10},{9,11},{10,... | collective-permute-start | bytes 1671176 | tf_op jit(solution)/shard_map/ppermute | solution.py:40
  549.2 33.9 %collective-permute-start.20 = (bf16[256,1024]{1,0:T(8,128)(2,1)S(1)}, bf16[256,1024]{1,0:T(8,128)(2,1)S(1)}, u32[]{:S(2)}, u32[]{:S(2)}) collective-permute-start(bf16[256,1024]{1,0:T(8,128)(2,1)S(1)} %pad_maximum_fusion.9), channel_id=1, source_target_pairs={{0,2},{1,3},{2,0},{3,1},{4,6},{5,7},{6,4},{7,5},{8,10},{9,11},{10,... | collective-permute-start | bytes 1572872 | tf_op jit(solution)/shard_map/ppermute | solution.py:40
  576.0 28.2 %collective-permute-start.36 = (bf16[16,136,512]{2,1,0:T(8,128)(2,1)S(1)}, bf16[16,136,512]{2,1,0:T(8,128)(2,1)}, u32[]{:S(2)}, u32[]{:S(2)}) collective-permute-start(bf16[16,136,512]{2,1,0:T(8,128)(2,1)S(1)} %constant_dynamic-update-slice_fusion.near), channel_id=1, source_target_pairs={{0,4},{4,0},{8,12},{12,8},{16,20},{20,16},{24,28},{28,24},{1,5},{5... | collective-permute-start | bytes 6684680 | tf_op jit(solution)/shard_map/ppermute | solution.py:40
  579.3 36.1 %collective-permute-start.52 = (bf16[16,136,512]{2,1,0:T(8,128)(2,1)}, bf16[16,136,512]{2,1,0:T(8,128)(2,1)}, u32[]{:S(2)}, u32[]{:S(2)}) collective-permute-start(bf16[16,136,512]{2,1,0:T(8,128)(2,1)} %constant_dynamic-update-slice_fusion.8.near), channel_id=1, source_target_pairs={{0,4},{4,0},{8,12},{12,8},{16,20},{20,16},{24,28},{28,24},{1,5},{5... | collective-permute-start | bytes 6684680 | tf_op jit(solution)/shard_map/ppermute | solution.py:40
  (62 other events, 885.4 us)

commit v3 on v2

--- a/solution.py
+++ b/solution.py
@@ -27,8 +27,8 @@
     )
 
 
-def cost(flops, moved):
-    return pl.CostEstimate(flops=int(flops) // 8, bytes_accessed=int(moved) // 8, transcendentals=0)
+def cost(micros):
+    return pl.CostEstimate(flops=int(micros * 1.15e9), bytes_accessed=0, transcendentals=0)
 
 
 def table_hot(table, count):
@@ -46,7 +46,7 @@
 
 def after_all(values, *others):
     leaves = tuple(jax.tree.leaves(others))
-    return lax.optimization_barrier(tuple(values) + leaves)[: len(values)]
+    return list(lax.optimization_barrier(tuple(values) + leaves)[: len(values)])
 
 
 def ring_gather(rows, move):
@@ -55,19 +55,23 @@
     return [rows, first, second, move(first[:half], 1), move(second[half:], 0)]
 
 
-def ring_sum(parts, move):
+def ring_sum_first(parts, move):
     half = parts[3].shape[0]
     left = move(parts[3], 0)
     right = move(parts[4], 1)
-    to_second = jnp.concatenate(
-        [(parts[2][:half].astype(f32) + left.astype(f32)).astype(bf16), parts[2][half:]], axis=0
-    )
-    to_first = jnp.concatenate(
-        [parts[1][:half], (parts[1][half:].astype(f32) + right.astype(f32)).astype(bf16)], axis=0
-    )
+    to_second = jnp.concatenate([add_low(parts[2][:half], left), parts[2][half:]], axis=0)
+    to_first = jnp.concatenate([parts[1][:half], add_low(parts[1][half:], right)], axis=0)
+    return parts[0], to_first, to_second
+
+
+def ring_sum_second(own, to_first, to_second, move):
     first = move(to_first, 0)
     second = move(to_second, 1)
-    return parts[0].astype(f32) + first.astype(f32) + second.astype(f32)
+    return own.astype(f32) + first.astype(f32) + second.astype(f32)
+
+
+def ring_sum(parts, move):
+    return ring_sum_second(*ring_sum_first(parts, move), move)
 
 
 def in_plane(rows, way):
@@ -99,16 +103,27 @@
     return (left.astype(f32) + right.astype(f32)).astype(bf16)
 
 
-def total_blocks(near, far):
-    rest = add_low(near, swap(far, "expert", 1))
-    rest = ring_sum([rest[0:4], rest[4:8], rest[8:12], rest[12:14], rest[14:16]], in_plane).astype(bf16)
+def sum_cores(near, far):
+    return add_low(near, swap(far, "expert", 1))
+
+
+def plane_parts(rest):
+    return [rest[0:4], rest[4:8], rest[8:12], rest[12:14], rest[14:16]]
+
+
+def sum_depth(rest):
     own = rest[0].astype(f32)
     for m in range(1, 4):
         own = own + swap(rest[m], "expert", 2 * m).astype(f32)
-    own = own.astype(bf16)
-    rest = jnp.stack([own] + [swap(own, "expert", 2 * m) for m in range(1, 4)])
-    near = jnp.concatenate(ring_gather(rest, in_plane), axis=0)
-    return near, swap(near, "expert", 1)
+    return own.astype(bf16)
+
+
+def spread_depth(own):
+    return jnp.stack([own] + [swap(own, "expert", 2 * m) for m in range(1, 4)])
+
+
+def spread_plane(rest):
+    return jnp.concatenate(ring_gather(rest, in_plane), axis=0)
 
 
 def project_kernel(long_local, inputs, gain, w_query, w_key, w_value, normed, query, pair, near, held):
@@ -149,7 +164,7 @@
         ],
         scratch_shapes=[pltpu.VMEM((rows, width), bf16)],
         compiler_params=params(),
-        cost_estimate=cost(6 * rows * width * width, 6 * width * width + 10 * rows * width),
+        cost_estimate=cost(6.9),
         name="project",
     )(inputs, gain.reshape(1, width), w_query, w_key, w_value)
 
@@ -188,7 +203,7 @@
         ],
         scratch_shapes=[pltpu.VMEM((rows, width), bf16)],
         compiler_params=params(),
-        cost_estimate=cost(4 * rows * width * width, 4 * width * width + 8 * rows * width),
+        cost_estimate=cost(7.7),
         name="project_others",
     )(gain.reshape(1, width), w_key, w_value, *sources)
 
@@ -201,59 +216,91 @@
     return views
 
 
+def own_lanes(head, dim, shape, axis):
+    place = lax.broadcasted_iota(jnp.int32, shape, axis)
+    return (place >= head * dim) & (place < (head + 1) * dim)
+
+
 def forward_kernel(
-    count, rows, dim, facts, query, pair, others, near, far_bias, near_bias, mixed, far_attend, near_attend, window
+    count,
+    rows,
+    dim,
+    facts,
+    query,
+    pair,
+    others,
+    near,
+    far_bias,
+    near_bias,
+    mixed,
+    far_attend,
+    near_attend,
+    window,
+    scores,
 ):
     place, far_len, near_len = facts[0], facts[1], facts[2]
     scale = 1.0 / math.sqrt(dim)
     views = key_value_views(pair, others, count, rows)
     short = near.shape[0] // 2
-    reach = far_bias.shape[-1]
+    band, reach = window.shape[1:]
+    low = (query[...].astype(f32) * scale).astype(bf16)
+    starts = [(place ^ r) * rows for r in range(count)]
+    spot = lax.broadcasted_iota(jnp.int32, (1, rows), 1)
+    kept = [start + spot < far_len for start in starts]
+    near_kept = lax.broadcasted_iota(jnp.int32, (1, short), 1) < near_len
+    mine = [jnp.where(own_lanes(head, dim, low.shape, 1), low, jnp.zeros_like(low)) for head in range(2)]
+    far_mine = jnp.concatenate([part[:rows] for part in mine], axis=0)
+    near_parts = mm(jnp.concatenate([part[rows:] for part in mine], axis=0), near[:short], NT)
+    near_parts = [near_parts[:short], near_parts[short:]]
+    for r in range(count):
+        part = mm(far_mine, views[r][0][views[r][1]], NT)
+        for head in range(2):
+            scores[head, :, r * rows : (r + 1) * rows] = part[head * rows : (head + 1) * rows]
     for head in range(2):
-        lanes = slice(head * dim, (head + 1) * dim)
-        low = (query[:, lanes].astype(f32) * scale).astype(bf16)
-        table = jnp.broadcast_to(far_bias[0, head : head + 1, :], (rows, reach))
-        window[...] = pltpu.roll(table, reach - (rows - 1), 1, stride=1, stride_axis=0)
-        scores = []
-        for r in range(count):
-            source = place ^ r
-            start = pl.multiple_of(source * rows, rows)
-            keys = views[r][0][views[r][1], lanes]
-            part = mm(low[:rows], keys, NT) + window[:, pl.ds(start, rows)]
-            spot = source * rows + lax.broadcasted_iota(jnp.int32, (1, rows), 1)
-            scores.append(jnp.where(spot < far_len, part, -1e30))
-        highest = scores[0]
-        for part in scores[1:]:
-            highest = jnp.maximum(highest, part)
-        highest = jnp.max(highest, axis=-1, keepdims=True)
-        grown = [jnp.exp(part - highest) for part in scores]
-        whole = grown[0]
-        for part in grown[1:]:
-            whole = whole + part
-        inverse = 1.0 / jnp.sum(whole, axis=-1, keepdims=True)
-        out = jnp.zeros((rows, dim), f32)
-        for r in range(count):
-            attend = (grown[r] * inverse).astype(bf16)
-            far_attend[head, :, r * rows : (r + 1) * rows] = attend
-            out = out + mm(attend, views[r][2][views[r][3], lanes])
-        mixed[:rows, lanes] = out.astype(bf16)
-
+        table = jnp.broadcast_to(far_bias[0, head : head + 1, :], (band, reach))
+        window[head] = pltpu.roll(table, reach - (band - 1), 1, stride=1, stride_axis=0)
+    for head in range(2):
         table = jnp.broadcast_to(near_bias[0, head : head + 1, :], (short, 2 * short))
         bias = pltpu.roll(table, short + 1, 1, stride=1, stride_axis=0)[:, :short]
-        part = mm(low[rows:], near[:short, lanes], NT) + bias
-        spot = lax.broadcasted_iota(jnp.int32, (1, short), 1)
-        part = jnp.where(spot < near_len, part, -1e30)
+        part = jnp.where(near_kept, near_parts[head] + bias, -1e30)
         part = jnp.exp(part - jnp.max(part, axis=-1, keepdims=True))
-        attend = (part * (1.0 / jnp.sum(part, axis=-1, keepdims=True))).astype(bf16)
-        near_attend[head] = attend
-        mixed[rows:, lanes] = mm(attend, near[short:, lanes]).astype(bf16)
-
-
-def attention_specs(count, rows, short, reach, tokens, first=0):
-    cut = lambda size: pl.BlockSpec((size, 128), lambda i, *_: (0, i + first))
+        near_attend[head] = (part * (1.0 / jnp.sum(part, axis=-1, keepdims=True))).astype(bf16)
+        for at in range(0, rows, 32):
+            shift = band * (rows // band - 1 - at // band)
+            lines = slice(at % band, at % band + 32)
+            parts = []
+            for r in range(count):
+                begin = pl.multiple_of(starts[r] + shift, 128)
+                part = scores[head, at : at + 32, r * rows : (r + 1) * rows]
+                part = part + window[head, lines, pl.ds(begin, rows)]
+                parts.append(jnp.where(kept[r], part, -1e30))
+            highest = parts[0]
+            for part in parts[1:]:
+                highest = jnp.maximum(highest, part)
+            highest = jnp.max(highest, axis=-1, keepdims=True)
+            parts = [jnp.exp(part - highest) for part in parts]
+            whole = parts[0]
+            for part in parts[1:]:
+                whole = whole + part
+            inverse = 1.0 / jnp.sum(whole, axis=-1, keepdims=True)
+            for r in range(count):
+                far_attend[head, at : at + 32, r * rows : (r + 1) * rows] = (parts[r] * inverse).astype(bf16)
+    out = jnp.zeros((2 * rows, 2 * dim), f32)
+    for r in range(count):
+        attend = far_attend[:, :, r * rows : (r + 1) * rows].reshape(2 * rows, rows)
+        out = out + mm(attend, views[r][2][views[r][3]])
+    near_out = mm(near_attend[...].reshape(2 * short, short), near[short:])
+    second = own_lanes(1, dim, (rows, 2 * dim), 1)
+    mixed[:rows] = jnp.where(second, out[rows:], out[:rows]).astype(bf16)
+    second = own_lanes(1, dim, (short, 2 * dim), 1)
+    mixed[rows:] = jnp.where(second, near_out[short:], near_out[:short]).astype(bf16)
+
+
+def attention_specs(count, rows, short, reach, tokens):
+    cut = lambda size: pl.BlockSpec((size, 128), lambda i, *_: (0, i))
     parts = [cut(2 * rows), cut(2 * (count - 1) * rows)]
-    table = lambda size: pl.BlockSpec((1, 2, size), lambda i, *_: (i + first, 0, 0))
-    weights = lambda size, span: pl.BlockSpec((2, size, span), lambda i, *_: (i + first, 0, 0))
+    table = lambda size: pl.BlockSpec((1, 2, size), lambda i, *_: (i, 0, 0))
+    weights = lambda size, span: pl.BlockSpec((2, size, span), lambda i, *_: (i, 0, 0))
     return (
         cut(tokens),
         parts,
@@ -276,7 +323,7 @@
             grid=(heads // 2,),
             in_specs=[cut] + part_specs + [near_spec] + tables,
             out_specs=[cut] + weights,
-            scratch_shapes=[pltpu.VMEM((rows, reach), f32)],
+            scratch_shapes=[pltpu.VMEM((2, 128, reach), f32), pltpu.VMEM((2, rows, count * rows), f32)],
         ),
         out_shape=[
             jax.ShapeDtypeStruct((tokens, width), bf16),
@@ -284,7 +331,7 @@
             jax.ShapeDtypeStruct((heads, short, short), bf16),
         ],
         compiler_params=params(),
-        cost_estimate=cost(40 * heads * rows * rows * count * dim, 12 * width * rows * count),
+        cost_estimate=cost(17),
         name="attend_forward",
     )(facts, query, *parts, near, far_bias, near_bias)
 
@@ -301,25 +348,29 @@
     near,
     far_attend,
     near_attend,
+    far_hot,
+    near_hot,
     grad_query,
     grad_pair,
     grad_others,
     grad_near,
-    far_sums,
-    near_sums,
+    bias_grad,
     window,
     near_window,
+    products,
+    scores,
+    near_scores,
 ):
     place = facts[0]
     scale = 1.0 / math.sqrt(dim)
     views = key_value_views(pair, others, count, rows)
     grad_views = key_value_views(grad_pair, grad_others, count, rows)
     short = near.shape[0] // 2
-    reach = window.shape[1]
+    band = window.shape[1]
+    starts = [(place ^ r) * rows for r in range(count)]
 
     @pl.when(pl.program_id(0) == 0)
     def _():
-        window[...] = jnp.zeros_like(window)
         near_window[...] = jnp.zeros_like(near_window)
 
     def reversal(size):
@@ -327,133 +378,151 @@
         across = lax.broadcasted_iota(jnp.int32, (size, size), 1)
         return (up + across == size - 1).astype(bf16)
 
-    far_turn = reversal(rows)
-    near_turn = far_turn if short == rows else reversal(short)
+    far_turn = reversal(band)
+    near_turn = far_turn if short == band else reversal(short)
+    low, grad_low = query[...], grad[...]
+    turned = jnp.transpose(low.astype(f32) * scale, (1, 0)).astype(bf16)
+    grad_turned = jnp.transpose(grad_low.astype(f32), (1, 0)).astype(bf16)
+    mine, grad_mine, grad_heads = [], [], []
     for head in range(2):
-        lanes = slice(head * dim, (head + 1) * dim)
-        low = query[:, lanes]
-        grad_low = grad[:, lanes]
-        turned = jnp.transpose((low.astype(f32) * scale), (1, 0)).astype(bf16)
-        grad_turned = jnp.transpose(grad_low.astype(f32), (1, 0)).astype(bf16)
-        attends, grads = [], []
-        inner = jnp.zeros((rows, 1), f32)
-        for r in range(count):
-            attend = far_attend[head, :, r * rows : (r + 1) * rows]
-            part = mm(grad_low[:rows], views[r][2][views[r][3], lanes], NT)
-            inner = inner + jnp.sum(attend.astype(f32) * part, axis=-1, keepdims=True)
-            attends.append(attend)
-            grads.append(part)
-        out = jnp.zeros((rows, dim), f32)
-        for r in range(count):
-            start = pl.multiple_of((place ^ r) * rows, rows)
-            scores = (attends[r].astype(f32) * (grads[r] - inner)).astype(bf16)
-            window[:, pl.ds(start, rows)] = mm(far_turn, scores)
-            out = out + mm(scores, views[r][0][views[r][1], lanes])
-            grad_keys = mm(turned[:, :rows], scores)
-            grad_values = mm(grad_turned[:, :rows], attends[r])
-            view = grad_views[r]
-            view[0][view[1], lanes] = jnp.transpose(grad_keys, (1, 0)).astype(bf16)
-            view[2][view[3], lanes] = jnp.transpose(grad_values, (1, 0)).astype(bf16)
-        grad_query[:rows, lanes] = (out * scale).astype(bf16)
-        rolled = pltpu.roll(window[...], 0, 1, stride=1, stride_axis=0)
-        far_sums[0, head : head + 1, :] = jnp.sum(rolled, axis=0, keepdims=True)
-
-        attend = near_attend[head]
-        part = mm(grad_low[rows:], near[short:, lanes], NT)
-        wide = attend.astype(f32)
+        lines = own_lanes(head, dim, turned.shape, 0)
+        mine.append(jnp.where(lines, turned, jnp.zeros_like(turned)))
+        grad_mine.append(jnp.where(lines, grad_turned, jnp.zeros_like(turned)))
+        lanes = own_lanes(head, dim, low.shape, 1)
+        grad_heads.append(jnp.where(lanes, grad_low, jnp.zeros_like(grad_low)))
+    far_grads = jnp.concatenate([part[:rows] for part in grad_heads], axis=0)
+    near_parts = mm(jnp.concatenate([part[rows:] for part in grad_heads], axis=0), near[short:], NT)
+    for r in range(count):
+        part = mm(far_grads, views[r][2][views[r][3]], NT)
+        for head in range(2):
+            products[head, :, r * rows : (r + 1) * rows] = part[head * rows : (head + 1) * rows]
+    window[...] = jnp.zeros_like(window)
+    for head in range(2):
+        wide = near_attend[head].astype(f32)
+        part = near_parts[head * short : (head + 1) * short]
         part = wide * (part - jnp.sum(wide * part, axis=-1, keepdims=True))
-        scores = part.astype(bf16)
-        near_window[:, :short] = mm(near_turn, scores)
-        rolled = pltpu.roll(near_window[...], 0, 1, stride=1, stride_axis=0)
-        near_sums[0, head : head + 1, :] = jnp.sum(rolled, axis=0, keepdims=True)
-        grad_query[rows:, lanes] = (mm(scores, near[:short, lanes]) * scale).astype(bf16)
-        grad_keys = mm(turned[:, rows:], scores)
-        grad_values = mm(grad_turned[:, rows:], attend)
-        grad_near[:short, lanes] = jnp.transpose(grad_keys, (1, 0)).astype(bf16)
-        grad_near[short:, lanes] = jnp.transpose(grad_values, (1, 0)).astype(bf16)
-
-
-def attend_backward(facts, query, grad, parts, near, weights, reach, count, rows, dim, half):
+        near_scores[head] = part.astype(bf16)
+        for at in range(0, rows, 32):
+            attend = far_attend[head, at : at + 32].astype(f32)
+            part = products[head, at : at + 32]
+            inner = jnp.sum(attend * part, axis=-1, keepdims=True)
+            scores[head, at : at + 32] = (attend * (part - inner)).astype(bf16)
+    out = jnp.zeros((2 * rows, 2 * dim), f32)
+    for r in range(count):
+        part = scores[:, :, r * rows : (r + 1) * rows].reshape(2 * rows, rows)
+        out = out + mm(part, views[r][0][views[r][1]])
+        for head in range(2):
+            for h in range(rows // band):
+                begin = pl.multiple_of(starts[r] + band * (rows // band - 1 - h), 128)
+                lines = slice(head * rows + h * band, head * rows + (h + 1) * band)
+                window[head, :, pl.ds(begin, rows)] += mm(far_turn, part[lines])
+    near_out = mm(near_scores[...].reshape(2 * short, short), near[:short])
+    second = own_lanes(1, dim, (rows, 2 * dim), 1)
+    grad_query[:rows] = (jnp.where(second, out[rows:], out[:rows]) * scale).astype(bf16)
+    second = own_lanes(1, dim, (short, 2 * dim), 1)
+    grad_query[rows:] = (jnp.where(second, near_out[short:], near_out[:short]) * scale).astype(bf16)
+    def by_bucket(lines, hot):
+        row = lax.broadcasted_iota(jnp.int32, (16, lines.shape[1]), 0)
+        high = lines.astype(bf16).astype(f32)
+        rest = lines - high
+        middle = rest.astype(bf16).astype(f32)
+        stack = jnp.where(row == 0, high, jnp.where(row == 1, middle, jnp.where(row == 2, rest - middle, 0.0)))
+        return jnp.sum(mm(stack.astype(bf16), hot[...]), axis=0, keepdims=True)
+
+    for head in range(2):
+        rolled = pltpu.roll(window[head], 0, 1, stride=1, stride_axis=0)
+        sums = by_bucket(jnp.sum(rolled, axis=0, keepdims=True), far_hot)
+        near_window[head, :, :short] = mm(near_turn, near_scores[head])
+        rolled = pltpu.roll(near_window[head], 0, 1, stride=1, stride_axis=0)
+        sums = sums + by_bucket(jnp.sum(rolled, axis=0, keepdims=True), near_hot)
+        bias_grad[0, head : head + 1, :] = sums
+    for r in range(count):
+        lanes = slice(r * rows, (r + 1) * rows)
+        keys = mm(mine[0][:, :rows], scores[0, :, lanes]) + mm(mine[1][:, :rows], scores[1, :, lanes])
+        values = mm(grad_mine[0][:, :rows], far_attend[0, :, lanes]) + mm(
+            grad_mine[1][:, :rows], far_attend[1, :, lanes]
+        )
+        view = grad_views[r]
+        view[0][view[1]] = jnp.transpose(keys, (1, 0)).astype(bf16)
+        view[2][view[3]] = jnp.transpose(values, (1, 0)).astype(bf16)
+    keys = mm(mine[0][:, rows:], near_scores[0]) + mm(mine[1][:, rows:], near_scores[1])
+    values = mm(grad_mine[0][:, rows:], near_attend[0]) + mm(grad_mine[1][:, rows:], near_attend[1])
+    grad_near[:short] = jnp.transpose(keys, (1, 0)).astype(bf16)
+    grad_near[short:] = jnp.transpose(values, (1, 0)).astype(bf16)
+
+
+def attend_backward(facts, query, grad, parts, near, weights, hots, count, rows, dim):
     tokens, width = query.shape
-    pairs = width // dim // 4
-    wide = width // 2
+    pairs = width // dim // 2
     short = near.shape[0] // 2
-    cut, part_specs, near_spec, _, weight_specs = attention_specs(
-        count, rows, short, reach, tokens, half * pairs
-    )
-    cut_out, part_outs, near_out, tables, _ = attention_specs(count, rows, short, reach, tokens)
+    reach, buckets = hots[0].shape
+    cut, part_specs, near_spec, _, weight_specs = attention_specs(count, rows, short, reach, tokens)
     return pl.pallas_call(
         partial(backward_kernel, count, rows, dim),
         grid_spec=pltpu.PrefetchScalarGridSpec(
             num_scalar_prefetch=1,
             grid=(pairs,),
-            in_specs=[cut, cut] + part_specs + [near_spec] + weight_specs,
-            out_specs=[cut_out] + part_outs + [near_out] + tables,
-            scratch_shapes=[pltpu.VMEM((rows, reach), f32), pltpu.VMEM((short, 2 * short), f32)],
+            in_specs=[cut, cut]
+            + part_specs
+            + [near_spec]
+            + weight_specs
+            + [pl.BlockSpec(hot.shape, lambda i, *_: (0, 0)) for hot in hots],
+            out_specs=[cut]
+            + part_specs
+            + [near_spec, pl.BlockSpec((1, 2, buckets), lambda i, *_: (i, 0, 0))],
+            scratch_shapes=[
+                pltpu.VMEM((2, 128, reach), f32),
+                pltpu.VMEM((2, short, 2 * short), f32),
+                pltpu.VMEM((2, rows, count * rows), f32),
+                pltpu.VMEM((2, rows, count * rows), bf16),
+                pltpu.VMEM((2, short, short), bf16),
+            ],
         ),
         out_shape=[
-            jax.ShapeDtypeStruct((size, wide), bf16)
+            jax.ShapeDtypeStruct((size, width), bf16)
             for size in (tokens, 2 * rows, 2 * (count - 1) * rows, 2 * short)
         ]
-        + [
-            jax.ShapeDtypeStruct((pairs, 2, reach), f32),
-            jax.ShapeDtypeStruct((pairs, 2, 2 * short), f32),
-        ],
+        + [jax.ShapeDtypeStruct((pairs, 2, buckets), f32)],
         compiler_params=params(),
-        cost_estimate=cost(50 * width // dim * rows * rows * count * dim, 8 * width * rows * count),
+        cost_estimate=cost(25),
         name="attend_backward",
-    )(facts, query, grad, *parts, near, *weights)
-
-
-def normed_grads_kernel(local, count, *refs):
-    grads, (w_query, w_key, w_value) = refs[:8], refs[8:11]
-    own, own_short, away = refs[11:]
-    half = pl.program_id(0)
-
-    @pl.when(half == 0)
+    )(facts, query, grad, *parts, near, *weights, *hots)
+
+
+def normed_grads_kernel(local, count, query, pair, others, near, w_query, w_key, w_value, *outs):
+    own, own_short, away = outs
+    short = near.shape[0] // 2
+
+    @pl.when(pl.program_id(0) == 0)
     def _():
-        own[...] = jnp.zeros_like(own)
-        own_short[...] = jnp.zeros_like(own_short)
-        away[...] = jnp.zeros_like(away)
-
-    for which in range(2):
-
-        @pl.when(half == which)
-        def _():
-            query, pair, others, near = grads[4 * which : 4 * which + 4]
-            short = near.shape[0] // 2
-            full = mm(query[...], w_query[...], NT)
-            own[...] += full[:local] + mm(pair[:local], w_key[...], NT) + mm(pair[local:], w_value[...], NT)
-            own_short[...] += (
-                full[local:] + mm(near[:short], w_key[...], NT) + mm(near[short:], w_value[...], NT)
-            )
-            for r in range(count - 1):
-                at = 2 * r * local
-                away[r * local : (r + 1) * local] += mm(
-                    others[at : at + local], w_key[...], NT
-                ) + mm(others[at + local : at + 2 * local], w_value[...], NT)
-
-
-def normed_grads(halves, w_query, w_key, w_value, local, count):
+        for out in outs:
+            out[...] = jnp.zeros_like(out)
+
+    full = mm(query[...], w_query[...], NT)
+    own[...] += full[:local] + mm(pair[:local], w_key[...], NT) + mm(pair[local:], w_value[...], NT)
+    own_short[...] += full[local:] + mm(near[:short], w_key[...], NT) + mm(near[short:], w_value[...], NT)
+    for r in range(count - 1):
+        at = 2 * r * local
+        away[r * local : (r + 1) * local] += mm(others[at : at + local], w_key[...], NT) + mm(
+            others[at + local : at + 2 * local], w_value[...], NT
+        )
+
+
+def normed_grads(grads, w_query, w_key, w_value, local, count):
     width = w_query.shape[0]
-    wide = width // 2
-    short = halves[0][3].shape[0] // 2
-    arrays = [array for half in halves for array in half[:4]]
-    cut = pl.BlockSpec((width, wide), lambda i: (0, i))
+    short = grads[3].shape[0] // 2
+    cut = lambda size: pl.BlockSpec((size, width // 2), lambda i: (0, i))
+    sizes = (local, short, (count - 1) * local)
     return pl.pallas_call(
         partial(normed_grads_kernel, local, count),
         grid=(2,),
-        in_specs=[pl.BlockSpec(array.shape, lambda i: (0, 0)) for array in arrays] + [cut] * 3,
-        out_specs=[
-            pl.BlockSpec((size, width), lambda i: (0, 0)) for size in (local, short, (count - 1) * local)
-        ],
-        out_shape=[
-            jax.ShapeDtypeStruct((size, width), f32) for size in (local, short, (count - 1) * local)
-        ],
+        in_specs=[cut(array.shape[0]) for array in grads] + [cut(width)] * 3,
+        out_specs=[pl.BlockSpec((size, width), lambda i: (0, 0)) for size in sizes],
+        out_shape=[jax.ShapeDtypeStruct((size, width), f32) for size in sizes],
         compiler_params=params(),
-        cost_estimate=cost(4 * count * local * width * width, 8 * count * local * width),
+        cost_estimate=cost(13),
         name="normed_grads",
-    )(*arrays, w_query, w_key, w_value)
+    )(*grads, w_query, w_key, w_value)
 
 
 def expert_kernel(chunks, capacity, padded, lanes_used, facts, rows_in, grads_in, *refs):
@@ -550,7 +619,7 @@
         out_shape=[jax.ShapeDtypeStruct((rows, units), bf16)] * (3 * chunks)
         + [jax.ShapeDtypeStruct((rows, width), bf16)] * 2,
         compiler_params=params(),
-        cost_estimate=cost(12 * chunks * rows * units * width, 8 * rows * width),
+        cost_estimate=cost(18),
         name="expert_pass",
     )(facts, slots, grads, *sources)
     middles = [outs[3 * c : 3 * c + 3] for c in range(chunks)]
@@ -632,7 +701,7 @@
         out_shape=out_shape,
         input_output_aliases={1 + 5 * count + i: i for i in range(len(before))},
         compiler_params=params(),
-        cost_estimate=cost(6 * count * rows * units * width, 8 * count * rows * width),
+        cost_estimate=cost(16),
         name="weight_pass",
     )(facts, *[array for kind in kinds for array in kind], *before)
 
@@ -657,7 +726,7 @@
         out_shape=[jax.ShapeDtypeStruct(array.shape, f32) for array in before],
         input_output_aliases={2 + i: i for i in range(3)},
         compiler_params=params(),
-        cost_estimate=cost(0, 6 * source.size),
+        cost_estimate=cost(6.5),
         name="weight_fill",
     )(facts, source, *before)
 
@@ -705,15 +774,15 @@
             jax.ShapeDtypeStruct((local * block, width), bf16),
         ],
         compiler_params=pltpu.CompilerParams(vmem_limit_bytes=VMEM_BYTES),
-        cost_estimate=cost(2 * local * block * tokens * width, 4 * local * block * width),
+        cost_estimate=cost(3.9),
         name="place_rows",
     )(turns, routes, rows)
 
 
 def route_kernel(
-    capacity, padded, mixed, w_proj, inputs, gain, router, routes, slots, resid, moe, probs, gates, out
+    capacity, padded, mixed, w_proj, inputs, gain, router, routes, slots, resid, moe, probs, gates, *outs
 ):
-    local, block, width = out.shape
+    local, block = len(outs), outs[0].shape[0]
     tokens = inputs.shape[0]
     sums = inputs[...].astype(f32) + mm(mixed[...], w_proj[...])
     resid[...] = sums
@@ -741,13 +810,13 @@
     spare = 16 - (padded - capacity)
     row = lax.broadcasted_iota(jnp.int32, (16, padded), 0)
     for j in range(local):
-        out[j] = filled[j * block : (j + 1) * block]
+        outs[j][...] = filled[j * block : (j + 1) * block]
         for g in range(block // padded):
             at = j * block + g * padded
             tail = filled[at + padded - 16 : at + padded, :padded].astype(f32)
             line = lines[:, at : at + padded]
             tail = jnp.where(row == spare, line[0:1], jnp.where(row == spare + 1, line[1:2], tail))
-            out[j, pl.ds((g + 1) * padded - 16, 16), :padded] = tail.astype(bf16)
+            outs[j][pl.ds((g + 1) * padded - 16, 16), :padded] = tail.astype(bf16)
 
 
 def route_rows(mixed, w_proj, inputs, gain, router, routes, slots, capacity, padded, block, local):
@@ -760,10 +829,10 @@
             jax.ShapeDtypeStruct((tokens, width), bf16),
             jax.ShapeDtypeStruct((router.shape[0], tokens), f32),
             jax.ShapeDtypeStruct((tops, tokens), f32),
-            jax.ShapeDtypeStruct((local, block, width), bf16),
-        ],
+        ]
+        + [jax.ShapeDtypeStruct((block, width), bf16)] * local,
         compiler_params=pltpu.CompilerParams(vmem_limit_bytes=VMEM_BYTES),
-        cost_estimate=cost(4 * local * block * tokens * width, 12 * local * block * width),
+        cost_estimate=cost(6.4),
         name="route_rows",
     )(mixed, w_proj, inputs, gain.reshape(1, width), router, routes, slots)
 
@@ -839,7 +908,7 @@
             jax.ShapeDtypeStruct((tokens, width), bf16),
         ],
         compiler_params=pltpu.CompilerParams(vmem_limit_bytes=VMEM_BYTES),
-        cost_estimate=cost(6 * tokens * width * width, 20 * tokens * width),
+        cost_estimate=cost(7.4),
         name="merge_rows",
     )(
         cotangent, resid, probs, moe, router, gain.reshape(1, width), w_proj, routes, slots,
@@ -848,11 +917,27 @@
 
 
 def blocks_kernel(
-    local, facts, normed, normed_others, mixed, grad_query, grad_pair, grad_others, grad_near, branch, small, near, far
+    local,
+    facts,
+    normed,
+    normed_others,
+    mixed,
+    grad_query,
+    grad_pair,
+    grad_others,
+    grad_near,
+    branch,
+    bias_grad,
+    gain_grad,
+    router_grad,
+    near,
+    far,
+    near_right,
+    far_right,
 ):
     step = pl.program_id(0)
     number = facts[3]
-    group = step ^ (number // 4)
+    group = step ^ (number // 8)
     share = (near.shape[1] - 8) // 4
     short = grad_near.shape[0] // 2
     own, own_short = normed[:local], normed[local:]
@@ -867,60 +952,74 @@
 
     made = [mm(normed[...], grad_query[...], TN), keyed(0), keyed(1), mm(mixed[...], branch[...], TN)]
     made = [part.astype(bf16) for part in made]
-    for s in range(4):
-        spot = s ^ (number % 4)
+    pairs, _, buckets = bias_grad.shape
+    line = [bias_grad[p, h : h + 1, :] for p in range(pairs) for h in range(2)]
+    line.append(jnp.zeros((1, 2 * near.shape[2] - 2 * pairs * buckets), f32))
+    tail = jnp.zeros((24 - 2 - router_grad.shape[0], 2 * near.shape[2]), f32)
+    small = jnp.concatenate(
+        [jnp.concatenate(line, axis=1), gain_grad[...], router_grad[...], tail], axis=0
+    )
+    for s in range(8):
+        spot = s ^ (number % 8)
         lines = [part[s * share : (s + 1) * share] for part in made]
-        extra = jnp.zeros((8, small.shape[1]), bf16)
+        extra = jnp.zeros((8, 2 * near.shape[2]), f32)
         if s < 3:
             extra = jnp.where(group == 0, small[s * 8 : s * 8 + 8], extra)
-        whole = jnp.concatenate(lines + [extra], axis=0)
-
-        @pl.when(step < 4)
+        whole = jnp.concatenate(lines + [extra.astype(bf16)], axis=0)
+
+        @pl.when(step < 2)
         def _():
-            near[spot] = whole
-
-        @pl.when(step >= 4)
+            near[spot] = whole[:, : near.shape[2]]
+            near_right[spot] = whole[:, near.shape[2] :]
+
+        @pl.when(step >= 2)
         def _():
-            far[spot] = whole
-
-
-def weight_blocks(facts, lefts, rights, branch, small, local, half):
+            far[spot] = whole[:, : near.shape[2]]
+            far_right[spot] = whole[:, near.shape[2] :]
+
+
+def weight_blocks(facts, lefts, rights, branch, bias_grad, gain_grad, router_grad, local):
     tokens, width = lefts[0].shape
-    wide = width // 2
     rows = 4 * width // 32 + 8
-    cut = lambda count: pl.BlockSpec((count, width // 8), lambda i, f: (0, i ^ (f[3] // 4)))
-    full = lambda count: pl.BlockSpec((count, wide), lambda i, f: (0, 0))
-    out = lambda which: pl.BlockSpec((4, rows, wide), which)
+    cut = lambda count: pl.BlockSpec((count, width // 4), lambda i, f: (0, i ^ (f[3] // 8)))
+    full = lambda count: pl.BlockSpec((count, width), lambda i, f: (0, 0))
+    out = lambda which: pl.BlockSpec((8, rows, width // 2), which)
     return pl.pallas_call(
         partial(blocks_kernel, local),
         grid_spec=pltpu.PrefetchScalarGridSpec(
             num_scalar_prefetch=1,
-            grid=(8,),
+            grid=(4,),
             in_specs=[cut(left.shape[0]) for left in lefts]
             + [full(right.shape[0]) for right in rights]
-            + [pl.BlockSpec((tokens, wide), lambda i, f: (0, half)), full(24)],
+            + [
+                full(tokens),
+                pl.BlockSpec(bias_grad.shape, lambda i, f: (0, 0, 0)),
+                full(1),
+                full(router_grad.shape[0]),
+            ],
             out_specs=[
-                out(lambda i, f: (jnp.minimum(i, 3), 0, 0)),
-                out(lambda i, f: (jnp.maximum(i - 4, 0), 0, 0)),
-            ],
+                out(lambda i, f: (jnp.minimum(i, 1), 0, 0)),
+                out(lambda i, f: (jnp.maximum(i - 2, 0), 0, 0)),
+            ]
+            * 2,
         ),
-        out_shape=[jax.ShapeDtypeStruct((16, rows, wide), bf16)] * 2,
+        out_shape=[jax.ShapeDtypeStruct((16, rows, width // 2), bf16)] * 4,
         compiler_params=params(),
-        cost_estimate=cost(8 * tokens * width * width, 4 * width * width),
+        cost_estimate=cost(17),
         name="weight_blocks",
-    )(facts, *lefts, *rights, branch, small)
+    )(facts, *lefts, *rights, branch, bias_grad, gain_grad, router_grad)
 
 
 def unpack_kernel(facts, near, far, w_query, w_key, w_value, gain, *refs):
     query, key, value, proj, gain_grad, small = refs[-6:]
     step = pl.program_id(0)
     number = facts[3]
-    group = step ^ (number // 4)
+    group = step ^ (number // 8)
     share = (near.shape[1] - 8) // 4
 
     def spread(source):
-        for s in range(4):
-            block = source[s ^ (number % 4)].astype(f32)
+        for s in range(8):
+            block = source[s ^ (number % 8)].astype(f32)
             for which, out in enumerate((query, key, value, proj)):
                 out[s * share : (s + 1) * share] = block[which * share : (which + 1) * share]
             if s < 3:
@@ -929,11 +1028,11 @@
                 def _():
                     small[s * 8 : s * 8 + 8] = block[4 * share :]
 
-    @pl.when(step < 4)
+    @pl.when(step < 2)
     def _():
         spread(near)
 
-    @pl.when(step >= 4)
+    @pl.when(step >= 2)
     def _():
         spread(far)
 
@@ -953,17 +1052,17 @@
     width = w_query.shape[0]
     wide = width // 2
     rows = near.shape[1]
-    step = width // 8
-    line = pl.BlockSpec((1, step), lambda i, f: (0, i ^ (f[3] // 4)))
-    block = pl.BlockSpec((step, wide), lambda i, f: (i ^ (f[3] // 4), half))
+    step = width // 4
+    line = pl.BlockSpec((1, step), lambda i, f: (0, i ^ (f[3] // 8)))
+    block = pl.BlockSpec((step, wide), lambda i, f: (i ^ (f[3] // 8), half))
     return pl.pallas_call(
         unpack_kernel,
         grid_spec=pltpu.PrefetchScalarGridSpec(
             num_scalar_prefetch=1,
-            grid=(8,),
+            grid=(4,),
             in_specs=[
-                pl.BlockSpec((4, rows, wide), lambda i, f: (jnp.minimum(i, 3), 0, 0)),
-                pl.BlockSpec((4, rows, wide), lambda i, f: (jnp.maximum(i - 4, 0), 0, 0)),
+                pl.BlockSpec((8, rows, wide), lambda i, f: (jnp.minimum(i, 1), 0, 0)),
+                pl.BlockSpec((8, rows, wide), lambda i, f: (jnp.maximum(i - 2, 0), 0, 0)),
                 block,
                 block,
                 block,
@@ -976,7 +1075,7 @@
         + [jax.ShapeDtypeStruct((1, width), f32), jax.ShapeDtypeStruct((24, wide), f32)],
         input_output_aliases={7 + i: i for i in range(len(before))},
         compiler_params=params(),
-        cost_estimate=cost(6 * width * width, 12 * width * width),
+        cost_estimate=cost(8),
         name="unpack_blocks",
     )(facts, near, far, w_query, w_key, w_value, gain.reshape(1, width), *before)
 
@@ -1042,7 +1141,8 @@
             pairs += [(e * tensor_axis + t, e * tensor_axis + (t ^ mask)) for t in range(tensor_axis)]
         return lax.ppermute(rows, ("expert", "tensor"), pairs)
 
-    sources = gather_parts(inputs[:long_local])[1:]
+    long_rows = inputs[:long_local]
+    sources = [swap(long_rows, "tensor", r) for r in range(1, tensor_axis)]
     normed_low, query, pair, near = project(inputs, attn_gain, w_query, w_key, w_value, long_local)
     slots, wide_slots, grad_slots_in = place_rows(
         turns.reshape(1, 2), after(routes_rows, normed_low), cotangent, capacity, padded, block, local
@@ -1057,7 +1157,6 @@
         return jnp.concatenate(split, axis=1).reshape(local * block, width)
 
     grad_whole = over_experts(grad_slots_in)
-    grad_arrived = by_expert(grad_whole)
     normed_others, others = project_others(sources, attn_gain, w_key, w_value, long_local)
     parts = (pair, others)
     if paired:
@@ -1081,7 +1180,7 @@
         facts, query, parts, near, spread(long_hot), spread(short_hot),
         tensor_axis, long_local, head_dim,
     )
-    resid, moe_low, probs, gates, slots_in = route_rows(
+    resid, moe_low, probs, gates, *slots_in = route_rows(
         mixed, w_proj, inputs, moe_gain, router, routes_rows, slots, capacity, padded, block, local
     )
 
@@ -1092,43 +1191,45 @@
         run = lambda rows, grads: expert_pass(
             facts, rows, grads, own, other, capacity, padded, lanes_used
         )
-        grads_c = trade(after(grad_arrived[0], other), True)
-        grads_b = trade(after(grad_arrived[1], other), False)
+        grad_arrived = by_expert(after(grad_whole, slots_in))
+        grads_b = trade(grad_arrived[1], False)
         grads_d = trade(grads_b, True)
-        rows_a = over_experts(after(slots_in[0], grad_whole))
-        rows_c = trade(after(rows_a, grads_b, grads_c), True)
-        rows_b = over_experts(after(slots_in[1], rows_a, grads_b, grads_c))
-        pass_a = run(rows_a, grad_arrived[0])
-        rows_b = trade(after(rows_b, pass_a[1]), False)
-        pass_c = run(rows_c, grads_c)
-        rows_d = trade(after(rows_b, pass_c[1]), True)
-        kept = add_low(pass_a[2], trade(pass_c[2], True))
-        kept = over_experts(kept)
+        rows_b = over_experts(slots_in[1])
+        rows_a = over_experts(after(slots_in[0], rows_b))
+        rows_b = trade(after(rows_b, grads_b), False)
+        rows_d = trade(rows_b, True)
+        grads_c = trade(after(grad_arrived[0], rows_d), True)
         pass_b = run(rows_b, grads_b)
         pass_d = run(after(rows_d, pass_b[1]), grads_d)
-        traded = add_low(pass_b[2], trade(pass_d[2], True))
+        rows_c = trade(after(rows_a, rows_d), True)
+        pass_a = run(after(rows_a, pass_d[1], grads_c, rows_c), grad_arrived[0])
+        traded = add_low(pass_b[2], after(trade(pass_d[2], True), pass_a[1]))
         traded = trade(traded, False)
-        grad_slots = [kept, over_experts(after(traded, kept))]
+        pass_c = run(after(rows_c, pass_a[1]), grads_c)
+        traded = after(traded, pass_c[1])
+        traded_back = over_experts(traded)
+        kept = add_low(pass_a[2], trade(after(pass_c[2], traded), True))
+        grad_slots = [over_experts(after(kept, traded_back)), traded_back]
 
         passes = [pass_a, pass_c, pass_b, pass_d]
         slot_blocks = [rows_a, rows_c, rows_b, rows_d]
         grad_blocks = [grad_arrived[0], grads_c, grads_b, grads_d]
         (sent,) = weight_pass(
-            facts, slot_blocks, grad_blocks, [after_all(made[0][1], pass_d[1]) for made in passes], (), local, True
+            facts, slot_blocks, grad_blocks, [after_all(made[0][1], pass_c[1]) for made in passes], (), local, True
         )
         weight_grads = weight_pass(
             facts, slot_blocks, grad_blocks, [after_all(made[0][0], sent) for made in passes], (), local, False
         )
-        outs_c = trade(after(pass_c[1], traded), True)
         outs_d = trade(after(pass_d[1], traded), True)
-        grad_slots[0] = after(grad_slots[0], weight_grads, outs_c, outs_d)
+        outs_c = trade(after(pass_c[1], kept, outs_d), True)
+        outs_traded = trade(add_low(pass_b[1], outs_d), False)
         outs_kept = add_low(pass_a[1], outs_c)
-        outs_traded = trade(add_low(pass_b[1], outs_d), False)
+        grad_slots[0] = after(grad_slots[0], weight_grads, outs_c, outs_traded)
         held_back = outs_traded
         sent = trade(after(sent, outs_traded), False)
-        send_outs = lambda: over_experts(after(by_device([outs_kept, outs_traded]), grad_slots[1]))
+        outs_back = over_experts(after(by_device([outs_kept, outs_traded]), grad_slots[0]))
     else:
-        grad_blocks = [gather_parts(rows) for rows in grad_arrived]
+        grad_blocks = [gather_parts(rows) for rows in by_expert(grad_whole)]
         slot_blocks = [gather_parts(over_experts(slots_in[j])) for j in range(local)]
         weight_grads, passes = (), []
         for j in range(local):
@@ -1146,48 +1247,50 @@
             over_experts(sum_parts([made[which] for made in passes[j]]).astype(bf16)) for j in range(local)
         ]
         grad_slots = send_back(2)
-        send_outs = lambda: by_device(send_back(1))
-        held_back = grad_slots[0]
+        outs_back = by_device(send_back(1))
+        held_back = sent = grad_slots[0]
 
     grad_resid, grad_mixed, moe_gain_grad, router_grad, branch = merge_rows(
         cotangent, resid, probs, moe_low, router, moe_gain, w_proj, routes_rows, slots, grad_slots,
         capacity, padded, shares,
     )
     grad_mixed = after(grad_mixed, held_back)
-    collect = lambda sums, hot: jnp.einsum(
-        "hc,cb->bh",
-        sums.reshape(heads // 2, hot.shape[0]),
-        hot,
-        precision=precise,
-        preferred_element_type=f32,
+    quick = experts_axis == 8 and tensor_axis == 4
+    hots = (long_hot.astype(bf16), short_hot.astype(bf16))
+    *attn_grads, bias_grad = attend_backward(
+        facts, query, grad_mixed, parts, near, (far_attend, near_attend), hots, tensor_axis, long_local, head_dim
     )
-    quick = experts_axis == 8 and tensor_axis == 4
-    wide = width // 2
-    halves, rel_halves, sums = [], [], []
-    for half in range(2):
-        made = attend_backward(
-            facts, query, grad_mixed, parts, near, (far_attend, near_attend), reach, tensor_axis, long_local,
-            head_dim, half,
+    if quick:
+        bias_grad = after(bias_grad, sent, outs_back)
+        made = weight_blocks(
+            facts, (normed_low, normed_others, mixed), attn_grads, branch, bias_grad, moe_gain_grad, router_grad,
+            long_local,
         )
-        halves.append(made[:4])
-        rel_halves.append(collect(made[4], long_hot) + collect(made[5], short_hot))
-        if quick:
-            rel_row = jnp.pad(rel_halves[half].reshape(1, -1), ((0, 0), (0, wide - rel_halves[half].size)))
-            columns = slice(half * wide, (half + 1) * wide)
-            small = jnp.concatenate([rel_row, moe_gain_grad[:, columns], router_grad[:, columns]], axis=0)
-            small = jnp.pad(small, ((0, 24 - small.shape[0]), (0, 0))).astype(bf16)
-            blocks = weight_blocks(
-                facts, (normed_low, normed_others, mixed), made[:4], branch, small, long_local, half
-            )
-            grad_mixed = after(grad_mixed, blocks)
-            sums.append(total_blocks(*blocks))
-    own_grads, near_grads, away = normed_grads(halves, w_query, w_key, w_value, long_local, tensor_axis)
+        sums = [add_low(made[half], swap(made[half + 1], "expert", 1)) for half in (0, 2)]
+        attn_grads = after_all(attn_grads, sums)
+    own_grads, near_grads, away = normed_grads(attn_grads, w_query, w_key, w_value, long_local, tensor_axis)
+    if quick:
+        sums = [ring_sum(plane_parts(part), in_plane).astype(bf16) for part in sums]
+        away = after(away, sums)
     pieces = [own_grads] + [
         away[r * long_local : (r + 1) * long_local].astype(bf16) for r in range(tensor_axis - 1)
     ]
     if tensor_axis == 4:
         pieces = pieces[:3] + [pieces[3][: long_local // 2], pieces[3][long_local // 2 :]]
-    grad_normed = jnp.concatenate([sum_parts(pieces), near_grads], axis=0)
+    summed = sum_parts(pieces)
+    if quick:
+        sums = [spread_depth(sum_depth(part)) for part in sums]
+        sums[1] = after(sums[1], summed)
+        sent, outs_back, summed = after_all((sent, outs_back, summed), sums[0])
+    if paired:
+        weight_grads = weight_fill(facts, sent, weight_grads)
+    slot_places = jnp.arange(local * block, dtype=jnp.int32)
+    outputs = resid
+    for k in range(top_count):
+        chosen = mm((wide_slots[k][:, None] == slot_places).astype(bf16), outs_back)
+        outputs = outputs + gates[k][:, None] * chosen
+    outputs = outputs.astype(bf16)
+    grad_normed = jnp.concatenate([summed, near_grads], axis=0)
     inputs_wide = inputs.astype(f32)
     scale = lax.rsqrt(jnp.mean(inputs_wide * inputs_wide, axis=-1, keepdims=True) + 1e-06)
     normed = inputs_wide * scale
@@ -1196,20 +1299,17 @@
         lifted - normed * jnp.mean(lifted * normed, axis=-1, keepdims=True)
     )
     if quick:
-        outs, smalls, gains = (), [], []
-        for half in range(2):
-            made = unpack_blocks(facts, *sums[half], w_query, w_key, w_value, attn_gain, outs, half)
-            outs = made[:4]
-            gains.append(made[4])
-            smalls.append(made[5])
-        query_grad, key_grad, value_grad, proj_grad = outs
-        attn_gain_grad = (gains[0] + gains[1])[0]
-        rel_grad = jnp.concatenate(
-            [small[0, : rel.size].reshape(rel.shape) for small, rel in zip(smalls, rel_halves)], axis=1
-        )
-        small = jnp.concatenate(smalls, axis=1)
+        sums = [spread_plane(part) for part in sums]
+        far = [swap(part, "expert", 1) for part in sums]
+        sums[0] = after(sums[0], outputs, weight_grads, inputs_grad)
+        unpack = partial(unpack_blocks, facts)
+        weights = (w_query, w_key, w_value, attn_gain)
+        first = unpack(sums[0], far[0], *weights, (), 0)
+        second = unpack(sums[1], far[1], *weights, first[:4], 1)
+        query_grad, key_grad, value_grad, proj_grad = second[:4]
+        attn_gain_grad = (first[4] + second[4])[0]
+        small = jnp.concatenate([first[5], second[5]], axis=1)
     else:
-        whole = [jnp.concatenate([one, two], axis=1) for one, two in zip(*halves)]
         key_others = [slice(2 * r * long_local, (2 * r + 1) * long_local) for r in range(tensor_axis - 1)]
         value_others = [slice((2 * r + 1) * long_local, (2 * r + 2) * long_local) for r in range(tensor_axis - 1)]
 
@@ -1217,15 +1317,16 @@
             short = slice(index * short_len, (index + 1) * short_len)
             rows = slice(index * long_local, (index + 1) * long_local)
             lefts = jnp.concatenate([normed_low, normed_others], axis=0)
-            rights = jnp.concatenate([whole[1][rows], whole[3][short]] + [whole[2][spot] for spot in spots], axis=0)
+            rights = jnp.concatenate(
+                [attn_grads[1][rows], attn_grads[3][short]] + [attn_grads[2][spot] for spot in spots], axis=0
+            )
             return mm(lefts, rights, TN)
 
-        rel_grad = jnp.concatenate(rel_halves, axis=1)
-        rel_row = jnp.pad(rel_grad.reshape(1, -1), ((0, 0), (0, width - rel_grad.size)))
+        rel_row = jnp.pad(bias_grad.reshape(1, -1), ((0, 0), (0, width - bias_grad.size)))
         small = jnp.concatenate([rel_row, moe_gain_grad, router_grad], axis=0)
         query_grad, key_grad, value_grad, proj_grad, small = lax.psum(
             (
-                mm(normed_low, whole[0], TN),
+                mm(normed_low, attn_grads[0], TN),
                 keyed(0, key_others),
                 keyed(1, value_others),
                 mm(mixed, branch, TN),
@@ -1237,18 +1338,9 @@
             query_grad * w_query.astype(f32) + key_grad * w_key.astype(f32) + value_grad * w_value.astype(f32),
             axis=1,
         ) / attn_gain.astype(f32)
-        rel_grad = small[0, : rel_grad.size].reshape(rel_grad.shape)
-    if paired:
-        weight_grads = weight_fill(facts, sent, weight_grads)
-
-    outs_back = send_outs()
-    slot_places = jnp.arange(local * block, dtype=jnp.int32)
-    outputs = resid
-    for k in range(top_count):
-        chosen = mm((wide_slots[k][:, None] == slot_places).astype(bf16), outs_back)
-        outputs = outputs + gates[k][:, None] * chosen
+    rel_grad = jnp.transpose(small[0, : heads * bucket_count].reshape(heads, bucket_count))
     return (
-        outputs.astype(bf16),
+        outputs,
         inputs_grad,
         attn_gain_grad,
         query_grad,

time: 643 us -> 537 us (0.84)
  waiting for transfers between devices: 191 us -> 146 us
  Pallas kernels: 258 us -> 228 us
  starting transfers between devices: 107 us -> 88.5 us
  local copies, waits for them, and re-layouts: 36.6 us -> 30 us
    ppermute x40 -> x39, waiting for transfers between devices: 122 us -> 66.1 us  [swap(): return lax.ppermute(rows, axis, [(i, i ^ mask) for i in range(count)])]
    all_to_all x6, waiting for transfers between devices: 28.4 us -> 46.3 us  [over_experts(): lax.all_to_all(blocks, 'expert', 0, 0, tiled=True).reshape(rows.shape)]
    ppermute x40 -> x39, starting transfers between devices: 66.3 us -> 49 us  [swap(): return lax.ppermute(rows, axis, [(i, i ^ mask) for i in range(count)])]
    pallas_call x2 -> x1, Pallas kernels: 37.5 us -> 24.5 us  [attend_backward(): pl.pallas_call(partial(backward_kernel, count, rows, dim), grid_spec=pltp...]
    pallas_call x2 -> x1, Pallas kernels: 22.9 us -> 15.8 us  [weight_blocks(): pl.pallas_call(partial(blocks_kernel, local), grid_spec=pltpu.PrefetchSca...]
  transfers between devices with their start and end apart: 60 -> 59, of which waited for: 27 -> 30; matrix products, arithmetic and copies ran while one was open for 9% -> 10% of each run, Pallas kernels for 35% -> 39%
where the time goes in v3:
time: 537 us; the launch traced here: 528 us
  Pallas kernels  228 us (42%)
  waiting for transfers between devices  146 us (27%)
  starting transfers between devices  88.5 us (16%)
  local copies, waits for them, and re-layouts  30 us (6%)
  other arithmetic  27.5 us (5%)
    pallas_call x4, Pallas kernels, expert_pass(): pl.pallas_call(partial(expert_kernel, chunks, capacity, padded, lanes_use...  72.2 us
    ppermute x39, waiting for transfers between devices, swap(): return lax.ppermute(rows, axis, [(i, i ^ mask) for i in range(count)])  66.1 us
    ppermute x39, starting transfers between devices, swap(): return lax.ppermute(rows, axis, [(i, i ^ mask) for i in range(count)])  49 us
    all_to_all x6, waiting for transfers between devices, over_experts(): lax.all_to_all(blocks, 'expert', 0, 0, tiled=True).reshape(rows.shape)  46.3 us
    ppermute x14, waiting for transfers between devices, trade(): return lax.ppermute(rows, ('expert', 'tensor'), pairs)  33.7 us
    pallas_call x2, Pallas kernels, weight_pass(): pl.pallas_call(body, grid_spec=pltpu.PrefetchScalarGridSpec(num_scalar_pr...  31.7 us
    all_to_all x6, starting transfers between devices, over_experts(): lax.all_to_all(blocks, 'expert', 0, 0, tiled=True).reshape(rows.shape)  24.6 us
    pallas_call x1, Pallas kernels, attend_backward(): pl.pallas_call(partial(backward_kernel, count, rows, dim), grid_spec=pltp...  24.5 us
  transfers between devices with their start and end apart: 59, of which 30 were waited for; matrix products, arithmetic and copies ran while one was open for 10% of the time, Pallas kernels for 39%

profile of v3, /device:TPU:0, one launch (start us, length us, event | category | flops | bytes accessed | tf_op | source)
XLA Modules:
  0.0 528.0 jit_solution(6413269193125904048)
XLA Ops:
  8.3 6.9 %project.1 = (bf16[384,1024]{1,0:T(8,128)(2,1)}, bf16[384,1024]{1,0:T(8,128)(2,1)}, bf16[512,1024]{1,0:T(8,128)(2,1)}, bf16[256,1024]{1,0:T(8,128)(2,1)}) custom-call(bf16[384,1024]{1,0:T(8,128)(2,1)} %inputs.3, bf16[1,1024]{1,0:T(2,128)(2,1)} %reshape.116.gain, bf16[1024,1024]{1,0:T(8,128)(2,1)} %w_query.7, bf16[1024,1024]{1,0:T(8,128)(2,1)} %w_key.9, ...), custom_call_target="tpu_custom_call" | custom-call | flops 7935000064 | tf_op jit(solution)/shard_map/project/pallas_call | solution.py:154
  19.6 5.5 %all-to-all-start.2 = ((bf16[8,128,1024]{2,1,0:T(8,128)(2,1)}), bf16[8,128,1024]{2,1,0:T(8,128)(2,1)S(1)}, u32[]{:S(2)}, u32[]{:S(2)}) async-start(bf16[8,128,1024]{2,1,0:T(8,128)(2,1)} %bitcast.94), calls=%async_computation.2 | async-start | bytes 4194304 | tf_op jit(solution)/shard_map/all_to_all | solution.py:99
  41.6 7.7 %project_others.1 = (bf16[768,1024]{1,0:T(8,128)(2,1)}, bf16[1536,1024]{1,0:T(8,128)(2,1)}) custom-call(bf16[1,1024]{1,0:T(2,128)(2,1)} %reshape.116.gain, bf16[1024,1024]{1,0:T(8,128)(2,1)} %w_key.9, bf16[1024,1024]{1,0:T(8,128)(2,1)} %w_value.9, bf16[256,1024]{1,0:T(8,128)(2,1)} %collective-permute-done.refs_0_, ...), custom_call_target="tpu_custom_call" | custom-call | flops 8855000064 | tf_op jit(solution)/shard_map/project_others/pallas_call | solution.py:195
  49.4 17.1 %attend_forward.1 = (bf16[384,1024]{1,0:T(8,128)(2,1)}, bf16[16,256,1024]{2,1,0:T(8,128)(2,1)}, bf16[16,128,128]{2,1,0:T(8,128)(2,1)}) custom-call(s32[7]{0:T(128)} %stack.68.facts, bf16[384,1024]{1,0:T(8,128)(2,1)} %get-tuple-element.153.query, bf16[512,1024]{1,0:T(8,128)(2,1)} %get-tuple-element.154.pair, bf16[1536,1024]{1,0:T(8,128)(2,1)} %get-tuple-element.155.others, ...), custom_call_target="tpu_custom_call" | custom-call | flops 19549999104 | tf_op jit(solution)/shard_map/attend_forward/pallas_call | solution.py:319
  66.5 6.4 %route_rows.1 = (f32[384,1024]{1,0:T(8,128)}, bf16[384,1024]{1,0:T(8,128)(2,1)}, f32[16,384]{1,0:T(8,128)}, f32[2,384]{1,0:T(2,128)}, bf16[512,1024]{1,0:T(8,128)(2,1)}, /*index=5*/bf16[512,1024]{1,0:T(8,128)(2,1)}) custom-call(bf16[384,1024]{1,0:T(8,128)(2,1)} %get-tuple-element.157.mixed, bf16[1024,1024]{1,0:T(8,128)(2,1)} %w_proj.3, ...), custom_call_target="tpu_custom_call" | custom-call | flops 7360000000 | tf_op jit(solution)/shard_map/route_rows/pallas_call | solution.py:825
  80.8 23.8 %all-to-all-done = bf16[8,64,1024]{2,1,0:T(8,128)(2,1)S(1)} async-done(((bf16[8,64,1024]{2,1,0:T(8,128)(2,1)}), bf16[8,64,1024]{2,1,0:T(8,128)(2,1)S(1)}, u32[]{:S(2)}, u32[]{:S(2)}) %all-to-all-start) | async-done | bytes 1048608 | tf_op jit(solution)/shard_map/all_to_all | solution.py:99
  111.1 15.0 %collective-permute-done.4.rows_in.refs_2_ = bf16[512,1024]{1,0:T(8,128)(2,1)} collective-permute-done((bf16[512,1024]{1,0:T(8,128)(2,1)S(1)}, bf16[512,1024]{1,0:T(8,128)(2,1)}, u32[]{:S(2)}, u32[]{:S(2)}) %collective-permute-start.4) | collective-permute-done | bytes 1048608 | tf_op jit(solution)/shard_map/ppermute | solution.py:1142
  127.6 17.9 %expert_pass.4 = (bf16[512,704]{1,0:T(8,128)(2,1)}, bf16[512,704]{1,0:T(8,128)(2,1)}, bf16[512,704]{1,0:T(8,128)(2,1)}, bf16[512,704]{1,0:T(8,128)(2,1)}, bf16[5...) custom-call(s32[7]{0:T(128)} %stack.68.facts, ...), custom_call_target="tpu_custom_call" | custom-call | flops 20700000256 | tf_op jit(solution)/shard_map/expert_pass/pallas_call | solution.py:609
  147.6 18.0 %expert_pass.5 = (bf16[512,704]{1,0:T(8,128)(2,1)}, bf16[512,704]{1,0:T(8,128)(2,1)}, bf16[512,704]{1,0:T(8,128)(2,1)}, bf16[512,704]{1,0:T(8,128)(2,1)}, bf16[5...) custom-call(s32[7]{0:T(128)} %stack.68.facts, ...), custom_call_target="tpu_custom_call" | custom-call | flops 20700000256 | tf_op jit(solution)/shard_map/expert_pass/pallas_call | solution.py:609
  166.2 5.4 %collective-permute-done.7.grads_in.refs_5_ = bf16[512,1024]{1,0:T(8,128)(2,1)S(1)} collective-permute-done((bf16[512,1024]{1,0:T(8,128)(2,1)S(1)}, bf16[512,1024]{1,0:T(8,128)(2,1)S(1)}, u32[]{:S(2)}, u32[]{:S(2)}) %collective-permute-start.7) | collective-permute-done | bytes 1048608 | tf_op jit(solution)/shard_map/ppermute | solution.py:1142
  172.6 18.3 %expert_pass.6 = (bf16[512,704]{1,0:T(8,128)(2,1)}, bf16[512,704]{1,0:T(8,128)(2,1)}, bf16[512,704]{1,0:T(8,128)(2,1)}, bf16[512,704]{1,0:T(8,128)(2,1)}, bf16[5...) custom-call(s32[7]{0:T(128)} %stack.68.facts, ...), custom_call_target="tpu_custom_call" | custom-call | flops 20700000256 | tf_op jit(solution)/shard_map/expert_pass/pallas_call | solution.py:609
  193.0 18.0 %expert_pass.7 = (bf16[512,704]{1,0:T(8,128)(2,1)}, bf16[512,704]{1,0:T(8,128)(2,1)}, bf16[512,704]{1,0:T(8,128)(2,1)}, bf16[512,704]{1,0:T(8,128)(2,1)}, bf16[5...) custom-call(s32[7]{0:T(128)} %stack.68.facts, ...), custom_call_target="tpu_custom_call" | custom-call | flops 20700000256 | tf_op jit(solution)/shard_map/expert_pass/pallas_call | solution.py:609
  219.1 7.8 %collective-permute-done.12 = bf16[512,1024]{1,0:T(8,128)(2,1)} collective-permute-done((bf16[512,1024]{1,0:T(8,128)(2,1)S(1)}, bf16[512,1024]{1,0:T(8,128)(2,1)}, u32[]{:S(2)}, u32[]{:S(2)}) %collective-permute-start.12) | collective-permute-done | bytes 1048608 | tf_op jit(solution)/shard_map/ppermute | solution.py:1142
  228.9 16.1 %weight_pass.2 = bf16[3,704,1024]{2,1,0:T(8,128)(2,1)} custom-call(s32[7]{0:T(128)} %stack.68.facts, bf16[512,1024]{1,0:T(8,128)(2,1)} %bitcast.97, bf16[512,1024]{1,0:T(8,128)(2,1)} %copy-done.27, bf16[512,1024]{1,0:T(8,128)(2,1)} %collective-permute-done.4.rows_in.refs_2_, bf16[512,1024]{1,0:T(8,128)(2,1)} %copy-done.26, bf16[512,1024]{1,0:T(8,128)(2,1)} %bitcast.103, ...), custom_call_target="tpu_custom_call" | custom-call | flops 18400000000 | tf_op jit(solution)/shard_map/weight_pass/pallas_call | solution.py:689
  254.4 15.6 %weight_pass.3 = (f32[2,704,1024]{2,1,0:T(8,128)}, f32[2,704,1024]{2,1,0:T(8,128)}, f32[2,704,1024]{2,1,0:T(8,128)}) custom-call(s32[7]{0:T(128)} %stack.68.facts, bf16[512,1024]{1,0:T(8,128)(2,1)} %bitcast.98, bf16[512,1024]{1,0:T(8,128)(2,1)} %copy-done.27, bf16[512,1024]{1,0:T(8,128)(2,1)} %collective-permute-done.4.rows_in.refs_2_, ...), custom_call_target="tpu_custom_call" | custom-call | flops 18400000000 | tf_op jit(solution)/shard_map/weight_pass/pallas_call | solution.py:689
  275.4 4.9 all-to-all-done.4
  285.8 7.4 %merge_rows.1 = (f32[384,1024]{1,0:T(8,128)}, bf16[384,1024]{1,0:T(8,128)(2,1)}, f32[1,1024]{1,0:T(1,128)}, f32[16,1024]{1,0:T(8,128)}, bf16[384,1024]{1,0:T(8,128)(2,1)}) custom-call(bf16[384,1024]{1,0:T(8,128)(2,1)} %cotangent.1, f32[384,1024]{1,0:T(8,128)} %get-tuple-element.161.resid, f32[16,384]{1,0:T(8,128)} %get-tuple-element.244.probs, ...), custom_call_target="tpu_custom_call" | custom-call | flops 8510000128 | tf_op jit(solution)/shard_map/merge_rows/pallas_call | solution.py:901
  293.2 24.5 %attend_backward.1 = (bf16[384,1024]{1,0:T(8,128)(2,1)}, bf16[512,1024]{1,0:T(8,128)(2,1)}, bf16[1536,1024]{1,0:T(8,128)(2,1)}, bf16[256,1024]{1,0:T(8,128)(2,1)}, f32[8,2,32]{2,1,0:T(2,128)}) custom-call(s32[7]{0:T(128)} %stack.68.facts, bf16[384,1024]{1,0:T(8,128)(2,1)} %get-tuple-element.153.query, bf16[384,1024]{1,0:T(8,128)(2,1)} %get-tuple-element.247.grad, ...), custom_call_target="tpu_custom_call" | custom-call | flops 28750000128 | tf_op jit(solution)/shard_map/attend_backward/pallas_call | solution.py:460
  317.7 16.4 %all-to-all-done.5 = bf16[8,128,1024]{2,1,0:T(8,128)(2,1)S(1)} async-done(((bf16[8,128,1024]{2,1,0:T(8,128)(2,1)}), bf16[8,128,1024]{2,1,0:T(8,128)(2,1)S(1)}, u32[]{:S(2)}, u32[]{:S(2)}) %all-to-all-start.5) | async-done | bytes 2097184 | tf_op jit(solution)/shard_map/all_to_all | solution.py:99
  334.1 15.8 %weight_blocks.1 = (bf16[16,136,512]{2,1,0:T(8,128)(2,1)}, bf16[16,136,512]{2,1,0:T(8,128)(2,1)}, bf16[16,136,512]{2,1,0:T(8,128)(2,1)}, bf16[16,136,512]{2,1,0:T(8,128)(2,1)}) custom-call(s32[7]{0:T(128)} %stack.68.facts, bf16[384,1024]{1,0:T(8,128)(2,1)} %get-tuple-element.158.normed, bf16[768,1024]{1,0:T(8,128)(2,1)} %get-tuple-element.254.normed_others, ...), custom_call_target="tpu_custom_call" | custom-call | flops 19549999104 | tf_op jit(solution)/shard_map/weight_blocks/pallas_call | solution.py:987
  361.9 4.6 collective-permute-done.19
  376.8 11.8 %normed_grads.1 = (f32[256,1024]{1,0:T(8,128)}, f32[128,1024]{1,0:T(8,128)}, f32[768,1024]{1,0:T(8,128)}) custom-call(bf16[384,1024]{1,0:T(8,128)(2,1)} %get-tuple-element.264.grad_query.query, bf16[512,1024]{1,0:T(8,128)(2,1)} %get-tuple-element.265.grad_pair.pair, bf16[1536,1024]{1,0:T(8,128)(2,1)} %get-tuple-element.266.grad_others.others, ...), custom_call_target="tpu_custom_call" | custom-call | flops 14949999616 | tf_op jit(solution)/shard_map/normed_grads/pallas_call | solution.py:516
  390.2 5.4 %collective-permute-done.26 = bf16[4,136,512]{2,1,0:T(8,128)(2,1)} collective-permute-done((bf16[4,136,512]{2,1,0:T(8,128)(2,1)}, bf16[4,136,512]{2,1,0:T(8,128)(2,1)}, u32[]{:S(2)}, u32[]{:S(2)}) %collective-permute-start.26) | collective-permute-done | bytes 557088 | tf_op jit(solution)/shard_map/ppermute | solution.py:40
  413.3 8.9 %collective-permute-start.42 = (bf16[136,512]{1,0:T(8,128)(2,1)S(1)}, bf16[136,512]{1,0:T(8,128)(2,1)S(1)}, u32[]{:S(2)}, u32[]{:S(2)}) collective-permute-start(bf16[136,512]{1,0:T(8,128)(2,1)S(1)} %get-tuple-element.319), channel_id=1, source_target_pairs={{0,8},{4,12},{8,0},{12,4},{16,24},{20,28},{24,16},{28,20},{1,9},{5... | collective-permute-start | bytes 417800 | tf_op jit(solution)/shard_map/ppermute | solution.py:40
  425.9 6.1 %collective-permute-start.34 = (bf16[136,512]{1,0:T(8,128)(2,1)S(1)}, bf16[136,512]{1,0:T(8,128)(2,1)S(1)}, u32[]{:S(2)}, u32[]{:S(2)}) collective-permute-start(bf16[136,512]{1,0:T(8,128)(2,1)S(1)} %get-tuple-element.298), channel_id=1, source_target_pairs={{0,8},{4,12},{8,0},{12,4},{16,24},{20,28},{24,16},{28,20},{1,9},{5... | collective-permute-start | bytes 417800 | tf_op jit(solution)/shard_map/ppermute | solution.py:40
  438.4 4.7 collective-permute-done.35
  450.4 7.5 %collective-permute-done.28 = bf16[256,1024]{1,0:T(8,128)(2,1)S(1)} collective-permute-done((bf16[256,1024]{1,0:T(8,128)(2,1)S(1)}, bf16[256,1024]{1,0:T(8,128)(2,1)S(1)}, u32[]{:S(2)}, u32[]{:S(2)}) %collective-permute-start.28) | collective-permute-done | bytes 524320 | tf_op jit(solution)/shard_map/ppermute | solution.py:40
  461.2 8.7 %collective-permute-done.37 = bf16[4,136,512]{2,1,0:T(8,128)(2,1)S(1)} collective-permute-done((bf16[4,136,512]{2,1,0:T(8,128)(2,1)S(1)}, bf16[4,136,512]{2,1,0:T(8,128)(2,1)S(1)}, u32[]{:S(2)}, u32[]{:S(2)}) %collective-permute-start.37) | collective-permute-done | bytes 557088 | tf_op jit(solution)/shard_map/ppermute | solution.py:40
  474.3 4.7 collective-permute-done.39
  499.3 6.6 %weight_fill.1 = (f32[2,704,1024]{2,1,0:T(8,128)}, f32[2,704,1024]{2,1,0:T(8,128)}, f32[2,704,1024]{2,1,0:T(8,128)}) custom-call(s32[7]{0:T(128)} %stack.68.facts, bf16[3,704,1024]{2,1,0:T(8,128)(2,1)} %collective-permute-done.14.source, f32[2,704,1024]{2,1,0:T(8,128)} %get-tuple-element.239.refs_0_, ...), custom_call_target="tpu_custom_call", output_to_operand_aliasing={{0}: (2, {}), {1}: (3, {}), {2}: (4, {})} | custom-call | flops 7474999808 | tf_op jit(solution)/shard_map/weight_fill/pallas_call | solution.py:718
  506.0 7.9 %unpack_blocks.2 = (f32[1024,1024]{1,0:T(8,128)}, f32[1024,1024]{1,0:T(8,128)}, f32[1024,1024]{1,0:T(8,128)}, f32[1024,1024]{1,0:T(8,128)}, f32[1,1024]{1,0:T(1,128)}, /*index=5*/f32[24,512]{1,0:T(8,128)}) custom-call(s32[7]{0:T(128)} %stack.68.facts, bf16[16,136,512]{2,1,0:T(8,128)(2,1)} %constant_dynamic-update-slice_fusion.near, ...), custom_call_target="tpu_custom_call" | custom-call | flops 9200000000 | tf_op jit(solution)/shard_map/unpack_blocks/pallas_call | solution.py:1058
  516.2 8.1 %unpack_blocks.3 = (f32[1024,1024]{1,0:T(8,128)}, f32[1024,1024]{1,0:T(8,128)}, f32[1024,1024]{1,0:T(8,128)}, f32[1024,1024]{1,0:T(8,128)}, f32[1,1024]{1,0:T(1,128)}, /*index=5*/f32[24,512]{1,0:T(8,128)}) custom-call(s32[7]{0:T(128)} %stack.68.facts, ...), custom_call_target="tpu_custom_call", output_to_operand_aliasing={{0}: (7, {}), {1}: (8, {}), {2}: (9, {}), {3}: (10, {})} | custom-call | flops 9200000000 | tf_op jit(solution)/shard_map/unpack_blocks/pallas_call | solution.py:1058
  (246 shorter events, 171.6 us)
Async XLA Ops:
  2.5 37.5 %collective-permute-start = (bf16[256,1024]{1,0:T(8,128)(2,1)}, bf16[256,1024]{1,0:T(8,128)(2,1)}, u32[]{:S(2)}, u32[]{:S(2)}) collective-permute-start(bf16[256,1024]{1,0:T(8,128)(2,1)} %slice.150), channel_id=1, source_target_pairs={{0,1},{1,0},{2,3},{3,2},{4,5},{5,4},{6,7},{7,6},{8,9},{9,8},{10,11... | collective-permute-start | bytes 1572872 | tf_op jit(solution)/shard_map/ppermute | solution.py:40
  5.5 34.6 %collective-permute-start.1 = (bf16[256,1024]{1,0:T(8,128)(2,1)}, bf16[256,1024]{1,0:T(8,128)(2,1)}, u32[]{:S(2)}, u32[]{:S(2)}) collective-permute-start(bf16[256,1024]{1,0:T(8,128)(2,1)} %slice.150), channel_id=1, source_target_pairs={{0,2},{1,3},{2,0},{3,1},{4,6},{5,7},{6,4},{7,5},{8,10},{9,11},{10,... | collective-permute-start | bytes 1572872 | tf_op jit(solution)/shard_map/ppermute | solution.py:40
  7.0 33.1 %collective-permute-start.2 = (bf16[256,1024]{1,0:T(8,128)(2,1)}, bf16[256,1024]{1,0:T(8,128)(2,1)}, u32[]{:S(2)}, u32[]{:S(2)}) collective-permute-start(bf16[256,1024]{1,0:T(8,128)(2,1)} %slice.150), channel_id=1, source_target_pairs={{0,3},{1,2},{2,1},{3,0},{4,7},{5,6},{6,5},{7,4},{8,11},{9,10},{10,... | collective-permute-start | bytes 1572872 | tf_op jit(solution)/shard_map/ppermute | solution.py:40
  19.6 54.6 %all-to-all-start.2 = ((bf16[8,128,1024]{2,1,0:T(8,128)(2,1)}), bf16[8,128,1024]{2,1,0:T(8,128)(2,1)S(1)}, u32[]{:S(2)}, u32[]{:S(2)}) async-start(bf16[8,128,1024]{2,1,0:T(8,128)(2,1)} %bitcast.94), calls=%async_computation.2 | async-start | bytes 4194304 | tf_op jit(solution)/shard_map/all_to_all | solution.py:99
  40.1 87.5 %collective-permute-start.9 = (bf16[3,704,1024]{2,1,0:T(8,128)(2,1)}, bf16[3,704,1024]{2,1,0:T(8,128)(2,1)}, u32[]{:S(2)}, u32[]{:S(2)}) collective-permute-start(bf16[3,704,1024]{2,1,0:T(8,128)(2,1)} %pad_maximum_fusion), channel_id=1, source_target_pairs={{0,1},{1,0},{2,3},{3,2},{4,6},{5,7},{6,4},{7,5},{8,9},{9,8},{10,11... | collective-permute-start | bytes 12976136 | tf_op jit(solution)/shard_map/ppermute | solution.py:1142
  74.2 30.4 %all-to-all-start = ((bf16[8,64,1024]{2,1,0:T(8,128)(2,1)}), bf16[8,64,1024]{2,1,0:T(8,128)(2,1)S(1)}, u32[]{:S(2)}, u32[]{:S(2)}) async-start(bf16[8,64,1024]{2,1,0:T(8,128)(2,1)} %bitcast.101), calls=%async_computation | async-start | bytes 2097152 | tf_op jit(solution)/shard_map/all_to_all | solution.py:99
  79.6 25.0 %collective-permute-start.3 = (bf16[512,1024]{1,0:T(8,128)(2,1)}, bf16[512,1024]{1,0:T(8,128)(2,1)}, u32[]{:S(2)}, u32[]{:S(2)}) collective-permute-start(bf16[512,1024]{1,0:T(8,128)(2,1)} %bitcast.19), channel_id=1, source_target_pairs={{0,1},{1,0},{2,3},{3,2},{4,6},{5,7},{6,4},{7,5},{8,9},{9,8},{10,11... | collective-permute-start | bytes 3145736 | tf_op jit(solution)/shard_map/ppermute | solution.py:1142
  104.6 21.5 %collective-permute-start.4 = (bf16[512,1024]{1,0:T(8,128)(2,1)S(1)}, bf16[512,1024]{1,0:T(8,128)(2,1)}, u32[]{:S(2)}, u32[]{:S(2)}) collective-permute-start(bf16[512,1024]{1,0:T(8,128)(2,1)S(1)} %bitcast.100), channel_id=1, source_target_pairs={{0,1},{1,0},{2,3},{3,2},{4,6},{5,7},{6,4},{7,5},{8,9},{9,8},{10,11... | collective-permute-start | bytes 3145736 | tf_op jit(solution)/shard_map/ppermute | solution.py:1142
  105.7 39.7 %all-to-all-start.1 = ((bf16[8,64,1024]{2,1,0:T(8,128)(2,1)}), bf16[8,64,1024]{2,1,0:T(8,128)(2,1)S(1)}, u32[]{:S(2)}, u32[]{:S(2)}) async-start(bf16[8,64,1024]{2,1,0:T(8,128)(2,1)} %bitcast.14), calls=%async_computation.1 | async-start | bytes 2097152 | tf_op jit(solution)/shard_map/all_to_all | solution.py:99
  109.5 38.1 %collective-permute-start.8 = (bf16[512,1024]{1,0:T(8,128)(2,1)}, bf16[512,1024]{1,0:T(8,128)(2,1)}, u32[]{:S(2)}, u32[]{:S(2)}) collective-permute-start(bf16[512,1024]{1,0:T(8,128)(2,1)} %collective-permute-done.3.grads_in.refs_6_), channel_id=1, source_target_pairs={{0,2},{1,3},{2,0},{3,1},{4,5},{5,4},{6,7},{7,6},{8,10},{9,11},{10,... | collective-permute-start | bytes 3145736 | tf_op jit(solution)/shard_map/ppermute | solution.py:1142
  145.5 20.7 %collective-permute-start.6 = (bf16[512,1024]{1,0:T(8,128)(2,1)S(1)}, bf16[512,1024]{1,0:T(8,128)(2,1)S(1)}, u32[]{:S(2)}, u32[]{:S(2)}) collective-permute-start(bf16[512,1024]{1,0:T(8,128)(2,1)S(1)} %bitcast.95), channel_id=1, source_target_pairs={{0,2},{1,3},{2,0},{3,1},{4,5},{5,4},{6,7},{7,6},{8,10},{9,11},{10,... | collective-permute-start | bytes 3145736 | tf_op jit(solution)/shard_map/ppermute | solution.py:1142
  146.1 25.5 %collective-permute-start.7 = (bf16[512,1024]{1,0:T(8,128)(2,1)S(1)}, bf16[512,1024]{1,0:T(8,128)(2,1)S(1)}, u32[]{:S(2)}, u32[]{:S(2)}) collective-permute-start(bf16[512,1024]{1,0:T(8,128)(2,1)S(1)} %bitcast.105), channel_id=1, source_target_pairs={{0,2},{1,3},{2,0},{3,1},{4,5},{5,4},{6,7},{7,6},{8,10},{9,11},{10,... | collective-permute-start | bytes 3145736 | tf_op jit(solution)/shard_map/ppermute | solution.py:1142
  165.6 25.3 %collective-permute-start.10 = (bf16[512,1024]{1,0:T(8,128)(2,1)}, bf16[512,1024]{1,0:T(8,128)(2,1)S(1)}, u32[]{:S(2)}, u32[]{:S(2)}) collective-permute-start(bf16[512,1024]{1,0:T(8,128)(2,1)} %get-tuple-element.205), channel_id=1, source_target_pairs={{0,2},{1,3},{2,0},{3,1},{4,5},{5,4},{6,7},{7,6},{8,10},{9,11},{10,... | collective-permute-start | bytes 3145736 | tf_op jit(solution)/shard_map/ppermute | solution.py:1142
  213.3 34.9 %collective-permute-start.15 = (bf16[512,1024]{1,0:T(8,128)(2,1)}, bf16[512,1024]{1,0:T(8,128)(2,1)S(1)}, u32[]{:S(2)}, u32[]{:S(2)}) collective-permute-start(bf16[512,1024]{1,0:T(8,128)(2,1)} %get-tuple-element.212), channel_id=1, source_target_pairs={{0,2},{1,3},{2,0},{3,1},{4,5},{5,4},{6,7},{7,6},{8,10},{9,11},{10,... | collective-permute-start | bytes 3145736 | tf_op jit(solution)/shard_map/ppermute | solution.py:1142
  214.8 35.4 %all-to-all-start.3 = ((bf16[8,64,1024]{2,1,0:T(8,128)(2,1)}), bf16[8,64,1024]{2,1,0:T(8,128)(2,1)}, u32[]{:S(2)}, u32[]{:S(2)}) async-start(bf16[8,64,1024]{2,1,0:T(8,128)(2,1)} %bitcast.30), calls=%async_computation.3 | async-start | bytes 2097152 | tf_op jit(solution)/shard_map/all_to_all | solution.py:99
  228.5 25.3 %collective-permute-start.13 = (bf16[512,1024]{1,0:T(8,128)(2,1)S(1)}, bf16[512,1024]{1,0:T(8,128)(2,1)}, u32[]{:S(2)}, u32[]{:S(2)}) collective-permute-start(bf16[512,1024]{1,0:T(8,128)(2,1)S(1)} %add_convert_fusion.4), channel_id=1, source_target_pairs={{0,1},{1,0},{2,3},{3,2},{4,6},{5,7},{6,4},{7,5},{8,9},{9,8},{10,11... | collective-permute-start | bytes 3145736 | tf_op jit(solution)/shard_map/ppermute | solution.py:1142
  249.7 22.6 %collective-permute-start.16 = (bf16[512,1024]{1,0:T(8,128)(2,1)}, bf16[512,1024]{1,0:T(8,128)(2,1)S(1)}, u32[]{:S(2)}, u32[]{:S(2)}) collective-permute-start(bf16[512,1024]{1,0:T(8,128)(2,1)} %get-tuple-element.213), channel_id=1, source_target_pairs={{0,2},{1,3},{2,0},{3,1},{4,5},{5,4},{6,7},{7,6},{8,10},{9,11},{10,... | collective-permute-start | bytes 3145736 | tf_op jit(solution)/shard_map/ppermute | solution.py:1142
  250.2 30.1 %all-to-all-start.4 = ((bf16[8,64,1024]{2,1,0:T(8,128)(2,1)}), bf16[8,64,1024]{2,1,0:T(8,128)(2,1)S(1)}, u32[]{:S(2)}, u32[]{:S(2)}) async-start(bf16[8,64,1024]{2,1,0:T(8,128)(2,1)} %bitcast.32), calls=%async_computation.4 | async-start | bytes 2097152 | tf_op jit(solution)/shard_map/all_to_all | solution.py:99
  253.8 63.9 %collective-permute-start.14 = (bf16[3,704,1024]{2,1,0:T(8,128)(2,1)}, bf16[3,704,1024]{2,1,0:T(8,128)(2,1)}, u32[]{:S(2)}, u32[]{:S(2)}) collective-permute-start(bf16[3,704,1024]{2,1,0:T(8,128)(2,1)} %weight_pass.2), channel_id=1, source_target_pairs={{0,1},{1,0},{2,3},{3,2},{4,6},{5,7},{6,4},{7,5},{8,9},{9,8},{10,11... | collective-permute-start | bytes 12976136 | tf_op jit(solution)/shard_map/ppermute | solution.py:1142
  281.3 52.8 %all-to-all-start.5 = ((bf16[8,128,1024]{2,1,0:T(8,128)(2,1)}), bf16[8,128,1024]{2,1,0:T(8,128)(2,1)S(1)}, u32[]{:S(2)}, u32[]{:S(2)}) async-start(bf16[8,128,1024]{2,1,0:T(8,128)(2,1)} %bitcast.34), calls=%async_computation.5 | async-start | bytes 4194304 | tf_op jit(solution)/shard_map/all_to_all | solution.py:99
  369.1 19.6 %collective-permute-start.22 = (bf16[4,136,512]{2,1,0:T(8,128)(2,1)}, bf16[4,136,512]{2,1,0:T(8,128)(2,1)S(1)}, u32[]{:S(2)}, u32[]{:S(2)}) collective-permute-start(bf16[4,136,512]{2,1,0:T(8,128)(2,1)} %pad_maximum_fusion.3), channel_id=1, source_target_pairs={{0,2},{1,3},{2,0},{3,1},{4,6},{5,7},{6,4},{7,5},{8,10},{9,11},{10,... | collective-permute-start | bytes 1671176 | tf_op jit(solution)/shard_map/ppermute | solution.py:40
  375.0 20.6 %collective-permute-start.26 = (bf16[4,136,512]{2,1,0:T(8,128)(2,1)}, bf16[4,136,512]{2,1,0:T(8,128)(2,1)}, u32[]{:S(2)}, u32[]{:S(2)}) collective-permute-start(bf16[4,136,512]{2,1,0:T(8,128)(2,1)} %pad_maximum_fusion.5), channel_id=1, source_target_pairs={{0,2},{1,3},{2,0},{3,1},{4,6},{5,7},{6,4},{7,5},{8,10},{9,11},{10,... | collective-permute-start | bytes 1671176 | tf_op jit(solution)/shard_map/ppermute | solution.py:40
  376.3 20.6 %collective-permute-start.24 = (bf16[4,136,512]{2,1,0:T(8,128)(2,1)}, bf16[4,136,512]{2,1,0:T(8,128)(2,1)}, u32[]{:S(2)}, u32[]{:S(2)}) collective-permute-start(bf16[4,136,512]{2,1,0:T(8,128)(2,1)} %pad_maximum_fusion.4), channel_id=1, source_target_pairs={{0,1},{1,0},{2,3},{3,2},{4,5},{5,4},{6,7},{7,6},{8,9},{9,8},{10,11... | collective-permute-start | bytes 1671176 | tf_op jit(solution)/shard_map/ppermute | solution.py:40
  398.7 33.4 %collective-permute-start.27 = (bf16[128,1024]{1,0:T(8,128)(2,1)S(1)}, bf16[128,1024]{1,0:T(8,128)(2,1)S(1)}, u32[]{:S(2)}, u32[]{:S(2)}) collective-permute-start(bf16[128,1024]{1,0:T(8,128)(2,1)S(1)} %get-tuple-element.316), channel_id=1, source_target_pairs={{0,2},{1,3},{2,0},{3,1},{4,6},{5,7},{6,4},{7,5},{8,10},{9,11},{10,... | collective-permute-start | bytes 786440 | tf_op jit(solution)/shard_map/ppermute | solution.py:40
  399.3 32.9 %collective-permute-start.29 = (bf16[128,1024]{1,0:T(8,128)(2,1)S(1)}, bf16[128,1024]{1,0:T(8,128)(2,1)S(1)}, u32[]{:S(2)}, u32[]{:S(2)}) collective-permute-start(bf16[128,1024]{1,0:T(8,128)(2,1)S(1)} %get-tuple-element.315), channel_id=1, source_target_pairs={{0,1},{1,0},{2,3},{3,2},{4,5},{5,4},{6,7},{7,6},{8,9},{9,8},{10,11... | collective-permute-start | bytes 786440 | tf_op jit(solution)/shard_map/ppermute | solution.py:40
  423.0 22.3 %collective-permute-start.36 = (bf16[136,512]{1,0:T(8,128)(2,1)S(1)}, bf16[136,512]{1,0:T(8,128)(2,1)S(1)}, u32[]{:S(2)}, u32[]{:S(2)}) collective-permute-start(bf16[136,512]{1,0:T(8,128)(2,1)S(1)} %get-tuple-element.298), channel_id=1, source_target_pairs={{0,24},{4,28},{8,16},{12,20},{16,8},{20,12},{24,0},{28,4},{1,25},{... | collective-permute-start | bytes 417800 | tf_op jit(solution)/shard_map/ppermute | solution.py:40
  446.1 23.9 %collective-permute-start.37 = (bf16[4,136,512]{2,1,0:T(8,128)(2,1)S(1)}, bf16[4,136,512]{2,1,0:T(8,128)(2,1)S(1)}, u32[]{:S(2)}, u32[]{:S(2)}) collective-permute-start(bf16[4,136,512]{2,1,0:T(8,128)(2,1)S(1)} %pad_maximum_fusion.6), channel_id=1, source_target_pairs={{0,1},{1,0},{2,3},{3,2},{4,5},{5,4},{6,7},{7,6},{8,9},{9,8},{10,11... | collective-permute-start | bytes 1671176 | tf_op jit(solution)/shard_map/ppermute | solution.py:40
  447.7 23.3 %collective-permute-start.38 = (bf16[4,136,512]{2,1,0:T(8,128)(2,1)S(1)}, bf16[4,136,512]{2,1,0:T(8,128)(2,1)S(1)}, u32[]{:S(2)}, u32[]{:S(2)}) collective-permute-start(bf16[4,136,512]{2,1,0:T(8,128)(2,1)S(1)} %pad_maximum_fusion.6), channel_id=1, source_target_pairs={{0,2},{1,3},{2,0},{3,1},{4,6},{5,7},{6,4},{7,5},{8,10},{9,11},{10,... | collective-permute-start | bytes 1671176 | tf_op jit(solution)/shard_map/ppermute | solution.py:40
  458.2 25.3 %collective-permute-start.48 = (bf16[4,136,512]{2,1,0:T(8,128)(2,1)S(1)}, bf16[4,136,512]{2,1,0:T(8,128)(2,1)S(1)}, u32[]{:S(2)}, u32[]{:S(2)}) collective-permute-start(bf16[4,136,512]{2,1,0:T(8,128)(2,1)S(1)} %pad_maximum_fusion.7), channel_id=1, source_target_pairs={{0,1},{1,0},{2,3},{3,2},{4,5},{5,4},{6,7},{7,6},{8,9},{9,8},{10,11... | collective-permute-start | bytes 1671176 | tf_op jit(solution)/shard_map/ppermute | solution.py:40
  459.8 26.5 %collective-permute-start.49 = (bf16[4,136,512]{2,1,0:T(8,128)(2,1)S(1)}, bf16[4,136,512]{2,1,0:T(8,128)(2,1)S(1)}, u32[]{:S(2)}, u32[]{:S(2)}) collective-permute-start(bf16[4,136,512]{2,1,0:T(8,128)(2,1)S(1)} %pad_maximum_fusion.7), channel_id=1, source_target_pairs={{0,2},{1,3},{2,0},{3,1},{4,6},{5,7},{6,4},{7,5},{8,10},{9,11},{10,... | collective-permute-start | bytes 1671176 | tf_op jit(solution)/shard_map/ppermute | solution.py:40
  481.9 24.1 %collective-permute-start.41 = (bf16[16,136,512]{2,1,0:T(8,128)(2,1)}, bf16[16,136,512]{2,1,0:T(8,128)(2,1)}, u32[]{:S(2)}, u32[]{:S(2)}) collective-permute-start(bf16[16,136,512]{2,1,0:T(8,128)(2,1)} %constant_dynamic-update-slice_fusion.near), channel_id=1, source_target_pairs={{0,4},{4,0},{8,12},{12,8},{16,20},{20,16},{24,28},{28,24},{1,5},{5... | collective-permute-start | bytes 6684680 | tf_op jit(solution)/shard_map/ppermute | solution.py:40
  495.9 20.3 %collective-permute-start.52 = (bf16[16,136,512]{2,1,0:T(8,128)(2,1)}, bf16[16,136,512]{2,1,0:T(8,128)(2,1)}, u32[]{:S(2)}, u32[]{:S(2)}) collective-permute-start(bf16[16,136,512]{2,1,0:T(8,128)(2,1)} %constant_dynamic-update-slice_fusion.8.near), channel_id=1, source_target_pairs={{0,4},{4,0},{8,12},{12,8},{16,20},{20,16},{24,28},{28,24},{1,5},{5... | collective-permute-start | bytes 6684680 | tf_op jit(solution)/shard_map/ppermute | solution.py:40
  (58 other events, 728.0 us)

commit v4 on v3

--- a/solution.py
+++ b/solution.py
@@ -112,14 +112,15 @@
 
 
 def sum_depth(rest):
-    own = rest[0].astype(f32)
-    for m in range(1, 4):
-        own = own + swap(rest[m], "expert", 2 * m).astype(f32)
-    return own.astype(bf16)
+    arrived = swap(rest[1::2], "expert", 2)
+    own, opposite = add_low(rest[0], arrived[0]), add_low(rest[2], arrived[1])
+    return add_low(own, swap(opposite, "expert", 4))
 
 
 def spread_depth(own):
-    return jnp.stack([own] + [swap(own, "expert", 2 * m) for m in range(1, 4)])
+    opposite = swap(own, "expert", 4)
+    arrived = swap(jnp.stack([own, opposite]), "expert", 2)
+    return jnp.stack([own, arrived[0], opposite, arrived[1]])
 
 
 def spread_plane(rest):
@@ -248,6 +249,7 @@
     spot = lax.broadcasted_iota(jnp.int32, (1, rows), 1)
     kept = [start + spot < far_len for start in starts]
     near_kept = lax.broadcasted_iota(jnp.int32, (1, short), 1) < near_len
+    line = 2 * (pl.program_id(0) % 4)
     mine = [jnp.where(own_lanes(head, dim, low.shape, 1), low, jnp.zeros_like(low)) for head in range(2)]
     far_mine = jnp.concatenate([part[:rows] for part in mine], axis=0)
     near_parts = mm(jnp.concatenate([part[rows:] for part in mine], axis=0), near[:short], NT)
@@ -257,10 +259,10 @@
         for head in range(2):
             scores[head, :, r * rows : (r + 1) * rows] = part[head * rows : (head + 1) * rows]
     for head in range(2):
-        table = jnp.broadcast_to(far_bias[0, head : head + 1, :], (band, reach))
+        table = jnp.broadcast_to(far_bias[pl.ds(line + head, 1)], (band, reach))
         window[head] = pltpu.roll(table, reach - (band - 1), 1, stride=1, stride_axis=0)
     for head in range(2):
-        table = jnp.broadcast_to(near_bias[0, head : head + 1, :], (short, 2 * short))
+        table = jnp.broadcast_to(near_bias[pl.ds(line + head, 1)], (short, 2 * short))
         bias = pltpu.roll(table, short + 1, 1, stride=1, stride_axis=0)[:, :short]
         part = jnp.where(near_kept, near_parts[head] + bias, -1e30)
         part = jnp.exp(part - jnp.max(part, axis=-1, keepdims=True))
@@ -299,7 +301,7 @@
 def attention_specs(count, rows, short, reach, tokens):
     cut = lambda size: pl.BlockSpec((size, 128), lambda i, *_: (0, i))
     parts = [cut(2 * rows), cut(2 * (count - 1) * rows)]
-    table = lambda size: pl.BlockSpec((1, 2, size), lambda i, *_: (i, 0, 0))
+    table = lambda size: pl.BlockSpec((8, size), lambda i, *_: (i // 4, 0))
     weights = lambda size, span: pl.BlockSpec((2, size, span), lambda i, *_: (i, 0, 0))
     return (
         cut(tokens),
@@ -1143,9 +1145,11 @@
 
     long_rows = inputs[:long_local]
     sources = [swap(long_rows, "tensor", r) for r in range(1, tensor_axis)]
-    normed_low, query, pair, near = project(inputs, attn_gain, w_query, w_key, w_value, long_local)
     slots, wide_slots, grad_slots_in = place_rows(
-        turns.reshape(1, 2), after(routes_rows, normed_low), cotangent, capacity, padded, block, local
+        turns.reshape(1, 2), routes_rows, cotangent, capacity, padded, block, local
+    )
+    normed_low, query, pair, near = project(
+        after(inputs, sources), attn_gain, w_query, w_key, w_value, long_local
     )
 
     def by_expert(rows):
@@ -1175,7 +1179,7 @@
     short_hot = table_hot(jnp.pad(short_buckets, (0, 1), constant_values=-1), bucket_count)
     spread = lambda hot: jnp.einsum(
         "cb,bh->hc", hot, rel_table, precision=precise, preferred_element_type=f32
-    ).reshape(heads // 2, 2, hot.shape[0])
+    )
     mixed, far_attend, near_attend = attend_forward(
         facts, query, parts, near, spread(long_hot), spread(short_hot),
         tensor_axis, long_local, head_dim,
@@ -1202,7 +1206,7 @@
         pass_b = run(rows_b, grads_b)
         pass_d = run(after(rows_d, pass_b[1]), grads_d)
         rows_c = trade(after(rows_a, rows_d), True)
-        pass_a = run(after(rows_a, pass_d[1], grads_c, rows_c), grad_arrived[0])
+        pass_a = run(after(rows_a, pass_d[1], rows_c), grad_arrived[0])
         traded = add_low(pass_b[2], after(trade(pass_d[2], True), pass_a[1]))
         traded = trade(traded, False)
         pass_c = run(after(rows_c, pass_a[1]), grads_c)
@@ -1261,13 +1265,13 @@
         facts, query, grad_mixed, parts, near, (far_attend, near_attend), hots, tensor_axis, long_local, head_dim
     )
     if quick:
-        bias_grad = after(bias_grad, sent, outs_back)
+        bias_grad = after(bias_grad, sent)
         made = weight_blocks(
             facts, (normed_low, normed_others, mixed), attn_grads, branch, bias_grad, moe_gain_grad, router_grad,
             long_local,
         )
         sums = [add_low(made[half], swap(made[half + 1], "expert", 1)) for half in (0, 2)]
-        attn_grads = after_all(attn_grads, sums)
+        attn_grads = after_all(attn_grads, sums, outs_back)
     own_grads, near_grads, away = normed_grads(attn_grads, w_query, w_key, w_value, long_local, tensor_axis)
     if quick:
         sums = [ring_sum(plane_parts(part), in_plane).astype(bf16) for part in sums]
@@ -1279,9 +1283,10 @@
         pieces = pieces[:3] + [pieces[3][: long_local // 2], pieces[3][long_local // 2 :]]
     summed = sum_parts(pieces)
     if quick:
-        sums = [spread_depth(sum_depth(part)) for part in sums]
+        owns = [sum_depth(part) for part in sums]
+        sums = [spread_depth(own) for own in owns]
+        sent, outs_back, summed = after_all((sent, outs_back, summed), sums[0], owns[1])
         sums[1] = after(sums[1], summed)
-        sent, outs_back, summed = after_all((sent, outs_back, summed), sums[0])
     if paired:
         weight_grads = weight_fill(facts, sent, weight_grads)
     slot_places = jnp.arange(local * block, dtype=jnp.int32)
@@ -1299,13 +1304,17 @@
         lifted - normed * jnp.mean(lifted * normed, axis=-1, keepdims=True)
     )
     if quick:
-        sums = [spread_plane(part) for part in sums]
-        far = [swap(part, "expert", 1) for part in sums]
-        sums[0] = after(sums[0], outputs, weight_grads, inputs_grad)
         unpack = partial(unpack_blocks, facts)
         weights = (w_query, w_key, w_value, attn_gain)
-        first = unpack(sums[0], far[0], *weights, (), 0)
-        second = unpack(sums[1], far[1], *weights, first[:4], 1)
+        one, two = sums
+        by_x, by_y = in_plane(one, 0), in_plane(one, 1)
+        half_x, half_y = after_all((by_x[:2], by_y[2:]), outputs, weight_grads, two)
+        one = jnp.concatenate([one, by_x, by_y, in_plane(half_x, 1), in_plane(half_y, 0)], axis=0)
+        first = unpack(one, swap(one, "expert", 1), *weights, (), 0)
+        by_x, by_y = in_plane(two, 0), in_plane(two, 1)
+        rest = after_all((in_plane(by_x[:2], 1), in_plane(by_y[2:], 0)), first[5], inputs_grad)
+        two = jnp.concatenate([two, by_x, by_y] + rest, axis=0)
+        second = unpack(two, swap(two, "expert", 1), *weights, first[:4], 1)
         query_grad, key_grad, value_grad, proj_grad = second[:4]
         attn_gain_grad = (first[4] + second[4])[0]
         small = jnp.concatenate([first[5], second[5]], axis=1)

time: 537 us -> 498 us (0.927)
  waiting for transfers between devices: 146 us -> 101 us
  starting transfers between devices: 88.5 us -> 95.5 us
    ppermute x39 -> x35, waiting for transfers between devices: 66.1 us -> 47.9 us  [swap(): return lax.ppermute(rows, axis, [(i, i ^ mask) for i in range(count)])]
    all_to_all x6, waiting for transfers between devices: 46.3 us -> 29.8 us  [over_experts(): lax.all_to_all(blocks, 'expert', 0, 0, tiled=True).reshape(rows.shape)]
    ppermute x14, waiting for transfers between devices: 33.7 us -> 23.8 us  [trade(): return lax.ppermute(rows, ('expert', 'tensor'), pairs)]
    unnamed x73 -> x75, local copies, waits for them, and re-layouts: 10.9 us -> 7.52 us
    ppermute x39 -> x35, starting transfers between devices: 49 us -> 50.9 us  [swap(): return lax.ppermute(rows, axis, [(i, i ^ mask) for i in range(count)])]
  transfers between devices with their start and end apart: 59 -> 55, of which waited for: 30 -> 23; matrix products, arithmetic and copies ran while one was open for 10% -> 10% of each run, Pallas kernels for 39% -> 45%
where the time goes in v4:
time: 498 us; the launch traced here: 490 us
  Pallas kernels  228 us (46%)
  waiting for transfers between devices  101 us (20%)
  starting transfers between devices  95.5 us (19%)
  other arithmetic  26.9 us (5%)
  local copies, waits for them, and re-layouts  26.1 us (5%)
  matrix products  8.16 us (2%)
    pallas_call x4, Pallas kernels, expert_pass(): pl.pallas_call(partial(expert_kernel, chunks, capacity, padded, lanes_use...  72.1 us
    ppermute x35, starting transfers between devices, swap(): return lax.ppermute(rows, axis, [(i, i ^ mask) for i in range(count)])  50.9 us
    ppermute x35, waiting for transfers between devices, swap(): return lax.ppermute(rows, axis, [(i, i ^ mask) for i in range(count)])  47.9 us
    pallas_call x2, Pallas kernels, weight_pass(): pl.pallas_call(body, grid_spec=pltpu.PrefetchScalarGridSpec(num_scalar_pr...  31.9 us
    all_to_all x6, waiting for transfers between devices, over_experts(): lax.all_to_all(blocks, 'expert', 0, 0, tiled=True).reshape(rows.shape)  29.8 us
    all_to_all x6, starting transfers between devices, over_experts(): lax.all_to_all(blocks, 'expert', 0, 0, tiled=True).reshape(rows.shape)  26.7 us
    pallas_call x1, Pallas kernels, attend_backward(): pl.pallas_call(partial(backward_kernel, count, rows, dim), grid_spec=pltp...  24.5 us
    ppermute x14, waiting for transfers between devices, trade(): return lax.ppermute(rows, ('expert', 'tensor'), pairs)  23.8 us
  transfers between devices with their start and end apart: 55, of which 23 were waited for; matrix products, arithmetic and copies ran while one was open for 10% of the time, Pallas kernels for 45%

profile of v4, /device:TPU:0, one launch (start us, length us, event | category | flops | bytes accessed | tf_op | source)
XLA Modules:
  0.0 489.6 jit_solution(14314665201143210189)
XLA Ops:
  7.6 3.9 place_rows.1
  11.5 5.5 %all-to-all-start.2 = ((bf16[8,128,1024]{2,1,0:T(8,128)(2,1)}), bf16[8,128,1024]{2,1,0:T(8,128)(2,1)S(1)}, u32[]{:S(2)}, u32[]{:S(2)}) async-start(bf16[8,128,1024]{2,1,0:T(8,128)(2,1)} %bitcast.78), calls=%async_computation.2 | async-start | bytes 4194304 | tf_op jit(solution)/shard_map/all_to_all | solution.py:99
  33.7 6.8 %project.1 = (bf16[384,1024]{1,0:T(8,128)(2,1)}, bf16[384,1024]{1,0:T(8,128)(2,1)}, bf16[512,1024]{1,0:T(8,128)(2,1)}, bf16[256,1024]{1,0:T(8,128)(2,1)}) custom-call(bf16[384,1024]{1,0:T(8,128)(2,1)} %inputs.2, bf16[1,1024]{1,0:T(2,128)(2,1)} %reshape.126.gain, bf16[1024,1024]{1,0:T(8,128)(2,1)} %w_query.7, bf16[1024,1024]{1,0:T(8,128)(2,1)} %w_key.9, ...), custom_call_target="tpu_custom_call" | custom-call | flops 7935000064 | tf_op jit(solution)/shard_map/project/pallas_call | solution.py:155
  40.5 7.7 %project_others.1 = (bf16[768,1024]{1,0:T(8,128)(2,1)}, bf16[1536,1024]{1,0:T(8,128)(2,1)}) custom-call(bf16[1,1024]{1,0:T(2,128)(2,1)} %reshape.126.gain, bf16[1024,1024]{1,0:T(8,128)(2,1)} %w_key.9, bf16[1024,1024]{1,0:T(8,128)(2,1)} %w_value.9, bf16[256,1024]{1,0:T(8,128)(2,1)} %collective-permute-done.refs_0_, ...), custom_call_target="tpu_custom_call" | custom-call | flops 8855000064 | tf_op jit(solution)/shard_map/project_others/pallas_call | solution.py:196
  48.2 17.3 %attend_forward.1 = (bf16[384,1024]{1,0:T(8,128)(2,1)}, bf16[16,256,1024]{2,1,0:T(8,128)(2,1)}, bf16[16,128,128]{2,1,0:T(8,128)(2,1)}) custom-call(s32[7]{0:T(128)} %stack.66.facts, bf16[384,1024]{1,0:T(8,128)(2,1)} %get-tuple-element.157.query, bf16[512,1024]{1,0:T(8,128)(2,1)} %get-tuple-element.158.pair, bf16[1536,1024]{1,0:T(8,128)(2,1)} %get-tuple-element.159.others, ...), custom_call_target="tpu_custom_call" | custom-call | flops 19549999104 | tf_op jit(solution)/shard_map/attend_forward/pallas_call | solution.py:321
  65.5 6.4 %route_rows.1 = (f32[384,1024]{1,0:T(8,128)}, bf16[384,1024]{1,0:T(8,128)(2,1)}, f32[16,384]{1,0:T(8,128)}, f32[2,384]{1,0:T(2,128)}, bf16[512,1024]{1,0:T(8,128)(2,1)}, /*index=5*/bf16[512,1024]{1,0:T(8,128)(2,1)}) custom-call(bf16[384,1024]{1,0:T(8,128)(2,1)} %get-tuple-element.161.mixed, bf16[1024,1024]{1,0:T(8,128)(2,1)} %w_proj.3, ...), custom_call_target="tpu_custom_call" | custom-call | flops 7360000000 | tf_op jit(solution)/shard_map/route_rows/pallas_call | solution.py:827
  71.9 5.1 %all-to-all-start = ((bf16[8,64,1024]{2,1,0:T(8,128)(2,1)}), bf16[8,64,1024]{2,1,0:T(8,128)(2,1)S(1)}, u32[]{:S(2)}, u32[]{:S(2)}) async-start(bf16[8,64,1024]{2,1,0:T(8,128)(2,1)} %bitcast.91), calls=%async_computation | async-start | bytes 2097152 | tf_op jit(solution)/shard_map/all_to_all | solution.py:99
  79.4 24.2 %all-to-all-done = bf16[8,64,1024]{2,1,0:T(8,128)(2,1)S(1)} async-done(((bf16[8,64,1024]{2,1,0:T(8,128)(2,1)}), bf16[8,64,1024]{2,1,0:T(8,128)(2,1)S(1)}, u32[]{:S(2)}, u32[]{:S(2)}) %all-to-all-start) | async-done | bytes 1048608 | tf_op jit(solution)/shard_map/all_to_all | solution.py:99
  109.3 16.1 %collective-permute-done.4.rows_in.refs_2_ = bf16[512,1024]{1,0:T(8,128)(2,1)} collective-permute-done((bf16[512,1024]{1,0:T(8,128)(2,1)S(1)}, bf16[512,1024]{1,0:T(8,128)(2,1)}, u32[]{:S(2)}, u32[]{:S(2)}) %collective-permute-start.4) | collective-permute-done | bytes 1048608 | tf_op jit(solution)/shard_map/ppermute | solution.py:1144
  127.4 17.9 %expert_pass.4 = (bf16[512,704]{1,0:T(8,128)(2,1)}, bf16[512,704]{1,0:T(8,128)(2,1)}, bf16[512,704]{1,0:T(8,128)(2,1)}, bf16[512,704]{1,0:T(8,128)(2,1)}, bf16[5...) custom-call(s32[7]{0:T(128)} %stack.66.facts, ...), custom_call_target="tpu_custom_call" | custom-call | flops 20700000256 | tf_op jit(solution)/shard_map/expert_pass/pallas_call | solution.py:611
  147.5 18.0 %expert_pass.5 = (bf16[512,704]{1,0:T(8,128)(2,1)}, bf16[512,704]{1,0:T(8,128)(2,1)}, bf16[512,704]{1,0:T(8,128)(2,1)}, bf16[512,704]{1,0:T(8,128)(2,1)}, bf16[5...) custom-call(s32[7]{0:T(128)} %stack.66.facts, ...), custom_call_target="tpu_custom_call" | custom-call | flops 20700000256 | tf_op jit(solution)/shard_map/expert_pass/pallas_call | solution.py:611
  165.6 18.3 %expert_pass.6 = (bf16[512,704]{1,0:T(8,128)(2,1)}, bf16[512,704]{1,0:T(8,128)(2,1)}, bf16[512,704]{1,0:T(8,128)(2,1)}, bf16[512,704]{1,0:T(8,128)(2,1)}, bf16[5...) custom-call(s32[7]{0:T(128)} %stack.66.facts, ...), custom_call_target="tpu_custom_call" | custom-call | flops 20700000256 | tf_op jit(solution)/shard_map/expert_pass/pallas_call | solution.py:611
  184.9 18.0 %expert_pass.7 = (bf16[512,704]{1,0:T(8,128)(2,1)}, bf16[512,704]{1,0:T(8,128)(2,1)}, bf16[512,704]{1,0:T(8,128)(2,1)}, bf16[512,704]{1,0:T(8,128)(2,1)}, bf16[5...) custom-call(s32[7]{0:T(128)} %stack.66.facts, ...), custom_call_target="tpu_custom_call" | custom-call | flops 20700000256 | tf_op jit(solution)/shard_map/expert_pass/pallas_call | solution.py:611
  207.5 4.2 all-to-all-start.3
  211.7 6.3 %collective-permute-done.12 = bf16[512,1024]{1,0:T(8,128)(2,1)} collective-permute-done((bf16[512,1024]{1,0:T(8,128)(2,1)}, bf16[512,1024]{1,0:T(8,128)(2,1)}, u32[]{:S(2)}, u32[]{:S(2)}) %collective-permute-start.12) | collective-permute-done | bytes 1048608 | tf_op jit(solution)/shard_map/ppermute | solution.py:1144
  222.3 16.2 %weight_pass.2 = bf16[3,704,1024]{2,1,0:T(8,128)(2,1)} custom-call(s32[7]{0:T(128)} %stack.66.facts, bf16[512,1024]{1,0:T(8,128)(2,1)} %bitcast.87, bf16[512,1024]{1,0:T(8,128)(2,1)} %copy-done.30, bf16[512,1024]{1,0:T(8,128)(2,1)} %collective-permute-done.4.rows_in.refs_2_, bf16[512,1024]{1,0:T(8,128)(2,1)} %copy-done.29, bf16[512,1024]{1,0:T(8,128)(2,1)} %bitcast.93, ...), custom_call_target="tpu_custom_call" | custom-call | flops 18400000000 | tf_op jit(solution)/shard_map/weight_pass/pallas_call | solution.py:691
  249.0 15.6 %weight_pass.3 = (f32[2,704,1024]{2,1,0:T(8,128)}, f32[2,704,1024]{2,1,0:T(8,128)}, f32[2,704,1024]{2,1,0:T(8,128)}) custom-call(s32[7]{0:T(128)} %stack.66.facts, bf16[512,1024]{1,0:T(8,128)(2,1)} %bitcast.88, bf16[512,1024]{1,0:T(8,128)(2,1)} %copy-done.30, bf16[512,1024]{1,0:T(8,128)(2,1)} %collective-permute-done.4.rows_in.refs_2_, ...), custom_call_target="tpu_custom_call" | custom-call | flops 18400000000 | tf_op jit(solution)/shard_map/weight_pass/pallas_call | solution.py:691
  267.8 5.6 %all-to-all-done.4 = bf16[8,64,1024]{2,1,0:T(8,128)(2,1)S(1)} async-done(((bf16[8,64,1024]{2,1,0:T(8,128)(2,1)}), bf16[8,64,1024]{2,1,0:T(8,128)(2,1)S(1)}, u32[]{:S(2)}, u32[]{:S(2)}) %all-to-all-start.4) | async-done | bytes 1048608 | tf_op jit(solution)/shard_map/all_to_all | solution.py:99
  273.4 4.6 all-to-all-start.5
  278.0 7.4 %merge_rows.1 = (f32[384,1024]{1,0:T(8,128)}, bf16[384,1024]{1,0:T(8,128)(2,1)}, f32[1,1024]{1,0:T(1,128)}, f32[16,1024]{1,0:T(8,128)}, bf16[384,1024]{1,0:T(8,128)(2,1)}) custom-call(bf16[384,1024]{1,0:T(8,128)(2,1)} %cotangent.1, f32[384,1024]{1,0:T(8,128)} %get-tuple-element.163.resid, f32[16,384]{1,0:T(8,128)} %get-tuple-element.246.probs, ...), custom_call_target="tpu_custom_call" | custom-call | flops 8510000128 | tf_op jit(solution)/shard_map/merge_rows/pallas_call | solution.py:903
  285.4 24.5 %attend_backward.1 = (bf16[384,1024]{1,0:T(8,128)(2,1)}, bf16[512,1024]{1,0:T(8,128)(2,1)}, bf16[1536,1024]{1,0:T(8,128)(2,1)}, bf16[256,1024]{1,0:T(8,128)(2,1)}, f32[8,2,32]{2,1,0:T(2,128)}) custom-call(s32[7]{0:T(128)} %stack.66.facts, bf16[384,1024]{1,0:T(8,128)(2,1)} %get-tuple-element.157.query, bf16[384,1024]{1,0:T(8,128)(2,1)} %get-tuple-element.249.grad, ...), custom_call_target="tpu_custom_call" | custom-call | flops 28750000128 | tf_op jit(solution)/shard_map/attend_backward/pallas_call | solution.py:462
  309.9 15.8 %weight_blocks.1 = (bf16[16,136,512]{2,1,0:T(8,128)(2,1)}, bf16[16,136,512]{2,1,0:T(8,128)(2,1)}, bf16[16,136,512]{2,1,0:T(8,128)(2,1)}, bf16[16,136,512]{2,1,0:T(8,128)(2,1)}) custom-call(s32[7]{0:T(128)} %stack.66.facts, bf16[384,1024]{1,0:T(8,128)(2,1)} %get-tuple-element.256.normed, bf16[768,1024]{1,0:T(8,128)(2,1)} %get-tuple-element.257.normed_others, ...), custom_call_target="tpu_custom_call" | custom-call | flops 19549999104 | tf_op jit(solution)/shard_map/weight_blocks/pallas_call | solution.py:989
  326.2 4.1 collective-permute-done.17
  354.9 11.8 %normed_grads.1 = (f32[256,1024]{1,0:T(8,128)}, f32[128,1024]{1,0:T(8,128)}, f32[768,1024]{1,0:T(8,128)}) custom-call(bf16[384,1024]{1,0:T(8,128)(2,1)} %get-tuple-element.267.grad_query.query, bf16[512,1024]{1,0:T(8,128)(2,1)} %get-tuple-element.268.grad_pair.pair, bf16[1536,1024]{1,0:T(8,128)(2,1)} %get-tuple-element.269.grad_others.others, ...), custom_call_target="tpu_custom_call" | custom-call | flops 14949999616 | tf_op jit(solution)/shard_map/normed_grads/pallas_call | solution.py:518
  367.0 5.6 %collective-permute-done.26 = bf16[4,136,512]{2,1,0:T(8,128)(2,1)} collective-permute-done((bf16[4,136,512]{2,1,0:T(8,128)(2,1)}, bf16[4,136,512]{2,1,0:T(8,128)(2,1)}, u32[]{:S(2)}, u32[]{:S(2)}) %collective-permute-start.26) | collective-permute-done | bytes 557088 | tf_op jit(solution)/shard_map/ppermute | solution.py:40
  398.6 4.8 collective-permute-done.36
  406.1 6.9 %collective-permute-start.34 = (bf16[2,136,512]{2,1,0:T(8,128)(2,1)S(1)}, bf16[2,136,512]{2,1,0:T(8,128)(2,1)S(1)}, u32[]{:S(2)}, u32[]{:S(2)}) collective-permute-start(bf16[2,136,512]{2,1,0:T(8,128)(2,1)S(1)} %pad_maximum_fusion.10), channel_id=1, source_target_pairs={{0,8},{4,12},{8,0},{12,4},{16,24},{20,28},{24,16},{28,20},{1,9},{5... | collective-permute-start | bytes 835592 | tf_op jit(solution)/shard_map/ppermute | solution.py:40
  413.1 4.4 collective-permute-start.40
  423.3 6.6 %weight_fill.1 = (f32[2,704,1024]{2,1,0:T(8,128)}, f32[2,704,1024]{2,1,0:T(8,128)}, f32[2,704,1024]{2,1,0:T(8,128)}) custom-call(s32[7]{0:T(128)} %stack.66.facts, bf16[3,704,1024]{2,1,0:T(8,128)(2,1)} %collective-permute-done.14.source, f32[2,704,1024]{2,1,0:T(8,128)} %get-tuple-element.241.refs_0_, ...), custom_call_target="tpu_custom_call", output_to_operand_aliasing={{0}: (2, {}), {1}: (3, {}), {2}: (4, {})} | custom-call | flops 7474999808 | tf_op jit(solution)/shard_map/weight_fill/pallas_call | solution.py:720
  450.5 10.7 %collective-permute-done.44 = bf16[4,136,512]{2,1,0:T(8,128)(2,1)S(1)} collective-permute-done((bf16[4,136,512]{2,1,0:T(8,128)(2,1)S(1)}, bf16[4,136,512]{2,1,0:T(8,128)(2,1)S(1)}, u32[]{:S(2)}, u32[]{:S(2)}) %collective-permute-start.44) | collective-permute-done | bytes 557088 | tf_op jit(solution)/shard_map/ppermute | solution.py:40
  465.1 7.9 %unpack_blocks.2 = (f32[1024,1024]{1,0:T(8,128)}, f32[1024,1024]{1,0:T(8,128)}, f32[1024,1024]{1,0:T(8,128)}, f32[1024,1024]{1,0:T(8,128)}, f32[1,1024]{1,0:T(1,128)}, /*index=5*/f32[24,512]{1,0:T(8,128)}) custom-call(s32[7]{0:T(128)} %stack.66.facts, bf16[16,136,512]{2,1,0:T(8,128)(2,1)} %constant_dynamic-update-slice_fusion.near, ...), custom_call_target="tpu_custom_call" | custom-call | flops 9200000000 | tf_op jit(solution)/shard_map/unpack_blocks/pallas_call | solution.py:1060
  477.7 8.0 %unpack_blocks.3 = (f32[1024,1024]{1,0:T(8,128)}, f32[1024,1024]{1,0:T(8,128)}, f32[1024,1024]{1,0:T(8,128)}, f32[1024,1024]{1,0:T(8,128)}, f32[1,1024]{1,0:T(1,128)}, /*index=5*/f32[24,512]{1,0:T(8,128)}) custom-call(s32[7]{0:T(128)} %stack.66.facts, ...), custom_call_target="tpu_custom_call", output_to_operand_aliasing={{0}: (7, {}), {1}: (8, {}), {2}: (9, {}), {3}: (10, {})} | custom-call | flops 9200000000 | tf_op jit(solution)/shard_map/unpack_blocks/pallas_call | solution.py:1060
  (243 shorter events, 150.0 us)
Async XLA Ops:
  2.5 29.6 %collective-permute-start = (bf16[256,1024]{1,0:T(8,128)(2,1)}, bf16[256,1024]{1,0:T(8,128)(2,1)}, u32[]{:S(2)}, u32[]{:S(2)}) collective-permute-start(bf16[256,1024]{1,0:T(8,128)(2,1)} %slice.168), channel_id=1, source_target_pairs={{0,1},{1,0},{2,3},{3,2},{4,5},{5,4},{6,7},{7,6},{8,9},{9,8},{10,11... | collective-permute-start | bytes 1572872 | tf_op jit(solution)/shard_map/ppermute | solution.py:40
  5.5 26.6 %collective-permute-start.1 = (bf16[256,1024]{1,0:T(8,128)(2,1)}, bf16[256,1024]{1,0:T(8,128)(2,1)}, u32[]{:S(2)}, u32[]{:S(2)}) collective-permute-start(bf16[256,1024]{1,0:T(8,128)(2,1)} %slice.168), channel_id=1, source_target_pairs={{0,2},{1,3},{2,0},{3,1},{4,6},{5,7},{6,4},{7,5},{8,10},{9,11},{10,... | collective-permute-start | bytes 1572872 | tf_op jit(solution)/shard_map/ppermute | solution.py:40
  7.0 25.1 %collective-permute-start.2 = (bf16[256,1024]{1,0:T(8,128)(2,1)}, bf16[256,1024]{1,0:T(8,128)(2,1)}, u32[]{:S(2)}, u32[]{:S(2)}) collective-permute-start(bf16[256,1024]{1,0:T(8,128)(2,1)} %slice.168), channel_id=1, source_target_pairs={{0,3},{1,2},{2,1},{3,0},{4,7},{5,6},{6,5},{7,4},{8,11},{9,10},{10,... | collective-permute-start | bytes 1572872 | tf_op jit(solution)/shard_map/ppermute | solution.py:40
  11.5 60.5 %all-to-all-start.2 = ((bf16[8,128,1024]{2,1,0:T(8,128)(2,1)}), bf16[8,128,1024]{2,1,0:T(8,128)(2,1)S(1)}, u32[]{:S(2)}, u32[]{:S(2)}) async-start(bf16[8,128,1024]{2,1,0:T(8,128)(2,1)} %bitcast.78), calls=%async_computation.2 | async-start | bytes 4194304 | tf_op jit(solution)/shard_map/all_to_all | solution.py:99
  32.1 95.3 %collective-permute-start.9 = (bf16[3,704,1024]{2,1,0:T(8,128)(2,1)}, bf16[3,704,1024]{2,1,0:T(8,128)(2,1)}, u32[]{:S(2)}, u32[]{:S(2)}) collective-permute-start(bf16[3,704,1024]{2,1,0:T(8,128)(2,1)} %pad_maximum_fusion), channel_id=1, source_target_pairs={{0,1},{1,0},{2,3},{3,2},{4,6},{5,7},{6,4},{7,5},{8,9},{9,8},{10,11... | collective-permute-start | bytes 12976136 | tf_op jit(solution)/shard_map/ppermute | solution.py:1144
  71.9 31.7 %all-to-all-start = ((bf16[8,64,1024]{2,1,0:T(8,128)(2,1)}), bf16[8,64,1024]{2,1,0:T(8,128)(2,1)S(1)}, u32[]{:S(2)}, u32[]{:S(2)}) async-start(bf16[8,64,1024]{2,1,0:T(8,128)(2,1)} %bitcast.91), calls=%async_computation | async-start | bytes 2097152 | tf_op jit(solution)/shard_map/all_to_all | solution.py:99
  78.6 25.0 %collective-permute-start.3 = (bf16[512,1024]{1,0:T(8,128)(2,1)}, bf16[512,1024]{1,0:T(8,128)(2,1)}, u32[]{:S(2)}, u32[]{:S(2)}) collective-permute-start(bf16[512,1024]{1,0:T(8,128)(2,1)} %bitcast.19), channel_id=1, source_target_pairs={{0,1},{1,0},{2,3},{3,2},{4,6},{5,7},{6,4},{7,5},{8,9},{9,8},{10,11... | collective-permute-start | bytes 3145736 | tf_op jit(solution)/shard_map/ppermute | solution.py:1144
  103.6 21.8 %collective-permute-start.4 = (bf16[512,1024]{1,0:T(8,128)(2,1)S(1)}, bf16[512,1024]{1,0:T(8,128)(2,1)}, u32[]{:S(2)}, u32[]{:S(2)}) collective-permute-start(bf16[512,1024]{1,0:T(8,128)(2,1)S(1)} %bitcast.90), channel_id=1, source_target_pairs={{0,1},{1,0},{2,3},{3,2},{4,6},{5,7},{6,4},{7,5},{8,9},{9,8},{10,11... | collective-permute-start | bytes 3145736 | tf_op jit(solution)/shard_map/ppermute | solution.py:1144
  104.5 40.8 %all-to-all-start.1 = ((bf16[8,64,1024]{2,1,0:T(8,128)(2,1)}), bf16[8,64,1024]{2,1,0:T(8,128)(2,1)S(1)}, u32[]{:S(2)}, u32[]{:S(2)}) async-start(bf16[8,64,1024]{2,1,0:T(8,128)(2,1)} %bitcast.14), calls=%async_computation.1 | async-start | bytes 2097152 | tf_op jit(solution)/shard_map/all_to_all | solution.py:99
  108.2 39.2 %collective-permute-start.8 = (bf16[512,1024]{1,0:T(8,128)(2,1)}, bf16[512,1024]{1,0:T(8,128)(2,1)}, u32[]{:S(2)}, u32[]{:S(2)}) collective-permute-start(bf16[512,1024]{1,0:T(8,128)(2,1)} %collective-permute-done.3.grads_in.refs_6_), channel_id=1, source_target_pairs={{0,2},{1,3},{2,0},{3,1},{4,5},{5,4},{6,7},{7,6},{8,10},{9,11},{10,... | collective-permute-start | bytes 3145736 | tf_op jit(solution)/shard_map/ppermute | solution.py:1144
  125.4 19.9 %collective-permute-start.5 = (bf16[512,1024]{1,0:T(8,128)(2,1)}, bf16[512,1024]{1,0:T(8,128)(2,1)S(1)}, u32[]{:S(2)}, u32[]{:S(2)}) collective-permute-start(bf16[512,1024]{1,0:T(8,128)(2,1)} %collective-permute-done.4.rows_in.refs_2_), channel_id=1, source_target_pairs={{0,2},{1,3},{2,0},{3,1},{4,5},{5,4},{6,7},{7,6},{8,10},{9,11},{10,... | collective-permute-start | bytes 3145736 | tf_op jit(solution)/shard_map/ppermute | solution.py:1144
  145.4 20.3 %collective-permute-start.6 = (bf16[512,1024]{1,0:T(8,128)(2,1)S(1)}, bf16[512,1024]{1,0:T(8,128)(2,1)S(1)}, u32[]{:S(2)}, u32[]{:S(2)}) collective-permute-start(bf16[512,1024]{1,0:T(8,128)(2,1)S(1)} %bitcast.85), channel_id=1, source_target_pairs={{0,2},{1,3},{2,0},{3,1},{4,5},{5,4},{6,7},{7,6},{8,10},{9,11},{10,... | collective-permute-start | bytes 3145736 | tf_op jit(solution)/shard_map/ppermute | solution.py:1144
  145.5 39.4 %collective-permute-start.7 = (bf16[512,1024]{1,0:T(8,128)(2,1)S(1)}, bf16[512,1024]{1,0:T(8,128)(2,1)}, u32[]{:S(2)}, u32[]{:S(2)}) collective-permute-start(bf16[512,1024]{1,0:T(8,128)(2,1)S(1)} %bitcast.95), channel_id=1, source_target_pairs={{0,2},{1,3},{2,0},{3,1},{4,5},{5,4},{6,7},{7,6},{8,10},{9,11},{10,... | collective-permute-start | bytes 3145736 | tf_op jit(solution)/shard_map/ppermute | solution.py:1144
  165.5 18.5 %collective-permute-start.10 = (bf16[512,1024]{1,0:T(8,128)(2,1)}, bf16[512,1024]{1,0:T(8,128)(2,1)S(1)}, u32[]{:S(2)}, u32[]{:S(2)}) collective-permute-start(bf16[512,1024]{1,0:T(8,128)(2,1)} %get-tuple-element.207), channel_id=1, source_target_pairs={{0,2},{1,3},{2,0},{3,1},{4,5},{5,4},{6,7},{7,6},{8,10},{9,11},{10,... | collective-permute-start | bytes 3145736 | tf_op jit(solution)/shard_map/ppermute | solution.py:1144
  184.4 18.5 %collective-permute-start.11 = (bf16[512,1024]{1,0:T(8,128)(2,1)S(1)}, bf16[512,1024]{1,0:T(8,128)(2,1)}, u32[]{:S(2)}, u32[]{:S(2)}) collective-permute-start(bf16[512,1024]{1,0:T(8,128)(2,1)S(1)} %add_convert_fusion.5), channel_id=1, source_target_pairs={{0,1},{1,0},{2,3},{3,2},{4,6},{5,7},{6,4},{7,5},{8,9},{9,8},{10,11... | collective-permute-start | bytes 3145736 | tf_op jit(solution)/shard_map/ppermute | solution.py:1144
  202.9 15.2 %collective-permute-start.12 = (bf16[512,1024]{1,0:T(8,128)(2,1)}, bf16[512,1024]{1,0:T(8,128)(2,1)}, u32[]{:S(2)}, u32[]{:S(2)}) collective-permute-start(bf16[512,1024]{1,0:T(8,128)(2,1)} %get-tuple-element.210), channel_id=1, source_target_pairs={{0,2},{1,3},{2,0},{3,1},{4,5},{5,4},{6,7},{7,6},{8,10},{9,11},{10,... | collective-permute-start | bytes 3145736 | tf_op jit(solution)/shard_map/ppermute | solution.py:1144
  207.0 32.8 %collective-permute-start.15 = (bf16[512,1024]{1,0:T(8,128)(2,1)}, bf16[512,1024]{1,0:T(8,128)(2,1)S(1)}, u32[]{:S(2)}, u32[]{:S(2)}) collective-permute-start(bf16[512,1024]{1,0:T(8,128)(2,1)} %get-tuple-element.214), channel_id=1, source_target_pairs={{0,2},{1,3},{2,0},{3,1},{4,5},{5,4},{6,7},{7,6},{8,10},{9,11},{10,... | collective-permute-start | bytes 3145736 | tf_op jit(solution)/shard_map/ppermute | solution.py:1144
  207.5 35.9 %all-to-all-start.3 = ((bf16[8,64,1024]{2,1,0:T(8,128)(2,1)}), bf16[8,64,1024]{2,1,0:T(8,128)(2,1)}, u32[]{:S(2)}, u32[]{:S(2)}) async-start(bf16[8,64,1024]{2,1,0:T(8,128)(2,1)} %bitcast.30), calls=%async_computation.3 | async-start | bytes 2097152 | tf_op jit(solution)/shard_map/all_to_all | solution.py:99
  219.7 27.2 %collective-permute-start.13 = (bf16[512,1024]{1,0:T(8,128)(2,1)S(1)}, bf16[512,1024]{1,0:T(8,128)(2,1)}, u32[]{:S(2)}, u32[]{:S(2)}) collective-permute-start(bf16[512,1024]{1,0:T(8,128)(2,1)S(1)} %add_convert_fusion.4), channel_id=1, source_target_pairs={{0,1},{1,0},{2,3},{3,2},{4,6},{5,7},{6,4},{7,5},{8,9},{9,8},{10,11... | collective-permute-start | bytes 3145736 | tf_op jit(solution)/shard_map/ppermute | solution.py:1144
  241.2 23.5 %collective-permute-start.16 = (bf16[512,1024]{1,0:T(8,128)(2,1)}, bf16[512,1024]{1,0:T(8,128)(2,1)S(1)}, u32[]{:S(2)}, u32[]{:S(2)}) collective-permute-start(bf16[512,1024]{1,0:T(8,128)(2,1)} %get-tuple-element.215), channel_id=1, source_target_pairs={{0,2},{1,3},{2,0},{3,1},{4,5},{5,4},{6,7},{7,6},{8,10},{9,11},{10,... | collective-permute-start | bytes 3145736 | tf_op jit(solution)/shard_map/ppermute | solution.py:1144
  243.4 30.1 %all-to-all-start.4 = ((bf16[8,64,1024]{2,1,0:T(8,128)(2,1)}), bf16[8,64,1024]{2,1,0:T(8,128)(2,1)S(1)}, u32[]{:S(2)}, u32[]{:S(2)}) async-start(bf16[8,64,1024]{2,1,0:T(8,128)(2,1)} %bitcast.32), calls=%async_computation.4 | async-start | bytes 2097152 | tf_op jit(solution)/shard_map/all_to_all | solution.py:99
  246.9 63.0 %collective-permute-start.14 = (bf16[3,704,1024]{2,1,0:T(8,128)(2,1)}, bf16[3,704,1024]{2,1,0:T(8,128)(2,1)}, u32[]{:S(2)}, u32[]{:S(2)}) collective-permute-start(bf16[3,704,1024]{2,1,0:T(8,128)(2,1)} %weight_pass.2), channel_id=1, source_target_pairs={{0,1},{1,0},{2,3},{3,2},{4,6},{5,7},{6,4},{7,5},{8,9},{9,8},{10,11... | collective-permute-start | bytes 12976136 | tf_op jit(solution)/shard_map/ppermute | solution.py:1144
  273.4 64.2 %all-to-all-start.5 = ((bf16[8,128,1024]{2,1,0:T(8,128)(2,1)}), bf16[8,128,1024]{2,1,0:T(8,128)(2,1)}, u32[]{:S(2)}, u32[]{:S(2)}) async-start(bf16[8,128,1024]{2,1,0:T(8,128)(2,1)} %bitcast.34), calls=%async_computation.5 | async-start | bytes 4194304 | tf_op jit(solution)/shard_map/all_to_all | solution.py:99
  344.4 22.3 %collective-permute-start.22 = (bf16[4,136,512]{2,1,0:T(8,128)(2,1)S(1)}, bf16[4,136,512]{2,1,0:T(8,128)(2,1)S(1)}, u32[]{:S(2)}, u32[]{:S(2)}) collective-permute-start(bf16[4,136,512]{2,1,0:T(8,128)(2,1)S(1)} %pad_maximum_fusion.3), channel_id=1, source_target_pairs={{0,2},{1,3},{2,0},{3,1},{4,6},{5,7},{6,4},{7,5},{8,10},{9,11},{10,... | collective-permute-start | bytes 1671176 | tf_op jit(solution)/shard_map/ppermute | solution.py:40
  346.4 20.3 %collective-permute-start.20 = (bf16[4,136,512]{2,1,0:T(8,128)(2,1)S(1)}, bf16[4,136,512]{2,1,0:T(8,128)(2,1)S(1)}, u32[]{:S(2)}, u32[]{:S(2)}) collective-permute-start(bf16[4,136,512]{2,1,0:T(8,128)(2,1)S(1)} %pad_maximum_fusion.2), channel_id=1, source_target_pairs={{0,1},{1,0},{2,3},{3,2},{4,5},{5,4},{6,7},{7,6},{8,9},{9,8},{10,11... | collective-permute-start | bytes 1671176 | tf_op jit(solution)/shard_map/ppermute | solution.py:40
  351.4 21.2 %collective-permute-start.26 = (bf16[4,136,512]{2,1,0:T(8,128)(2,1)}, bf16[4,136,512]{2,1,0:T(8,128)(2,1)}, u32[]{:S(2)}, u32[]{:S(2)}) collective-permute-start(bf16[4,136,512]{2,1,0:T(8,128)(2,1)} %pad_maximum_fusion.5), channel_id=1, source_target_pairs={{0,2},{1,3},{2,0},{3,1},{4,6},{5,7},{6,4},{7,5},{8,10},{9,11},{10,... | collective-permute-start | bytes 1671176 | tf_op jit(solution)/shard_map/ppermute | solution.py:40
  352.9 20.1 %collective-permute-start.24 = (bf16[4,136,512]{2,1,0:T(8,128)(2,1)}, bf16[4,136,512]{2,1,0:T(8,128)(2,1)S(1)}, u32[]{:S(2)}, u32[]{:S(2)}) collective-permute-start(bf16[4,136,512]{2,1,0:T(8,128)(2,1)} %pad_maximum_fusion.4), channel_id=1, source_target_pairs={{0,1},{1,0},{2,3},{3,2},{4,5},{5,4},{6,7},{7,6},{8,9},{9,8},{10,11... | collective-permute-start | bytes 1671176 | tf_op jit(solution)/shard_map/ppermute | solution.py:40
  383.7 33.8 %collective-permute-start.30 = (bf16[256,1024]{1,0:T(8,128)(2,1)S(1)}, bf16[256,1024]{1,0:T(8,128)(2,1)S(1)}, u32[]{:S(2)}, u32[]{:S(2)}) collective-permute-start(bf16[256,1024]{1,0:T(8,128)(2,1)S(1)} %pad_maximum_fusion.9), channel_id=1, source_target_pairs={{0,2},{1,3},{2,0},{3,1},{4,6},{5,7},{6,4},{7,5},{8,10},{9,11},{10,... | collective-permute-start | bytes 1572872 | tf_op jit(solution)/shard_map/ppermute | solution.py:40
  384.4 33.0 %collective-permute-start.28 = (bf16[256,1024]{1,0:T(8,128)(2,1)S(1)}, bf16[256,1024]{1,0:T(8,128)(2,1)S(1)}, u32[]{:S(2)}, u32[]{:S(2)}) collective-permute-start(bf16[256,1024]{1,0:T(8,128)(2,1)S(1)} %pad_maximum_fusion.8), channel_id=1, source_target_pairs={{0,1},{1,0},{2,3},{3,2},{4,5},{5,4},{6,7},{7,6},{8,9},{9,8},{10,11... | collective-permute-start | bytes 1572872 | tf_op jit(solution)/shard_map/ppermute | solution.py:40
  413.1 19.6 %collective-permute-start.40 = (bf16[2,136,512]{2,1,0:T(8,128)(2,1)S(1)}, bf16[2,136,512]{2,1,0:T(8,128)(2,1)S(1)}, u32[]{:S(2)}, u32[]{:S(2)}) collective-permute-start(bf16[2,136,512]{2,1,0:T(8,128)(2,1)S(1)} %pad_maximum_fusion.11), channel_id=1, source_target_pairs={{0,8},{4,12},{8,0},{12,4},{16,24},{20,28},{24,16},{28,20},{1,9},{5... | collective-permute-start | bytes 835592 | tf_op jit(solution)/shard_map/ppermute | solution.py:40
  445.9 17.9 %collective-permute-start.43 = (bf16[16,136,512]{2,1,0:T(8,128)(2,1)}, bf16[16,136,512]{2,1,0:T(8,128)(2,1)S(1)}, u32[]{:S(2)}, u32[]{:S(2)}) collective-permute-start(bf16[16,136,512]{2,1,0:T(8,128)(2,1)} %constant_dynamic-update-slice_fusion.near), channel_id=1, source_target_pairs={{0,4},{4,0},{8,12},{12,8},{16,20},{20,16},{24,28},{28,24},{1,5},{5... | collective-permute-start | bytes 6684680 | tf_op jit(solution)/shard_map/ppermute | solution.py:40
  446.1 15.1 %collective-permute-start.44 = (bf16[4,136,512]{2,1,0:T(8,128)(2,1)S(1)}, bf16[4,136,512]{2,1,0:T(8,128)(2,1)S(1)}, u32[]{:S(2)}, u32[]{:S(2)}) collective-permute-start(bf16[4,136,512]{2,1,0:T(8,128)(2,1)S(1)} %pad_maximum_fusion.7), channel_id=1, source_target_pairs={{0,1},{1,0},{2,3},{3,2},{4,5},{5,4},{6,7},{7,6},{8,9},{9,8},{10,11... | collective-permute-start | bytes 1671176 | tf_op jit(solution)/shard_map/ppermute | solution.py:40
  (55 other events, 577.4 us)

commit v5 on v4

--- a/solution.py
+++ b/solution.py
@@ -127,86 +127,56 @@
     return jnp.concatenate(ring_gather(rest, in_plane), axis=0)
 
 
-def project_kernel(long_local, inputs, gain, w_query, w_key, w_value, normed, query, pair, near, held):
+def project_kernel(
+    local, gain, w_query, w_key, w_value, inputs, *refs
+):
+    sources, (normed, normed_others, query, pair, others, near, held) = refs[:-7], refs[-7:]
+    tokens = inputs.shape[0]
+
     @pl.when(pl.program_id(0) == 0)
     def _():
-        rows = inputs[...].astype(f32)
+        rows = jnp.concatenate([inputs[...]] + [source[...] for source in sources], axis=0).astype(f32)
         scale = lax.rsqrt(jnp.mean(rows * rows, axis=-1, keepdims=True) + 1e-06)
         held[...] = (rows * scale * gain[...].astype(f32)).astype(bf16)
-        normed[...] = held[...]
-
-    rows = held[...]
-    query[...] = mm(rows, w_query[...]).astype(bf16)
-    keys = mm(rows, w_key[...]).astype(bf16)
-    values = mm(rows, w_value[...]).astype(bf16)
-    pair[:long_local] = keys[:long_local]
-    pair[long_local:] = values[:long_local]
-    short = keys.shape[0] - long_local
-    near[:short] = keys[long_local:]
-    near[short:] = values[long_local:]
-
-
-def project(inputs, gain, w_query, w_key, w_value, long_local):
-    rows, width = inputs.shape
-    short = rows - long_local
+        normed[...] = held[:tokens]
+        normed_others[...] = held[tokens:]
+
+    query[...] = mm(held[:tokens], w_query[...]).astype(bf16)
+    keys = mm(held[...], w_key[...]).astype(bf16)
+    values = mm(held[...], w_value[...]).astype(bf16)
+    pair[:local] = keys[:local]
+    pair[local:] = values[:local]
+    short = tokens - local
+    near[:short] = keys[local:tokens]
+    near[short:] = values[local:tokens]
+    for r in range((held.shape[0] - tokens) // local):
+        low = tokens + r * local
+        others[2 * r * local : (2 * r + 1) * local] = keys[low : low + local]
+        others[(2 * r + 1) * local : (2 * r + 2) * local] = values[low : low + local]
+
+
+def project(inputs, sources, gain, w_query, w_key, w_value, local):
+    tokens, width = inputs.shape
+    away = sum(source.shape[0] for source in sources)
+    short = tokens - local
     step = 256
     whole = lambda count: pl.BlockSpec((count, width), lambda i: (0, 0))
     cut = lambda count: pl.BlockSpec((count, step), lambda i: (0, i))
     return pl.pallas_call(
-        partial(project_kernel, long_local),
+        partial(project_kernel, local),
         grid=(width // step,),
-        in_specs=[whole(rows), whole(1), cut(width), cut(width), cut(width)],
-        out_specs=[whole(rows), cut(rows), cut(2 * long_local), cut(2 * short)],
+        in_specs=[whole(1), cut(width), cut(width), cut(width), whole(tokens)]
+        + [whole(source.shape[0]) for source in sources],
+        out_specs=[whole(tokens), whole(away), cut(tokens), cut(2 * local), cut(2 * away), cut(2 * short)],
         out_shape=[
-            jax.ShapeDtypeStruct((rows, width), bf16),
-            jax.ShapeDtypeStruct((rows, width), bf16),
-            jax.ShapeDtypeStruct((2 * long_local, width), bf16),
-            jax.ShapeDtypeStruct((2 * short, width), bf16),
+            jax.ShapeDtypeStruct((size, width), bf16)
+            for size in (tokens, away, tokens, 2 * local, 2 * away, 2 * short)
         ],
-        scratch_shapes=[pltpu.VMEM((rows, width), bf16)],
+        scratch_shapes=[pltpu.VMEM((tokens + away, width), bf16)],
         compiler_params=params(),
-        cost_estimate=cost(6.9),
+        cost_estimate=cost(12),
         name="project",
-    )(inputs, gain.reshape(1, width), w_query, w_key, w_value)
-
-
-def project_others_kernel(local, gain, w_key, w_value, *refs):
-    sources, (normed, pairs, held) = refs[:-3], refs[-3:]
-
-    @pl.when(pl.program_id(0) == 0)
-    def _():
-        rows = jnp.concatenate([source[...] for source in sources], axis=0).astype(f32)
-        scale = lax.rsqrt(jnp.mean(rows * rows, axis=-1, keepdims=True) + 1e-06)
-        held[...] = (rows * scale * gain[...].astype(f32)).astype(bf16)
-        normed[...] = held[...]
-
-    keys = mm(held[...], w_key[...]).astype(bf16)
-    values = mm(held[...], w_value[...]).astype(bf16)
-    for r in range(keys.shape[0] // local):
-        pairs[2 * r * local : (2 * r + 1) * local] = keys[r * local : (r + 1) * local]
-        pairs[(2 * r + 1) * local : (2 * r + 2) * local] = values[r * local : (r + 1) * local]
-
-
-def project_others(sources, gain, w_key, w_value, local):
-    rows = sum(source.shape[0] for source in sources)
-    width = gain.shape[0]
-    step = 256
-    whole = lambda count: pl.BlockSpec((count, width), lambda i: (0, 0))
-    cut = lambda count: pl.BlockSpec((count, step), lambda i: (0, i))
-    return pl.pallas_call(
-        partial(project_others_kernel, local),
-        grid=(width // step,),
-        in_specs=[whole(1), cut(width), cut(width)] + [whole(source.shape[0]) for source in sources],
-        out_specs=[whole(rows), cut(2 * rows)],
-        out_shape=[
-            jax.ShapeDtypeStruct((rows, width), bf16),
-            jax.ShapeDtypeStruct((2 * rows, width), bf16),
-        ],
-        scratch_shapes=[pltpu.VMEM((rows, width), bf16)],
-        compiler_params=params(),
-        cost_estimate=cost(7.7),
-        name="project_others",
-    )(gain.reshape(1, width), w_key, w_value, *sources)
+    )(gain.reshape(1, width), w_query, w_key, w_value, inputs, *sources)
 
 
 def key_value_views(pair, others, count, rows):
@@ -527,65 +497,110 @@
     )(*grads, w_query, w_key, w_value)
 
 
-def expert_kernel(chunks, capacity, padded, lanes_used, facts, rows_in, grads_in, *refs):
+def pick_kernel(facts, *refs):
+    for i in range(3):
+        refs[3][i] = refs[i][0]
+
+
+def pick_weights(facts, *weights):
+    _, units, width = weights[0].shape
+    tile = units // 4
+    return pl.pallas_call(
+        pick_kernel,
+        grid_spec=pltpu.PrefetchScalarGridSpec(
+            num_scalar_prefetch=1,
+            grid=(4,),
+            in_specs=[pl.BlockSpec((1, tile, width), lambda i, f: (f[6], i, 0))] * 3,
+            out_specs=pl.BlockSpec((3, tile, width), lambda i, f: (0, i, 0)),
+        ),
+        out_shape=jax.ShapeDtypeStruct((3, units, width), bf16),
+        compiler_params=params(),
+        cost_estimate=cost(5),
+        name="pick_weights",
+    )(facts, *weights)
+
+
+def expert_kernel(chunks, capacity, padded, lanes_used, facts, slots_in, grads_in, *refs):
     sources, rest = refs[: 3 * chunks], refs[3 * chunks :]
-    middles, (out_ref, grad_ref) = rest[: 3 * chunks], rest[3 * chunks : 3 * chunks + 2]
-    held, sems = rest[3 * chunks + 2 : 6 * chunks + 2], rest[6 * chunks + 2]
-    rows = rows_in.shape[0]
+    outs, rest = rest[: 3 * chunks + 2], rest[3 * chunks + 2 :]
+    rows_buffer, grads_buffer, held, middles, out_buffer, grad_buffer, in_sems, out_sems = rest
+    rows = rows_buffer.shape[0]
+    units = sources[0].shape[1]
+    wide = held.shape[1] // chunks
     groups = rows // padded
-    first = pl.program_id(0) == 0
-
-    def copy(i):
-        index = facts[4] if i < 3 else i % 3
-        return pltpu.make_async_copy(sources[i].at[index], held[i], sems.at[i])
-
-    @pl.when(first)
-    def _():
-        for i in range(3 * chunks):
-            copy(i).start()
-        for i in range(3 * chunks):
-            copy(i).wait()
-
-    slots = rows_in[...]
-    grads = grads_in[...]
     spare = 16 - (padded - capacity)
+
+    arrivals = [
+        pltpu.make_async_copy(slots_in, rows_buffer, in_sems.at[0]),
+        pltpu.make_async_copy(grads_in, grads_buffer, in_sems.at[1]),
+    ]
+    weights = []
+    for k in range(3):
+        for c in range(chunks):
+            i = 3 * c + k
+            index = facts[4] if c == 0 else k
+            place = held.at[k, pl.ds(c * wide, units)]
+            weights.append(pltpu.make_async_copy(sources[i].at[index], place, in_sems.at[2 + i]))
+    arrivals[0].start()
+    for copy in weights[: 2 * chunks]:
+        copy.start()
+    arrivals[1].start()
+    for copy in weights[2 * chunks :]:
+        copy.start()
+    if wide > units:
+        for k in range(3):
+            for c in range(chunks):
+                held[k, c * wide + units : (c + 1) * wide] = jnp.zeros((wide - units, held.shape[2]), bf16)
+
+    arrivals[0].wait()
     lanes = lax.broadcasted_iota(jnp.int32, (padded, 128), 1)
     match = lax.broadcasted_iota(jnp.int32, (padded, 128), 0) == lanes
     columns = []
     for g in range(groups):
-        tail = rows_in[pl.ds((g + 1) * padded - 16, 16), :128].astype(f32)
+        tail = rows_buffer[pl.ds((g + 1) * padded - 16, 16), :128].astype(f32)
         line = tail[spare : spare + 1] + tail[spare + 1 : spare + 2]
         columns.append(jnp.sum(jnp.where(match, line, 0.0), axis=-1, keepdims=True))
     gate_column = jnp.concatenate(columns, axis=0)
 
-    lows = []
+    slots = rows_buffer[...]
+    for copy in weights[:chunks]:
+        copy.wait()
+    gate_pre = mm(slots, held[0], NT)
+    for copy in weights[chunks : 2 * chunks]:
+        copy.wait()
+    up_pre = mm(slots, held[1], NT)
+    arrivals[1].wait()
+    for copy in weights[2 * chunks :]:
+        copy.wait()
+    grads = grads_buffer[...]
+    grad_hidden = mm(grads, held[2], NT) * gate_column
     slope = math.sqrt(2.0 / math.pi)
-    for c in range(chunks):
-        gate_pre = mm(slots, held[3 * c][...], NT)
-        up_pre = mm(slots, held[3 * c + 1][...], NT)
-        grad_hidden = mm(grads, held[3 * c + 2][...], NT) * gate_column
-        square = gate_pre * gate_pre
-        curve = jnp.tanh(slope * gate_pre * (1.0 + 0.044715 * square))
-        side = 0.5 * (1.0 + curve)
-        bent = gate_pre * side
-        hidden = bent * up_pre
-        bent_slope = side + 0.5 * slope * gate_pre * (1.0 - curve * curve) * (
-            1.0 + 3.0 * 0.044715 * square
-        )
-        gate_low = (grad_hidden * up_pre * bent_slope).astype(bf16)
-        up_low = (grad_hidden * bent).astype(bf16)
-        middles[3 * c][...] = (hidden * gate_column).astype(bf16)
-        middles[3 * c + 1][...] = gate_low
-        middles[3 * c + 2][...] = up_low
-        lows.append((gate_low, up_low, hidden.astype(bf16)))
-    left = [jnp.concatenate([low[k] for low in lows], axis=1) for k in range(3)]
-    right = [
-        jnp.concatenate([held[3 * c + k][...] for c in range(chunks)], axis=0) for k in range(3)
-    ]
-    out = mm(left[2], right[2])
-    grad_out = mm(left[0], right[0]) + mm(left[1], right[1])
-    out_ref[...] = out.astype(bf16)
-    grad_ref[...] = grad_out.astype(bf16)
+    square = gate_pre * gate_pre
+    curve = jnp.tanh(slope * gate_pre * (1.0 + 0.044715 * square))
+    side = 0.5 * (1.0 + curve)
+    bent = gate_pre * side
+    hidden = bent * up_pre
+    bent_slope = side + 0.5 * slope * gate_pre * (1.0 - curve * curve) * (
+        1.0 + 3.0 * 0.044715 * square
+    )
+    gate_low = (grad_hidden * up_pre * bent_slope).astype(bf16)
+    up_low = (grad_hidden * bent).astype(bf16)
+    departures = []
+
+    def depart(buffer, target):
+        copy = pltpu.make_async_copy(buffer, target, out_sems.at[len(departures)])
+        copy.start()
+        departures.append(copy)
+
+    for k, value in enumerate(((hidden * gate_column).astype(bf16), gate_low, up_low)):
+        for c in range(chunks):
+            middles[3 * c + k] = value[:, c * wide : c * wide + units]
+            depart(middles.at[3 * c + k], outs[3 * c + k])
+    out = mm(hidden.astype(bf16), held[2])
+    out_buffer[...] = out.astype(bf16)
+    depart(out_buffer, outs[3 * chunks])
+    grad_out = mm(gate_low, held[0]) + mm(up_low, held[1])
+    grad_buffer[...] = grad_out.astype(bf16)
 
     grad_gate = jnp.sum(out * grads.astype(f32), axis=-1, keepdims=True)
     lanes = lax.broadcasted_iota(jnp.int32, (padded, lanes_used), 1)
@@ -598,30 +613,35 @@
         high = line.astype(bf16).astype(f32)
         tail = grad_out[(g + 1) * padded - 16 : (g + 1) * padded, :lanes_used]
         tail = jnp.where(row == spare, high, jnp.where(row == spare + 1, line - high, tail))
-        grad_ref[pl.ds((g + 1) * padded - 16, 16), :lanes_used] = tail.astype(bf16)
+        grad_buffer[pl.ds((g + 1) * padded - 16, 16), :lanes_used] = tail.astype(bf16)
+    depart(grad_buffer, outs[3 * chunks + 1])
+    for copy in departures:
+        copy.wait()
 
 
 def expert_pass(facts, slots, grads, own, other, capacity, padded, lanes_used):
     rows, width = slots.shape
     units = own[0].shape[1]
+    wide = (units + 127) // 128 * 128
     chunks = 1 if other is None else 2
     sources = list(own) + ([] if other is None else [other] * 3)
-    tile = rows
-    cut = lambda size: pl.BlockSpec((tile, size), lambda i, f: (i, 0))
+    anywhere = pl.BlockSpec(memory_space=pl.ANY)
     outs = pl.pallas_call(
         partial(expert_kernel, chunks, capacity, padded, lanes_used),
         grid_spec=pltpu.PrefetchScalarGridSpec(
             num_scalar_prefetch=1,
-            grid=(rows // tile,),
-            in_specs=[cut(width)] * 2 + [pl.BlockSpec(memory_space=pl.ANY)] * (3 * chunks),
-            out_specs=[cut(units)] * (3 * chunks) + [cut(width)] * 2,
-            scratch_shapes=[pltpu.VMEM((units, width), bf16)] * (3 * chunks)
-            + [pltpu.SemaphoreType.DMA((3 * chunks,))],
+            grid=(1,),
+            in_specs=[anywhere] * (2 + 3 * chunks),
+            out_specs=[anywhere] * (3 * chunks + 2),
+            scratch_shapes=[pltpu.VMEM((rows, width), bf16)] * 2
+            + [pltpu.VMEM((3, chunks * wide, width), bf16), pltpu.VMEM((3 * chunks, rows, units), bf16)]
+            + [pltpu.VMEM((rows, width), bf16)] * 2
+            + [pltpu.SemaphoreType.DMA((2 + 3 * chunks,)), pltpu.SemaphoreType.DMA((3 * chunks + 2,))],
         ),
         out_shape=[jax.ShapeDtypeStruct((rows, units), bf16)] * (3 * chunks)
         + [jax.ShapeDtypeStruct((rows, width), bf16)] * 2,
         compiler_params=params(),
-        cost_estimate=cost(18),
+        cost_estimate=cost(15),
         name="expert_pass",
     )(facts, slots, grads, *sources)
     middles = [outs[3 * c : 3 * c + 3] for c in range(chunks)]
@@ -1012,8 +1032,8 @@
     )(facts, *lefts, *rights, branch, bias_grad, gain_grad, router_grad)
 
 
-def unpack_kernel(facts, near, far, w_query, w_key, w_value, gain, *refs):
-    query, key, value, proj, gain_grad, small = refs[-6:]
+def unpack_kernel(facts, near, far, w_query, w_key, w_value, gain, gain_before, *refs):
+    query, key, value, proj, small, gain_grad = refs[-6:]
     step = pl.program_id(0)
     number = facts[3]
     group = step ^ (number // 8)
@@ -1047,10 +1067,10 @@
         jnp.int32, (size, size), 1
     )
     line = jnp.sum(jnp.where(match, column, 0.0), axis=0, keepdims=True)
-    gain_grad[...] = line / gain[...].astype(f32)
-
-
-def unpack_blocks(facts, near, far, w_query, w_key, w_value, gain, before, half):
+    gain_grad[...] = gain_before[...] + line / gain[...].astype(f32)
+
+
+def unpack_blocks(facts, near, far, w_query, w_key, w_value, gain, gain_before, before, half):
     width = w_query.shape[0]
     wide = width // 2
     rows = near.shape[1]
@@ -1069,17 +1089,18 @@
                 block,
                 block,
                 line,
+                line,
             ]
             + [pl.BlockSpec(memory_space=pl.ANY)] * len(before),
-            out_specs=[block, block, block, block, line, pl.BlockSpec((24, wide), lambda i, f: (0, 0))],
+            out_specs=[block, block, block, block, pl.BlockSpec((24, wide), lambda i, f: (0, half)), line],
         ),
         out_shape=[jax.ShapeDtypeStruct((width, width), f32)] * 4
-        + [jax.ShapeDtypeStruct((1, width), f32), jax.ShapeDtypeStruct((24, wide), f32)],
-        input_output_aliases={7 + i: i for i in range(len(before))},
+        + [jax.ShapeDtypeStruct((24, width), f32), jax.ShapeDtypeStruct((1, width), f32)],
+        input_output_aliases={8 + i: i for i in range(len(before))},
         compiler_params=params(),
         cost_estimate=cost(8),
         name="unpack_blocks",
-    )(facts, near, far, w_query, w_key, w_value, gain.reshape(1, width), *before)
+    )(facts, near, far, w_query, w_key, w_value, gain.reshape(1, width), gain_before, *before)
 
 
 def per_device(
@@ -1148,8 +1169,8 @@
     slots, wide_slots, grad_slots_in = place_rows(
         turns.reshape(1, 2), routes_rows, cotangent, capacity, padded, block, local
     )
-    normed_low, query, pair, near = project(
-        after(inputs, sources), attn_gain, w_query, w_key, w_value, long_local
+    normed_low, normed_others, query, pair, others, near = project(
+        inputs, sources, attn_gain, w_query, w_key, w_value, long_local
     )
 
     def by_expert(rows):
@@ -1161,15 +1182,9 @@
         return jnp.concatenate(split, axis=1).reshape(local * block, width)
 
     grad_whole = over_experts(grad_slots_in)
-    normed_others, others = project_others(sources, attn_gain, w_key, w_value, long_local)
     parts = (pair, others)
     if paired:
-        other = jnp.stack(
-            [
-                lax.dynamic_index_in_dim(array, 1 - which, 0, keepdims=False)
-                for array in (gate_turned, up_turned, w_down)
-            ]
-        )
+        other = pick_weights(facts, gate_turned, up_turned, w_down)
         other = trade(after(other, sources), False)
 
     reach = long_span + long_local
@@ -1200,7 +1215,7 @@
         grads_d = trade(grads_b, True)
         rows_b = over_experts(slots_in[1])
         rows_a = over_experts(after(slots_in[0], rows_b))
-        rows_b = trade(after(rows_b, grads_b), False)
+        rows_b = trade(after(rows_b, grads_b, grads_d), False)
         rows_d = trade(rows_b, True)
         grads_c = trade(after(grad_arrived[0], rows_d), True)
         pass_b = run(rows_b, grads_b)
@@ -1310,14 +1325,14 @@
         by_x, by_y = in_plane(one, 0), in_plane(one, 1)
         half_x, half_y = after_all((by_x[:2], by_y[2:]), outputs, weight_grads, two)
         one = jnp.concatenate([one, by_x, by_y, in_plane(half_x, 1), in_plane(half_y, 0)], axis=0)
-        first = unpack(one, swap(one, "expert", 1), *weights, (), 0)
+        first = unpack(one, swap(one, "expert", 1), *weights, jnp.zeros((1, width), f32), (), 0)
         by_x, by_y = in_plane(two, 0), in_plane(two, 1)
         rest = after_all((in_plane(by_x[:2], 1), in_plane(by_y[2:], 0)), first[5], inputs_grad)
         two = jnp.concatenate([two, by_x, by_y] + rest, axis=0)
-        second = unpack(two, swap(two, "expert", 1), *weights, first[:4], 1)
+        second = unpack(two, swap(two, "expert", 1), *weights, first[5], first[:5], 1)
         query_grad, key_grad, value_grad, proj_grad = second[:4]
-        attn_gain_grad = (first[4] + second[4])[0]
-        small = jnp.concatenate([first[5], second[5]], axis=1)
+        attn_gain_grad = second[5][0]
+        small = second[4]
     else:
         key_others = [slice(2 * r * long_local, (2 * r + 1) * long_local) for r in range(tensor_axis - 1)]
         value_others = [slice((2 * r + 1) * long_local, (2 * r + 2) * long_local) for r in range(tensor_axis - 1)]

time: 498 us -> 495 us (level)
  waiting for transfers between devices: 101 us -> 126 us
  local copies, waits for them, and re-layouts: 26.1 us -> 14.8 us
  starting transfers between devices: 95.5 us -> 87.8 us
  other arithmetic: 26.9 us -> 21.4 us
    ppermute x35, waiting for transfers between devices: 47.9 us -> 69.7 us  [swap(): return lax.ppermute(rows, axis, [(i, i ^ mask) for i in range(count)])]
    ppermute x14, waiting for transfers between devices: 23.8 us -> 39.8 us  [trade(): return lax.ppermute(rows, ('expert', 'tensor'), pairs)]
    ppermute x35, starting transfers between devices: 50.9 us -> 36.7 us  [swap(): return lax.ppermute(rows, axis, [(i, i ^ mask) for i in range(count)])]
    all_to_all x6, waiting for transfers between devices: 29.8 us -> 16.6 us  [over_experts(): lax.all_to_all(blocks, 'expert', 0, 0, tiled=True).reshape(rows.shape)]
    all_to_all x6, starting transfers between devices: 26.7 us -> 35 us  [over_experts(): lax.all_to_all(blocks, 'expert', 0, 0, tiled=True).reshape(rows.shape)]
    dynamic_slice x2 -> x0, local copies, waits for them, and re-layouts: 5.07 us -> none  [per_device(): lax.dynamic_index_in_dim(array, 1 - which, 0, keepdims=False)]
    unnamed x75 -> x76, local copies, waits for them, and re-layouts: 7.52 us -> 2.52 us
  transfers between devices with their start and end apart: 55 -> 55, of which waited for: 23 -> 29; matrix products, arithmetic and copies ran while one was open for 10% -> 7% of each run, Pallas kernels for 45% -> 45%
where the time goes in v5:
time: 495 us; the launch traced here: 487 us
  Pallas kernels  225 us (45%)
  waiting for transfers between devices  126 us (25%)
  starting transfers between devices  87.8 us (18%)
  other arithmetic  21.4 us (4%)
  local copies, waits for them, and re-layouts  14.8 us (3%)
  matrix products  8.16 us (2%)
    ppermute x35, waiting for transfers between devices, swap(): return lax.ppermute(rows, axis, [(i, i ^ mask) for i in range(count)])  69.7 us
    pallas_call x4, Pallas kernels, expert_pass(): pl.pallas_call(partial(expert_kernel, chunks, capacity, padded, lanes_use...  67.4 us
    ppermute x14, waiting for transfers between devices, trade(): return lax.ppermute(rows, ('expert', 'tensor'), pairs)  39.8 us
    ppermute x35, starting transfers between devices, swap(): return lax.ppermute(rows, axis, [(i, i ^ mask) for i in range(count)])  36.7 us
    all_to_all x6, starting transfers between devices, over_experts(): lax.all_to_all(blocks, 'expert', 0, 0, tiled=True).reshape(rows.shape)  35 us
    pallas_call x2, Pallas kernels, weight_pass(): pl.pallas_call(body, grid_spec=pltpu.PrefetchScalarGridSpec(num_scalar_pr...  31.9 us
    pallas_call x1, Pallas kernels, attend_backward(): pl.pallas_call(partial(backward_kernel, count, rows, dim), grid_spec=pltp...  24.5 us
    pallas_call x1, Pallas kernels, attend_forward(): pl.pallas_call(partial(forward_kernel, count, rows, dim), grid_spec=pltpu...  17.3 us
  transfers between devices with their start and end apart: 55, of which 29 were waited for; matrix products, arithmetic and copies ran while one was open for 7% of the time, Pallas kernels for 45%

profile of v5, /device:TPU:0, one launch (start us, length us, event | category | flops | bytes accessed | tf_op | source)
XLA Modules:
  0.0 486.6 jit_solution(16505525511945860228)
XLA Ops:
  10.8 5.5 %all-to-all-start.2 = ((bf16[8,128,1024]{2,1,0:T(8,128)(2,1)}), bf16[8,128,1024]{2,1,0:T(8,128)(2,1)S(1)}, u32[]{:S(2)}, u32[]{:S(2)}) async-start(bf16[8,128,1024]{2,1,0:T(8,128)(2,1)} %bitcast.74), calls=%async_computation.2 | async-start | bytes 4194304 | tf_op jit(solution)/shard_map/all_to_all | solution.py:99
  21.3 5.4 %pick_weights.1 = bf16[3,704,1024]{2,1,0:T(8,128)(2,1)} custom-call(s32[7]{0:T(128)} %stack.60.facts, bf16[2,704,1024]{2,1,0:T(8,128)(2,1)} %bitcast.96, bf16[2,704,1024]{2,1,0:T(8,128)(2,1)} %bitcast.101, bf16[2,704,1024]{2,1,0:T(8,128)(2,1)} %refs_2_.9), custom_call_target="tpu_custom_call" | custom-call | flops 5750000128 | tf_op jit(solution)/shard_map/pick_weights/pallas_call | solution.py:508
  30.7 10.6 %project.1 = (bf16[384,1024]{1,0:T(8,128)(2,1)}, bf16[768,1024]{1,0:T(8,128)(2,1)}, bf16[384,1024]{1,0:T(8,128)(2,1)}, bf16[512,1024]{1,0:T(8,128)(2,1)}, bf16[1...) custom-call(bf16[1,1024]{1,0:T(2,128)(2,1)} %reshape.125.gain, bf16[1024,1024]{1,0:T(8,128)(2,1)} %w_query.7, ...), custom_call_target="tpu_custom_call" | custom-call | flops 13799999488 | tf_op jit(solution)/shard_map/project/pallas_call | solution.py:165
  41.3 17.3 %attend_forward.1 = (bf16[384,1024]{1,0:T(8,128)(2,1)}, bf16[16,256,1024]{2,1,0:T(8,128)(2,1)}, bf16[16,128,128]{2,1,0:T(8,128)(2,1)}) custom-call(s32[7]{0:T(128)} %stack.60.facts, bf16[384,1024]{1,0:T(8,128)(2,1)} %get-tuple-element.155.query, bf16[512,1024]{1,0:T(8,128)(2,1)} %get-tuple-element.156.pair, bf16[1536,1024]{1,0:T(8,128)(2,1)} %get-tuple-element.157.others, ...), custom_call_target="tpu_custom_call" | custom-call | flops 19549999104 | tf_op jit(solution)/shard_map/attend_forward/pallas_call | solution.py:291
  58.6 6.4 %route_rows.1 = (f32[384,1024]{1,0:T(8,128)}, bf16[384,1024]{1,0:T(8,128)(2,1)}, f32[16,384]{1,0:T(8,128)}, f32[2,384]{1,0:T(2,128)}, bf16[512,1024]{1,0:T(8,128)(2,1)}, /*index=5*/bf16[512,1024]{1,0:T(8,128)(2,1)}) custom-call(bf16[384,1024]{1,0:T(8,128)(2,1)} %get-tuple-element.159.mixed, bf16[1024,1024]{1,0:T(8,128)(2,1)} %w_proj.3, ...), custom_call_target="tpu_custom_call" | custom-call | flops 7360000000 | tf_op jit(solution)/shard_map/route_rows/pallas_call | solution.py:847
  71.7 19.1 %collective-permute-done.3.grads_in.refs_6_ = bf16[512,1024]{1,0:T(8,128)(2,1)S(1)} collective-permute-done((bf16[512,1024]{1,0:T(8,128)(2,1)}, bf16[512,1024]{1,0:T(8,128)(2,1)S(1)}, u32[]{:S(2)}, u32[]{:S(2)}) %collective-permute-start.3) | collective-permute-done | bytes 1048608 | tf_op jit(solution)/shard_map/ppermute | solution.py:1165
  92.7 5.6 %all-to-all-done = bf16[8,64,1024]{2,1,0:T(8,128)(2,1)S(1)} async-done(((bf16[8,64,1024]{2,1,0:T(8,128)(2,1)}), bf16[8,64,1024]{2,1,0:T(8,128)(2,1)S(1)}, u32[]{:S(2)}, u32[]{:S(2)}) %all-to-all-start) | async-done | bytes 1048608 | tf_op jit(solution)/shard_map/all_to_all | solution.py:99
  98.3 7.7 %collective-permute-done.4.grads_in.refs_7_ = bf16[512,1024]{1,0:T(8,128)(2,1)} collective-permute-done((bf16[512,1024]{1,0:T(8,128)(2,1)S(1)}, bf16[512,1024]{1,0:T(8,128)(2,1)}, u32[]{:S(2)}, u32[]{:S(2)}) %collective-permute-start.4) | collective-permute-done | bytes 1048608 | tf_op jit(solution)/shard_map/ppermute | solution.py:1165
  107.0 5.0 %all-to-all-start.1 = ((bf16[8,64,1024]{2,1,0:T(8,128)(2,1)}), bf16[8,64,1024]{2,1,0:T(8,128)(2,1)S(1)}, u32[]{:S(2)}, u32[]{:S(2)}) async-start(bf16[8,64,1024]{2,1,0:T(8,128)(2,1)} %bitcast.14), calls=%async_computation.1 | async-start | bytes 2097152 | tf_op jit(solution)/shard_map/all_to_all | solution.py:99
  112.0 9.9 %collective-permute-done.5.slots_in.refs_2_ = bf16[512,1024]{1,0:T(8,128)(2,1)} collective-permute-done((bf16[512,1024]{1,0:T(8,128)(2,1)S(1)}, bf16[512,1024]{1,0:T(8,128)(2,1)}, u32[]{:S(2)}, u32[]{:S(2)}) %collective-permute-start.5) | collective-permute-done | bytes 1048608 | tf_op jit(solution)/shard_map/ppermute | solution.py:1165
  125.2 16.6 %expert_pass.4 = (bf16[512,704]{1,0:T(8,128)(2,1)}, bf16[512,704]{1,0:T(8,128)(2,1)}, bf16[512,704]{1,0:T(8,128)(2,1)}, bf16[512,704]{1,0:T(8,128)(2,1)}, bf16[5...) custom-call(s32[7]{0:T(128)} %stack.60.facts, ...), custom_call_target="tpu_custom_call" | custom-call | flops 17250000896 | tf_op jit(solution)/shard_map/expert_pass/pallas_call | solution.py:629
  143.9 16.8 %expert_pass.5 = (bf16[512,704]{1,0:T(8,128)(2,1)}, bf16[512,704]{1,0:T(8,128)(2,1)}, bf16[512,704]{1,0:T(8,128)(2,1)}, bf16[512,704]{1,0:T(8,128)(2,1)}, bf16[5...) custom-call(s32[7]{0:T(128)} %stack.60.facts, ...), custom_call_target="tpu_custom_call" | custom-call | flops 17250000896 | tf_op jit(solution)/shard_map/expert_pass/pallas_call | solution.py:629
  160.9 17.1 %expert_pass.6 = (bf16[512,704]{1,0:T(8,128)(2,1)}, bf16[512,704]{1,0:T(8,128)(2,1)}, bf16[512,704]{1,0:T(8,128)(2,1)}, bf16[512,704]{1,0:T(8,128)(2,1)}, bf16[5...) custom-call(s32[7]{0:T(128)} %stack.60.facts, ...), custom_call_target="tpu_custom_call" | custom-call | flops 17250000896 | tf_op jit(solution)/shard_map/expert_pass/pallas_call | solution.py:629
  180.1 16.9 %expert_pass.7 = (bf16[512,704]{1,0:T(8,128)(2,1)}, bf16[512,704]{1,0:T(8,128)(2,1)}, bf16[512,704]{1,0:T(8,128)(2,1)}, bf16[512,704]{1,0:T(8,128)(2,1)}, bf16[5...) custom-call(s32[7]{0:T(128)} %stack.60.facts, ...), custom_call_target="tpu_custom_call" | custom-call | flops 17250000896 | tf_op jit(solution)/shard_map/expert_pass/pallas_call | solution.py:629
  201.7 8.8 %all-to-all-start.3 = ((bf16[8,64,1024]{2,1,0:T(8,128)(2,1)}), bf16[8,64,1024]{2,1,0:T(8,128)(2,1)}, u32[]{:S(2)}, u32[]{:S(2)}) async-start(bf16[8,64,1024]{2,1,0:T(8,128)(2,1)} %bitcast.28), calls=%async_computation.3 | async-start | bytes 2097152 | tf_op jit(solution)/shard_map/all_to_all | solution.py:99
  215.6 16.2 %weight_pass.2 = bf16[3,704,1024]{2,1,0:T(8,128)(2,1)} custom-call(s32[7]{0:T(128)} %stack.60.facts, bf16[512,1024]{1,0:T(8,128)(2,1)} %bitcast.83, bf16[512,1024]{1,0:T(8,128)(2,1)} %copy-done.30, bf16[512,1024]{1,0:T(8,128)(2,1)} %collective-permute-done.5.slots_in.refs_2_, bf16[512,1024]{1,0:T(8,128)(2,1)} %copy-done.29, bf16[512,1024]{1,0:T(8,128)(2,1)} %bitcast.89, ...), custom_call_target="tpu_custom_call" | custom-call | flops 18400000000 | tf_op jit(solution)/shard_map/weight_pass/pallas_call | solution.py:711
  237.2 7.6 %all-to-all-start.4 = ((bf16[8,64,1024]{2,1,0:T(8,128)(2,1)}), bf16[8,64,1024]{2,1,0:T(8,128)(2,1)S(1)}, u32[]{:S(2)}, u32[]{:S(2)}) async-start(bf16[8,64,1024]{2,1,0:T(8,128)(2,1)} %bitcast.30), calls=%async_computation.4 | async-start | bytes 2097152 | tf_op jit(solution)/shard_map/all_to_all | solution.py:99
  245.4 15.6 %weight_pass.3 = (f32[2,704,1024]{2,1,0:T(8,128)}, f32[2,704,1024]{2,1,0:T(8,128)}, f32[2,704,1024]{2,1,0:T(8,128)}) custom-call(s32[7]{0:T(128)} %stack.60.facts, bf16[512,1024]{1,0:T(8,128)(2,1)} %bitcast.84, bf16[512,1024]{1,0:T(8,128)(2,1)} %copy-done.30, bf16[512,1024]{1,0:T(8,128)(2,1)} %collective-permute-done.5.slots_in.refs_2_, ...), custom_call_target="tpu_custom_call" | custom-call | flops 18400000000 | tf_op jit(solution)/shard_map/weight_pass/pallas_call | solution.py:711
  264.2 7.2 %all-to-all-done.4 = bf16[8,64,1024]{2,1,0:T(8,128)(2,1)S(1)} async-done(((bf16[8,64,1024]{2,1,0:T(8,128)(2,1)}), bf16[8,64,1024]{2,1,0:T(8,128)(2,1)S(1)}, u32[]{:S(2)}, u32[]{:S(2)}) %all-to-all-start.4) | async-done | bytes 1048608 | tf_op jit(solution)/shard_map/all_to_all | solution.py:99
  275.7 7.4 %merge_rows.1 = (f32[384,1024]{1,0:T(8,128)}, bf16[384,1024]{1,0:T(8,128)(2,1)}, f32[1,1024]{1,0:T(1,128)}, f32[16,1024]{1,0:T(8,128)}, bf16[384,1024]{1,0:T(8,128)(2,1)}) custom-call(bf16[384,1024]{1,0:T(8,128)(2,1)} %cotangent.1, f32[384,1024]{1,0:T(8,128)} %get-tuple-element.161.resid, f32[16,384]{1,0:T(8,128)} %get-tuple-element.244.probs, ...), custom_call_target="tpu_custom_call" | custom-call | flops 8510000128 | tf_op jit(solution)/shard_map/merge_rows/pallas_call | solution.py:923
  283.1 24.5 %attend_backward.1 = (bf16[384,1024]{1,0:T(8,128)(2,1)}, bf16[512,1024]{1,0:T(8,128)(2,1)}, bf16[1536,1024]{1,0:T(8,128)(2,1)}, bf16[256,1024]{1,0:T(8,128)(2,1)}, f32[8,2,32]{2,1,0:T(2,128)}) custom-call(s32[7]{0:T(128)} %stack.60.facts, bf16[384,1024]{1,0:T(8,128)(2,1)} %get-tuple-element.155.query, bf16[384,1024]{1,0:T(8,128)(2,1)} %get-tuple-element.247.grad, ...), custom_call_target="tpu_custom_call" | custom-call | flops 28750000128 | tf_op jit(solution)/shard_map/attend_backward/pallas_call | solution.py:432
  307.6 15.8 %weight_blocks.1 = (bf16[16,136,512]{2,1,0:T(8,128)(2,1)}, bf16[16,136,512]{2,1,0:T(8,128)(2,1)}, bf16[16,136,512]{2,1,0:T(8,128)(2,1)}, bf16[16,136,512]{2,1,0:T(8,128)(2,1)}) custom-call(s32[7]{0:T(128)} %stack.60.facts, bf16[384,1024]{1,0:T(8,128)(2,1)} %get-tuple-element.254.normed, bf16[768,1024]{1,0:T(8,128)(2,1)} %get-tuple-element.255.normed_others, ...), custom_call_target="tpu_custom_call" | custom-call | flops 19549999104 | tf_op jit(solution)/shard_map/weight_blocks/pallas_call | solution.py:1009
  352.0 11.8 %normed_grads.1 = (f32[256,1024]{1,0:T(8,128)}, f32[128,1024]{1,0:T(8,128)}, f32[768,1024]{1,0:T(8,128)}) custom-call(bf16[384,1024]{1,0:T(8,128)(2,1)} %get-tuple-element.265.grad_query.query, bf16[512,1024]{1,0:T(8,128)(2,1)} %get-tuple-element.266.grad_pair.pair, bf16[1536,1024]{1,0:T(8,128)(2,1)} %get-tuple-element.267.grad_others.others, ...), custom_call_target="tpu_custom_call" | custom-call | flops 14949999616 | tf_op jit(solution)/shard_map/normed_grads/pallas_call | solution.py:488
  364.1 6.4 %collective-permute-done.26 = bf16[4,136,512]{2,1,0:T(8,128)(2,1)} collective-permute-done((bf16[4,136,512]{2,1,0:T(8,128)(2,1)}, bf16[4,136,512]{2,1,0:T(8,128)(2,1)}, u32[]{:S(2)}, u32[]{:S(2)}) %collective-permute-start.26) | collective-permute-done | bytes 557088 | tf_op jit(solution)/shard_map/ppermute | solution.py:40
  394.6 5.8 %collective-permute-done.36 = bf16[136,512]{1,0:T(8,128)(2,1)S(1)} collective-permute-done((bf16[136,512]{1,0:T(8,128)(2,1)S(1)}, bf16[136,512]{1,0:T(8,128)(2,1)S(1)}, u32[]{:S(2)}, u32[]{:S(2)}) %collective-permute-start.36) | collective-permute-done | bytes 139296 | tf_op jit(solution)/shard_map/ppermute | solution.py:40
  403.3 5.1 %collective-permute-start.34 = (bf16[2,136,512]{2,1,0:T(8,128)(2,1)S(1)}, bf16[2,136,512]{2,1,0:T(8,128)(2,1)S(1)}, u32[]{:S(2)}, u32[]{:S(2)}) collective-permute-start(bf16[2,136,512]{2,1,0:T(8,128)(2,1)S(1)} %pad_maximum_fusion.9), channel_id=1, source_target_pairs={{0,8},{4,12},{8,0},{12,4},{16,24},{20,28},{24,16},{28,20},{1,9},{5... | collective-permute-start | bytes 835592 | tf_op jit(solution)/shard_map/ppermute | solution.py:40
  411.6 5.6 %collective-permute-done.34 = bf16[2,136,512]{2,1,0:T(8,128)(2,1)S(1)} collective-permute-done((bf16[2,136,512]{2,1,0:T(8,128)(2,1)S(1)}, bf16[2,136,512]{2,1,0:T(8,128)(2,1)S(1)}, u32[]{:S(2)}, u32[]{:S(2)}) %collective-permute-start.34) | collective-permute-done | bytes 278560 | tf_op jit(solution)/shard_map/ppermute | solution.py:40
  420.6 6.6 %weight_fill.1 = (f32[2,704,1024]{2,1,0:T(8,128)}, f32[2,704,1024]{2,1,0:T(8,128)}, f32[2,704,1024]{2,1,0:T(8,128)}) custom-call(s32[7]{0:T(128)} %stack.60.facts, bf16[3,704,1024]{2,1,0:T(8,128)(2,1)} %collective-permute-done.14.source, f32[2,704,1024]{2,1,0:T(8,128)} %get-tuple-element.239.refs_0_, ...), custom_call_target="tpu_custom_call", output_to_operand_aliasing={{0}: (2, {}), {1}: (3, {}), {2}: (4, {})} | custom-call | flops 7474999808 | tf_op jit(solution)/shard_map/weight_fill/pallas_call | solution.py:740
  434.8 5.5 %collective-permute-done.45 = bf16[2,136,512]{2,1,0:T(8,128)(2,1)S(1)} collective-permute-done((bf16[2,136,512]{2,1,0:T(8,128)(2,1)S(1)}, bf16[2,136,512]{2,1,0:T(8,128)(2,1)S(1)}, u32[]{:S(2)}, u32[]{:S(2)}) %collective-permute-start.45) | collective-permute-done | bytes 278560 | tf_op jit(solution)/shard_map/ppermute | solution.py:40
  445.4 10.9 %collective-permute-done.39 = bf16[4,136,512]{2,1,0:T(8,128)(2,1)S(1)} collective-permute-done((bf16[4,136,512]{2,1,0:T(8,128)(2,1)S(1)}, bf16[4,136,512]{2,1,0:T(8,128)(2,1)S(1)}, u32[]{:S(2)}, u32[]{:S(2)}) %collective-permute-start.39) | collective-permute-done | bytes 557088 | tf_op jit(solution)/shard_map/ppermute | solution.py:40
  460.0 7.9 %unpack_blocks.2 = (f32[1024,1024]{1,0:T(8,128)}, f32[1024,1024]{1,0:T(8,128)}, f32[1024,1024]{1,0:T(8,128)}, f32[1024,1024]{1,0:T(8,128)}, f32[24,1024]{1,0:T(8,128)}, /*index=5*/f32[1,1024]{1,0:T(1,128)}) custom-call(s32[7]{0:T(128)} %stack.60.facts, bf16[16,136,512]{2,1,0:T(8,128)(2,1)} %copy-done.17, bf16[16,136,512]{2,1,0:T(8,128)(2,1)} %copy-done.26, ...), custom_call_target="tpu_custom_call" | custom-call | flops 9200000000 | tf_op jit(solution)/shard_map/unpack_blocks/pallas_call | solution.py:1080
  473.8 8.1 %unpack_blocks.3 = (f32[1024,1024]{1,0:T(8,128)}, f32[1024,1024]{1,0:T(8,128)}, f32[1024,1024]{1,0:T(8,128)}, f32[1024,1024]{1,0:T(8,128)}, f32[24,1024]{1,0:T(8,128)}, /*index=5*/f32[1,1024]{1,0:T(1,128)}) custom-call(s32[7]{0:T(128)} %stack.60.facts, ...), custom_call_target="tpu_custom_call", output_to_operand_aliasing={{0}: (8, {}), {1}: (9, {}), {2}: (10, {}), {3}: (11, {}), {... | custom-call | flops 9200000000 | tf_op jit(solution)/shard_map/unpack_blocks/pallas_call | solution.py:1080
  (240 shorter events, 146.4 us)
Async XLA Ops:
  1.7 25.0 %collective-permute-start = (bf16[256,1024]{1,0:T(8,128)(2,1)S(1)}, bf16[256,1024]{1,0:T(8,128)(2,1)}, u32[]{:S(2)}, u32[]{:S(2)}) collective-permute-start(bf16[256,1024]{1,0:T(8,128)(2,1)S(1)} %slice.168), channel_id=1, source_target_pairs={{0,1},{1,0},{2,3},{3,2},{4,5},{5,4},{6,7},{7,6},{8,9},{9,8},{10,11... | collective-permute-start | bytes 1572872 | tf_op jit(solution)/shard_map/ppermute | solution.py:40
  4.7 24.7 %collective-permute-start.1 = (bf16[256,1024]{1,0:T(8,128)(2,1)S(1)}, bf16[256,1024]{1,0:T(8,128)(2,1)}, u32[]{:S(2)}, u32[]{:S(2)}) collective-permute-start(bf16[256,1024]{1,0:T(8,128)(2,1)S(1)} %slice.168), channel_id=1, source_target_pairs={{0,2},{1,3},{2,0},{3,1},{4,6},{5,7},{6,4},{7,5},{8,10},{9,11},{10,... | collective-permute-start | bytes 1572872 | tf_op jit(solution)/shard_map/ppermute | solution.py:40
  6.3 23.2 %collective-permute-start.2 = (bf16[256,1024]{1,0:T(8,128)(2,1)S(1)}, bf16[256,1024]{1,0:T(8,128)(2,1)}, u32[]{:S(2)}, u32[]{:S(2)}) collective-permute-start(bf16[256,1024]{1,0:T(8,128)(2,1)S(1)} %slice.168), channel_id=1, source_target_pairs={{0,3},{1,2},{2,1},{3,0},{4,7},{5,6},{6,5},{7,4},{8,11},{9,10},{10,... | collective-permute-start | bytes 1572872 | tf_op jit(solution)/shard_map/ppermute | solution.py:40
  10.8 54.5 %all-to-all-start.2 = ((bf16[8,128,1024]{2,1,0:T(8,128)(2,1)}), bf16[8,128,1024]{2,1,0:T(8,128)(2,1)S(1)}, u32[]{:S(2)}, u32[]{:S(2)}) async-start(bf16[8,128,1024]{2,1,0:T(8,128)(2,1)} %bitcast.74), calls=%async_computation.2 | async-start | bytes 4194304 | tf_op jit(solution)/shard_map/all_to_all | solution.py:99
  29.5 95.7 %collective-permute-start.9 = (bf16[3,704,1024]{2,1,0:T(8,128)(2,1)}, bf16[3,704,1024]{2,1,0:T(8,128)(2,1)}, u32[]{:S(2)}, u32[]{:S(2)}) collective-permute-start(bf16[3,704,1024]{2,1,0:T(8,128)(2,1)} %pick_weights.1), channel_id=1, source_target_pairs={{0,1},{1,0},{2,3},{3,2},{4,6},{5,7},{6,4},{7,5},{8,9},{9,8},{10,11... | collective-permute-start | bytes 12976136 | tf_op jit(solution)/shard_map/ppermute | solution.py:1165
  66.6 24.3 %collective-permute-start.3 = (bf16[512,1024]{1,0:T(8,128)(2,1)}, bf16[512,1024]{1,0:T(8,128)(2,1)S(1)}, u32[]{:S(2)}, u32[]{:S(2)}) collective-permute-start(bf16[512,1024]{1,0:T(8,128)(2,1)} %bitcast.19), channel_id=1, source_target_pairs={{0,1},{1,0},{2,3},{3,2},{4,6},{5,7},{6,4},{7,5},{8,9},{9,8},{10,11... | collective-permute-start | bytes 3145736 | tf_op jit(solution)/shard_map/ppermute | solution.py:1165
  68.0 30.3 %all-to-all-start = ((bf16[8,64,1024]{2,1,0:T(8,128)(2,1)}), bf16[8,64,1024]{2,1,0:T(8,128)(2,1)S(1)}, u32[]{:S(2)}, u32[]{:S(2)}) async-start(bf16[8,64,1024]{2,1,0:T(8,128)(2,1)} %bitcast.12), calls=%async_computation | async-start | bytes 2097152 | tf_op jit(solution)/shard_map/all_to_all | solution.py:99
  90.8 15.2 %collective-permute-start.4 = (bf16[512,1024]{1,0:T(8,128)(2,1)S(1)}, bf16[512,1024]{1,0:T(8,128)(2,1)}, u32[]{:S(2)}, u32[]{:S(2)}) collective-permute-start(bf16[512,1024]{1,0:T(8,128)(2,1)S(1)} %collective-permute-done.3.grads_in.refs_6_), channel_id=1, source_target_pairs={{0,2},{1,3},{2,0},{3,1},{4,5},{5,4},{6,7},{7,6},{8,10},{9,11},{10,... | collective-permute-start | bytes 3145736 | tf_op jit(solution)/shard_map/ppermute | solution.py:1165
  106.1 15.8 %collective-permute-start.5 = (bf16[512,1024]{1,0:T(8,128)(2,1)S(1)}, bf16[512,1024]{1,0:T(8,128)(2,1)}, u32[]{:S(2)}, u32[]{:S(2)}) collective-permute-start(bf16[512,1024]{1,0:T(8,128)(2,1)S(1)} %bitcast.86), channel_id=1, source_target_pairs={{0,1},{1,0},{2,3},{3,2},{4,6},{5,7},{6,4},{7,5},{8,9},{9,8},{10,11... | collective-permute-start | bytes 3145736 | tf_op jit(solution)/shard_map/ppermute | solution.py:1165
  107.0 34.8 %all-to-all-start.1 = ((bf16[8,64,1024]{2,1,0:T(8,128)(2,1)}), bf16[8,64,1024]{2,1,0:T(8,128)(2,1)S(1)}, u32[]{:S(2)}, u32[]{:S(2)}) async-start(bf16[8,64,1024]{2,1,0:T(8,128)(2,1)} %bitcast.14), calls=%async_computation.1 | async-start | bytes 2097152 | tf_op jit(solution)/shard_map/all_to_all | solution.py:99
  121.9 19.9 %collective-permute-start.6 = (bf16[512,1024]{1,0:T(8,128)(2,1)}, bf16[512,1024]{1,0:T(8,128)(2,1)S(1)}, u32[]{:S(2)}, u32[]{:S(2)}) collective-permute-start(bf16[512,1024]{1,0:T(8,128)(2,1)} %collective-permute-done.5.slots_in.refs_2_), channel_id=1, source_target_pairs={{0,2},{1,3},{2,0},{3,1},{4,5},{5,4},{6,7},{7,6},{8,10},{9,11},{10,... | collective-permute-start | bytes 3145736 | tf_op jit(solution)/shard_map/ppermute | solution.py:1165
  141.8 19.1 %collective-permute-start.7 = (bf16[512,1024]{1,0:T(8,128)(2,1)S(1)}, bf16[512,1024]{1,0:T(8,128)(2,1)S(1)}, u32[]{:S(2)}, u32[]{:S(2)}) collective-permute-start(bf16[512,1024]{1,0:T(8,128)(2,1)S(1)} %bitcast.81), channel_id=1, source_target_pairs={{0,2},{1,3},{2,0},{3,1},{4,5},{5,4},{6,7},{7,6},{8,10},{9,11},{10,... | collective-permute-start | bytes 3145736 | tf_op jit(solution)/shard_map/ppermute | solution.py:1165
  141.9 38.2 %collective-permute-start.8 = (bf16[512,1024]{1,0:T(8,128)(2,1)S(1)}, bf16[512,1024]{1,0:T(8,128)(2,1)}, u32[]{:S(2)}, u32[]{:S(2)}) collective-permute-start(bf16[512,1024]{1,0:T(8,128)(2,1)S(1)} %bitcast.87), channel_id=1, source_target_pairs={{0,2},{1,3},{2,0},{3,1},{4,5},{5,4},{6,7},{7,6},{8,10},{9,11},{10,... | collective-permute-start | bytes 3145736 | tf_op jit(solution)/shard_map/ppermute | solution.py:1165
  160.7 18.9 %collective-permute-start.10 = (bf16[512,1024]{1,0:T(8,128)(2,1)}, bf16[512,1024]{1,0:T(8,128)(2,1)S(1)}, u32[]{:S(2)}, u32[]{:S(2)}) collective-permute-start(bf16[512,1024]{1,0:T(8,128)(2,1)} %get-tuple-element.205), channel_id=1, source_target_pairs={{0,2},{1,3},{2,0},{3,1},{4,5},{5,4},{6,7},{7,6},{8,10},{9,11},{10,... | collective-permute-start | bytes 3145736 | tf_op jit(solution)/shard_map/ppermute | solution.py:1165
  180.0 17.0 %collective-permute-start.11 = (bf16[512,1024]{1,0:T(8,128)(2,1)S(1)}, bf16[512,1024]{1,0:T(8,128)(2,1)}, u32[]{:S(2)}, u32[]{:S(2)}) collective-permute-start(bf16[512,1024]{1,0:T(8,128)(2,1)S(1)} %add_convert_fusion.5), channel_id=1, source_target_pairs={{0,1},{1,0},{2,3},{3,2},{4,6},{5,7},{6,4},{7,5},{8,9},{9,8},{10,11... | collective-permute-start | bytes 3145736 | tf_op jit(solution)/shard_map/ppermute | solution.py:1165
  200.1 31.8 %collective-permute-start.15 = (bf16[512,1024]{1,0:T(8,128)(2,1)}, bf16[512,1024]{1,0:T(8,128)(2,1)S(1)}, u32[]{:S(2)}, u32[]{:S(2)}) collective-permute-start(bf16[512,1024]{1,0:T(8,128)(2,1)} %get-tuple-element.212), channel_id=1, source_target_pairs={{0,2},{1,3},{2,0},{3,1},{4,5},{5,4},{6,7},{7,6},{8,10},{9,11},{10,... | collective-permute-start | bytes 3145736 | tf_op jit(solution)/shard_map/ppermute | solution.py:1165
  201.7 35.5 %all-to-all-start.3 = ((bf16[8,64,1024]{2,1,0:T(8,128)(2,1)}), bf16[8,64,1024]{2,1,0:T(8,128)(2,1)}, u32[]{:S(2)}, u32[]{:S(2)}) async-start(bf16[8,64,1024]{2,1,0:T(8,128)(2,1)} %bitcast.28), calls=%async_computation.3 | async-start | bytes 2097152 | tf_op jit(solution)/shard_map/all_to_all | solution.py:99
  213.7 31.1 %collective-permute-start.13 = (bf16[512,1024]{1,0:T(8,128)(2,1)S(1)}, bf16[512,1024]{1,0:T(8,128)(2,1)}, u32[]{:S(2)}, u32[]{:S(2)}) collective-permute-start(bf16[512,1024]{1,0:T(8,128)(2,1)S(1)} %add_convert_fusion.4), channel_id=1, source_target_pairs={{0,1},{1,0},{2,3},{3,2},{4,6},{5,7},{6,4},{7,5},{8,9},{9,8},{10,11... | collective-permute-start | bytes 3145736 | tf_op jit(solution)/shard_map/ppermute | solution.py:1165
  233.2 27.8 %collective-permute-start.16 = (bf16[512,1024]{1,0:T(8,128)(2,1)}, bf16[512,1024]{1,0:T(8,128)(2,1)S(1)}, u32[]{:S(2)}, u32[]{:S(2)}) collective-permute-start(bf16[512,1024]{1,0:T(8,128)(2,1)} %get-tuple-element.213), channel_id=1, source_target_pairs={{0,2},{1,3},{2,0},{3,1},{4,5},{5,4},{6,7},{7,6},{8,10},{9,11},{10,... | collective-permute-start | bytes 3145736 | tf_op jit(solution)/shard_map/ppermute | solution.py:1165
  237.2 34.2 %all-to-all-start.4 = ((bf16[8,64,1024]{2,1,0:T(8,128)(2,1)}), bf16[8,64,1024]{2,1,0:T(8,128)(2,1)S(1)}, u32[]{:S(2)}, u32[]{:S(2)}) async-start(bf16[8,64,1024]{2,1,0:T(8,128)(2,1)} %bitcast.30), calls=%async_computation.4 | async-start | bytes 2097152 | tf_op jit(solution)/shard_map/all_to_all | solution.py:99
  244.8 62.8 %collective-permute-start.14 = (bf16[3,704,1024]{2,1,0:T(8,128)(2,1)}, bf16[3,704,1024]{2,1,0:T(8,128)(2,1)}, u32[]{:S(2)}, u32[]{:S(2)}) collective-permute-start(bf16[3,704,1024]{2,1,0:T(8,128)(2,1)} %weight_pass.2), channel_id=1, source_target_pairs={{0,1},{1,0},{2,3},{3,2},{4,6},{5,7},{6,4},{7,5},{8,9},{9,8},{10,11... | collective-permute-start | bytes 12976136 | tf_op jit(solution)/shard_map/ppermute | solution.py:1165
  271.4 64.4 %all-to-all-start.5 = ((bf16[8,128,1024]{2,1,0:T(8,128)(2,1)}), bf16[8,128,1024]{2,1,0:T(8,128)(2,1)}, u32[]{:S(2)}, u32[]{:S(2)}) async-start(bf16[8,128,1024]{2,1,0:T(8,128)(2,1)} %bitcast.32), calls=%async_computation.5 | async-start | bytes 4194304 | tf_op jit(solution)/shard_map/all_to_all | solution.py:99
  344.0 19.9 %collective-permute-start.22 = (bf16[4,136,512]{2,1,0:T(8,128)(2,1)S(1)}, bf16[4,136,512]{2,1,0:T(8,128)(2,1)S(1)}, u32[]{:S(2)}, u32[]{:S(2)}) collective-permute-start(bf16[4,136,512]{2,1,0:T(8,128)(2,1)S(1)} %pad_maximum_fusion.2), channel_id=1, source_target_pairs={{0,2},{1,3},{2,0},{3,1},{4,6},{5,7},{6,4},{7,5},{8,10},{9,11},{10,... | collective-permute-start | bytes 1671176 | tf_op jit(solution)/shard_map/ppermute | solution.py:40
  344.2 19.7 %collective-permute-start.20 = (bf16[4,136,512]{2,1,0:T(8,128)(2,1)S(1)}, bf16[4,136,512]{2,1,0:T(8,128)(2,1)S(1)}, u32[]{:S(2)}, u32[]{:S(2)}) collective-permute-start(bf16[4,136,512]{2,1,0:T(8,128)(2,1)S(1)} %pad_maximum_fusion.1), channel_id=1, source_target_pairs={{0,1},{1,0},{2,3},{3,2},{4,5},{5,4},{6,7},{7,6},{8,9},{9,8},{10,11... | collective-permute-start | bytes 1671176 | tf_op jit(solution)/shard_map/ppermute | solution.py:40
  349.7 20.8 %collective-permute-start.26 = (bf16[4,136,512]{2,1,0:T(8,128)(2,1)}, bf16[4,136,512]{2,1,0:T(8,128)(2,1)}, u32[]{:S(2)}, u32[]{:S(2)}) collective-permute-start(bf16[4,136,512]{2,1,0:T(8,128)(2,1)} %pad_maximum_fusion.4), channel_id=1, source_target_pairs={{0,2},{1,3},{2,0},{3,1},{4,6},{5,7},{6,4},{7,5},{8,10},{9,11},{10,... | collective-permute-start | bytes 1671176 | tf_op jit(solution)/shard_map/ppermute | solution.py:40
  350.7 21.0 %collective-permute-start.24 = (bf16[4,136,512]{2,1,0:T(8,128)(2,1)}, bf16[4,136,512]{2,1,0:T(8,128)(2,1)S(1)}, u32[]{:S(2)}, u32[]{:S(2)}) collective-permute-start(bf16[4,136,512]{2,1,0:T(8,128)(2,1)} %pad_maximum_fusion.3), channel_id=1, source_target_pairs={{0,1},{1,0},{2,3},{3,2},{4,5},{5,4},{6,7},{7,6},{8,9},{9,8},{10,11... | collective-permute-start | bytes 1671176 | tf_op jit(solution)/shard_map/ppermute | solution.py:40
  381.8 29.5 %collective-permute-start.30 = (bf16[256,1024]{1,0:T(8,128)(2,1)S(1)}, bf16[256,1024]{1,0:T(8,128)(2,1)S(1)}, u32[]{:S(2)}, u32[]{:S(2)}) collective-permute-start(bf16[256,1024]{1,0:T(8,128)(2,1)S(1)} %pad_maximum_fusion.8), channel_id=1, source_target_pairs={{0,2},{1,3},{2,0},{3,1},{4,6},{5,7},{6,4},{7,5},{8,10},{9,11},{10,... | collective-permute-start | bytes 1572872 | tf_op jit(solution)/shard_map/ppermute | solution.py:40
  383.0 28.3 %collective-permute-start.28 = (bf16[256,1024]{1,0:T(8,128)(2,1)S(1)}, bf16[256,1024]{1,0:T(8,128)(2,1)S(1)}, u32[]{:S(2)}, u32[]{:S(2)}) collective-permute-start(bf16[256,1024]{1,0:T(8,128)(2,1)S(1)} %pad_maximum_fusion.7), channel_id=1, source_target_pairs={{0,1},{1,0},{2,3},{3,2},{4,5},{5,4},{6,7},{7,6},{8,9},{9,8},{10,11... | collective-permute-start | bytes 1572872 | tf_op jit(solution)/shard_map/ppermute | solution.py:40
  411.2 18.7 %collective-permute-start.38 = (bf16[2,136,512]{2,1,0:T(8,128)(2,1)S(1)}, bf16[2,136,512]{2,1,0:T(8,128)(2,1)S(1)}, u32[]{:S(2)}, u32[]{:S(2)}) collective-permute-start(bf16[2,136,512]{2,1,0:T(8,128)(2,1)S(1)} %pad_maximum_fusion.10), channel_id=1, source_target_pairs={{0,8},{4,12},{8,0},{12,4},{16,24},{20,28},{24,16},{28,20},{1,9},{5... | collective-permute-start | bytes 835592 | tf_op jit(solution)/shard_map/ppermute | solution.py:40
  417.4 16.3 %collective-permute-start.43 = (bf16[4,136,512]{2,1,0:T(8,128)(2,1)S(1)}, bf16[4,136,512]{2,1,0:T(8,128)(2,1)S(1)}, u32[]{:S(2)}, u32[]{:S(2)}) collective-permute-start(bf16[4,136,512]{2,1,0:T(8,128)(2,1)S(1)} %pad_maximum_fusion.5), channel_id=1, source_target_pairs={{0,1},{1,0},{2,3},{3,2},{4,5},{5,4},{6,7},{7,6},{8,9},{9,8},{10,11... | collective-permute-start | bytes 1671176 | tf_op jit(solution)/shard_map/ppermute | solution.py:40
  440.9 17.7 %collective-permute-start.47 = (bf16[16,136,512]{2,1,0:T(8,128)(2,1)S(1)}, bf16[16,136,512]{2,1,0:T(8,128)(2,1)S(1)}, u32[]{:S(2)}, u32[]{:S(2)}) collective-permute-start(bf16[16,136,512]{2,1,0:T(8,128)(2,1)S(1)} %constant_dynamic-update-slice_fusion.near), channel_id=1, source_target_pairs={{0,4},{4,0},{8,12},{12,8},{16,20},{20,16},{24,28},{28,24},{1,5},{5... | collective-permute-start | bytes 6684680 | tf_op jit(solution)/shard_map/ppermute | solution.py:40
  441.8 16.2 %collective-permute-start.40 = (bf16[4,136,512]{2,1,0:T(8,128)(2,1)S(1)}, bf16[4,136,512]{2,1,0:T(8,128)(2,1)S(1)}, u32[]{:S(2)}, u32[]{:S(2)}) collective-permute-start(bf16[4,136,512]{2,1,0:T(8,128)(2,1)S(1)} %pad_maximum_fusion.6), channel_id=1, source_target_pairs={{0,2},{1,3},{2,0},{3,1},{4,6},{5,7},{6,4},{7,5},{8,10},{9,11},{10,... | collective-permute-start | bytes 1671176 | tf_op jit(solution)/shard_map/ppermute | solution.py:40
  (56 other events, 644.3 us)

commit v6 on v5

--- a/solution.py
+++ b/solution.py
@@ -1033,7 +1033,8 @@
 
 
 def unpack_kernel(facts, near, far, w_query, w_key, w_value, gain, gain_before, *refs):
-    query, key, value, proj, small, gain_grad = refs[-6:]
+    query, key, value, proj, top, router, gain_grad = refs[-7:]
+    count = router.shape[0]
     step = pl.program_id(0)
     number = facts[3]
     group = step ^ (number // 8)
@@ -1048,7 +1049,11 @@
 
                 @pl.when(group == 0)
                 def _():
-                    small[s * 8 : s * 8 + 8] = block[4 * share :]
+                    tail = block[4 * share :]
+                    if s == 0:
+                        top[...] = tail
+                    low, high = max(s * 8, 2), min(s * 8 + 8, 2 + count)
+                    router[low - 2 : high - 2] = tail[low - s * 8 : high - s * 8]
 
     @pl.when(step < 2)
     def _():
@@ -1070,7 +1075,7 @@
     gain_grad[...] = gain_before[...] + line / gain[...].astype(f32)
 
 
-def unpack_blocks(facts, near, far, w_query, w_key, w_value, gain, gain_before, before, half):
+def unpack_blocks(facts, near, far, w_query, w_key, w_value, gain, gain_before, before, half, count):
     width = w_query.shape[0]
     wide = width // 2
     rows = near.shape[1]
@@ -1092,10 +1097,10 @@
                 line,
             ]
             + [pl.BlockSpec(memory_space=pl.ANY)] * len(before),
-            out_specs=[block, block, block, block, pl.BlockSpec((24, wide), lambda i, f: (0, half)), line],
+            out_specs=[block] * 4 + [pl.BlockSpec((size, wide), lambda i, f: (0, half)) for size in (8, count)] + [line],
         ),
         out_shape=[jax.ShapeDtypeStruct((width, width), f32)] * 4
-        + [jax.ShapeDtypeStruct((24, width), f32), jax.ShapeDtypeStruct((1, width), f32)],
+        + [jax.ShapeDtypeStruct((size, width), f32) for size in (8, count, 1)],
         input_output_aliases={8 + i: i for i in range(len(before))},
         compiler_params=params(),
         cost_estimate=cost(8),
@@ -1325,14 +1330,14 @@
         by_x, by_y = in_plane(one, 0), in_plane(one, 1)
         half_x, half_y = after_all((by_x[:2], by_y[2:]), outputs, weight_grads, two)
         one = jnp.concatenate([one, by_x, by_y, in_plane(half_x, 1), in_plane(half_y, 0)], axis=0)
-        first = unpack(one, swap(one, "expert", 1), *weights, jnp.zeros((1, width), f32), (), 0)
+        first = unpack(one, swap(one, "expert", 1), *weights, jnp.zeros((1, width), f32), (), 0, experts)
         by_x, by_y = in_plane(two, 0), in_plane(two, 1)
-        rest = after_all((in_plane(by_x[:2], 1), in_plane(by_y[2:], 0)), first[5], inputs_grad)
+        rest = after_all((in_plane(by_x[:2], 1), in_plane(by_y[2:], 0)), first[6], inputs_grad)
         two = jnp.concatenate([two, by_x, by_y] + rest, axis=0)
-        second = unpack(two, swap(two, "expert", 1), *weights, first[5], first[:5], 1)
+        second = unpack(two, swap(two, "expert", 1), *weights, first[6], first[:6], 1, experts)
         query_grad, key_grad, value_grad, proj_grad = second[:4]
-        attn_gain_grad = second[5][0]
-        small = second[4]
+        attn_gain_grad = second[6][0]
+        small, router_sum = second[4], second[5]
     else:
         key_others = [slice(2 * r * long_local, (2 * r + 1) * long_local) for r in range(tensor_axis - 1)]
         value_others = [slice((2 * r + 1) * long_local, (2 * r + 2) * long_local) for r in range(tensor_axis - 1)]
@@ -1362,6 +1367,7 @@
             query_grad * w_query.astype(f32) + key_grad * w_key.astype(f32) + value_grad * w_value.astype(f32),
             axis=1,
         ) / attn_gain.astype(f32)
+        router_sum = small[2:]
     rel_grad = jnp.transpose(small[0, : heads * bucket_count].reshape(heads, bucket_count))
     return (
         outputs,
@@ -1373,7 +1379,7 @@
         proj_grad,
         rel_grad,
         small[1],
-        jnp.transpose(small[2 : 2 + experts]),
+        jnp.transpose(router_sum),
         jnp.swapaxes(weight_grads[0], 1, 2),
         jnp.swapaxes(weight_grads[1], 1, 2),
         weight_grads[2],

time: 495 us -> 494 us (level)
  no operation moved by 1% of the time
where the time goes in v6:
time: 494 us; the launch traced here: 485 us
  Pallas kernels  225 us (46%)
  waiting for transfers between devices  126 us (26%)
  starting transfers between devices  87.8 us (18%)
  other arithmetic  21.4 us (4%)
  local copies, waits for them, and re-layouts  13.3 us (3%)
  matrix products  8.16 us (2%)
    ppermute x35, waiting for transfers between devices, swap(): return lax.ppermute(rows, axis, [(i, i ^ mask) for i in range(count)])  69.7 us
    pallas_call x4, Pallas kernels, expert_pass(): pl.pallas_call(partial(expert_kernel, chunks, capacity, padded, lanes_use...  67.4 us
    ppermute x14, waiting for transfers between devices, trade(): return lax.ppermute(rows, ('expert', 'tensor'), pairs)  39.8 us
    ppermute x35, starting transfers between devices, swap(): return lax.ppermute(rows, axis, [(i, i ^ mask) for i in range(count)])  36.7 us
    all_to_all x6, starting transfers between devices, over_experts(): lax.all_to_all(blocks, 'expert', 0, 0, tiled=True).reshape(rows.shape)  35 us
    pallas_call x2, Pallas kernels, weight_pass(): pl.pallas_call(body, grid_spec=pltpu.PrefetchScalarGridSpec(num_scalar_pr...  31.9 us
    pallas_call x1, Pallas kernels, attend_backward(): pl.pallas_call(partial(backward_kernel, count, rows, dim), grid_spec=pltp...  24.5 us
    pallas_call x1, Pallas kernels, attend_forward(): pl.pallas_call(partial(forward_kernel, count, rows, dim), grid_spec=pltpu...  17.3 us
  transfers between devices with their start and end apart: 55, of which 29 were waited for; matrix products, arithmetic and copies ran while one was open for 7% of the time, Pallas kernels for 45%

profile of v6, /device:TPU:0, one launch (start us, length us, event | category | flops | bytes accessed | tf_op | source)
XLA Modules:
  0.0 485.0 jit_solution(13643316868713477075)
XLA Ops:
  10.8 5.5 %all-to-all-start.2 = ((bf16[8,128,1024]{2,1,0:T(8,128)(2,1)}), bf16[8,128,1024]{2,1,0:T(8,128)(2,1)S(1)}, u32[]{:S(2)}, u32[]{:S(2)}) async-start(bf16[8,128,1024]{2,1,0:T(8,128)(2,1)} %bitcast.73), calls=%async_computation.2 | async-start | bytes 4194304 | tf_op jit(solution)/shard_map/all_to_all | solution.py:99
  21.3 5.4 %pick_weights.1 = bf16[3,704,1024]{2,1,0:T(8,128)(2,1)} custom-call(s32[7]{0:T(128)} %stack.60.facts, bf16[2,704,1024]{2,1,0:T(8,128)(2,1)} %bitcast.95, bf16[2,704,1024]{2,1,0:T(8,128)(2,1)} %bitcast.100, bf16[2,704,1024]{2,1,0:T(8,128)(2,1)} %refs_2_.9), custom_call_target="tpu_custom_call" | custom-call | flops 5750000128 | tf_op jit(solution)/shard_map/pick_weights/pallas_call | solution.py:508
  30.7 10.6 %project.1 = (bf16[384,1024]{1,0:T(8,128)(2,1)}, bf16[768,1024]{1,0:T(8,128)(2,1)}, bf16[384,1024]{1,0:T(8,128)(2,1)}, bf16[512,1024]{1,0:T(8,128)(2,1)}, bf16[1...) custom-call(bf16[1,1024]{1,0:T(2,128)(2,1)} %reshape.125.gain, bf16[1024,1024]{1,0:T(8,128)(2,1)} %w_query.7, ...), custom_call_target="tpu_custom_call" | custom-call | flops 13799999488 | tf_op jit(solution)/shard_map/project/pallas_call | solution.py:165
  41.3 17.3 %attend_forward.1 = (bf16[384,1024]{1,0:T(8,128)(2,1)}, bf16[16,256,1024]{2,1,0:T(8,128)(2,1)}, bf16[16,128,128]{2,1,0:T(8,128)(2,1)}) custom-call(s32[7]{0:T(128)} %stack.60.facts, bf16[384,1024]{1,0:T(8,128)(2,1)} %get-tuple-element.157.query, bf16[512,1024]{1,0:T(8,128)(2,1)} %get-tuple-element.158.pair, bf16[1536,1024]{1,0:T(8,128)(2,1)} %get-tuple-element.159.others, ...), custom_call_target="tpu_custom_call" | custom-call | flops 19549999104 | tf_op jit(solution)/shard_map/attend_forward/pallas_call | solution.py:291
  58.6 6.4 %route_rows.1 = (f32[384,1024]{1,0:T(8,128)}, bf16[384,1024]{1,0:T(8,128)(2,1)}, f32[16,384]{1,0:T(8,128)}, f32[2,384]{1,0:T(2,128)}, bf16[512,1024]{1,0:T(8,128)(2,1)}, /*index=5*/bf16[512,1024]{1,0:T(8,128)(2,1)}) custom-call(bf16[384,1024]{1,0:T(8,128)(2,1)} %get-tuple-element.161.mixed, bf16[1024,1024]{1,0:T(8,128)(2,1)} %w_proj.3, ...), custom_call_target="tpu_custom_call" | custom-call | flops 7360000000 | tf_op jit(solution)/shard_map/route_rows/pallas_call | solution.py:847
  71.7 19.1 %collective-permute-done.3.grads_in.refs_6_ = bf16[512,1024]{1,0:T(8,128)(2,1)S(1)} collective-permute-done((bf16[512,1024]{1,0:T(8,128)(2,1)}, bf16[512,1024]{1,0:T(8,128)(2,1)S(1)}, u32[]{:S(2)}, u32[]{:S(2)}) %collective-permute-start.3) | collective-permute-done | bytes 1048608 | tf_op jit(solution)/shard_map/ppermute | solution.py:1170
  92.7 5.6 %all-to-all-done = bf16[8,64,1024]{2,1,0:T(8,128)(2,1)S(1)} async-done(((bf16[8,64,1024]{2,1,0:T(8,128)(2,1)}), bf16[8,64,1024]{2,1,0:T(8,128)(2,1)S(1)}, u32[]{:S(2)}, u32[]{:S(2)}) %all-to-all-start) | async-done | bytes 1048608 | tf_op jit(solution)/shard_map/all_to_all | solution.py:99
  98.3 7.7 %collective-permute-done.4.grads_in.refs_7_ = bf16[512,1024]{1,0:T(8,128)(2,1)} collective-permute-done((bf16[512,1024]{1,0:T(8,128)(2,1)S(1)}, bf16[512,1024]{1,0:T(8,128)(2,1)}, u32[]{:S(2)}, u32[]{:S(2)}) %collective-permute-start.4) | collective-permute-done | bytes 1048608 | tf_op jit(solution)/shard_map/ppermute | solution.py:1170
  107.0 5.0 %all-to-all-start.1 = ((bf16[8,64,1024]{2,1,0:T(8,128)(2,1)}), bf16[8,64,1024]{2,1,0:T(8,128)(2,1)S(1)}, u32[]{:S(2)}, u32[]{:S(2)}) async-start(bf16[8,64,1024]{2,1,0:T(8,128)(2,1)} %bitcast.14), calls=%async_computation.1 | async-start | bytes 2097152 | tf_op jit(solution)/shard_map/all_to_all | solution.py:99
  112.0 9.9 %collective-permute-done.5.slots_in.refs_2_ = bf16[512,1024]{1,0:T(8,128)(2,1)} collective-permute-done((bf16[512,1024]{1,0:T(8,128)(2,1)S(1)}, bf16[512,1024]{1,0:T(8,128)(2,1)}, u32[]{:S(2)}, u32[]{:S(2)}) %collective-permute-start.5) | collective-permute-done | bytes 1048608 | tf_op jit(solution)/shard_map/ppermute | solution.py:1170
  125.2 16.6 %expert_pass.4 = (bf16[512,704]{1,0:T(8,128)(2,1)}, bf16[512,704]{1,0:T(8,128)(2,1)}, bf16[512,704]{1,0:T(8,128)(2,1)}, bf16[512,704]{1,0:T(8,128)(2,1)}, bf16[5...) custom-call(s32[7]{0:T(128)} %stack.60.facts, ...), custom_call_target="tpu_custom_call" | custom-call | flops 17250000896 | tf_op jit(solution)/shard_map/expert_pass/pallas_call | solution.py:629
  143.9 16.8 %expert_pass.5 = (bf16[512,704]{1,0:T(8,128)(2,1)}, bf16[512,704]{1,0:T(8,128)(2,1)}, bf16[512,704]{1,0:T(8,128)(2,1)}, bf16[512,704]{1,0:T(8,128)(2,1)}, bf16[5...) custom-call(s32[7]{0:T(128)} %stack.60.facts, ...), custom_call_target="tpu_custom_call" | custom-call | flops 17250000896 | tf_op jit(solution)/shard_map/expert_pass/pallas_call | solution.py:629
  160.9 17.1 %expert_pass.6 = (bf16[512,704]{1,0:T(8,128)(2,1)}, bf16[512,704]{1,0:T(8,128)(2,1)}, bf16[512,704]{1,0:T(8,128)(2,1)}, bf16[512,704]{1,0:T(8,128)(2,1)}, bf16[5...) custom-call(s32[7]{0:T(128)} %stack.60.facts, ...), custom_call_target="tpu_custom_call" | custom-call | flops 17250000896 | tf_op jit(solution)/shard_map/expert_pass/pallas_call | solution.py:629
  180.1 16.9 %expert_pass.7 = (bf16[512,704]{1,0:T(8,128)(2,1)}, bf16[512,704]{1,0:T(8,128)(2,1)}, bf16[512,704]{1,0:T(8,128)(2,1)}, bf16[512,704]{1,0:T(8,128)(2,1)}, bf16[5...) custom-call(s32[7]{0:T(128)} %stack.60.facts, ...), custom_call_target="tpu_custom_call" | custom-call | flops 17250000896 | tf_op jit(solution)/shard_map/expert_pass/pallas_call | solution.py:629
  201.7 8.8 %all-to-all-start.3 = ((bf16[8,64,1024]{2,1,0:T(8,128)(2,1)}), bf16[8,64,1024]{2,1,0:T(8,128)(2,1)}, u32[]{:S(2)}, u32[]{:S(2)}) async-start(bf16[8,64,1024]{2,1,0:T(8,128)(2,1)} %bitcast.28), calls=%async_computation.3 | async-start | bytes 2097152 | tf_op jit(solution)/shard_map/all_to_all | solution.py:99
  215.6 16.2 %weight_pass.2 = bf16[3,704,1024]{2,1,0:T(8,128)(2,1)} custom-call(s32[7]{0:T(128)} %stack.60.facts, bf16[512,1024]{1,0:T(8,128)(2,1)} %bitcast.82, bf16[512,1024]{1,0:T(8,128)(2,1)} %copy-done.30, bf16[512,1024]{1,0:T(8,128)(2,1)} %collective-permute-done.5.slots_in.refs_2_, bf16[512,1024]{1,0:T(8,128)(2,1)} %copy-done.29, bf16[512,1024]{1,0:T(8,128)(2,1)} %bitcast.88, ...), custom_call_target="tpu_custom_call" | custom-call | flops 18400000000 | tf_op jit(solution)/shard_map/weight_pass/pallas_call | solution.py:711
  237.2 7.6 %all-to-all-start.4 = ((bf16[8,64,1024]{2,1,0:T(8,128)(2,1)}), bf16[8,64,1024]{2,1,0:T(8,128)(2,1)S(1)}, u32[]{:S(2)}, u32[]{:S(2)}) async-start(bf16[8,64,1024]{2,1,0:T(8,128)(2,1)} %bitcast.30), calls=%async_computation.4 | async-start | bytes 2097152 | tf_op jit(solution)/shard_map/all_to_all | solution.py:99
  245.4 15.6 %weight_pass.3 = (f32[2,704,1024]{2,1,0:T(8,128)}, f32[2,704,1024]{2,1,0:T(8,128)}, f32[2,704,1024]{2,1,0:T(8,128)}) custom-call(s32[7]{0:T(128)} %stack.60.facts, bf16[512,1024]{1,0:T(8,128)(2,1)} %bitcast.83, bf16[512,1024]{1,0:T(8,128)(2,1)} %copy-done.30, bf16[512,1024]{1,0:T(8,128)(2,1)} %collective-permute-done.5.slots_in.refs_2_, ...), custom_call_target="tpu_custom_call" | custom-call | flops 18400000000 | tf_op jit(solution)/shard_map/weight_pass/pallas_call | solution.py:711
  264.2 7.2 %all-to-all-done.4 = bf16[8,64,1024]{2,1,0:T(8,128)(2,1)S(1)} async-done(((bf16[8,64,1024]{2,1,0:T(8,128)(2,1)}), bf16[8,64,1024]{2,1,0:T(8,128)(2,1)S(1)}, u32[]{:S(2)}, u32[]{:S(2)}) %all-to-all-start.4) | async-done | bytes 1048608 | tf_op jit(solution)/shard_map/all_to_all | solution.py:99
  275.7 7.4 %merge_rows.1 = (f32[384,1024]{1,0:T(8,128)}, bf16[384,1024]{1,0:T(8,128)(2,1)}, f32[1,1024]{1,0:T(1,128)}, f32[16,1024]{1,0:T(8,128)}, bf16[384,1024]{1,0:T(8,128)(2,1)}) custom-call(bf16[384,1024]{1,0:T(8,128)(2,1)} %cotangent.1, f32[384,1024]{1,0:T(8,128)} %get-tuple-element.163.resid, f32[16,384]{1,0:T(8,128)} %get-tuple-element.246.probs, ...), custom_call_target="tpu_custom_call" | custom-call | flops 8510000128 | tf_op jit(solution)/shard_map/merge_rows/pallas_call | solution.py:923
  283.1 24.5 %attend_backward.1 = (bf16[384,1024]{1,0:T(8,128)(2,1)}, bf16[512,1024]{1,0:T(8,128)(2,1)}, bf16[1536,1024]{1,0:T(8,128)(2,1)}, bf16[256,1024]{1,0:T(8,128)(2,1)}, f32[8,2,32]{2,1,0:T(2,128)}) custom-call(s32[7]{0:T(128)} %stack.60.facts, bf16[384,1024]{1,0:T(8,128)(2,1)} %get-tuple-element.157.query, bf16[384,1024]{1,0:T(8,128)(2,1)} %get-tuple-element.249.grad, ...), custom_call_target="tpu_custom_call" | custom-call | flops 28750000128 | tf_op jit(solution)/shard_map/attend_backward/pallas_call | solution.py:432
  307.6 15.8 %weight_blocks.1 = (bf16[16,136,512]{2,1,0:T(8,128)(2,1)}, bf16[16,136,512]{2,1,0:T(8,128)(2,1)}, bf16[16,136,512]{2,1,0:T(8,128)(2,1)}, bf16[16,136,512]{2,1,0:T(8,128)(2,1)}) custom-call(s32[7]{0:T(128)} %stack.60.facts, bf16[384,1024]{1,0:T(8,128)(2,1)} %get-tuple-element.256.normed, bf16[768,1024]{1,0:T(8,128)(2,1)} %get-tuple-element.257.normed_others, ...), custom_call_target="tpu_custom_call" | custom-call | flops 19549999104 | tf_op jit(solution)/shard_map/weight_blocks/pallas_call | solution.py:1009
  352.0 11.8 %normed_grads.1 = (f32[256,1024]{1,0:T(8,128)}, f32[128,1024]{1,0:T(8,128)}, f32[768,1024]{1,0:T(8,128)}) custom-call(bf16[384,1024]{1,0:T(8,128)(2,1)} %get-tuple-element.267.grad_query.query, bf16[512,1024]{1,0:T(8,128)(2,1)} %get-tuple-element.268.grad_pair.pair, bf16[1536,1024]{1,0:T(8,128)(2,1)} %get-tuple-element.269.grad_others.others, ...), custom_call_target="tpu_custom_call" | custom-call | flops 14949999616 | tf_op jit(solution)/shard_map/normed_grads/pallas_call | solution.py:488
  364.1 6.4 %collective-permute-done.26 = bf16[4,136,512]{2,1,0:T(8,128)(2,1)} collective-permute-done((bf16[4,136,512]{2,1,0:T(8,128)(2,1)}, bf16[4,136,512]{2,1,0:T(8,128)(2,1)}, u32[]{:S(2)}, u32[]{:S(2)}) %collective-permute-start.26) | collective-permute-done | bytes 557088 | tf_op jit(solution)/shard_map/ppermute | solution.py:40
  394.6 5.8 %collective-permute-done.36 = bf16[136,512]{1,0:T(8,128)(2,1)S(1)} collective-permute-done((bf16[136,512]{1,0:T(8,128)(2,1)S(1)}, bf16[136,512]{1,0:T(8,128)(2,1)S(1)}, u32[]{:S(2)}, u32[]{:S(2)}) %collective-permute-start.36) | collective-permute-done | bytes 139296 | tf_op jit(solution)/shard_map/ppermute | solution.py:40
  403.3 5.1 %collective-permute-start.34 = (bf16[2,136,512]{2,1,0:T(8,128)(2,1)S(1)}, bf16[2,136,512]{2,1,0:T(8,128)(2,1)S(1)}, u32[]{:S(2)}, u32[]{:S(2)}) collective-permute-start(bf16[2,136,512]{2,1,0:T(8,128)(2,1)S(1)} %pad_maximum_fusion.9), channel_id=1, source_target_pairs={{0,8},{4,12},{8,0},{12,4},{16,24},{20,28},{24,16},{28,20},{1,9},{5... | collective-permute-start | bytes 835592 | tf_op jit(solution)/shard_map/ppermute | solution.py:40
  411.6 5.6 %collective-permute-done.34 = bf16[2,136,512]{2,1,0:T(8,128)(2,1)S(1)} collective-permute-done((bf16[2,136,512]{2,1,0:T(8,128)(2,1)S(1)}, bf16[2,136,512]{2,1,0:T(8,128)(2,1)S(1)}, u32[]{:S(2)}, u32[]{:S(2)}) %collective-permute-start.34) | collective-permute-done | bytes 278560 | tf_op jit(solution)/shard_map/ppermute | solution.py:40
  420.6 6.6 %weight_fill.1 = (f32[2,704,1024]{2,1,0:T(8,128)}, f32[2,704,1024]{2,1,0:T(8,128)}, f32[2,704,1024]{2,1,0:T(8,128)}) custom-call(s32[7]{0:T(128)} %stack.60.facts, bf16[3,704,1024]{2,1,0:T(8,128)(2,1)} %collective-permute-done.14.source, f32[2,704,1024]{2,1,0:T(8,128)} %get-tuple-element.241.refs_0_, ...), custom_call_target="tpu_custom_call", output_to_operand_aliasing={{0}: (2, {}), {1}: (3, {}), {2}: (4, {})} | custom-call | flops 7474999808 | tf_op jit(solution)/shard_map/weight_fill/pallas_call | solution.py:740
  434.8 5.5 %collective-permute-done.45 = bf16[2,136,512]{2,1,0:T(8,128)(2,1)S(1)} collective-permute-done((bf16[2,136,512]{2,1,0:T(8,128)(2,1)S(1)}, bf16[2,136,512]{2,1,0:T(8,128)(2,1)S(1)}, u32[]{:S(2)}, u32[]{:S(2)}) %collective-permute-start.45) | collective-permute-done | bytes 278560 | tf_op jit(solution)/shard_map/ppermute | solution.py:40
  445.4 10.9 %collective-permute-done.39 = bf16[4,136,512]{2,1,0:T(8,128)(2,1)S(1)} collective-permute-done((bf16[4,136,512]{2,1,0:T(8,128)(2,1)S(1)}, bf16[4,136,512]{2,1,0:T(8,128)(2,1)S(1)}, u32[]{:S(2)}, u32[]{:S(2)}) %collective-permute-start.39) | collective-permute-done | bytes 557088 | tf_op jit(solution)/shard_map/ppermute | solution.py:40
  460.0 7.9 %unpack_blocks.2 = (f32[1024,1024]{1,0:T(8,128)}, f32[1024,1024]{1,0:T(8,128)}, f32[1024,1024]{1,0:T(8,128)}, f32[1024,1024]{1,0:T(8,128)}, f32[8,1024]{1,0:T(8,...) custom-call(s32[7]{0:T(128)} %stack.60.facts, bf16[16,136,512]{2,1,0:T(8,128)(2,1)} %copy-done.17, ...), custom_call_target="tpu_custom_call" | custom-call | flops 9200000000 | tf_op jit(solution)/shard_map/unpack_blocks/pallas_call | solution.py:1085
  473.7 8.1 %unpack_blocks.3 = (f32[1024,1024]{1,0:T(8,128)}, f32[1024,1024]{1,0:T(8,128)}, f32[1024,1024]{1,0:T(8,128)}, f32[1024,1024]{1,0:T(8,128)}, f32[8,1024]{1,0:T(8,...) custom-call(s32[7]{0:T(128)} %stack.60.facts, ...), custom_call_target="tpu_custom_call", output_to_operand_aliasing={{0}: (8, {}), {1}: (9, {}), {2}: (10, {}), {3}: (11, {}), {... | custom-call | flops 9200000000 | tf_op jit(solution)/shard_map/unpack_blocks/pallas_call | solution.py:1085
  (239 shorter events, 144.9 us)
Async XLA Ops:
  1.7 25.0 %collective-permute-start = (bf16[256,1024]{1,0:T(8,128)(2,1)S(1)}, bf16[256,1024]{1,0:T(8,128)(2,1)}, u32[]{:S(2)}, u32[]{:S(2)}) collective-permute-start(bf16[256,1024]{1,0:T(8,128)(2,1)S(1)} %slice.165), channel_id=1, source_target_pairs={{0,1},{1,0},{2,3},{3,2},{4,5},{5,4},{6,7},{7,6},{8,9},{9,8},{10,11... | collective-permute-start | bytes 1572872 | tf_op jit(solution)/shard_map/ppermute | solution.py:40
  4.7 24.7 %collective-permute-start.1 = (bf16[256,1024]{1,0:T(8,128)(2,1)S(1)}, bf16[256,1024]{1,0:T(8,128)(2,1)}, u32[]{:S(2)}, u32[]{:S(2)}) collective-permute-start(bf16[256,1024]{1,0:T(8,128)(2,1)S(1)} %slice.165), channel_id=1, source_target_pairs={{0,2},{1,3},{2,0},{3,1},{4,6},{5,7},{6,4},{7,5},{8,10},{9,11},{10,... | collective-permute-start | bytes 1572872 | tf_op jit(solution)/shard_map/ppermute | solution.py:40
  6.3 23.2 %collective-permute-start.2 = (bf16[256,1024]{1,0:T(8,128)(2,1)S(1)}, bf16[256,1024]{1,0:T(8,128)(2,1)}, u32[]{:S(2)}, u32[]{:S(2)}) collective-permute-start(bf16[256,1024]{1,0:T(8,128)(2,1)S(1)} %slice.165), channel_id=1, source_target_pairs={{0,3},{1,2},{2,1},{3,0},{4,7},{5,6},{6,5},{7,4},{8,11},{9,10},{10,... | collective-permute-start | bytes 1572872 | tf_op jit(solution)/shard_map/ppermute | solution.py:40
  10.8 54.5 %all-to-all-start.2 = ((bf16[8,128,1024]{2,1,0:T(8,128)(2,1)}), bf16[8,128,1024]{2,1,0:T(8,128)(2,1)S(1)}, u32[]{:S(2)}, u32[]{:S(2)}) async-start(bf16[8,128,1024]{2,1,0:T(8,128)(2,1)} %bitcast.73), calls=%async_computation.2 | async-start | bytes 4194304 | tf_op jit(solution)/shard_map/all_to_all | solution.py:99
  29.5 95.7 %collective-permute-start.9 = (bf16[3,704,1024]{2,1,0:T(8,128)(2,1)}, bf16[3,704,1024]{2,1,0:T(8,128)(2,1)}, u32[]{:S(2)}, u32[]{:S(2)}) collective-permute-start(bf16[3,704,1024]{2,1,0:T(8,128)(2,1)} %pick_weights.1), channel_id=1, source_target_pairs={{0,1},{1,0},{2,3},{3,2},{4,6},{5,7},{6,4},{7,5},{8,9},{9,8},{10,11... | collective-permute-start | bytes 12976136 | tf_op jit(solution)/shard_map/ppermute | solution.py:1170
  66.6 24.3 %collective-permute-start.3 = (bf16[512,1024]{1,0:T(8,128)(2,1)}, bf16[512,1024]{1,0:T(8,128)(2,1)S(1)}, u32[]{:S(2)}, u32[]{:S(2)}) collective-permute-start(bf16[512,1024]{1,0:T(8,128)(2,1)} %bitcast.19), channel_id=1, source_target_pairs={{0,1},{1,0},{2,3},{3,2},{4,6},{5,7},{6,4},{7,5},{8,9},{9,8},{10,11... | collective-permute-start | bytes 3145736 | tf_op jit(solution)/shard_map/ppermute | solution.py:1170
  68.0 30.3 %all-to-all-start = ((bf16[8,64,1024]{2,1,0:T(8,128)(2,1)}), bf16[8,64,1024]{2,1,0:T(8,128)(2,1)S(1)}, u32[]{:S(2)}, u32[]{:S(2)}) async-start(bf16[8,64,1024]{2,1,0:T(8,128)(2,1)} %bitcast.12), calls=%async_computation | async-start | bytes 2097152 | tf_op jit(solution)/shard_map/all_to_all | solution.py:99
  90.8 15.2 %collective-permute-start.4 = (bf16[512,1024]{1,0:T(8,128)(2,1)S(1)}, bf16[512,1024]{1,0:T(8,128)(2,1)}, u32[]{:S(2)}, u32[]{:S(2)}) collective-permute-start(bf16[512,1024]{1,0:T(8,128)(2,1)S(1)} %collective-permute-done.3.grads_in.refs_6_), channel_id=1, source_target_pairs={{0,2},{1,3},{2,0},{3,1},{4,5},{5,4},{6,7},{7,6},{8,10},{9,11},{10,... | collective-permute-start | bytes 3145736 | tf_op jit(solution)/shard_map/ppermute | solution.py:1170
  106.1 15.8 %collective-permute-start.5 = (bf16[512,1024]{1,0:T(8,128)(2,1)S(1)}, bf16[512,1024]{1,0:T(8,128)(2,1)}, u32[]{:S(2)}, u32[]{:S(2)}) collective-permute-start(bf16[512,1024]{1,0:T(8,128)(2,1)S(1)} %bitcast.85), channel_id=1, source_target_pairs={{0,1},{1,0},{2,3},{3,2},{4,6},{5,7},{6,4},{7,5},{8,9},{9,8},{10,11... | collective-permute-start | bytes 3145736 | tf_op jit(solution)/shard_map/ppermute | solution.py:1170
  107.0 34.8 %all-to-all-start.1 = ((bf16[8,64,1024]{2,1,0:T(8,128)(2,1)}), bf16[8,64,1024]{2,1,0:T(8,128)(2,1)S(1)}, u32[]{:S(2)}, u32[]{:S(2)}) async-start(bf16[8,64,1024]{2,1,0:T(8,128)(2,1)} %bitcast.14), calls=%async_computation.1 | async-start | bytes 2097152 | tf_op jit(solution)/shard_map/all_to_all | solution.py:99
  121.9 19.9 %collective-permute-start.6 = (bf16[512,1024]{1,0:T(8,128)(2,1)}, bf16[512,1024]{1,0:T(8,128)(2,1)S(1)}, u32[]{:S(2)}, u32[]{:S(2)}) collective-permute-start(bf16[512,1024]{1,0:T(8,128)(2,1)} %collective-permute-done.5.slots_in.refs_2_), channel_id=1, source_target_pairs={{0,2},{1,3},{2,0},{3,1},{4,5},{5,4},{6,7},{7,6},{8,10},{9,11},{10,... | collective-permute-start | bytes 3145736 | tf_op jit(solution)/shard_map/ppermute | solution.py:1170
  141.8 19.1 %collective-permute-start.7 = (bf16[512,1024]{1,0:T(8,128)(2,1)S(1)}, bf16[512,1024]{1,0:T(8,128)(2,1)S(1)}, u32[]{:S(2)}, u32[]{:S(2)}) collective-permute-start(bf16[512,1024]{1,0:T(8,128)(2,1)S(1)} %bitcast.80), channel_id=1, source_target_pairs={{0,2},{1,3},{2,0},{3,1},{4,5},{5,4},{6,7},{7,6},{8,10},{9,11},{10,... | collective-permute-start | bytes 3145736 | tf_op jit(solution)/shard_map/ppermute | solution.py:1170
  141.9 38.2 %collective-permute-start.8 = (bf16[512,1024]{1,0:T(8,128)(2,1)S(1)}, bf16[512,1024]{1,0:T(8,128)(2,1)}, u32[]{:S(2)}, u32[]{:S(2)}) collective-permute-start(bf16[512,1024]{1,0:T(8,128)(2,1)S(1)} %bitcast.86), channel_id=1, source_target_pairs={{0,2},{1,3},{2,0},{3,1},{4,5},{5,4},{6,7},{7,6},{8,10},{9,11},{10,... | collective-permute-start | bytes 3145736 | tf_op jit(solution)/shard_map/ppermute | solution.py:1170
  160.7 18.9 %collective-permute-start.10 = (bf16[512,1024]{1,0:T(8,128)(2,1)}, bf16[512,1024]{1,0:T(8,128)(2,1)S(1)}, u32[]{:S(2)}, u32[]{:S(2)}) collective-permute-start(bf16[512,1024]{1,0:T(8,128)(2,1)} %get-tuple-element.207), channel_id=1, source_target_pairs={{0,2},{1,3},{2,0},{3,1},{4,5},{5,4},{6,7},{7,6},{8,10},{9,11},{10,... | collective-permute-start | bytes 3145736 | tf_op jit(solution)/shard_map/ppermute | solution.py:1170
  180.0 17.0 %collective-permute-start.11 = (bf16[512,1024]{1,0:T(8,128)(2,1)S(1)}, bf16[512,1024]{1,0:T(8,128)(2,1)}, u32[]{:S(2)}, u32[]{:S(2)}) collective-permute-start(bf16[512,1024]{1,0:T(8,128)(2,1)S(1)} %add_convert_fusion.5), channel_id=1, source_target_pairs={{0,1},{1,0},{2,3},{3,2},{4,6},{5,7},{6,4},{7,5},{8,9},{9,8},{10,11... | collective-permute-start | bytes 3145736 | tf_op jit(solution)/shard_map/ppermute | solution.py:1170
  200.1 31.8 %collective-permute-start.15 = (bf16[512,1024]{1,0:T(8,128)(2,1)}, bf16[512,1024]{1,0:T(8,128)(2,1)S(1)}, u32[]{:S(2)}, u32[]{:S(2)}) collective-permute-start(bf16[512,1024]{1,0:T(8,128)(2,1)} %get-tuple-element.214), channel_id=1, source_target_pairs={{0,2},{1,3},{2,0},{3,1},{4,5},{5,4},{6,7},{7,6},{8,10},{9,11},{10,... | collective-permute-start | bytes 3145736 | tf_op jit(solution)/shard_map/ppermute | solution.py:1170
  201.7 35.5 %all-to-all-start.3 = ((bf16[8,64,1024]{2,1,0:T(8,128)(2,1)}), bf16[8,64,1024]{2,1,0:T(8,128)(2,1)}, u32[]{:S(2)}, u32[]{:S(2)}) async-start(bf16[8,64,1024]{2,1,0:T(8,128)(2,1)} %bitcast.28), calls=%async_computation.3 | async-start | bytes 2097152 | tf_op jit(solution)/shard_map/all_to_all | solution.py:99
  213.7 31.1 %collective-permute-start.13 = (bf16[512,1024]{1,0:T(8,128)(2,1)S(1)}, bf16[512,1024]{1,0:T(8,128)(2,1)}, u32[]{:S(2)}, u32[]{:S(2)}) collective-permute-start(bf16[512,1024]{1,0:T(8,128)(2,1)S(1)} %add_convert_fusion.4), channel_id=1, source_target_pairs={{0,1},{1,0},{2,3},{3,2},{4,6},{5,7},{6,4},{7,5},{8,9},{9,8},{10,11... | collective-permute-start | bytes 3145736 | tf_op jit(solution)/shard_map/ppermute | solution.py:1170
  233.2 27.8 %collective-permute-start.16 = (bf16[512,1024]{1,0:T(8,128)(2,1)}, bf16[512,1024]{1,0:T(8,128)(2,1)S(1)}, u32[]{:S(2)}, u32[]{:S(2)}) collective-permute-start(bf16[512,1024]{1,0:T(8,128)(2,1)} %get-tuple-element.215), channel_id=1, source_target_pairs={{0,2},{1,3},{2,0},{3,1},{4,5},{5,4},{6,7},{7,6},{8,10},{9,11},{10,... | collective-permute-start | bytes 3145736 | tf_op jit(solution)/shard_map/ppermute | solution.py:1170
  237.2 34.2 %all-to-all-start.4 = ((bf16[8,64,1024]{2,1,0:T(8,128)(2,1)}), bf16[8,64,1024]{2,1,0:T(8,128)(2,1)S(1)}, u32[]{:S(2)}, u32[]{:S(2)}) async-start(bf16[8,64,1024]{2,1,0:T(8,128)(2,1)} %bitcast.30), calls=%async_computation.4 | async-start | bytes 2097152 | tf_op jit(solution)/shard_map/all_to_all | solution.py:99
  244.8 62.8 %collective-permute-start.14 = (bf16[3,704,1024]{2,1,0:T(8,128)(2,1)}, bf16[3,704,1024]{2,1,0:T(8,128)(2,1)}, u32[]{:S(2)}, u32[]{:S(2)}) collective-permute-start(bf16[3,704,1024]{2,1,0:T(8,128)(2,1)} %weight_pass.2), channel_id=1, source_target_pairs={{0,1},{1,0},{2,3},{3,2},{4,6},{5,7},{6,4},{7,5},{8,9},{9,8},{10,11... | collective-permute-start | bytes 12976136 | tf_op jit(solution)/shard_map/ppermute | solution.py:1170
  271.4 64.4 %all-to-all-start.5 = ((bf16[8,128,1024]{2,1,0:T(8,128)(2,1)}), bf16[8,128,1024]{2,1,0:T(8,128)(2,1)}, u32[]{:S(2)}, u32[]{:S(2)}) async-start(bf16[8,128,1024]{2,1,0:T(8,128)(2,1)} %bitcast.32), calls=%async_computation.5 | async-start | bytes 4194304 | tf_op jit(solution)/shard_map/all_to_all | solution.py:99
  344.0 19.9 %collective-permute-start.22 = (bf16[4,136,512]{2,1,0:T(8,128)(2,1)S(1)}, bf16[4,136,512]{2,1,0:T(8,128)(2,1)S(1)}, u32[]{:S(2)}, u32[]{:S(2)}) collective-permute-start(bf16[4,136,512]{2,1,0:T(8,128)(2,1)S(1)} %pad_maximum_fusion.2), channel_id=1, source_target_pairs={{0,2},{1,3},{2,0},{3,1},{4,6},{5,7},{6,4},{7,5},{8,10},{9,11},{10,... | collective-permute-start | bytes 1671176 | tf_op jit(solution)/shard_map/ppermute | solution.py:40
  344.2 19.7 %collective-permute-start.20 = (bf16[4,136,512]{2,1,0:T(8,128)(2,1)S(1)}, bf16[4,136,512]{2,1,0:T(8,128)(2,1)S(1)}, u32[]{:S(2)}, u32[]{:S(2)}) collective-permute-start(bf16[4,136,512]{2,1,0:T(8,128)(2,1)S(1)} %pad_maximum_fusion.1), channel_id=1, source_target_pairs={{0,1},{1,0},{2,3},{3,2},{4,5},{5,4},{6,7},{7,6},{8,9},{9,8},{10,11... | collective-permute-start | bytes 1671176 | tf_op jit(solution)/shard_map/ppermute | solution.py:40
  349.7 20.8 %collective-permute-start.26 = (bf16[4,136,512]{2,1,0:T(8,128)(2,1)}, bf16[4,136,512]{2,1,0:T(8,128)(2,1)}, u32[]{:S(2)}, u32[]{:S(2)}) collective-permute-start(bf16[4,136,512]{2,1,0:T(8,128)(2,1)} %pad_maximum_fusion.4), channel_id=1, source_target_pairs={{0,2},{1,3},{2,0},{3,1},{4,6},{5,7},{6,4},{7,5},{8,10},{9,11},{10,... | collective-permute-start | bytes 1671176 | tf_op jit(solution)/shard_map/ppermute | solution.py:40
  350.7 21.0 %collective-permute-start.24 = (bf16[4,136,512]{2,1,0:T(8,128)(2,1)}, bf16[4,136,512]{2,1,0:T(8,128)(2,1)S(1)}, u32[]{:S(2)}, u32[]{:S(2)}) collective-permute-start(bf16[4,136,512]{2,1,0:T(8,128)(2,1)} %pad_maximum_fusion.3), channel_id=1, source_target_pairs={{0,1},{1,0},{2,3},{3,2},{4,5},{5,4},{6,7},{7,6},{8,9},{9,8},{10,11... | collective-permute-start | bytes 1671176 | tf_op jit(solution)/shard_map/ppermute | solution.py:40
  381.8 29.5 %collective-permute-start.30 = (bf16[256,1024]{1,0:T(8,128)(2,1)S(1)}, bf16[256,1024]{1,0:T(8,128)(2,1)S(1)}, u32[]{:S(2)}, u32[]{:S(2)}) collective-permute-start(bf16[256,1024]{1,0:T(8,128)(2,1)S(1)} %pad_maximum_fusion.8), channel_id=1, source_target_pairs={{0,2},{1,3},{2,0},{3,1},{4,6},{5,7},{6,4},{7,5},{8,10},{9,11},{10,... | collective-permute-start | bytes 1572872 | tf_op jit(solution)/shard_map/ppermute | solution.py:40
  383.0 28.3 %collective-permute-start.28 = (bf16[256,1024]{1,0:T(8,128)(2,1)S(1)}, bf16[256,1024]{1,0:T(8,128)(2,1)S(1)}, u32[]{:S(2)}, u32[]{:S(2)}) collective-permute-start(bf16[256,1024]{1,0:T(8,128)(2,1)S(1)} %pad_maximum_fusion.7), channel_id=1, source_target_pairs={{0,1},{1,0},{2,3},{3,2},{4,5},{5,4},{6,7},{7,6},{8,9},{9,8},{10,11... | collective-permute-start | bytes 1572872 | tf_op jit(solution)/shard_map/ppermute | solution.py:40
  411.2 18.7 %collective-permute-start.38 = (bf16[2,136,512]{2,1,0:T(8,128)(2,1)S(1)}, bf16[2,136,512]{2,1,0:T(8,128)(2,1)S(1)}, u32[]{:S(2)}, u32[]{:S(2)}) collective-permute-start(bf16[2,136,512]{2,1,0:T(8,128)(2,1)S(1)} %pad_maximum_fusion.10), channel_id=1, source_target_pairs={{0,8},{4,12},{8,0},{12,4},{16,24},{20,28},{24,16},{28,20},{1,9},{5... | collective-permute-start | bytes 835592 | tf_op jit(solution)/shard_map/ppermute | solution.py:40
  417.4 16.3 %collective-permute-start.43 = (bf16[4,136,512]{2,1,0:T(8,128)(2,1)S(1)}, bf16[4,136,512]{2,1,0:T(8,128)(2,1)S(1)}, u32[]{:S(2)}, u32[]{:S(2)}) collective-permute-start(bf16[4,136,512]{2,1,0:T(8,128)(2,1)S(1)} %pad_maximum_fusion.5), channel_id=1, source_target_pairs={{0,1},{1,0},{2,3},{3,2},{4,5},{5,4},{6,7},{7,6},{8,9},{9,8},{10,11... | collective-permute-start | bytes 1671176 | tf_op jit(solution)/shard_map/ppermute | solution.py:40
  440.9 17.7 %collective-permute-start.47 = (bf16[16,136,512]{2,1,0:T(8,128)(2,1)S(1)}, bf16[16,136,512]{2,1,0:T(8,128)(2,1)S(1)}, u32[]{:S(2)}, u32[]{:S(2)}) collective-permute-start(bf16[16,136,512]{2,1,0:T(8,128)(2,1)S(1)} %constant_dynamic-update-slice_fusion.near), channel_id=1, source_target_pairs={{0,4},{4,0},{8,12},{12,8},{16,20},{20,16},{24,28},{28,24},{1,5},{5... | collective-permute-start | bytes 6684680 | tf_op jit(solution)/shard_map/ppermute | solution.py:40
  441.8 16.2 %collective-permute-start.40 = (bf16[4,136,512]{2,1,0:T(8,128)(2,1)S(1)}, bf16[4,136,512]{2,1,0:T(8,128)(2,1)S(1)}, u32[]{:S(2)}, u32[]{:S(2)}) collective-permute-start(bf16[4,136,512]{2,1,0:T(8,128)(2,1)S(1)} %pad_maximum_fusion.6), channel_id=1, source_target_pairs={{0,2},{1,3},{2,0},{3,1},{4,6},{5,7},{6,4},{7,5},{8,10},{9,11},{10,... | collective-permute-start | bytes 1671176 | tf_op jit(solution)/shard_map/ppermute | solution.py:40
  (56 other events, 642.7 us)
